TPU v7x, 128 devices: a whole 4x4x4 slice. The times are simulated.
128 devices in a mesh: dp: 16 (over z_hi, y, core), mp: 8 (over z_lo, x).
Axes of the slice: x: 4, y: 4, z: 4 (z_hi: 2, z_lo: 2; z = z_hi * 2 + z_lo), core: 2. Of those that a mesh axis runs over, the one named last changes fastest.
Arguments:
- patches: bfloat16 [8192, 6144], P('dp'), may hold values from -6 to 6
- norm_gain: float32 [6144], replicated, may hold values from 0.1 to 1.9
- qkv_weight: bfloat16 [6144, 24, 384], P('dp', 'mp'), may hold values from -0.078125 to 0.078125
- qk_gain: float32 [2, 24, 128], P(None, 'mp'), may hold values from 0.1 to 24, as said below
- out_weight: bfloat16 [6144, 3072], P('dp', 'mp'), may hold values from -0.109375 to 0.109375
- final_gain: float32 [6144], replicated, may hold values from 0.1 to 1.9
- proj_weight: bfloat16 [6144, 4096], P('dp', 'mp'), may hold values from -0.078125 to 0.078125
- text_embed: bfloat16 [16, 1024, 4096], P('dp', 'mp'), may hold values from -6 to 6
- slot_offset: int32 [32], P('dp'), may hold values from 0 to 768, as said below
- text_len: int32 [16], P('dp'), may hold values from 0 to 512
Outputs:
- block_out: bfloat16 [8192, 6144], P('dp', 'mp')
- sequence: bfloat16 [16, 1024, 4096], P('dp', 'mp')
Inputs may be any that keep to these rules, and one draw needn't show every extreme that they name: `slot_offset`: images 2r and 2r + 1 lie in packed row r; every offset is a multiple of half of 256; image 2r + 1 starts at or after the end of image 2r, and both end inside the row. `qk_gain`: positive gains.
All inputs are finite; a program needn't handle non-finite values.
Results may differ from a plain program's by a relative error of at most 0.015.
The roundings to bfloat16 on the way count: a program that leaves them out, or rounds other values in their place, can miss the bound.
Values may be sent and summed in bfloat16 or wider, within the bound.
No kernel may reach another device: no remote copies, remote signals or barrier semaphores. Data moves between devices by JAX's collectives and lax.ppermute only.
A program may use at most 128 MiB of HBM per device.

v0:
```python
import functools
import math

import jax
import jax.numpy as jnp
import numpy as np
from jax import lax
from jax.experimental import pallas as pl
from jax.experimental.pallas import tpu as pltpu
from jax.sharding import PartitionSpec as P

PATCHES = 256
HALF = 128
AXES = ("dp", "mp")
VMEM = 40 * 1024 * 1024
epsilon = 1e-06


def coordinates():
    return [
        (zh, y, c, zl, x)
        for zh in range(2)
        for y in range(4)
        for c in range(2)
        for zl in range(2)
        for x in range(4)
    ]


def device_index(zh, y, c, zl, x):
    return ((zh * 4 + y) * 2 + c) * 8 + zl * 4 + x


def move(values, target):
    pairs = [(device_index(*at), device_index(*target(*at))) for at in coordinates()]
    return lax.ppermute(values, AXES, pairs)


def swap_core(values):
    return move(values, lambda zh, y, c, zl, x: (zh, y, 1 - c, zl, x))


def swap_zh(values):
    return move(values, lambda zh, y, c, zl, x: (1 - zh, y, c, zl, x))


def swap_zl(values):
    return move(values, lambda zh, y, c, zl, x: (zh, y, c, 1 - zl, x))


def spread_y(values):
    return move(values, lambda zh, y, c, zl, x: (zh, (y + 1 - 2 * c) % 4, c, zl, x))


def shift_x(values, step):
    return move(values, lambda zh, y, c, zl, x: (zh, y, c, zl, (x + step) % 4))


def transpose_mesh(values):
    return move(values, lambda zh, y, c, zl, x: (zl, x, c, zh, y))


def per_device(order):
    table = np.zeros((16, 16), np.int32)
    for zh in range(2):
        for y in range(4):
            for c in range(2):
                met = order(zh, y, c, 2 * c - 1)
                table[zh * 8 + y * 2 + c] = [r % 2 * 8 + yy % 4 * 2 + cc % 2 for r, yy, cc in met]
    return table


def early_order(zh, y, c, step):
    order = []
    for row in (zh, zh + 1):
        order += [(row, y, c), (row, y, c + 1)]
    for row in (zh, zh + 1):
        order += [(row, y + step, c), (row, y + step, c + 1)]
        order += [(row, y - step, c + 1), (row, y - step, c)]
    for row in (zh, zh + 1):
        order += [(row, y + 2, c), (row, y + 2, c + 1)]
    return order


def late_order(zh, y, c, step):
    order = []
    for yy, cores in (
        (y, (c, c + 1)),
        (y + step, (c, c + 1)),
        (y - step, (c + 1, c)),
        (y + 2, (c, c + 1)),
    ):
        for core in cores:
            order += [(zh, yy, core), (zh + 1, yy, core)]
    return order


NEAR = [(0, 0), (1, 0), (0, 1), (0, 3), (1, 1), (1, 3), (0, 2), (1, 2)]


def place_tables():
    met = per_device(late_order)
    groups = np.zeros((8, 8), np.int32)
    shards = np.zeros((16, 8, 16), np.int32)
    for mp in range(8):
        for r, (dz, dx) in enumerate(NEAR):
            group = (mp // 4 ^ dz) * 4 + (mp + dx) % 4
            groups[mp, r] = group
            for dp in range(16):
                for half in range(2):
                    shards[dp, mp, 2 * r + half] = np.argmax(met[dp] == 2 * group + half)
    return groups, shards


def norm_kernel(values_ref, gain_ref, out_ref):
    values = values_ref[...].astype(jnp.float32)
    width = values.shape[1]
    row_mean = jnp.sum(values, -1, keepdims=True) / width
    squares = jnp.sum(values * values, -1, keepdims=True) / width
    scale = lax.rsqrt(squares - row_mean * row_mean + epsilon)
    normed = ((values - row_mean) * scale * gain_ref[...]).astype(jnp.bfloat16)
    depth = out_ref.shape[2]
    for k in range(out_ref.shape[0]):
        out_ref[k] = normed[:, k * depth : (k + 1) * depth]


def norm_columns(values, gain, chunks):
    rows, width = values.shape
    block = 64
    return pl.pallas_call(
        norm_kernel,
        grid=(rows // block,),
        in_specs=[
            pl.BlockSpec((block, width), lambda i: (i, 0)),
            pl.BlockSpec((1, width), lambda i: (0, 0)),
        ],
        out_specs=pl.BlockSpec((chunks, block, width // chunks), lambda i: (0, i, 0)),
        out_shape=jax.ShapeDtypeStruct((chunks, rows, width // chunks), jnp.bfloat16),
        compiler_params=pltpu.CompilerParams(vmem_limit_bytes=VMEM),
        cost_estimate=pl.CostEstimate(
            flops=8 * rows * width, bytes_accessed=4 * rows * width, transcendentals=rows
        ),
        name="norm_columns",
    )(values, gain.reshape(1, width))


def row_norm(values, gain):
    row_mean = jnp.mean(values, -1, keepdims=True)
    squares = jnp.mean(values * values, -1, keepdims=True)
    return (values - row_mean) * lax.rsqrt(squares - row_mean * row_mean + epsilon) * gain


def accumulate_kernel(shard_counts, has_total, attend, index_ref, *refs):
    del index_ref
    count = sum(shard_counts)
    columns, refs = refs[:count], refs[count:]
    shards, refs = refs[: len(shard_counts)], refs[len(shard_counts) :]
    total = None
    if has_total:
        total, refs = refs[0][0], refs[1:]
    at = 0
    for held, number in zip(shards, shard_counts):
        for k in range(number):
            term = jnp.dot(columns[at][0], held[k, 0], preferred_element_type=jnp.float32)
            total = term if total is None else total + term
            at += 1
    if not attend:
        refs[0][0] = total
        return
    gain_ref, out_ref = refs
    size = gain_ref.shape[2]
    gains = gain_ref[0]
    query = row_norm(total[:, :size], gains[0:1]).astype(jnp.bfloat16)
    key = row_norm(total[:, size : 2 * size], gains[1:2]).astype(jnp.bfloat16)
    value = total[:, 2 * size :].astype(jnp.bfloat16)
    for image in range(total.shape[0] // PATCHES):
        rows = slice(image * PATCHES, (image + 1) * PATCHES)
        scores = lax.dot_general(
            query[rows], key[rows], (((1,), (1,)), ((), ())), preferred_element_type=jnp.float32
        ) / math.sqrt(size)
        raised = jnp.exp(scores - jnp.max(scores, -1, keepdims=True))
        weights = (raised / jnp.sum(raised, -1, keepdims=True)).astype(jnp.bfloat16)
        out_ref[rows, :] = jnp.dot(
            weights, value[rows], preferred_element_type=jnp.float32
        ).astype(jnp.bfloat16)


def accumulate(columns, shards, index, total=None, gains=None):
    shards = [held if held.ndim == 4 else held[None] for held in shards]
    counts = tuple(held.shape[0] for held in shards)
    _, rows, depth = columns.shape
    heads, wide = shards[0].shape[1], shards[0].shape[3]
    in_specs = [
        pl.BlockSpec((1, rows, depth), functools.partial(lambda k, h, index: (index[k], 0, 0), k))
        for k in range(sum(counts))
    ]
    in_specs += [
        pl.BlockSpec((number, 1, depth, wide), lambda h, index: (0, h, 0, 0)) for number in counts
    ]
    operands = [columns] * sum(counts) + shards
    total_spec = pl.BlockSpec((1, rows, wide), lambda h, index: (h, 0, 0))
    if total is not None:
        in_specs.append(total_spec)
        operands.append(total)
    aliases = {}
    if gains is None:
        out_spec = total_spec
        out_shape = jax.ShapeDtypeStruct((heads, rows, wide), jnp.float32)
        if total is not None:
            aliases = {len(operands): 0}
    else:
        in_specs.append(pl.BlockSpec((1, 2, wide // 3), lambda h, index: (h, 0, 0)))
        operands.append(gains)
        out_spec = pl.BlockSpec((rows, wide // 3), lambda h, index: (0, h))
        out_shape = jax.ShapeDtypeStruct((rows, heads * wide // 3), jnp.bfloat16)
    flops = 2 * sum(counts) * rows * depth * wide * heads
    return pl.pallas_call(
        functools.partial(accumulate_kernel, counts, total is not None, gains is not None),
        grid_spec=pltpu.PrefetchScalarGridSpec(
            num_scalar_prefetch=1, grid=(heads,), in_specs=in_specs, out_specs=out_spec
        ),
        out_shape=out_shape,
        input_output_aliases=aliases,
        compiler_params=pltpu.CompilerParams(vmem_limit_bytes=VMEM),
        cost_estimate=pl.CostEstimate(
            flops=flops,
            bytes_accessed=2 * sum(counts) * (rows + heads * wide) * depth,
            transcendentals=0,
        ),
        name="accumulate",
    )(index, *operands)


def out_kernel(split, has_total, finish, index_ref, *refs):
    del index_ref
    near, refs = refs[: sum(split)], refs[sum(split) :]
    shards, refs = refs[: 2 * len(split)], refs[2 * len(split) :]
    total = [refs[0][0], refs[0][1]] if has_total else [None, None]
    refs = refs[1:] if has_total else refs
    at = 0
    for piece, number in enumerate(split):
        values = near[at][...]
        if number == 2:
            values = jnp.concatenate([values, near[at + 1][...]], 0)
        at += number
        for half in range(2):
            term = lax.dot_general(
                values,
                shards[2 * piece + half][0],
                (((1,), (1,)), ((), ())),
                preferred_element_type=jnp.float32,
            )
            term = term.astype(jnp.bfloat16).astype(jnp.float32)
            total[half] = term if total[half] is None else total[half] + term
    if not finish:
        refs[0][0] = total[0]
        refs[0][1] = total[1]
        return
    patches_ref, block_ref, stats_ref = refs
    depth = total[0].shape[1]
    rows = total[0].shape[0]
    sums, squares = 0.0, 0.0
    for half in range(2):
        cols = slice(half * depth, (half + 1) * depth)
        block = (patches_ref[:, cols].astype(jnp.float32) + total[half]).astype(jnp.bfloat16)
        block_ref[:, cols] = block
        block = block.astype(jnp.float32)
        sums += jnp.sum(block, 1, keepdims=True)
        squares += jnp.sum(block * block, 1, keepdims=True)
    lane = lax.broadcasted_iota(jnp.int32, (rows, 128), 1)
    both = jnp.where(lane == 0, sums, squares)
    stats_ref[...] = both.T[:8]


def out_project(near, shards, index, total=None, patches=None):
    split = tuple(len(piece) for piece in near)
    pieces = [part for piece in near for part in piece]
    rows, depth = near[0][0].shape
    whole = lambda shape: pl.BlockSpec(shape, lambda i, index: (0,) * len(shape))
    in_specs = [whole(part.shape) for part in pieces]
    in_specs += [
        pl.BlockSpec(
            (1, depth, depth), functools.partial(lambda k, i, index: (index[k], 0, 0), k)
        )
        for k in range(2 * len(near))
    ]
    operands = pieces + [shards] * (2 * len(near))
    if total is not None:
        in_specs.append(whole(total.shape))
        operands.append(total)
    if patches is None:
        out_shape = jax.ShapeDtypeStruct((2, rows, depth), jnp.float32)
        out_specs = whole(out_shape.shape)
    else:
        in_specs.append(
            pl.BlockSpec((rows, 2 * depth), lambda i, index: (0, index[2 * len(near)]))
        )
        operands.append(patches)
        out_shape = [
            jax.ShapeDtypeStruct((rows, 2 * depth), jnp.bfloat16),
            jax.ShapeDtypeStruct((8, rows), jnp.float32),
        ]
        out_specs = [whole(out.shape) for out in out_shape]
    return pl.pallas_call(
        functools.partial(out_kernel, split, total is not None, patches is not None),
        grid_spec=pltpu.PrefetchScalarGridSpec(
            num_scalar_prefetch=1, grid=(1,), in_specs=in_specs, out_specs=out_specs
        ),
        out_shape=out_shape,
        compiler_params=pltpu.CompilerParams(vmem_limit_bytes=VMEM),
        cost_estimate=pl.CostEstimate(
            flops=4 * len(near) * rows * depth * depth,
            bytes_accessed=4 * len(near) * (rows + depth) * depth,
            transcendentals=0,
        ),
        name="out_project",
    )(index, *operands)


def project_kernel(split, has_total, finish, width, index_ref, *refs):
    near, refs = refs[: sum(split)], refs[sum(split) :]
    stats_ref, refs = refs[0], refs[1:]
    gains, refs = refs[: len(split)], refs[len(split) :]
    shards, refs = refs[: 2 * len(split)], refs[2 * len(split) :]
    total = None
    if has_total:
        total, refs = refs[0][...], refs[1:]
    rows = stats_ref.shape[1]
    row = lax.broadcasted_iota(jnp.int32, (128, rows), 0)
    stats = jnp.where(row == 0, stats_ref[0:1], stats_ref[1:2]).T
    row_mean = stats[:, 0:1] / width
    scale = lax.rsqrt(stats[:, 1:2] / width - row_mean * row_mean + epsilon)
    depth = shards[0].shape[1]
    at = 0
    for piece, number in enumerate(split):
        values = near[at][...]
        if number == 2:
            values = jnp.concatenate([values, near[at + 1][...]], 0)
        at += number
        values = values.astype(jnp.float32)
        normed = ((values - row_mean) * scale * gains[piece][...]).astype(jnp.bfloat16)
        for half in range(2):
            term = jnp.dot(
                normed[:, half * depth : (half + 1) * depth],
                shards[2 * piece + half][0],
                preferred_element_type=jnp.float32,
            )
            total = term if total is None else total + term
    if not finish:
        refs[0][...] = total
        return
    out_ref, held_ref = refs
    held_ref[...] = total.astype(jnp.bfloat16).reshape(held_ref.shape)
    at = 3 * len(split)
    for block in range(out_ref.shape[0]):
        source = index_ref[at + block]
        value = held_ref[jnp.maximum(source, 0)]
        out_ref[block] = jnp.where(source >= 0, value, jnp.zeros_like(value))


def project(near, stats, gain, shards, index, total=None, finish=False):
    split = tuple(len(piece) for piece in near)
    pieces = [part for piece in near for part in piece]
    rows = stats.shape[1]
    width = gain.shape[0]
    depth, wide = shards.shape[1:]
    count = len(near)
    whole = lambda shape: pl.BlockSpec(shape, lambda i, index: (0,) * len(shape))
    in_specs = [whole(part.shape) for part in pieces]
    in_specs.append(whole(stats.shape))
    in_specs += [
        pl.BlockSpec((1, 2 * depth), functools.partial(lambda k, i, index: (0, index[k]), k))
        for k in range(2 * count, 3 * count)
    ]
    in_specs += [
        pl.BlockSpec((1, depth, wide), functools.partial(lambda k, i, index: (index[k], 0, 0), k))
        for k in range(2 * count)
    ]
    operands = pieces + [stats] + [gain.reshape(1, width)] * count + [shards] * (2 * count)
    if total is not None:
        in_specs.append(whole(total.shape))
        operands.append(total)
    scratch = []
    if finish:
        out_shape = jax.ShapeDtypeStruct((8, HALF, wide), jnp.bfloat16)
        scratch = [pltpu.VMEM((rows // HALF, HALF, wide), jnp.bfloat16)]
    else:
        out_shape = jax.ShapeDtypeStruct((rows, wide), jnp.float32)
    return pl.pallas_call(
        functools.partial(project_kernel, split, total is not None, finish, width),
        grid_spec=pltpu.PrefetchScalarGridSpec(
            num_scalar_prefetch=1,
            grid=(1,),
            in_specs=in_specs,
            out_specs=whole(out_shape.shape),
            scratch_shapes=scratch,
        ),
        out_shape=out_shape,
        compiler_params=pltpu.CompilerParams(vmem_limit_bytes=VMEM),
        cost_estimate=pl.CostEstimate(
            flops=4 * count * rows * depth * wide,
            bytes_accessed=4 * count * (rows + wide) * depth,
            transcendentals=rows,
        ),
        name="project",
    )(index, *operands)


def pack_kernel(place_ref, arrived_ref, text_ref, out_ref):
    start, first, second, length = (place_ref[k] for k in range(4))
    rows, wide = arrived_ref.shape[1:]
    covered = ((start >= first) & (start < first + PATCHES)) | (
        (start >= second) & (start < second + PATCHES)
    )

    @pl.when(covered)
    def _():
        for k in range(arrived_ref.shape[0]):
            out_ref[:, k * wide : (k + 1) * wide] = arrived_ref[k]

    @pl.when(jnp.logical_not(covered))
    def _():
        position = start + lax.broadcasted_iota(jnp.int32, (rows, wide), 0)
        before = jnp.clip(position - first, 0, PATCHES) + jnp.clip(position - second, 0, PATCHES)
        is_text = position - before < length
        for k in range(arrived_ref.shape[0]):
            text = text_ref[:, k * wide : (k + 1) * wide].astype(jnp.float32)
            out_ref[:, k * wide : (k + 1) * wide] = jnp.where(is_text, text, 0.0).astype(
                jnp.bfloat16
            )


def pack(arrived, text, place):
    whole = lambda shape: pl.BlockSpec(shape, lambda i, index: (0,) * len(shape))
    return pl.pallas_call(
        pack_kernel,
        grid_spec=pltpu.PrefetchScalarGridSpec(
            num_scalar_prefetch=1,
            grid=(1,),
            in_specs=[whole(arrived.shape), whole(text.shape)],
            out_specs=whole(text.shape),
        ),
        out_shape=jax.ShapeDtypeStruct(text.shape, text.dtype),
        compiler_params=pltpu.CompilerParams(vmem_limit_bytes=VMEM),
        cost_estimate=pl.CostEstimate(
            flops=text.size, bytes_accessed=6 * text.size, transcendentals=0
        ),
        name="pack",
    )(place, arrived, text)


def after(values, *others):
    return lax.optimization_barrier((values, *others))[0]


def spread_x(mine):
    half = mine.shape[0] // 2
    right, left = shift_x(mine, -1), shift_x(mine, 1)
    return right, left, (shift_x(left[:half], 1), shift_x(right[half:], -1))


def local(
    patches,
    norm_gain,
    qkv_weight,
    qk_gain,
    out_weight,
    final_gain,
    proj_weight,
    text_embed,
    slot_offset,
    text_len,
):
    dp = lax.axis_index("dp")
    mp = lax.axis_index("mp")
    met = jnp.asarray(per_device(early_order))[dp]
    groups, shards = place_tables()
    groups, shards = jnp.asarray(groups)[mp], jnp.asarray(shards)[dp, mp]

    own = qkv_weight.transpose(1, 0, 2)
    other = swap_core(own)
    pair = jnp.stack([own, other])
    first = spread_y(pair)
    far = swap_zh(after(own, pair))
    columns = norm_columns(after(patches, pair), norm_gain, 16)
    total = accumulate(columns, [own, other], met[0:2])
    far_other = swap_core(after(far, total))
    far_first = spread_y(jnp.stack([far, far_other]))

    def prepare(own, far):
        mine = jnp.stack([own, far])
        return jnp.concatenate([mine, swap_core(mine)])

    turned = transpose_mesh(after(out_weight, far_other))
    proj_far = swap_zh(after(proj_weight, far_other))

    total = accumulate(columns, [far, far_other], met[2:4], total)
    first, total = lax.optimization_barrier((first, total))
    second = spread_y(first[0])
    first_other = swap_core(first)
    total = accumulate(columns, [first, first_other], met[4:8], total)

    turned_far = swap_zh(after(turned, first_other))
    far_first, total = lax.optimization_barrier((far_first, total))
    far_second = spread_y(far_first[0])
    far_first_other = swap_core(far_first)
    second_other = swap_core(second)
    out_quad = prepare(turned, turned_far)
    out_first = spread_y(after(out_quad, far_first_other))
    proj_quad = prepare(proj_weight, after(proj_far, far_first_other))
    total = accumulate(columns, [far_first, far_first_other], met[8:12], total)
    total = accumulate(columns, [second, second_other], met[12:14], total)
    far_second, total = lax.optimization_barrier((far_second, total))
    far_second_other = swap_core(far_second)
    attended = accumulate(
        columns, [far_second, far_second_other], met[14:16], total, qk_gain.transpose(1, 0, 2)
    )

    near_att = {(0, 0): (attended,)}
    att_z = swap_zl(attended)
    right, left, beyond = spread_x(attended)
    near_att[0, 1], near_att[0, 3], near_att[0, 2] = (right,), (left,), beyond
    near_att[1, 0] = (att_z,)
    right, left, beyond = spread_x(att_z)
    near_att[1, 1], near_att[1, 3], near_att[1, 2] = (right,), (left,), beyond

    out_first = after(out_first, attended)
    out_second = spread_y(out_first[:2])
    out_all = jnp.concatenate(
        [out_quad, out_first, swap_core(out_first), out_second, swap_core(out_second)]
    )
    proj_first = spread_y(after(proj_quad, out_first))
    proj_second = spread_y(proj_first[:2])
    proj_all = jnp.concatenate(
        [proj_quad, proj_first, swap_core(proj_first), proj_second, swap_core(proj_second)]
    )

    mp_slot = mp[None].astype(jnp.int32)
    partial = out_project([near_att[r] for r in NEAR[:4]], out_all, shards[:8])
    block_out, stats = out_project(
        [near_att[r] for r in NEAR[4:]],
        out_all,
        jnp.concatenate([shards[8:], mp_slot]),
        partial,
        patches,
    )

    near = {(0, 0): (block_out,)}
    block_z = swap_zl(block_out)
    right, left, beyond = spread_x(block_out)
    near[0, 1], near[0, 3], near[0, 2] = (right,), (left,), beyond
    stats = stats + swap_zl(stats)
    stats = stats + shift_x(stats, 1) + shift_x(stats, -1) + shift_x(stats, 2)
    near[1, 0] = (block_z,)
    right, left, beyond = spread_x(block_z)
    near[1, 1], near[1, 3], near[1, 2] = (right,), (left,), beyond

    slot = slot_offset // HALF
    block = jnp.arange(8, dtype=jnp.int32)
    in_first = (block >= slot[0]) & (block < slot[0] + 2)
    in_second = (block >= slot[1]) & (block < slot[1] + 2)
    source = jnp.where(in_first, block - slot[0], jnp.where(in_second, block - slot[1] + 2, -1))

    total = None
    for at in range(0, 8, 2):
        index = [shards[2 * at : 2 * at + 4], groups[at : at + 2]]
        index = jnp.concatenate(index + [source])
        total = project(
            [near[r] for r in NEAR[at : at + 2]], stats, final_gain, proj_all, index, total, at == 6
        )
    arrived = lax.all_to_all(total, "mp", split_axis=0, concat_axis=0, tiled=True)
    place = jnp.concatenate([mp_slot * HALF, slot_offset, text_len])
    sequence = pack(arrived, text_embed[0], place)
    return (block_out, sequence[None])


def solution(mesh):
    in_specs = (
        P("dp", None),
        P(),
        P("dp", "mp", None),
        P(None, "mp", None),
        P("dp", "mp"),
        P(),
        P("dp", "mp"),
        P("dp", "mp", None),
        P("dp"),
        P("dp"),
    )
    out_specs = (P("dp", "mp"), P("dp", "mp", None))
    return jax.shard_map(local, mesh=mesh, in_specs=in_specs, out_specs=out_specs, check_vma=False)
```

profile of v0, /device:TPU:0, one launch (start us, length us, event | category | flops | bytes accessed | tf_op | source)
XLA Modules:
  0.0 275.6 jit_solution(4678450845643541497)
XLA Ops:
  0.7 2.6 collective-permute-done
  3.3 2.6 pad_maximum_fusion
  6.9 4.0 %collective-permute-start.1 = (bf16[3,384,384]{2,1,0:T(8,128)(2,1)}, bf16[3,384,384]{2,1,0:T(8,128)(2,1)S(1)}, u32[]{:S(2)}, u32[]{:S(2)}) collective-permute-start(bf16[3,384,384]{2,1,0:T(8,128)(2,1)} %bitcast.64), channel_id=1, source_target_pairs={{0,64},{1,65},{2,66},{3,67},{4,68},{5,69},{6,70},{7,71},{8,72},{9,... | collective-permute-start | bytes 2654216 | tf_op jit(solution)/shard_map/ppermute | solution.py:36
  13.2 2.8 %copy-done.3 = bf16[512,6144]{1,0:T(8,128)(2,1)S(1)} copy-done((bf16[512,6144]{1,0:T(8,128)(2,1)S(1)}, bf16[512,6144]{1,0:T(8,128)(2,1)}, u32[]{:S(2)}) %copy-start.3) | copy-done | bytes 6291480
  16.7 6.1 %norm_columns.1.refs_0_.refs_1_.refs_2_.refs_3_ = bf16[16,512,384]{2,1,0:T(8,128)(2,1)S(1)} custom-call(bf16[512,6144]{1,0:T(8,128)(2,1)S(1)} %copy-done.3, f32[1,6144]{1,0:T(1,128)S(1)} %bitcast.84), custom_call_target="tpu_custom_call" | custom-call | flops 25165824 | bytes 12582912 | tf_op jit(solution)/shard_map/norm_columns/pallas_call | solution.py:130
  22.9 2.5 accumulate.6.refs_4_
  25.4 5.6 %collective-permute-done.1 = bf16[3,384,384]{2,1,0:T(8,128)(2,1)S(1)} collective-permute-done((bf16[3,384,384]{2,1,0:T(8,128)(2,1)}, bf16[3,384,384]{2,1,0:T(8,128)(2,1)S(1)}, u32[]{:S(2)}, u32[]{:S(2)}) %collective-permute-start.1) | collective-permute-done | bytes 884768 | tf_op jit(solution)/shard_map/ppermute | solution.py:36
  31.0 2.4 collective-permute-done.2
  33.4 2.5 accumulate.7.refs_6_
  41.0 5.1 %accumulate.8.refs_6_ = f32[3,512,384]{2,1,0:T(8,128)S(1)} custom-call(s32[4]{0:T(128)S(1)} %get-tuple-element.54.index_ref, bf16[16,512,384]{2,1,0:T(8,128)(2,1)S(1)} %norm_columns.1.refs_0_.refs_1_.refs_2_.refs_3_, bf16[16,512,384]{2,1,0:T(8,128)(2,1)S(1)} %norm_columns.1.refs_0_.refs_1_.refs_2_.refs_3_, ...), custom_call_target="tpu_custom_call", output_to_operand_aliasing={{}: (7, {})} | custom-call | flops 1811939328 | bytes 5111808 | tf_op jit(solution)/shard_map/accumulate/pallas_call | solution.py:217
  46.1 14.0 %collective-permute-done.3.refs_4_ = bf16[2,3,384,384]{3,2,1,0:T(8,128)(2,1)S(1)} collective-permute-done((bf16[2,3,384,384]{3,2,1,0:T(8,128)(2,1)S(1)}, bf16[2,3,384,384]{3,2,1,0:T(8,128)(2,1)S(1)}, u32[]{:S(2)}, u32[]{:S(2)}) %collective-permute-start.3) | collective-permute-done | bytes 1769504 | tf_op jit(solution)/shard_map/ppermute | solution.py:36
  60.8 19.3 %collective-permute-done.7 = bf16[3,384,384]{2,1,0:T(8,128)(2,1)S(1)} collective-permute-done((bf16[3,384,384]{2,1,0:T(8,128)(2,1)S(1)}, bf16[3,384,384]{2,1,0:T(8,128)(2,1)S(1)}, u32[]{:S(2)}, u32[]{:S(2)}) %collective-permute-start.7) | collective-permute-done | bytes 884768 | tf_op jit(solution)/shard_map/ppermute | solution.py:36
  80.2 3.3 %collective-permute-start.21 = (bf16[384,384]{1,0:T(8,128)(2,1)S(1)}, bf16[384,384]{1,0:T(8,128)(2,1)S(1)}, u32[]{:S(2)}, u32[]{:S(2)}) collective-permute-start(bf16[384,384]{1,0:T(8,128)(2,1)S(1)} %collective-permute-done.20), channel_id=1, source_target_pairs={{0,64},{1,65},{2,66},{3,67},{4,68},{5,69},{6,70},{7,71},{8,72},{9,... | collective-permute-start | bytes 884744 | tf_op jit(solution)/shard_map/ppermute | solution.py:36
  83.6 2.6 collective-permute-start.6
  86.1 5.0 %collective-permute-done.21 = bf16[384,384]{1,0:T(8,128)(2,1)S(1)} collective-permute-done((bf16[384,384]{1,0:T(8,128)(2,1)S(1)}, bf16[384,384]{1,0:T(8,128)(2,1)S(1)}, u32[]{:S(2)}, u32[]{:S(2)}) %collective-permute-start.21) | collective-permute-done | bytes 294944 | tf_op jit(solution)/shard_map/ppermute | solution.py:36
  91.3 3.3 %collective-permute-start.40 = (bf16[384,512]{1,0:T(8,128)(2,1)}, bf16[384,512]{1,0:T(8,128)(2,1)}, u32[]{:S(2)}, u32[]{:S(2)}) collective-permute-start(bf16[384,512]{1,0:T(8,128)(2,1)} %param.19), channel_id=1, source_target_pairs={{0,64},{1,65},{2,66},{3,67},{4,68},{5,69},{6,70},{7,71},{8,72},{9,... | collective-permute-start | bytes 1179656 | tf_op jit(solution)/shard_map/ppermute | solution.py:36
  94.6 4.4 %accumulate.9.refs_4_ = f32[3,512,384]{2,1,0:T(8,128)S(1)} custom-call(s32[4]{0:T(128)S(1)} %get-tuple-element.53.index_ref, bf16[16,512,384]{2,1,0:T(8,128)(2,1)S(1)} %norm_columns.1.refs_0_.refs_1_.refs_2_.refs_3_, bf16[16,512,384]{2,1,0:T(8,128)(2,1)S(1)} %norm_columns.1.refs_0_.refs_1_.refs_2_.refs_3_, ...), custom_call_target="tpu_custom_call", output_to_operand_aliasing={{}: (7, {})} | custom-call | flops 1811939328 | bytes 5111808 | tf_op jit(solution)/shard_map/accumulate/pallas_call | solution.py:217
  99.0 2.5 accumulate.10.refs_4_
  103.0 2.5 collective-permute-start.23
  109.7 2.8 %copy-done.1 = bf16[16,512,384]{2,1,0:T(8,128)(2,1)S(1)} copy-done((bf16[16,512,384]{2,1,0:T(8,128)(2,1)S(1)}, bf16[16,512,384]{2,1,0:T(8,128)(2,1)}, u32[]{:S(2)}) %copy-start.1) | copy-done | bytes 6291480
  112.5 5.8 %accumulate.11.refs_0_ = bf16[512,384]{1,0:T(8,128)(2,1)S(1)} custom-call(s32[2]{0:T(128)S(1)} %get-tuple-element.58.index_ref, bf16[16,512,384]{2,1,0:T(8,128)(2,1)S(1)} %copy-done.1, bf16[16,512,384]{2,1,0:T(8,128)(2,1)S(1)} %copy-done.1, bf16[1,3,384,384]{3,2,1,0:T(8,128)(2,1)S(1)} %bitcast.81, bf16[1,3,384,384]{3,2,1,0:T(8,128)(2,1)} %bitcast.20.refs_3_, ...), custom_call_target="tpu_custom_call" | custom-call | flops 905969664 | bytes 2555904 | tf_op jit(solution)/shard_map/accumulate/pallas_call | solution.py:217
  123.3 3.2 %collective-permute-start.16 = (bf16[512,384]{1,0:T(8,128)(2,1)S(1)}, bf16[512,384]{1,0:T(8,128)(2,1)S(1)}, u32[]{:S(2)}, u32[]{:S(2)}) collective-permute-start(bf16[512,384]{1,0:T(8,128)(2,1)S(1)} %accumulate.11.refs_0_), channel_id=1, source_target_pairs={{0,3},{1,0},{2,1},{3,2},{4,7},{5,4},{6,5},{7,6},{8,11},{9,8},{10,9... | collective-permute-start | bytes 1179656 | tf_op jit(solution)/shard_map/ppermute | solution.py:36
  131.4 4.5 %collective-permute-done.14.refs_3_ = bf16[512,384]{1,0:T(8,128)(2,1)S(1)} collective-permute-done((bf16[512,384]{1,0:T(8,128)(2,1)S(1)}, bf16[512,384]{1,0:T(8,128)(2,1)S(1)}, u32[]{:S(2)}, u32[]{:S(2)}) %collective-permute-start.14) | collective-permute-done | bytes 393248 | tf_op jit(solution)/shard_map/ppermute | solution.py:36
  136.0 3.2 %collective-permute-start.12 = (bf16[512,384]{1,0:T(8,128)(2,1)S(1)}, bf16[512,384]{1,0:T(8,128)(2,1)S(1)}, u32[]{:S(2)}, u32[]{:S(2)}) collective-permute-start(bf16[512,384]{1,0:T(8,128)(2,1)S(1)} %collective-permute-done.11.refs_1_), channel_id=1, source_target_pairs={{0,3},{1,0},{2,1},{3,2},{4,7},{5,4},{6,5},{7,6},{8,11},{9,8},{10,9... | collective-permute-start | bytes 1179656 | tf_op jit(solution)/shard_map/ppermute | solution.py:36
  140.9 7.0 %collective-permute-done.13.refs_1_ = bf16[512,384]{1,0:T(8,128)(2,1)S(1)} collective-permute-done((bf16[512,384]{1,0:T(8,128)(2,1)S(1)}, bf16[512,384]{1,0:T(8,128)(2,1)S(1)}, u32[]{:S(2)}, u32[]{:S(2)}) %collective-permute-start.13) | collective-permute-done | bytes 393248 | tf_op jit(solution)/shard_map/ppermute | solution.py:36
  148.0 3.3 %collective-permute-start.17 = (bf16[256,384]{1,0:T(8,128)(2,1)S(1)}, bf16[256,384]{1,0:T(8,128)(2,1)S(1)}, u32[]{:S(2)}, u32[]{:S(2)}) collective-permute-start(bf16[256,384]{1,0:T(8,128)(2,1)S(1)} %slice.189), channel_id=1, source_target_pairs={{0,3},{1,0},{2,1},{3,2},{4,7},{5,4},{6,5},{7,6},{8,11},{9,8},{10,9... | collective-permute-start | bytes 589832 | tf_op jit(solution)/shard_map/ppermute | solution.py:36
  151.8 3.3 %collective-permute-start.19 = (bf16[256,384]{1,0:T(8,128)(2,1)S(1)}, bf16[256,384]{1,0:T(8,128)(2,1)S(1)}, u32[]{:S(2)}, u32[]{:S(2)}) collective-permute-start(bf16[256,384]{1,0:T(8,128)(2,1)S(1)} %slice.191), channel_id=1, source_target_pairs={{0,3},{1,0},{2,1},{3,2},{4,7},{5,4},{6,5},{7,6},{8,11},{9,8},{10,9... | collective-permute-start | bytes 589832 | tf_op jit(solution)/shard_map/ppermute | solution.py:36
  155.2 2.7 out_project.2.refs_14_
  159.2 2.8 %copy-done.4 = bf16[512,6144]{1,0:T(8,128)(2,1)S(1)} copy-done((bf16[512,6144]{1,0:T(8,128)(2,1)S(1)}, bf16[512,6144]{1,0:T(8,128)(2,1)}, u32[]{:S(2)}) %copy-start.4) | copy-done | bytes 6291480
  161.9 3.7 %out_project.3 = (bf16[512,768]{1,0:T(8,128)(2,1)}, f32[8,512]{1,0:T(8,128)S(1)}) custom-call(s32[9]{0:T(128)S(1)} %pad_add_fusion.index_ref, bf16[512,384]{1,0:T(8,128)(2,1)S(1)} %collective-permute-done.12.refs_0_, bf16[512,384]{1,0:T(8,128)(2,1)S(1)} %collective-permute-done.13.refs_1_, bf16[256,384]{1,0:T(8,128)(2,1)S(1)} %collective-permute-done.15.refs_2_, ...), custom_call_target="tpu_custom_call" | custom-call | flops 1207959552 | bytes 5505024 | tf_op jit(solution)/shard_map/out_project/pallas_call | solution.py:304
  171.4 13.0 %collective-permute-done.36 = f32[8,512]{1,0:T(8,128)S(1)} collective-permute-done((f32[8,512]{1,0:T(8,128)S(1)}, f32[8,512]{1,0:T(8,128)S(1)}, u32[]{:S(2)}, u32[]{:S(2)}) %collective-permute-start.36) | collective-permute-done | bytes 16416 | tf_op jit(solution)/shard_map/ppermute | solution.py:36
  194.5 4.0 %collective-permute-done.39 = f32[8,512]{1,0:T(8,128)S(1)} collective-permute-done((f32[8,512]{1,0:T(8,128)S(1)}, f32[8,512]{1,0:T(8,128)S(1)}, u32[]{:S(2)}, u32[]{:S(2)}) %collective-permute-start.39) | collective-permute-done | bytes 16416 | tf_op jit(solution)/shard_map/ppermute | solution.py:36
  198.5 2.9 %collective-permute-start.29 = (bf16[512,768]{1,0:T(8,128)(2,1)}, bf16[512,768]{1,0:T(8,128)(2,1)S(1)}, u32[]{:S(2)}, u32[]{:S(2)}) collective-permute-start(bf16[512,768]{1,0:T(8,128)(2,1)} %get-tuple-element.18.refs_0_), channel_id=1, source_target_pairs={{0,3},{1,0},{2,1},{3,2},{4,7},{5,4},{6,5},{7,6},{8,11},{9,8},{10,9... | collective-permute-start | bytes 2359304 | tf_op jit(solution)/shard_map/ppermute | solution.py:36
  201.5 3.2 %collective-permute-start.34 = (bf16[512,768]{1,0:T(8,128)(2,1)S(1)}, bf16[512,768]{1,0:T(8,128)(2,1)S(1)}, u32[]{:S(2)}, u32[]{:S(2)}) collective-permute-start(bf16[512,768]{1,0:T(8,128)(2,1)S(1)} %collective-permute-done.31.refs_1_), channel_id=1, source_target_pairs={{0,3},{1,0},{2,1},{3,2},{4,7},{5,4},{6,5},{7,6},{8,11},{9,8},{10,9... | collective-permute-start | bytes 2359304 | tf_op jit(solution)/shard_map/ppermute | solution.py:36
  207.6 2.7 constant_dynamic-update-slice_fusion.10
  210.2 9.5 %collective-permute-done.29.refs_0_ = bf16[512,768]{1,0:T(8,128)(2,1)S(1)} collective-permute-done((bf16[512,768]{1,0:T(8,128)(2,1)}, bf16[512,768]{1,0:T(8,128)(2,1)S(1)}, u32[]{:S(2)}, u32[]{:S(2)}) %collective-permute-start.29) | collective-permute-done | bytes 786464 | tf_op jit(solution)/shard_map/ppermute | solution.py:36
  219.8 3.7 %collective-permute-start.30 = (bf16[256,768]{1,0:T(8,128)(2,1)S(1)}, bf16[256,768]{1,0:T(8,128)(2,1)S(1)}, u32[]{:S(2)}, u32[]{:S(2)}) collective-permute-start(bf16[256,768]{1,0:T(8,128)(2,1)S(1)} %slice.193), channel_id=1, source_target_pairs={{0,3},{1,0},{2,1},{3,2},{4,7},{5,4},{6,5},{7,6},{8,11},{9,8},{10,9... | collective-permute-start | bytes 1179656 | tf_op jit(solution)/shard_map/ppermute | solution.py:36
  223.5 13.0 %collective-permute-done.34.refs_0_ = bf16[512,768]{1,0:T(8,128)(2,1)S(1)} collective-permute-done((bf16[512,768]{1,0:T(8,128)(2,1)S(1)}, bf16[512,768]{1,0:T(8,128)(2,1)S(1)}, u32[]{:S(2)}, u32[]{:S(2)}) %collective-permute-start.34) | collective-permute-done | bytes 786464 | tf_op jit(solution)/shard_map/ppermute | solution.py:36
  236.6 3.8 %collective-permute-start.35 = (bf16[256,768]{1,0:T(8,128)(2,1)S(1)}, bf16[256,768]{1,0:T(8,128)(2,1)S(1)}, u32[]{:S(2)}, u32[]{:S(2)}) collective-permute-start(bf16[256,768]{1,0:T(8,128)(2,1)S(1)} %slice.195), channel_id=1, source_target_pairs={{0,3},{1,0},{2,1},{3,2},{4,7},{5,4},{6,5},{7,6},{8,11},{9,8},{10,9... | collective-permute-start | bytes 1179656 | tf_op jit(solution)/shard_map/ppermute | solution.py:36
  240.3 2.7 constant_dynamic-update-slice_fusion.9
  243.0 2.1 constant_dynamic-update-slice_fusion.8
  246.1 2.8 %copy-done.2 = bf16[16,384,512]{2,1,0:T(8,128)(2,1)S(1)} copy-done((bf16[16,384,512]{2,1,0:T(8,128)(2,1)S(1)}, bf16[16,384,512]{2,1,0:T(8,128)(2,1)}, u32[]{:S(2)}) %copy-start.2) | copy-done | bytes 6291480
  248.8 2.2 project.4.refs_9_
  251.1 2.3 project.5.refs_9_
  253.4 2.3 project.6.refs_11_
  255.7 3.3 %project.7 = bf16[8,128,512]{2,1,0:T(8,128)(2,1)} custom-call(s32[14]{0:T(128)S(1)} %add_add_fusion.1.index_ref, bf16[256,768]{1,0:T(8,128)(2,1)S(1)} %collective-permute-done.28.refs_0_, bf16[256,768]{1,0:T(8,128)(2,1)S(1)} %collective-permute-done.30.refs_1_, bf16[256,768]{1,0:T(8,128)(2,1)S(1)} %collective-permute-done.33.refs_2_, ...), custom_call_target="tpu_custom_call" | custom-call | flops 805306368 | bytes 3145728 | tf_op jit(solution)/shard_map/project/pallas_call | solution.py:389
  259.0 3.6 %all-to-all-start = ((bf16[8,128,512]{2,1,0:T(8,128)(2,1)}), bf16[8,128,512]{2,1,0:T(8,128)(2,1)S(1)}, u32[]{:S(2)}, u32[]{:S(2)}) async-start(bf16[8,128,512]{2,1,0:T(8,128)(2,1)} %project.7), calls=%async_computation | async-start | bytes 2097152 | tf_op jit(solution)/shard_map/all_to_all | solution.py:571
  263.3 10.7 %all-to-all-done.arrived_ref = bf16[8,128,512]{2,1,0:T(8,128)(2,1)S(1)} async-done(((bf16[8,128,512]{2,1,0:T(8,128)(2,1)}), bf16[8,128,512]{2,1,0:T(8,128)(2,1)S(1)}, u32[]{:S(2)}, u32[]{:S(2)}) %all-to-all-start) | async-done | bytes 1048608 | tf_op jit(solution)/shard_map/all_to_all | solution.py:571
  (151 shorter events, 49.3 us)
Async XLA Ops:
  0.6 2.7 collective-permute-start
  6.9 24.1 %collective-permute-start.1 = (bf16[3,384,384]{2,1,0:T(8,128)(2,1)}, bf16[3,384,384]{2,1,0:T(8,128)(2,1)S(1)}, u32[]{:S(2)}, u32[]{:S(2)}) collective-permute-start(bf16[3,384,384]{2,1,0:T(8,128)(2,1)} %bitcast.64), channel_id=1, source_target_pairs={{0,64},{1,65},{2,66},{3,67},{4,68},{5,69},{6,70},{7,71},{8,72},{9,... | collective-permute-start | bytes 2654216 | tf_op jit(solution)/shard_map/ppermute | solution.py:36
  10.8 25.1 %collective-permute-start.4 = (bf16[2,3,384,384]{3,2,1,0:T(8,128)(2,1)}, bf16[2,3,384,384]{3,2,1,0:T(8,128)(2,1)}, u32[]{:S(2)}, u32[]{:S(2)}) collective-permute-start(bf16[2,3,384,384]{3,2,1,0:T(8,128)(2,1)} %pad_maximum_fusion), channel_id=1, source_target_pairs={{0,16},{1,17},{2,18},{3,19},{4,20},{5,21},{6,22},{7,23},{8,56},{9,... | collective-permute-start | bytes 5308424 | tf_op jit(solution)/shard_map/ppermute | solution.py:36
  22.8 76.1 %copy-start = (bf16[16,512,384]{2,1,0:T(8,128)(2,1)}, bf16[16,512,384]{2,1,0:T(8,128)(2,1)S(1)}, u32[]{:S(2)}) copy-start(bf16[16,512,384]{2,1,0:T(8,128)(2,1)S(1)} %norm_columns.1.refs_0_.refs_1_.refs_2_.refs_3_) | copy-start | bytes 18874372
  31.0 2.4 collective-permute-start.2
  35.9 5.0 %collective-permute-start.5 = (bf16[2,3,384,384]{3,2,1,0:T(8,128)(2,1)}, bf16[2,3,384,384]{3,2,1,0:T(8,128)(2,1)S(1)}, u32[]{:S(2)}, u32[]{:S(2)}) collective-permute-start(bf16[2,3,384,384]{3,2,1,0:T(8,128)(2,1)} %collective-permute-done.4.refs_4_), channel_id=1, source_target_pairs={{0,8},{1,9},{2,10},{3,11},{4,12},{5,13},{6,14},{7,15},{8,0},{9,1},... | collective-permute-start | bytes 5308424 | tf_op jit(solution)/shard_map/ppermute | solution.py:36
  36.3 23.8 %collective-permute-start.3 = (bf16[2,3,384,384]{3,2,1,0:T(8,128)(2,1)S(1)}, bf16[2,3,384,384]{3,2,1,0:T(8,128)(2,1)S(1)}, u32[]{:S(2)}, u32[]{:S(2)}) collective-permute-start(bf16[2,3,384,384]{3,2,1,0:T(8,128)(2,1)S(1)} %pad_maximum_fusion.1), channel_id=1, source_target_pairs={{0,16},{1,17},{2,18},{3,19},{4,20},{5,21},{6,22},{7,23},{8,56},{9,... | collective-permute-start | bytes 5308424 | tf_op jit(solution)/shard_map/ppermute | solution.py:36
  39.3 40.8 %collective-permute-start.7 = (bf16[3,384,384]{2,1,0:T(8,128)(2,1)S(1)}, bf16[3,384,384]{2,1,0:T(8,128)(2,1)S(1)}, u32[]{:S(2)}, u32[]{:S(2)}) collective-permute-start(bf16[3,384,384]{2,1,0:T(8,128)(2,1)S(1)} %slice_bitcast_fusion), channel_id=1, source_target_pairs={{0,16},{1,17},{2,18},{3,19},{4,20},{5,21},{6,22},{7,23},{8,56},{9,... | collective-permute-start | bytes 2654216 | tf_op jit(solution)/shard_map/ppermute | solution.py:36
  60.1 34.4 %collective-permute-start.9 = (bf16[2,3,384,384]{3,2,1,0:T(8,128)(2,1)S(1)}, bf16[2,3,384,384]{3,2,1,0:T(8,128)(2,1)S(1)}, u32[]{:S(2)}, u32[]{:S(2)}) collective-permute-start(bf16[2,3,384,384]{3,2,1,0:T(8,128)(2,1)S(1)} %collective-permute-done.3.refs_4_), channel_id=1, source_target_pairs={{0,8},{1,9},{2,10},{3,11},{4,12},{5,13},{6,14},{7,15},{8,0},{9,1},... | collective-permute-start | bytes 5308424 | tf_op jit(solution)/shard_map/ppermute | solution.py:36
  60.1 20.0 %collective-permute-start.20 = (bf16[384,384]{1,0:T(8,128)(2,1)S(1)}, bf16[384,384]{1,0:T(8,128)(2,1)S(1)}, u32[]{:S(2)}, u32[]{:S(2)}) collective-permute-start(bf16[384,384]{1,0:T(8,128)(2,1)S(1)} %copy-done.20), channel_id=1, source_target_pairs={{0,0},{1,16},{2,32},{3,48},{4,64},{5,80},{6,96},{7,112},{8,8},{9,2... | collective-permute-start | bytes 884744 | tf_op jit(solution)/shard_map/ppermute | solution.py:36
  80.1 18.8 %collective-permute-start.8 = (bf16[3,384,384]{2,1,0:T(8,128)(2,1)S(1)}, bf16[3,384,384]{2,1,0:T(8,128)(2,1)S(1)}, u32[]{:S(2)}, u32[]{:S(2)}) collective-permute-start(bf16[3,384,384]{2,1,0:T(8,128)(2,1)S(1)} %collective-permute-done.7), channel_id=1, source_target_pairs={{0,8},{1,9},{2,10},{3,11},{4,12},{5,13},{6,14},{7,15},{8,0},{9,1},... | collective-permute-start | bytes 2654216 | tf_op jit(solution)/shard_map/ppermute | solution.py:36
  80.2 10.9 %collective-permute-start.21 = (bf16[384,384]{1,0:T(8,128)(2,1)S(1)}, bf16[384,384]{1,0:T(8,128)(2,1)S(1)}, u32[]{:S(2)}, u32[]{:S(2)}) collective-permute-start(bf16[384,384]{1,0:T(8,128)(2,1)S(1)} %collective-permute-done.20), channel_id=1, source_target_pairs={{0,64},{1,65},{2,66},{3,67},{4,68},{5,69},{6,70},{7,71},{8,72},{9,... | collective-permute-start | bytes 884744 | tf_op jit(solution)/shard_map/ppermute | solution.py:36
  83.6 17.9 %collective-permute-start.6 = (bf16[3,384,384]{2,1,0:T(8,128)(2,1)S(1)}, bf16[3,384,384]{2,1,0:T(8,128)(2,1)S(1)}, u32[]{:S(2)}, u32[]{:S(2)}) collective-permute-start(bf16[3,384,384]{2,1,0:T(8,128)(2,1)S(1)} %slice_bitcast_fusion.1), channel_id=1, source_target_pairs={{0,16},{1,17},{2,18},{3,19},{4,20},{5,21},{6,22},{7,23},{8,56},{9,... | collective-permute-start | bytes 2654216 | tf_op jit(solution)/shard_map/ppermute | solution.py:36
  91.2 10.6 %collective-permute-start.22 = (bf16[2,384,384]{2,1,0:T(8,128)(2,1)S(1)}, bf16[2,384,384]{2,1,0:T(8,128)(2,1)S(1)}, u32[]{:S(2)}, u32[]{:S(2)}) collective-permute-start(bf16[2,384,384]{2,1,0:T(8,128)(2,1)S(1)} %pad_maximum_fusion.5), channel_id=1, source_target_pairs={{0,8},{1,9},{2,10},{3,11},{4,12},{5,13},{6,14},{7,15},{8,0},{9,1},... | collective-permute-start | bytes 1769480 | tf_op jit(solution)/shard_map/ppermute | solution.py:36
  91.3 14.2 %collective-permute-start.40 = (bf16[384,512]{1,0:T(8,128)(2,1)}, bf16[384,512]{1,0:T(8,128)(2,1)}, u32[]{:S(2)}, u32[]{:S(2)}) collective-permute-start(bf16[384,512]{1,0:T(8,128)(2,1)} %param.19), channel_id=1, source_target_pairs={{0,64},{1,65},{2,66},{3,67},{4,68},{5,69},{6,70},{7,71},{8,72},{9,... | collective-permute-start | bytes 1179656 | tf_op jit(solution)/shard_map/ppermute | solution.py:36
  101.5 8.2 %collective-permute-start.10 = (bf16[3,384,384]{2,1,0:T(8,128)(2,1)S(1)}, bf16[3,384,384]{2,1,0:T(8,128)(2,1)}, u32[]{:S(2)}, u32[]{:S(2)}) collective-permute-start(bf16[3,384,384]{2,1,0:T(8,128)(2,1)S(1)} %collective-permute-done.6), channel_id=1, source_target_pairs={{0,8},{1,9},{2,10},{3,11},{4,12},{5,13},{6,14},{7,15},{8,0},{9,1},... | collective-permute-start | bytes 2654216 | tf_op jit(solution)/shard_map/ppermute | solution.py:36
  103.0 17.7 %collective-permute-start.23 = (bf16[4,384,384]{2,1,0:T(8,128)(2,1)}, bf16[4,384,384]{2,1,0:T(8,128)(2,1)}, u32[]{:S(2)}, u32[]{:S(2)}) collective-permute-start(bf16[4,384,384]{2,1,0:T(8,128)(2,1)} %pad_maximum_fusion.3), channel_id=1, source_target_pairs={{0,16},{1,17},{2,18},{3,19},{4,20},{5,21},{6,22},{7,23},{8,56},{9,... | collective-permute-start | bytes 3538952 | tf_op jit(solution)/shard_map/ppermute | solution.py:36
  106.7 16.6 %collective-permute-start.41 = (bf16[2,384,512]{2,1,0:T(8,128)(2,1)S(1)}, bf16[2,384,512]{2,1,0:T(8,128)(2,1)S(1)}, u32[]{:S(2)}, u32[]{:S(2)}) collective-permute-start(bf16[2,384,512]{2,1,0:T(8,128)(2,1)S(1)} %pad_maximum_fusion.4), channel_id=1, source_target_pairs={{0,8},{1,9},{2,10},{3,11},{4,12},{5,13},{6,14},{7,15},{8,0},{9,1},... | collective-permute-start | bytes 2359304 | tf_op jit(solution)/shard_map/ppermute | solution.py:36
  118.4 11.3 %collective-permute-start.11 = (bf16[512,384]{1,0:T(8,128)(2,1)S(1)}, bf16[512,384]{1,0:T(8,128)(2,1)S(1)}, u32[]{:S(2)}, u32[]{:S(2)}) collective-permute-start(bf16[512,384]{1,0:T(8,128)(2,1)S(1)} %accumulate.11.refs_0_), channel_id=1, source_target_pairs={{0,4},{1,5},{2,6},{3,7},{4,0},{5,1},{6,2},{7,3},{8,12},{9,13},{10,... | collective-permute-start | bytes 1179656 | tf_op jit(solution)/shard_map/ppermute | solution.py:36
  120.7 30.6 %collective-permute-start.24 = (bf16[4,384,384]{2,1,0:T(8,128)(2,1)}, bf16[4,384,384]{2,1,0:T(8,128)(2,1)S(1)}, u32[]{:S(2)}, u32[]{:S(2)}) collective-permute-start(bf16[4,384,384]{2,1,0:T(8,128)(2,1)} %collective-permute-done.23), channel_id=1, source_target_pairs={{0,8},{1,9},{2,10},{3,11},{4,12},{5,13},{6,14},{7,15},{8,0},{9,1},... | collective-permute-start | bytes 3538952 | tf_op jit(solution)/shard_map/ppermute | solution.py:36
  121.9 17.3 %collective-permute-start.25 = (bf16[2,384,384]{2,1,0:T(8,128)(2,1)S(1)}, bf16[2,384,384]{2,1,0:T(8,128)(2,1)S(1)}, u32[]{:S(2)}, u32[]{:S(2)}) collective-permute-start(bf16[2,384,384]{2,1,0:T(8,128)(2,1)S(1)} %slice.162), channel_id=1, source_target_pairs={{0,16},{1,17},{2,18},{3,19},{4,20},{5,21},{6,22},{7,23},{8,56},{9,... | collective-permute-start | bytes 1769480 | tf_op jit(solution)/shard_map/ppermute | solution.py:36
  123.3 12.7 %collective-permute-start.14 = (bf16[512,384]{1,0:T(8,128)(2,1)S(1)}, bf16[512,384]{1,0:T(8,128)(2,1)S(1)}, u32[]{:S(2)}, u32[]{:S(2)}) collective-permute-start(bf16[512,384]{1,0:T(8,128)(2,1)S(1)} %accumulate.11.refs_0_), channel_id=1, source_target_pairs={{0,1},{1,2},{2,3},{3,0},{4,5},{5,6},{6,7},{7,4},{8,9},{9,10},{10,1... | collective-permute-start | bytes 1179656 | tf_op jit(solution)/shard_map/ppermute | solution.py:36
  123.3 12.7 %collective-permute-start.16 = (bf16[512,384]{1,0:T(8,128)(2,1)S(1)}, bf16[512,384]{1,0:T(8,128)(2,1)S(1)}, u32[]{:S(2)}, u32[]{:S(2)}) collective-permute-start(bf16[512,384]{1,0:T(8,128)(2,1)S(1)} %accumulate.11.refs_0_), channel_id=1, source_target_pairs={{0,3},{1,0},{2,1},{3,2},{4,7},{5,4},{6,5},{7,6},{8,11},{9,8},{10,9... | collective-permute-start | bytes 1179656 | tf_op jit(solution)/shard_map/ppermute | solution.py:36
  129.7 38.5 %collective-permute-start.42 = (bf16[4,384,512]{2,1,0:T(8,128)(2,1)S(1)}, bf16[4,384,512]{2,1,0:T(8,128)(2,1)}, u32[]{:S(2)}, u32[]{:S(2)}) collective-permute-start(bf16[4,384,512]{2,1,0:T(8,128)(2,1)S(1)} %pad_maximum_fusion.2), channel_id=1, source_target_pairs={{0,16},{1,17},{2,18},{3,19},{4,20},{5,21},{6,22},{7,23},{8,56},{9,... | collective-permute-start | bytes 4718600 | tf_op jit(solution)/shard_map/ppermute | solution.py:36
  136.0 12.0 %collective-permute-start.13 = (bf16[512,384]{1,0:T(8,128)(2,1)S(1)}, bf16[512,384]{1,0:T(8,128)(2,1)S(1)}, u32[]{:S(2)}, u32[]{:S(2)}) collective-permute-start(bf16[512,384]{1,0:T(8,128)(2,1)S(1)} %collective-permute-done.11.refs_1_), channel_id=1, source_target_pairs={{0,1},{1,2},{2,3},{3,0},{4,5},{5,6},{6,7},{7,4},{8,9},{9,10},{10,1... | collective-permute-start | bytes 1179656 | tf_op jit(solution)/shard_map/ppermute | solution.py:36
  136.0 12.0 %collective-permute-start.12 = (bf16[512,384]{1,0:T(8,128)(2,1)S(1)}, bf16[512,384]{1,0:T(8,128)(2,1)S(1)}, u32[]{:S(2)}, u32[]{:S(2)}) collective-permute-start(bf16[512,384]{1,0:T(8,128)(2,1)S(1)} %collective-permute-done.11.refs_1_), channel_id=1, source_target_pairs={{0,3},{1,0},{2,1},{3,2},{4,7},{5,4},{6,5},{7,6},{8,11},{9,8},{10,9... | collective-permute-start | bytes 1179656 | tf_op jit(solution)/shard_map/ppermute | solution.py:36
  139.2 12.6 %collective-permute-start.26 = (bf16[2,384,384]{2,1,0:T(8,128)(2,1)S(1)}, bf16[2,384,384]{2,1,0:T(8,128)(2,1)S(1)}, u32[]{:S(2)}, u32[]{:S(2)}) collective-permute-start(bf16[2,384,384]{2,1,0:T(8,128)(2,1)S(1)} %collective-permute-done.25), channel_id=1, source_target_pairs={{0,8},{1,9},{2,10},{3,11},{4,12},{5,13},{6,14},{7,15},{8,0},{9,1},... | collective-permute-start | bytes 1769480 | tf_op jit(solution)/shard_map/ppermute | solution.py:36
  147.9 9.9 %collective-permute-start.15 = (bf16[256,384]{1,0:T(8,128)(2,1)S(1)}, bf16[256,384]{1,0:T(8,128)(2,1)S(1)}, u32[]{:S(2)}, u32[]{:S(2)}) collective-permute-start(bf16[256,384]{1,0:T(8,128)(2,1)S(1)} %slice.188), channel_id=1, source_target_pairs={{0,1},{1,2},{2,3},{3,0},{4,5},{5,6},{6,7},{7,4},{8,9},{9,10},{10,1... | collective-permute-start | bytes 589832 | tf_op jit(solution)/shard_map/ppermute | solution.py:36
  148.0 9.9 %collective-permute-start.17 = (bf16[256,384]{1,0:T(8,128)(2,1)S(1)}, bf16[256,384]{1,0:T(8,128)(2,1)S(1)}, u32[]{:S(2)}, u32[]{:S(2)}) collective-permute-start(bf16[256,384]{1,0:T(8,128)(2,1)S(1)} %slice.189), channel_id=1, source_target_pairs={{0,3},{1,0},{2,1},{3,2},{4,7},{5,4},{6,5},{7,6},{8,11},{9,8},{10,9... | collective-permute-start | bytes 589832 | tf_op jit(solution)/shard_map/ppermute | solution.py:36
  151.3 7.8 %collective-permute-start.18 = (bf16[256,384]{1,0:T(8,128)(2,1)S(1)}, bf16[256,384]{1,0:T(8,128)(2,1)S(1)}, u32[]{:S(2)}, u32[]{:S(2)}) collective-permute-start(bf16[256,384]{1,0:T(8,128)(2,1)S(1)} %slice.190), channel_id=1, source_target_pairs={{0,1},{1,2},{2,3},{3,0},{4,5},{5,6},{6,7},{7,4},{8,9},{9,10},{10,1... | collective-permute-start | bytes 589832 | tf_op jit(solution)/shard_map/ppermute | solution.py:36
  151.8 7.4 %collective-permute-start.19 = (bf16[256,384]{1,0:T(8,128)(2,1)S(1)}, bf16[256,384]{1,0:T(8,128)(2,1)S(1)}, u32[]{:S(2)}, u32[]{:S(2)}) collective-permute-start(bf16[256,384]{1,0:T(8,128)(2,1)S(1)} %slice.191), channel_id=1, source_target_pairs={{0,3},{1,0},{2,1},{3,2},{4,7},{5,4},{6,5},{7,6},{8,11},{9,8},{10,9... | collective-permute-start | bytes 589832 | tf_op jit(solution)/shard_map/ppermute | solution.py:36
  165.7 35.8 %collective-permute-start.31 = (bf16[512,768]{1,0:T(8,128)(2,1)}, bf16[512,768]{1,0:T(8,128)(2,1)S(1)}, u32[]{:S(2)}, u32[]{:S(2)}) collective-permute-start(bf16[512,768]{1,0:T(8,128)(2,1)} %get-tuple-element.18.refs_0_), channel_id=1, source_target_pairs={{0,4},{1,5},{2,6},{3,7},{4,0},{5,1},{6,2},{7,3},{8,12},{9,13},{10,... | collective-permute-start | bytes 2359304 | tf_op jit(solution)/shard_map/ppermute | solution.py:36
  165.8 35.7 %collective-permute-start.27 = (bf16[512,768]{1,0:T(8,128)(2,1)}, bf16[512,768]{1,0:T(8,128)(2,1)S(1)}, u32[]{:S(2)}, u32[]{:S(2)}) collective-permute-start(bf16[512,768]{1,0:T(8,128)(2,1)} %get-tuple-element.18.refs_0_), channel_id=1, source_target_pairs={{0,1},{1,2},{2,3},{3,0},{4,5},{5,6},{6,7},{7,4},{8,9},{9,10},{10,1... | collective-permute-start | bytes 2359304 | tf_op jit(solution)/shard_map/ppermute | solution.py:36
  168.2 68.4 %collective-permute-start.43 = (bf16[4,384,512]{2,1,0:T(8,128)(2,1)}, bf16[4,384,512]{2,1,0:T(8,128)(2,1)}, u32[]{:S(2)}, u32[]{:S(2)}) collective-permute-start(bf16[4,384,512]{2,1,0:T(8,128)(2,1)} %collective-permute-done.42), channel_id=1, source_target_pairs={{0,8},{1,9},{2,10},{3,11},{4,12},{5,13},{6,14},{7,15},{8,0},{9,1},... | collective-permute-start | bytes 4718600 | tf_op jit(solution)/shard_map/ppermute | solution.py:36
  168.3 16.2 %collective-permute-start.36 = (f32[8,512]{1,0:T(8,128)S(1)}, f32[8,512]{1,0:T(8,128)S(1)}, u32[]{:S(2)}, u32[]{:S(2)}) collective-permute-start(f32[8,512]{1,0:T(8,128)S(1)} %get-tuple-element.34), channel_id=1, source_target_pairs={{0,4},{1,5},{2,6},{3,7},{4,0},{5,1},{6,2},{7,3},{8,12},{9,13},{10,... | collective-permute-start | bytes 49160 | tf_op jit(solution)/shard_map/ppermute | solution.py:36
  170.4 36.1 %collective-permute-start.44 = (bf16[2,384,512]{2,1,0:T(8,128)(2,1)S(1)}, bf16[2,384,512]{2,1,0:T(8,128)(2,1)}, u32[]{:S(2)}, u32[]{:S(2)}) collective-permute-start(bf16[2,384,512]{2,1,0:T(8,128)(2,1)S(1)} %slice.196), channel_id=1, source_target_pairs={{0,16},{1,17},{2,18},{3,19},{4,20},{5,21},{6,22},{7,23},{8,56},{9,... | collective-permute-start | bytes 2359304 | tf_op jit(solution)/shard_map/ppermute | solution.py:36
  184.5 4.9 %collective-permute-start.37 = (f32[8,512]{1,0:T(8,128)S(1)}, f32[8,512]{1,0:T(8,128)S(1)}, u32[]{:S(2)}, u32[]{:S(2)}) collective-permute-start(f32[8,512]{1,0:T(8,128)S(1)} %add.35), channel_id=1, source_target_pairs={{0,1},{1,2},{2,3},{3,0},{4,5},{5,6},{6,7},{7,4},{8,9},{9,10},{10,1... | collective-permute-start | bytes 49160 | tf_op jit(solution)/shard_map/ppermute | solution.py:36
  189.4 3.7 %collective-permute-start.38 = (f32[8,512]{1,0:T(8,128)S(1)}, f32[8,512]{1,0:T(8,128)S(1)}, u32[]{:S(2)}, u32[]{:S(2)}) collective-permute-start(f32[8,512]{1,0:T(8,128)S(1)} %add.35), channel_id=1, source_target_pairs={{0,3},{1,0},{2,1},{3,2},{4,7},{5,4},{6,5},{7,6},{8,11},{9,8},{10,9... | collective-permute-start | bytes 49160 | tf_op jit(solution)/shard_map/ppermute | solution.py:36
  193.1 5.4 %collective-permute-start.39 = (f32[8,512]{1,0:T(8,128)S(1)}, f32[8,512]{1,0:T(8,128)S(1)}, u32[]{:S(2)}, u32[]{:S(2)}) collective-permute-start(f32[8,512]{1,0:T(8,128)S(1)} %add.35), channel_id=1, source_target_pairs={{0,2},{1,3},{2,0},{3,1},{4,6},{5,7},{6,4},{7,5},{8,10},{9,11},{10,... | collective-permute-start | bytes 49160 | tf_op jit(solution)/shard_map/ppermute | solution.py:36
  198.5 21.3 %collective-permute-start.29 = (bf16[512,768]{1,0:T(8,128)(2,1)}, bf16[512,768]{1,0:T(8,128)(2,1)S(1)}, u32[]{:S(2)}, u32[]{:S(2)}) collective-permute-start(bf16[512,768]{1,0:T(8,128)(2,1)} %get-tuple-element.18.refs_0_), channel_id=1, source_target_pairs={{0,3},{1,0},{2,1},{3,2},{4,7},{5,4},{6,5},{7,6},{8,11},{9,8},{10,9... | collective-permute-start | bytes 2359304 | tf_op jit(solution)/shard_map/ppermute | solution.py:36
  201.5 18.3 %collective-permute-start.32 = (bf16[512,768]{1,0:T(8,128)(2,1)S(1)}, bf16[512,768]{1,0:T(8,128)(2,1)S(1)}, u32[]{:S(2)}, u32[]{:S(2)}) collective-permute-start(bf16[512,768]{1,0:T(8,128)(2,1)S(1)} %collective-permute-done.31.refs_1_), channel_id=1, source_target_pairs={{0,1},{1,2},{2,3},{3,0},{4,5},{5,6},{6,7},{7,4},{8,9},{9,10},{10,1... | collective-permute-start | bytes 2359304 | tf_op jit(solution)/shard_map/ppermute | solution.py:36
  201.5 35.0 %collective-permute-start.34 = (bf16[512,768]{1,0:T(8,128)(2,1)S(1)}, bf16[512,768]{1,0:T(8,128)(2,1)S(1)}, u32[]{:S(2)}, u32[]{:S(2)}) collective-permute-start(bf16[512,768]{1,0:T(8,128)(2,1)S(1)} %collective-permute-done.31.refs_1_), channel_id=1, source_target_pairs={{0,3},{1,0},{2,1},{3,2},{4,7},{5,4},{6,5},{7,6},{8,11},{9,8},{10,9... | collective-permute-start | bytes 2359304 | tf_op jit(solution)/shard_map/ppermute | solution.py:36
  206.6 38.5 %collective-permute-start.45 = (bf16[2,384,512]{2,1,0:T(8,128)(2,1)}, bf16[2,384,512]{2,1,0:T(8,128)(2,1)S(1)}, u32[]{:S(2)}, u32[]{:S(2)}) collective-permute-start(bf16[2,384,512]{2,1,0:T(8,128)(2,1)} %collective-permute-done.44), channel_id=1, source_target_pairs={{0,8},{1,9},{2,10},{3,11},{4,12},{5,13},{6,14},{7,15},{8,0},{9,1},... | collective-permute-start | bytes 2359304 | tf_op jit(solution)/shard_map/ppermute | solution.py:36
  219.8 35.9 %collective-permute-start.28 = (bf16[256,768]{1,0:T(8,128)(2,1)S(1)}, bf16[256,768]{1,0:T(8,128)(2,1)S(1)}, u32[]{:S(2)}, u32[]{:S(2)}) collective-permute-start(bf16[256,768]{1,0:T(8,128)(2,1)S(1)} %slice.192), channel_id=1, source_target_pairs={{0,1},{1,2},{2,3},{3,0},{4,5},{5,6},{6,7},{7,4},{8,9},{9,10},{10,1... | collective-permute-start | bytes 1179656 | tf_op jit(solution)/shard_map/ppermute | solution.py:36
  219.8 35.8 %collective-permute-start.30 = (bf16[256,768]{1,0:T(8,128)(2,1)S(1)}, bf16[256,768]{1,0:T(8,128)(2,1)S(1)}, u32[]{:S(2)}, u32[]{:S(2)}) collective-permute-start(bf16[256,768]{1,0:T(8,128)(2,1)S(1)} %slice.193), channel_id=1, source_target_pairs={{0,3},{1,0},{2,1},{3,2},{4,7},{5,4},{6,5},{7,6},{8,11},{9,8},{10,9... | collective-permute-start | bytes 1179656 | tf_op jit(solution)/shard_map/ppermute | solution.py:36
  236.5 19.1 %collective-permute-start.33 = (bf16[256,768]{1,0:T(8,128)(2,1)S(1)}, bf16[256,768]{1,0:T(8,128)(2,1)S(1)}, u32[]{:S(2)}, u32[]{:S(2)}) collective-permute-start(bf16[256,768]{1,0:T(8,128)(2,1)S(1)} %slice.194), channel_id=1, source_target_pairs={{0,1},{1,2},{2,3},{3,0},{4,5},{5,6},{6,7},{7,4},{8,9},{9,10},{10,1... | collective-permute-start | bytes 1179656 | tf_op jit(solution)/shard_map/ppermute | solution.py:36
  236.6 19.1 %collective-permute-start.35 = (bf16[256,768]{1,0:T(8,128)(2,1)S(1)}, bf16[256,768]{1,0:T(8,128)(2,1)S(1)}, u32[]{:S(2)}, u32[]{:S(2)}) collective-permute-start(bf16[256,768]{1,0:T(8,128)(2,1)S(1)} %slice.195), channel_id=1, source_target_pairs={{0,3},{1,0},{2,1},{3,2},{4,7},{5,4},{6,5},{7,6},{8,11},{9,8},{10,9... | collective-permute-start | bytes 1179656 | tf_op jit(solution)/shard_map/ppermute | solution.py:36
  259.0 15.0 %all-to-all-start = ((bf16[8,128,512]{2,1,0:T(8,128)(2,1)}), bf16[8,128,512]{2,1,0:T(8,128)(2,1)S(1)}, u32[]{:S(2)}, u32[]{:S(2)}) async-start(bf16[8,128,512]{2,1,0:T(8,128)(2,1)} %project.7), calls=%async_computation | async-start | bytes 2097152 | tf_op jit(solution)/shard_map/all_to_all | solution.py:571
  (20 other events, 280.9 us)
where the time goes:
time: 277 us; the launch traced here: 276 us
  waiting for transfers between devices  118 us (43%)
  starting transfers between devices  64.2 us (23%)
  Pallas kernels  47 us (17%)
  local copies, waits for them, and re-layouts  34.7 us (13%)
  other arithmetic  8.13 us (3%)
  between operations  3.01 us (1%)
    ppermute x46, waiting for transfers between devices, move(): return lax.ppermute(values, AXES, pairs)  108 us
    ppermute x46, starting transfers between devices, move(): return lax.ppermute(values, AXES, pairs)  60.6 us
    unnamed x54, local copies, waits for them, and re-layouts  26.8 us
    pallas_call x6, Pallas kernels, accumulate(): pl.pallas_call(functools.partial(accumulate_kernel, counts, total is not...  22.8 us
    all_to_all x1, waiting for transfers between devices, local(): lax.all_to_all(total, 'mp', split_axis=0, concat_axis=0, tiled=True)  10.7 us
    pallas_call x4, Pallas kernels, project(): pl.pallas_call(functools.partial(project_kernel, split, total is not None...  10.1 us
    pallas_call x2, Pallas kernels, out_project(): pl.pallas_call(functools.partial(out_kernel, split, total is not None, pa...  6.42 us
    pallas_call x1, Pallas kernels, norm_columns(): pl.pallas_call(norm_kernel, grid=(rows // block,), in_specs=[pl.BlockSpec...  6.14 us
  transfers between devices with their start and end apart: 47, of which 18 were waited for; matrix products, arithmetic and copies ran while one was open for 10% of the time, Pallas kernels for 15%

commit v1 on v0

v1 whole, which is shorter than its diff:
```python
import functools
import math

import jax
import jax.numpy as jnp
import numpy as np
from jax import lax
from jax.experimental import pallas as pl
from jax.experimental.pallas import tpu as pltpu
from jax.sharding import PartitionSpec as P

PATCHES = 256
HALF = 128
AXES = ("dp", "mp")
VMEM = 40 * 1024 * 1024
epsilon = 1e-06
SMALL = pl.CostEstimate(flops=1, bytes_accessed=1, transcendentals=0)


def coordinates():
    return [
        (zh, y, c, zl, x)
        for zh in range(2)
        for y in range(4)
        for c in range(2)
        for zl in range(2)
        for x in range(4)
    ]


def device_index(zh, y, c, zl, x):
    return ((zh * 4 + y) * 2 + c) * 8 + zl * 4 + x


def move(values, target):
    pairs = [(device_index(*at), device_index(*target(*at))) for at in coordinates()]
    return lax.ppermute(values, AXES, pairs)


def swap_core(values):
    return move(values, lambda zh, y, c, zl, x: (zh, y, 1 - c, zl, x))


def swap_zh(values):
    return move(values, lambda zh, y, c, zl, x: (1 - zh, y, c, zl, x))


def swap_zl(values):
    return move(values, lambda zh, y, c, zl, x: (zh, y, c, 1 - zl, x))


def spread_y(values):
    return move(values, lambda zh, y, c, zl, x: (zh, (y + 1 - 2 * c) % 4, c, zl, x))


def shift_x(values, step):
    return move(values, lambda zh, y, c, zl, x: (zh, y, c, zl, (x + step) % 4))


def transpose_mesh(values):
    return move(values, lambda zh, y, c, zl, x: (zl, x, c, zh, y))


def per_device(order):
    table = np.zeros((16, 16), np.int32)
    for zh in range(2):
        for y in range(4):
            for c in range(2):
                met = order(zh, y, c, 2 * c - 1)
                table[zh * 8 + y * 2 + c] = [r % 2 * 8 + yy % 4 * 2 + cc % 2 for r, yy, cc in met]
    return table


def early_order(zh, y, c, step):
    return [
        (zh, y, c),
        (zh, y, c + 1),
        (zh + 1, y, c),
        (zh + 1, y, c + 1),
        (zh, y + step, c),
        (zh, y - step, c + 1),
        (zh, y + step, c + 1),
        (zh, y - step, c),
        (zh + 1, y + step, c),
        (zh + 1, y - step, c + 1),
        (zh, y + 2, c),
        (zh, y + 2, c + 1),
        (zh + 1, y + step, c + 1),
        (zh + 1, y - step, c),
        (zh + 1, y + 2, c),
        (zh + 1, y + 2, c + 1),
    ]


def late_order(zh, y, c, step):
    order = []
    for yy, cores in (
        (y, (c, c + 1)),
        (y + step, (c, c + 1)),
        (y - step, (c + 1, c)),
        (y + 2, (c, c + 1)),
    ):
        for core in cores:
            order += [(zh, yy, core), (zh + 1, yy, core)]
    return order


NEAR = [(0, 0), (1, 0), (0, 1), (0, 3), (1, 1), (1, 3), (0, 2), (1, 2)]


def place_tables():
    met = per_device(late_order)
    groups = np.zeros((8, 8), np.int32)
    shards = np.zeros((16, 8, 16), np.int32)
    for mp in range(8):
        for r, (dz, dx) in enumerate(NEAR):
            group = (mp // 4 ^ dz) * 4 + (mp + dx) % 4
            groups[mp, r] = group
            for dp in range(16):
                for half in range(2):
                    shards[dp, mp, 2 * r + half] = np.argmax(met[dp] == 2 * group + half)
    return groups, shards


def norm_kernel(values_ref, gain_ref, out_ref):
    values = values_ref[...].astype(jnp.float32)
    width = values.shape[1]
    row_mean = jnp.sum(values, -1, keepdims=True) / width
    squares = jnp.sum(values * values, -1, keepdims=True) / width
    scale = lax.rsqrt(squares - row_mean * row_mean + epsilon)
    normed = ((values - row_mean) * scale * gain_ref[...]).astype(jnp.bfloat16)
    depth = out_ref.shape[2]
    for k in range(out_ref.shape[0]):
        out_ref[k] = normed[:, k * depth : (k + 1) * depth]


def norm_columns(values, gain, chunks):
    rows, width = values.shape
    block = 64
    return pl.pallas_call(
        norm_kernel,
        grid=(rows // block,),
        in_specs=[
            pl.BlockSpec((block, width), lambda i: (i, 0)),
            pl.BlockSpec((1, width), lambda i: (0, 0)),
        ],
        out_specs=pl.BlockSpec((chunks, block, width // chunks), lambda i: (0, i, 0)),
        out_shape=jax.ShapeDtypeStruct((chunks, rows, width // chunks), jnp.bfloat16),
        compiler_params=pltpu.CompilerParams(vmem_limit_bytes=VMEM),
        cost_estimate=SMALL,
        name="norm_columns",
    )(values, gain.reshape(1, width))


def row_norm(values, gain):
    row_mean = jnp.mean(values, -1, keepdims=True)
    squares = jnp.mean(values * values, -1, keepdims=True)
    return (values - row_mean) * lax.rsqrt(squares - row_mean * row_mean + epsilon) * gain


def accumulate_kernel(shard_counts, has_total, attend, index_ref, *refs):
    del index_ref
    count = sum(shard_counts)
    columns, refs = refs[:count], refs[count:]
    shards, refs = refs[: len(shard_counts)], refs[len(shard_counts) :]
    total = None
    if has_total:
        total, refs = refs[0][0], refs[1:]
    at = 0
    for held, number in zip(shards, shard_counts):
        for k in range(number):
            term = jnp.dot(columns[at][0], held[k, 0], preferred_element_type=jnp.float32)
            total = term if total is None else total + term
            at += 1
    if not attend:
        refs[0][0] = total
        return
    gain_ref, out_ref = refs
    size = gain_ref.shape[2]
    gains = gain_ref[0]
    query = row_norm(total[:, :size], gains[0:1]).astype(jnp.bfloat16)
    key = row_norm(total[:, size : 2 * size], gains[1:2]).astype(jnp.bfloat16)
    value = total[:, 2 * size :].astype(jnp.bfloat16)
    for image in range(total.shape[0] // PATCHES):
        rows = slice(image * PATCHES, (image + 1) * PATCHES)
        scores = lax.dot_general(
            query[rows], key[rows], (((1,), (1,)), ((), ())), preferred_element_type=jnp.float32
        ) / math.sqrt(size)
        raised = jnp.exp(scores - jnp.max(scores, -1, keepdims=True))
        weights = (raised / jnp.sum(raised, -1, keepdims=True)).astype(jnp.bfloat16)
        out_ref[rows, :] = jnp.dot(
            weights, value[rows], preferred_element_type=jnp.float32
        ).astype(jnp.bfloat16)


def accumulate(columns, shards, index, total=None, gains=None):
    shards = [held if held.ndim == 4 else held[None] for held in shards]
    counts = tuple(held.shape[0] for held in shards)
    _, rows, depth = columns.shape
    heads, wide = shards[0].shape[1], shards[0].shape[3]
    in_specs = [
        pl.BlockSpec((1, rows, depth), functools.partial(lambda k, h, index: (index[k], 0, 0), k))
        for k in range(sum(counts))
    ]
    in_specs += [
        pl.BlockSpec((number, 1, depth, wide), lambda h, index: (0, h, 0, 0)) for number in counts
    ]
    operands = [columns] * sum(counts) + shards
    total_spec = pl.BlockSpec((1, rows, wide), lambda h, index: (h, 0, 0))
    if total is not None:
        in_specs.append(total_spec)
        operands.append(total)
    aliases = {}
    if gains is None:
        out_spec = total_spec
        out_shape = jax.ShapeDtypeStruct((heads, rows, wide), jnp.float32)
        if total is not None:
            aliases = {len(operands): 0}
    else:
        in_specs.append(pl.BlockSpec((1, 2, wide // 3), lambda h, index: (h, 0, 0)))
        operands.append(gains)
        out_spec = pl.BlockSpec((rows, wide // 3), lambda h, index: (0, h))
        out_shape = jax.ShapeDtypeStruct((rows, heads * wide // 3), jnp.bfloat16)
    return pl.pallas_call(
        functools.partial(accumulate_kernel, counts, total is not None, gains is not None),
        grid_spec=pltpu.PrefetchScalarGridSpec(
            num_scalar_prefetch=1, grid=(heads,), in_specs=in_specs, out_specs=out_spec
        ),
        out_shape=out_shape,
        input_output_aliases=aliases,
        compiler_params=pltpu.CompilerParams(vmem_limit_bytes=VMEM),
        cost_estimate=SMALL,
        name="accumulate",
    )(index, *operands)


def load_shards(parts, held_ref, sems):
    at = 0
    copies = []
    for k, part in enumerate(parts):
        number = part.shape[0]
        copies.append(pltpu.make_async_copy(part, held_ref.at[pl.ds(at, number)], sems.at[k]))
        at += number
    for copy in copies:
        copy.start()
    for copy in copies:
        copy.wait()


def read_piece(piece, refs):
    parts = [refs[k][first:last] for k, first, last in piece]
    return parts[0] if len(parts) == 1 else jnp.concatenate(parts, 0)


def out_kernel(pieces, held, count, index_ref, *refs):
    near, refs = refs[:held], refs[held:]
    parts, refs = refs[:count], refs[count:]
    patches_ref, block_ref, stats_ref, held_ref, sems = refs
    load_shards(parts, held_ref, sems)
    depth = held_ref.shape[1]
    rows = patches_ref.shape[0]
    sums, squares = 0.0, 0.0
    for half in range(2):
        total = None
        for k, piece in enumerate(pieces):
            term = lax.dot_general(
                read_piece(piece, near),
                held_ref[index_ref[2 * k + half]],
                (((1,), (1,)), ((), ())),
                preferred_element_type=jnp.float32,
            )
            term = term.astype(jnp.bfloat16).astype(jnp.float32)
            total = term if total is None else total + term
        cols = slice(half * depth, (half + 1) * depth)
        block = (patches_ref[:, cols].astype(jnp.float32) + total).astype(jnp.bfloat16)
        block_ref[:, cols] = block
        block = block.astype(jnp.float32)
        sums += jnp.sum(block, 1, keepdims=True)
        squares += jnp.sum(block * block, 1, keepdims=True)
    lane = lax.broadcasted_iota(jnp.int32, (rows, 128), 1)
    both = jnp.where(lane == 0, sums, squares)
    stats_ref[...] = both.T[:8]


def whole(shape):
    return pl.BlockSpec(shape, lambda i, index: (0,) * len(shape))


def out_project(near, pieces, parts, index, patches):
    rows, depth = near[0].shape
    in_specs = [whole(part.shape) for part in near]
    in_specs += [pl.BlockSpec(memory_space=pl.ANY) for _ in parts]
    in_specs.append(pl.BlockSpec((rows, 2 * depth), lambda i, index: (0, index[16])))
    out_shape = [
        jax.ShapeDtypeStruct((rows, 2 * depth), jnp.bfloat16),
        jax.ShapeDtypeStruct((8, rows), jnp.float32),
    ]
    return pl.pallas_call(
        functools.partial(out_kernel, pieces, len(near), len(parts)),
        grid_spec=pltpu.PrefetchScalarGridSpec(
            num_scalar_prefetch=1,
            grid=(1,),
            in_specs=in_specs,
            out_specs=[whole(out.shape) for out in out_shape],
            scratch_shapes=[
                pltpu.VMEM((16, depth, depth), jnp.bfloat16),
                pltpu.SemaphoreType.DMA((len(parts),)),
            ],
        ),
        out_shape=out_shape,
        compiler_params=pltpu.CompilerParams(vmem_limit_bytes=VMEM),
        cost_estimate=SMALL,
        name="out_project",
    )(index, *near, *parts, patches)


def project_kernel(pieces, held, count, kept, finish, width, index_ref, *refs):
    near, refs = refs[:held], refs[held:]
    stats_ref, refs = refs[0], refs[1:]
    gains, refs = refs[: len(pieces)], refs[len(pieces) :]
    parts, refs = refs[:count], refs[count:]
    if finish:
        total, (out_ref, held_ref, sems, blocks_ref) = refs[0][...], refs[1:]
    else:
        total, (out_ref, kept_ref, held_ref, sems) = None, refs
    load_shards(parts, held_ref, sems)
    rows = stats_ref.shape[1]
    row = lax.broadcasted_iota(jnp.int32, (128, rows), 0)
    stats = jnp.where(row == 0, stats_ref[0:1], stats_ref[1:2]).T
    row_mean = stats[:, 0:1] / width
    scale = lax.rsqrt(stats[:, 1:2] / width - row_mean * row_mean + epsilon)
    depth = held_ref.shape[1]
    for k, piece in enumerate(pieces):
        values = read_piece(piece, near).astype(jnp.float32)
        normed = ((values - row_mean) * scale * gains[k][...]).astype(jnp.bfloat16)
        for half in range(2):
            at = 2 * k + half if finish else index_ref[2 * k + half]
            term = jnp.dot(
                normed[:, half * depth : (half + 1) * depth],
                held_ref[at],
                preferred_element_type=jnp.float32,
            )
            total = term if total is None else total + term
    if not finish:
        out_ref[...] = total
        for k in range(kept):
            kept_ref[k] = held_ref[index_ref[2 * len(pieces) + k]]
        return
    blocks_ref[...] = total.astype(jnp.bfloat16).reshape(blocks_ref.shape)
    for block in range(out_ref.shape[0]):
        source = index_ref[len(pieces) + block]
        value = blocks_ref[jnp.maximum(source, 0)]
        out_ref[block] = jnp.where(source >= 0, value, jnp.zeros_like(value))


def project(near, pieces, stats, gain, parts, index, kept=0, total=None):
    rows = stats.shape[1]
    width = gain.shape[0]
    depth, wide = parts[0].shape[1:]
    count = len(pieces)
    finish = total is not None
    at = 0 if finish else 2 * count + kept
    in_specs = [whole(part.shape) for part in near]
    in_specs.append(whole(stats.shape))
    in_specs += [
        pl.BlockSpec((1, 2 * depth), functools.partial(lambda k, i, index: (0, index[k]), k))
        for k in range(at, at + count)
    ]
    in_specs += [pl.BlockSpec(memory_space=pl.ANY) for _ in parts]
    operands = list(near) + [stats] + [gain.reshape(1, width)] * count + list(parts)
    scratch = [
        pltpu.VMEM((sum(part.shape[0] for part in parts), depth, wide), jnp.bfloat16),
        pltpu.SemaphoreType.DMA((len(parts),)),
    ]
    if finish:
        in_specs.append(whole(total.shape))
        operands.append(total)
        out_shape = [jax.ShapeDtypeStruct((8, HALF, wide), jnp.bfloat16)]
        scratch.append(pltpu.VMEM((rows // HALF, HALF, wide), jnp.bfloat16))
    else:
        out_shape = [
            jax.ShapeDtypeStruct((rows, wide), jnp.float32),
            jax.ShapeDtypeStruct((kept, depth, wide), jnp.bfloat16),
        ]
    return pl.pallas_call(
        functools.partial(
            project_kernel, pieces, len(near), len(parts), kept, finish, width
        ),
        grid_spec=pltpu.PrefetchScalarGridSpec(
            num_scalar_prefetch=1,
            grid=(1,),
            in_specs=in_specs,
            out_specs=[whole(out.shape) for out in out_shape],
            scratch_shapes=scratch,
        ),
        out_shape=out_shape,
        compiler_params=pltpu.CompilerParams(vmem_limit_bytes=VMEM),
        cost_estimate=SMALL,
        name="project",
    )(index, *operands)


def pack_kernel(place_ref, arrived_ref, text_ref, out_ref):
    start, first, second, length = (place_ref[k] for k in range(4))
    rows, wide = arrived_ref.shape[1:]
    covered = ((start >= first) & (start < first + PATCHES)) | (
        (start >= second) & (start < second + PATCHES)
    )

    @pl.when(covered)
    def _():
        for k in range(arrived_ref.shape[0]):
            out_ref[:, k * wide : (k + 1) * wide] = arrived_ref[k]

    @pl.when(jnp.logical_not(covered))
    def _():
        position = start + lax.broadcasted_iota(jnp.int32, (rows, wide), 0)
        before = jnp.clip(position - first, 0, PATCHES) + jnp.clip(position - second, 0, PATCHES)
        is_text = position - before < length
        for k in range(arrived_ref.shape[0]):
            text = text_ref[:, k * wide : (k + 1) * wide].astype(jnp.float32)
            out_ref[:, k * wide : (k + 1) * wide] = jnp.where(is_text, text, 0.0).astype(
                jnp.bfloat16
            )


def pack(arrived, text, place):
    return pl.pallas_call(
        pack_kernel,
        grid_spec=pltpu.PrefetchScalarGridSpec(
            num_scalar_prefetch=1,
            grid=(1,),
            in_specs=[whole(arrived.shape), whole(text.shape)],
            out_specs=whole(text.shape),
        ),
        out_shape=jax.ShapeDtypeStruct(text.shape, text.dtype),
        compiler_params=pltpu.CompilerParams(vmem_limit_bytes=VMEM),
        cost_estimate=SMALL,
        name="pack",
    )(place, arrived, text)


def join(*values):
    return lax.optimization_barrier(values)


def local(
    patches,
    norm_gain,
    qkv_weight,
    qk_gain,
    out_weight,
    final_gain,
    proj_weight,
    text_embed,
    slot_offset,
    text_len,
):
    dp = lax.axis_index("dp")
    mp = lax.axis_index("mp")
    met = jnp.asarray(per_device(early_order))[dp]
    groups, shards = place_tables()
    groups, shards = jnp.asarray(groups)[mp], jnp.asarray(shards)[dp, mp]
    mp_slot = mp[None].astype(jnp.int32)

    own = qkv_weight.transpose(1, 0, 2)
    turned = transpose_mesh(out_weight)
    (other,) = join(swap_core(own))
    first = spread_y(join(own, other)[0])
    beside = spread_y(other)
    far = swap_zh(join(own, other)[0])
    columns = norm_columns(join(patches, other)[0], norm_gain, 16)
    total = accumulate(columns, [own, other], met[0:2])

    far, first, beside, turned, total = join(far, first, beside, turned, total)
    far_first = spread_y(far)
    second = spread_y(first)
    far_other, first_other, beside_other = join(
        swap_core(far), swap_core(first), swap_core(beside)
    )
    far_beside = spread_y(far_other)
    turned_far = swap_zh(join(turned, far_other)[0])
    proj_far = swap_zh(join(proj_weight, far_other)[0])
    total = accumulate(
        columns,
        [far, far_other, first, first_other, beside, beside_other],
        met[2:8],
        total,
    )

    far_first, second, far_beside, turned_far, proj_far, total = join(
        far_first, second, far_beside, turned_far, proj_far, total
    )
    far_second = spread_y(far_first)
    far_first_other, second_other, far_beside_other = join(
        swap_core(far_first), swap_core(second), swap_core(far_beside)
    )
    out_mine = jnp.stack([turned, join(turned_far, second_other)[0]])
    proj_mine = jnp.stack([proj_weight, join(proj_far, second_other)[0]])
    out_other = swap_core(out_mine)
    proj_other = swap_core(proj_mine)
    total = accumulate(
        columns,
        [far_first, far_first_other, second, second_other, far_beside, far_beside_other],
        met[8:14],
        total,
    )

    far_second, out_other, proj_other, total = join(far_second, out_other, proj_other, total)
    far_second_other = swap_core(far_second)
    out_quad = jnp.concatenate([out_mine, out_other])
    proj_quad = jnp.concatenate([proj_mine, proj_other])
    out_first = spread_y(out_quad)
    attended = accumulate(
        columns, [far_second, far_second_other], met[14:16], total, qk_gain.transpose(1, 0, 2)
    )

    out_quad, proj_quad = join(out_quad, proj_quad)
    rows = attended.shape[0]
    half = rows // 2
    middle = rows * 9 // 16
    quarter = middle // 2
    late = middle - half
    pieces = (
        ((0, 0, rows),),
        ((1, 0, rows),),
        ((2, 0, rows),),
        ((3, 0, rows),),
        ((5, half, half + middle), (6, 0, rows - middle)),
        ((4, half, half + middle), (6, rows - middle, 2 * (rows - middle))),
        ((4, 0, half), (5, 0, half)),
        ((7, 0, quarter), (8, 0, quarter), (9, 0, rows - middle)),
    )

    def gather_first(mine):
        return [swap_zl(mine), shift_x(mine, -1), shift_x(mine, 1)]

    def gather_second(far, right, left):
        return [
            shift_x(jnp.concatenate([left[:half], far[:middle]]), 1),
            shift_x(jnp.concatenate([right[half:], far[:middle]]), -1),
            swap_zl(jnp.concatenate([right[middle:], left[middle:]])),
        ]

    def gather_third(from_left, from_right):
        return [
            shift_x(from_left[half : half + quarter], 1),
            shift_x(from_right[half + quarter :], -1),
            swap_zl(from_right[late:half]),
        ]

    near = [attended]
    *got, out_first = join(*gather_first(attended), out_first)
    near += got
    out_second = spread_y(out_first[:2])
    out_first_other = swap_core(out_first)
    *got, out_second, out_first_other = join(*gather_second(*got), out_second, out_first_other)
    near += got
    proj_first = spread_y(join(proj_quad, out_second)[0])
    out_second_other = swap_core(out_second)
    *got, out_second_other = join(*gather_third(*got[:2]), out_second_other)
    near += got
    block_out, stats = out_project(
        near,
        pieces,
        [out_quad, out_first, out_first_other, out_second, out_second_other],
        jnp.concatenate([shards, mp_slot]),
        patches,
    )

    near = [block_out]
    sent = gather_first(block_out)
    stats_x = join(shift_x(stats, 1), shift_x(stats, -1), shift_x(stats, 2))
    stats = stats + stats_x[0] + stats_x[1] + stats_x[2]
    *got, proj_first, stats = join(*sent, proj_first, stats)
    near += got
    proj_second = spread_y(proj_first[:2])
    proj_first_other = swap_core(proj_first)
    *got, proj_second, proj_first_other, stats_z = join(
        *gather_second(*got), proj_second, proj_first_other, swap_zl(stats)
    )
    near += got
    stats = stats + stats_z
    last = gather_third(*got[:2])
    proj_second_other = swap_core(proj_second)

    slot = slot_offset // HALF
    block = jnp.arange(8, dtype=jnp.int32)
    in_first = (block >= slot[0]) & (block < slot[0] + 2)
    in_second = (block >= slot[1]) & (block < slot[1] + 2)
    source = jnp.where(in_first, block - slot[0], jnp.where(in_second, block - slot[1] + 2, -1))

    total, left = project(
        near,
        pieces[:7],
        stats,
        final_gain,
        [proj_quad, proj_first, proj_first_other, proj_second, proj_second_other],
        jnp.concatenate([shards, groups[:7]]),
        kept=2,
    )
    (outgoing,) = project(
        last,
        (tuple((k - 7, first, last) for k, first, last in pieces[7]),),
        stats,
        final_gain,
        [left],
        jnp.concatenate([groups[7:], source]),
        total=total,
    )
    arrived = lax.all_to_all(outgoing, "mp", split_axis=0, concat_axis=0, tiled=True)
    place = jnp.concatenate([mp_slot * HALF, slot_offset, text_len])
    sequence = pack(arrived, text_embed[0], place)
    return (block_out, sequence[None])


def solution(mesh):
    in_specs = (
        P("dp", None),
        P(),
        P("dp", "mp", None),
        P(None, "mp", None),
        P("dp", "mp"),
        P(),
        P("dp", "mp"),
        P("dp", "mp", None),
        P("dp"),
        P("dp"),
    )
    out_specs = (P("dp", "mp"), P("dp", "mp", None))
    return jax.shard_map(local, mesh=mesh, in_specs=in_specs, out_specs=out_specs, check_vma=False)
```

time: 277 us -> 274 us (0.989)
  waiting for transfers between devices: 118 us -> 129 us
  starting transfers between devices: 64.2 us -> 54.5 us
  Pallas kernels: 47 us -> 43.6 us
  other arithmetic: 8.13 us -> 4.82 us
  local copies, waits for them, and re-layouts: 34.7 us -> 37.7 us
    ppermute x46 -> x50, starting transfers between devices: 60.6 us -> 50.8 us  [move(): return lax.ppermute(values, AXES, pairs)]
    ppermute x46 -> x50, waiting for transfers between devices: 108 us -> 114 us  [move(): return lax.ppermute(values, AXES, pairs)]
    slice x13 -> x22, local copies, waits for them, and re-layouts: 0.55 us -> 5.62 us  [the longest x2 1.87 us: gather_third(): from_left[half:half + quarter]]
    pallas_call x6 -> x4, Pallas kernels: 22.8 us -> 18.2 us  [accumulate(): pl.pallas_call(functools.partial(accumulate_kernel, counts, total is not...]
    all_to_all x1, waiting for transfers between devices: 10.7 us -> 14.7 us  [local(): lax.all_to_all(outgoing, 'mp', split_axis=0, concat_axis=0, tiled=True)]
    another operation x4 -> x2, other arithmetic: 4.06 us -> 1.1 us  [the longest x1 1.03 us: local(): out_mine = jnp.stack([turned, join(turned_far, second_other)[0]])]
    unnamed x54 -> x76, local copies, waits for them, and re-layouts: 26.8 us -> 28.1 us
    pallas_call x6 -> x3, Pallas kernels: 16.5 us -> 17.5 us  [the longest x2 9.86 us: project(): pl.pallas_call(functools.partial(project_kernel, pieces, len(near), len(p...]
  transfers between devices with their start and end apart: 47 -> 51, of which waited for: 18 -> 24; matrix products, arithmetic and copies ran while one was open for 10% -> 5% of each run, Pallas kernels for 15% -> 14%
where the time goes in v1:
time: 274 us; the launch traced here: 272 us
  waiting for transfers between devices  129 us (47%)
  starting transfers between devices  54.5 us (20%)
  Pallas kernels  43.6 us (16%)
  local copies, waits for them, and re-layouts  37.7 us (14%)
  other arithmetic  4.82 us (2%)
  between operations  3.13 us (1%)
    ppermute x50, waiting for transfers between devices, move(): return lax.ppermute(values, AXES, pairs)  114 us
    ppermute x50, starting transfers between devices, move(): return lax.ppermute(values, AXES, pairs)  50.8 us
    unnamed x76, local copies, waits for them, and re-layouts  28.1 us
    pallas_call x4, Pallas kernels, accumulate(): pl.pallas_call(functools.partial(accumulate_kernel, counts, total is not...  18.2 us
    all_to_all x1, waiting for transfers between devices, local(): lax.all_to_all(outgoing, 'mp', split_axis=0, concat_axis=0, tiled=True)  14.7 us
    pallas_call x2, Pallas kernels, project(): pl.pallas_call(functools.partial(project_kernel, pieces, len(near), len(p...  9.86 us
    pallas_call x1, Pallas kernels, out_project(): pl.pallas_call(functools.partial(out_kernel, pieces, len(near), len(parts...  7.67 us
    pallas_call x1, Pallas kernels, norm_columns(): pl.pallas_call(norm_kernel, grid=(rows // block,), in_specs=[pl.BlockSpec...  6.15 us
  transfers between devices with their start and end apart: 51, of which 24 were waited for; matrix products, arithmetic and copies ran while one was open for 5% of the time, Pallas kernels for 14%

profile of v1, /device:TPU:0, one launch (start us, length us, event | category | flops | bytes accessed | tf_op | source)
XLA Modules:
  0.0 272.4 jit_solution(3776271177291870989)
XLA Ops:
  0.7 2.6 collective-permute-done
  3.3 4.0 %collective-permute-start.1 = (bf16[3,384,384]{2,1,0:T(8,128)(2,1)}, bf16[3,384,384]{2,1,0:T(8,128)(2,1)S(1)}, u32[]{:S(2)}, u32[]{:S(2)}) collective-permute-start(bf16[3,384,384]{2,1,0:T(8,128)(2,1)} %bitcast.65), channel_id=1, source_target_pairs={{0,64},{1,65},{2,66},{3,67},{4,68},{5,69},{6,70},{7,71},{8,72},{9,... | collective-permute-start | bytes 2654216 | tf_op jit(solution)/shard_map/ppermute | solution.py:37
  7.3 1.6 collective-permute-start.2
  8.9 1.6 collective-permute-start.3
  10.5 3.8 %collective-permute-start.4 = (bf16[384,384]{1,0:T(8,128)(2,1)}, bf16[384,384]{1,0:T(8,128)(2,1)}, u32[]{:S(2)}, u32[]{:S(2)}) collective-permute-start(bf16[384,384]{1,0:T(8,128)(2,1)} %param.17), channel_id=1, source_target_pairs={{0,0},{1,16},{2,32},{3,48},{4,64},{5,80},{6,96},{7,112},{8,8},{9,2... | collective-permute-start | bytes 884744 | tf_op jit(solution)/shard_map/ppermute | solution.py:37
  15.0 2.8 %copy-done = bf16[512,6144]{1,0:T(8,128)(2,1)S(1)} copy-done((bf16[512,6144]{1,0:T(8,128)(2,1)S(1)}, bf16[512,6144]{1,0:T(8,128)(2,1)}, u32[]{:S(2)}) %copy-start) | copy-done | bytes 6291480
  18.5 6.1 %norm_columns.1.refs_0_.refs_1_.refs_2_.refs_3_.refs_4_.refs_5_ = bf16[16,512,384]{2,1,0:T(8,128)(2,1)S(1)} custom-call(bf16[512,6144]{1,0:T(8,128)(2,1)S(1)} %copy-done, f32[1,6144]{1,0:T(1,128)S(1)} %bitcast.71), custom_call_target="tpu_custom_call" | custom-call | flops 1 | bytes 1 | tf_op jit(solution)/shard_map/norm_columns/pallas_call | solution.py:140
  24.7 2.5 accumulate.4.refs_12_
  27.5 4.9 %collective-permute-done.2 = bf16[3,384,384]{2,1,0:T(8,128)(2,1)S(1)} collective-permute-done((bf16[3,384,384]{2,1,0:T(8,128)(2,1)}, bf16[3,384,384]{2,1,0:T(8,128)(2,1)S(1)}, u32[]{:S(2)}, u32[]{:S(2)}) %collective-permute-start.2) | collective-permute-done | bytes 884768 | tf_op jit(solution)/shard_map/ppermute | solution.py:37
  32.4 9.4 %collective-permute-done.3 = bf16[3,384,384]{2,1,0:T(8,128)(2,1)S(1)} collective-permute-done((bf16[3,384,384]{2,1,0:T(8,128)(2,1)S(1)}, bf16[3,384,384]{2,1,0:T(8,128)(2,1)S(1)}, u32[]{:S(2)}, u32[]{:S(2)}) %collective-permute-start.3) | collective-permute-done | bytes 884768 | tf_op jit(solution)/shard_map/ppermute | solution.py:37
  42.3 2.5 collective-permute-start.5
  45.5 1.3 collective-permute-done.9
  46.7 2.5 collective-permute-start.10
  49.2 3.5 %collective-permute-start.11 = (bf16[384,384]{1,0:T(8,128)(2,1)}, bf16[384,384]{1,0:T(8,128)(2,1)S(1)}, u32[]{:S(2)}, u32[]{:S(2)}) collective-permute-start(bf16[384,384]{1,0:T(8,128)(2,1)} %collective-permute-done.4), channel_id=1, source_target_pairs={{0,64},{1,65},{2,66},{3,67},{4,68},{5,69},{6,70},{7,71},{8,72},{9,... | collective-permute-start | bytes 884744 | tf_op jit(solution)/shard_map/ppermute | solution.py:37
  52.8 5.4 %accumulate.5.refs_12_ = f32[3,512,384]{2,1,0:T(8,128)S(1)} custom-call(s32[6]{0:T(128)S(1)} %get-tuple-element.131.index_ref, bf16[16,512,384]{2,1,0:T(8,128)(2,1)S(1)} %norm_columns.1.refs_0_.refs_1_.refs_2_.refs_3_.refs_4_.refs_5_, ...), custom_call_target="tpu_custom_call", output_to_operand_aliasing={{}: (13, {})} | custom-call | flops 1 | bytes 1 | tf_op jit(solution)/shard_map/accumulate/pallas_call | solution.py:224
  58.3 7.7 %collective-permute-done.6 = bf16[3,384,384]{2,1,0:T(8,128)(2,1)S(1)} collective-permute-done((bf16[3,384,384]{2,1,0:T(8,128)(2,1)S(1)}, bf16[3,384,384]{2,1,0:T(8,128)(2,1)S(1)}, u32[]{:S(2)}, u32[]{:S(2)}) %collective-permute-start.6) | collective-permute-done | bytes 884768 | tf_op jit(solution)/shard_map/ppermute | solution.py:37
  66.0 9.5 %collective-permute-done.10 = bf16[3,384,384]{2,1,0:T(8,128)(2,1)S(1)} collective-permute-done((bf16[3,384,384]{2,1,0:T(8,128)(2,1)S(1)}, bf16[3,384,384]{2,1,0:T(8,128)(2,1)S(1)}, u32[]{:S(2)}, u32[]{:S(2)}) %collective-permute-start.10) | collective-permute-done | bytes 884768 | tf_op jit(solution)/shard_map/ppermute | solution.py:37
  76.0 1.3 collective-permute-start.13
  77.9 1.3 collective-permute-done.15
  79.2 1.3 collective-permute-done.16
  82.2 5.4 %accumulate.6.refs_4_ = f32[3,512,384]{2,1,0:T(8,128)S(1)} custom-call(s32[6]{0:T(128)S(1)} %get-tuple-element.130.index_ref, bf16[16,512,384]{2,1,0:T(8,128)(2,1)S(1)} %norm_columns.1.refs_0_.refs_1_.refs_2_.refs_3_.refs_4_.refs_5_, ...), custom_call_target="tpu_custom_call", output_to_operand_aliasing={{}: (13, {})} | custom-call | flops 1 | bytes 1 | tf_op jit(solution)/shard_map/accumulate/pallas_call | solution.py:224
  87.7 2.6 collective-permute-done.13
  92.7 4.9 %accumulate.7.refs_0_ = bf16[512,384]{1,0:T(8,128)(2,1)S(1)} custom-call(s32[2]{0:T(128)S(1)} %get-tuple-element.133.index_ref, bf16[16,512,384]{2,1,0:T(8,128)(2,1)S(1)} %norm_columns.1.refs_0_.refs_1_.refs_2_.refs_3_.refs_4_.refs_5_, bf16[16,512,384]{2,1,0:T(8,128)(2,1)S(1)} %norm_columns.1.refs_0_.refs_1_.refs_2_.refs_3_.refs_4_.refs_5_, ...), custom_call_target="tpu_custom_call" | custom-call | flops 1 | bytes 1 | tf_op jit(solution)/shard_map/accumulate/pallas_call | solution.py:224
  99.4 1.3 collective-permute-start.22
  100.7 8.4 %collective-permute-done.23.refs_11_ = bf16[4,384,384]{2,1,0:T(8,128)(2,1)S(1)} collective-permute-done((bf16[4,384,384]{2,1,0:T(8,128)(2,1)S(1)}, bf16[4,384,384]{2,1,0:T(8,128)(2,1)S(1)}, u32[]{:S(2)}, u32[]{:S(2)}) %collective-permute-start.23) | collective-permute-done | bytes 1179680 | tf_op jit(solution)/shard_map/ppermute | solution.py:37
  109.5 2.7 collective-permute-done.22.refs_3_
  113.3 3.2 %collective-permute-start.25 = (bf16[544,384]{1,0:T(8,128)(2,1)S(1)}, bf16[544,384]{1,0:T(8,128)(2,1)S(1)}, u32[]{:S(2)}, u32[]{:S(2)}) collective-permute-start(bf16[544,384]{1,0:T(8,128)(2,1)S(1)} %get-tuple-element.126), channel_id=1, source_target_pairs={{0,3},{1,0},{2,1},{3,2},{4,7},{5,4},{6,5},{7,6},{8,11},{9,8},{10,9... | collective-permute-start | bytes 1253384 | tf_op jit(solution)/shard_map/ppermute | solution.py:37
  117.8 8.8 %collective-permute-done.26.refs_6_ = bf16[448,384]{1,0:T(8,128)(2,1)S(1)} collective-permute-done((bf16[448,384]{1,0:T(8,128)(2,1)S(1)}, bf16[448,384]{1,0:T(8,128)(2,1)S(1)}, u32[]{:S(2)}, u32[]{:S(2)}) %collective-permute-start.26) | collective-permute-done | bytes 344096 | tf_op jit(solution)/shard_map/ppermute | solution.py:37
  134.9 3.2 %collective-permute-start.30 = (bf16[144,384]{1,0:T(8,128)(2,1)S(1)}, bf16[144,384]{1,0:T(8,128)(2,1)S(1)}, u32[]{:S(2)}, u32[]{:S(2)}) collective-permute-start(bf16[144,384]{1,0:T(8,128)(2,1)S(1)} %slice.117), channel_id=1, source_target_pairs={{0,3},{1,0},{2,1},{3,2},{4,7},{5,4},{6,5},{7,6},{8,11},{9,8},{10,9... | collective-permute-start | bytes 331784 | tf_op jit(solution)/shard_map/ppermute | solution.py:37
  138.2 3.1 %collective-permute-done.29.refs_7_ = bf16[144,384]{1,0:T(8,128)(2,1)S(1)} collective-permute-done((bf16[144,384]{1,0:T(8,128)(2,1)S(1)}, bf16[144,384]{1,0:T(8,128)(2,1)S(1)}, u32[]{:S(2)}, u32[]{:S(2)}) %collective-permute-start.29) | collective-permute-done | bytes 110624 | tf_op jit(solution)/shard_map/ppermute | solution.py:37
  141.3 2.8 %copy-done.1 = bf16[512,6144]{1,0:T(8,128)(2,1)S(1)} copy-done((bf16[512,6144]{1,0:T(8,128)(2,1)S(1)}, bf16[512,6144]{1,0:T(8,128)(2,1)}, u32[]{:S(2)}) %copy-start.1) | copy-done | bytes 6291480
  144.0 1.3 copy-done.7
  146.3 1.3 copy-done.20
  151.6 7.7 %out_project.1 = (bf16[512,768]{1,0:T(8,128)(2,1)}, f32[8,512]{1,0:T(8,128)S(1)}) custom-call(s32[17]{0:T(128)S(1)} %pad_add_fusion.index_ref, bf16[512,384]{1,0:T(8,128)(2,1)S(1)} %accumulate.7.refs_0_, bf16[512,384]{1,0:T(8,128)(2,1)S(1)} %copy-done.25, bf16[512,384]{1,0:T(8,128)(2,1)S(1)} %collective-permute-done.21.refs_2_, ...), custom_call_target="tpu_custom_call" | custom-call | flops 1 | bytes 1 | tf_op jit(solution)/shard_map/out_project/pallas_call | solution.py:298
  160.3 3.0 %collective-permute-start.34 = (bf16[512,768]{1,0:T(8,128)(2,1)}, bf16[512,768]{1,0:T(8,128)(2,1)S(1)}, u32[]{:S(2)}, u32[]{:S(2)}) collective-permute-start(bf16[512,768]{1,0:T(8,128)(2,1)} %get-tuple-element.61.refs_0_), channel_id=1, source_target_pairs={{0,3},{1,0},{2,1},{3,2},{4,7},{5,4},{6,5},{7,6},{8,11},{9,8},{10,9... | collective-permute-start | bytes 2359304 | tf_op jit(solution)/shard_map/ppermute | solution.py:37
  163.3 19.8 %collective-permute-done.37 = f32[8,512]{1,0:T(8,128)S(1)} collective-permute-done((f32[8,512]{1,0:T(8,128)S(1)}, f32[8,512]{1,0:T(8,128)S(1)}, u32[]{:S(2)}, u32[]{:S(2)}) %collective-permute-start.37) | collective-permute-done | bytes 16416 | tf_op jit(solution)/shard_map/ppermute | solution.py:37
  183.1 3.7 %collective-permute-done.38 = f32[8,512]{1,0:T(8,128)S(1)} collective-permute-done((f32[8,512]{1,0:T(8,128)S(1)}, f32[8,512]{1,0:T(8,128)S(1)}, u32[]{:S(2)}, u32[]{:S(2)}) %collective-permute-start.38) | collective-permute-done | bytes 16416 | tf_op jit(solution)/shard_map/ppermute | solution.py:37
  186.9 5.2 %collective-permute-done.39 = f32[8,512]{1,0:T(8,128)S(1)} collective-permute-done((f32[8,512]{1,0:T(8,128)S(1)}, f32[8,512]{1,0:T(8,128)S(1)}, u32[]{:S(2)}, u32[]{:S(2)}) %collective-permute-start.39) | collective-permute-done | bytes 16416 | tf_op jit(solution)/shard_map/ppermute | solution.py:37
  193.7 3.2 %collective-permute-start.41 = (bf16[544,768]{1,0:T(8,128)(2,1)S(1)}, bf16[544,768]{1,0:T(8,128)(2,1)S(1)}, u32[]{:S(2)}, u32[]{:S(2)}) collective-permute-start(bf16[544,768]{1,0:T(8,128)(2,1)S(1)} %get-tuple-element.124), channel_id=1, source_target_pairs={{0,3},{1,0},{2,1},{3,2},{4,7},{5,4},{6,5},{7,6},{8,11},{9,8},{10,9... | collective-permute-start | bytes 2506760 | tf_op jit(solution)/shard_map/ppermute | solution.py:37
  199.9 2.8 %collective-permute-done.45 = f32[8,512]{1,0:T(8,128)S(1)} collective-permute-done((f32[8,512]{1,0:T(8,128)S(1)}, f32[8,512]{1,0:T(8,128)S(1)}, u32[]{:S(2)}, u32[]{:S(2)}) %collective-permute-start.45) | collective-permute-done | bytes 16416 | tf_op jit(solution)/shard_map/ppermute | solution.py:37
  204.3 15.8 %collective-permute-done.42.refs_6_ = bf16[448,768]{1,0:T(8,128)(2,1)S(1)} collective-permute-done((bf16[448,768]{1,0:T(8,128)(2,1)S(1)}, bf16[448,768]{1,0:T(8,128)(2,1)S(1)}, u32[]{:S(2)}, u32[]{:S(2)}) %collective-permute-start.42) | collective-permute-done | bytes 688160 | tf_op jit(solution)/shard_map/ppermute | solution.py:37
  228.2 3.2 %collective-permute-start.47 = (bf16[144,768]{1,0:T(8,128)(2,1)S(1)}, bf16[144,768]{1,0:T(8,128)(2,1)S(1)}, u32[]{:S(2)}, u32[]{:S(2)}) collective-permute-start(bf16[144,768]{1,0:T(8,128)(2,1)S(1)} %slice.130), channel_id=1, source_target_pairs={{0,3},{1,0},{2,1},{3,2},{4,7},{5,4},{6,5},{7,6},{8,11},{9,8},{10,9... | collective-permute-start | bytes 663560 | tf_op jit(solution)/shard_map/ppermute | solution.py:37
  236.9 1.4 copy-done.13
  241.6 7.0 %project.2 = (f32[512,512]{1,0:T(8,128)S(1)}, bf16[2,384,512]{2,1,0:T(8,128)(2,1)S(1)}) custom-call(s32[23]{0:T(128)S(1)} %pad_add_fusion.3.index_ref, bf16[512,768]{1,0:T(8,128)(2,1)S(1)} %copy-done.27, bf16[512,768]{1,0:T(8,128)(2,1)S(1)} %copy-done.11, bf16[512,768]{1,0:T(8,128)(2,1)S(1)} %copy-done.3, bf16[512,768]{1,0:T(8,128)(2,1)S(1)} %copy-done.5, ...), custom_call_target="tpu_custom_call" | custom-call | flops 1 | bytes 1 | tf_op jit(solution)/shard_map/project/pallas_call | solution.py:385
  248.7 2.9 %project.3 = bf16[8,128,512]{2,1,0:T(8,128)(2,1)} custom-call(s32[9]{0:T(128)S(1)} %pad_add_fusion.2.index_ref, bf16[144,768]{1,0:T(8,128)(2,1)S(1)} %collective-permute-done.46.refs_0_, bf16[144,768]{1,0:T(8,128)(2,1)S(1)} %collective-permute-done.47.refs_1_, bf16[224,768]{1,0:T(8,128)(2,1)S(1)} %collective-permute-done.48.refs_2_, ...), custom_call_target="tpu_custom_call" | custom-call | flops 1 | bytes 1 | tf_op jit(solution)/shard_map/project/pallas_call | solution.py:385
  251.6 3.7 %all-to-all-start = ((bf16[8,128,512]{2,1,0:T(8,128)(2,1)}), bf16[8,128,512]{2,1,0:T(8,128)(2,1)S(1)}, u32[]{:S(2)}, u32[]{:S(2)}) async-start(bf16[8,128,512]{2,1,0:T(8,128)(2,1)} %project.3), calls=%async_computation | async-start | bytes 2097152 | tf_op jit(solution)/shard_map/all_to_all | solution.py:611
  256.0 14.7 %all-to-all-done.arrived_ref = bf16[8,128,512]{2,1,0:T(8,128)(2,1)S(1)} async-done(((bf16[8,128,512]{2,1,0:T(8,128)(2,1)}), bf16[8,128,512]{2,1,0:T(8,128)(2,1)S(1)}, u32[]{:S(2)}, u32[]{:S(2)}) %all-to-all-start) | async-done | bytes 1048608 | tf_op jit(solution)/shard_map/all_to_all | solution.py:611
  270.7 1.7 pack.1
  (183 shorter events, 49.1 us)
Async XLA Ops:
  3.3 24.1 %collective-permute-start.1 = (bf16[3,384,384]{2,1,0:T(8,128)(2,1)}, bf16[3,384,384]{2,1,0:T(8,128)(2,1)S(1)}, u32[]{:S(2)}, u32[]{:S(2)}) collective-permute-start(bf16[3,384,384]{2,1,0:T(8,128)(2,1)} %bitcast.65), channel_id=1, source_target_pairs={{0,64},{1,65},{2,66},{3,67},{4,68},{5,69},{6,70},{7,71},{8,72},{9,... | collective-permute-start | bytes 2654216 | tf_op jit(solution)/shard_map/ppermute | solution.py:37
  7.3 25.1 %collective-permute-start.2 = (bf16[3,384,384]{2,1,0:T(8,128)(2,1)}, bf16[3,384,384]{2,1,0:T(8,128)(2,1)S(1)}, u32[]{:S(2)}, u32[]{:S(2)}) collective-permute-start(bf16[3,384,384]{2,1,0:T(8,128)(2,1)} %bitcast.66), channel_id=1, source_target_pairs={{0,16},{1,17},{2,18},{3,19},{4,20},{5,21},{6,22},{7,23},{8,56},{9,... | collective-permute-start | bytes 2654216 | tf_op jit(solution)/shard_map/ppermute | solution.py:37
  8.9 32.9 %collective-permute-start.3 = (bf16[3,384,384]{2,1,0:T(8,128)(2,1)S(1)}, bf16[3,384,384]{2,1,0:T(8,128)(2,1)S(1)}, u32[]{:S(2)}, u32[]{:S(2)}) collective-permute-start(bf16[3,384,384]{2,1,0:T(8,128)(2,1)S(1)} %collective-permute-done), channel_id=1, source_target_pairs={{0,16},{1,17},{2,18},{3,19},{4,20},{5,21},{6,22},{7,23},{8,56},{9,... | collective-permute-start | bytes 2654216 | tf_op jit(solution)/shard_map/ppermute | solution.py:37
  10.5 16.7 %collective-permute-start.4 = (bf16[384,384]{1,0:T(8,128)(2,1)}, bf16[384,384]{1,0:T(8,128)(2,1)}, u32[]{:S(2)}, u32[]{:S(2)}) collective-permute-start(bf16[384,384]{1,0:T(8,128)(2,1)} %param.17), channel_id=1, source_target_pairs={{0,0},{1,16},{2,32},{3,48},{4,64},{5,80},{6,96},{7,112},{8,8},{9,2... | collective-permute-start | bytes 884744 | tf_op jit(solution)/shard_map/ppermute | solution.py:37
  41.8 3.0 %collective-permute-start.7 = (bf16[3,384,384]{2,1,0:T(8,128)(2,1)S(1)}, bf16[3,384,384]{2,1,0:T(8,128)(2,1)S(1)}, u32[]{:S(2)}, u32[]{:S(2)}) collective-permute-start(bf16[3,384,384]{2,1,0:T(8,128)(2,1)S(1)} %collective-permute-done.1), channel_id=1, source_target_pairs={{0,8},{1,9},{2,10},{3,11},{4,12},{5,13},{6,14},{7,15},{8,0},{9,1},... | collective-permute-start | bytes 2654216 | tf_op jit(solution)/shard_map/ppermute | solution.py:37
  41.8 3.7 %collective-permute-start.8 = (bf16[3,384,384]{2,1,0:T(8,128)(2,1)S(1)}, bf16[3,384,384]{2,1,0:T(8,128)(2,1)S(1)}, u32[]{:S(2)}, u32[]{:S(2)}) collective-permute-start(bf16[3,384,384]{2,1,0:T(8,128)(2,1)S(1)} %collective-permute-done.2), channel_id=1, source_target_pairs={{0,8},{1,9},{2,10},{3,11},{4,12},{5,13},{6,14},{7,15},{8,0},{9,1},... | collective-permute-start | bytes 2654216 | tf_op jit(solution)/shard_map/ppermute | solution.py:37
  42.3 4.4 %collective-permute-start.9 = (bf16[3,384,384]{2,1,0:T(8,128)(2,1)S(1)}, bf16[3,384,384]{2,1,0:T(8,128)(2,1)S(1)}, u32[]{:S(2)}, u32[]{:S(2)}) collective-permute-start(bf16[3,384,384]{2,1,0:T(8,128)(2,1)S(1)} %collective-permute-done.3), channel_id=1, source_target_pairs={{0,8},{1,9},{2,10},{3,11},{4,12},{5,13},{6,14},{7,15},{8,0},{9,1},... | collective-permute-start | bytes 2654216 | tf_op jit(solution)/shard_map/ppermute | solution.py:37
  42.3 16.0 %collective-permute-start.5 = (bf16[3,384,384]{2,1,0:T(8,128)(2,1)S(1)}, bf16[3,384,384]{2,1,0:T(8,128)(2,1)S(1)}, u32[]{:S(2)}, u32[]{:S(2)}) collective-permute-start(bf16[3,384,384]{2,1,0:T(8,128)(2,1)S(1)} %collective-permute-done.1), channel_id=1, source_target_pairs={{0,16},{1,17},{2,18},{3,19},{4,20},{5,21},{6,22},{7,23},{8,56},{9,... | collective-permute-start | bytes 2654216 | tf_op jit(solution)/shard_map/ppermute | solution.py:37
  44.8 21.3 %collective-permute-start.6 = (bf16[3,384,384]{2,1,0:T(8,128)(2,1)S(1)}, bf16[3,384,384]{2,1,0:T(8,128)(2,1)S(1)}, u32[]{:S(2)}, u32[]{:S(2)}) collective-permute-start(bf16[3,384,384]{2,1,0:T(8,128)(2,1)S(1)} %collective-permute-done.2), channel_id=1, source_target_pairs={{0,16},{1,17},{2,18},{3,19},{4,20},{5,21},{6,22},{7,23},{8,56},{9,... | collective-permute-start | bytes 2654216 | tf_op jit(solution)/shard_map/ppermute | solution.py:37
  46.7 28.8 %collective-permute-start.10 = (bf16[3,384,384]{2,1,0:T(8,128)(2,1)S(1)}, bf16[3,384,384]{2,1,0:T(8,128)(2,1)S(1)}, u32[]{:S(2)}, u32[]{:S(2)}) collective-permute-start(bf16[3,384,384]{2,1,0:T(8,128)(2,1)S(1)} %collective-permute-done.7), channel_id=1, source_target_pairs={{0,16},{1,17},{2,18},{3,19},{4,20},{5,21},{6,22},{7,23},{8,56},{9,... | collective-permute-start | bytes 2654216 | tf_op jit(solution)/shard_map/ppermute | solution.py:37
  49.2 16.8 %collective-permute-start.12 = (bf16[384,512]{1,0:T(8,128)(2,1)S(1)}, bf16[384,512]{1,0:T(8,128)(2,1)S(1)}, u32[]{:S(2)}, u32[]{:S(2)}) collective-permute-start(bf16[384,512]{1,0:T(8,128)(2,1)S(1)} %copy-done.36), channel_id=1, source_target_pairs={{0,64},{1,65},{2,66},{3,67},{4,68},{5,69},{6,70},{7,71},{8,72},{9,... | collective-permute-start | bytes 1179656 | tf_op jit(solution)/shard_map/ppermute | solution.py:37
  49.2 16.8 %collective-permute-start.11 = (bf16[384,384]{1,0:T(8,128)(2,1)}, bf16[384,384]{1,0:T(8,128)(2,1)S(1)}, u32[]{:S(2)}, u32[]{:S(2)}) collective-permute-start(bf16[384,384]{1,0:T(8,128)(2,1)} %collective-permute-done.4), channel_id=1, source_target_pairs={{0,64},{1,65},{2,66},{3,67},{4,68},{5,69},{6,70},{7,71},{8,72},{9,... | collective-permute-start | bytes 884744 | tf_op jit(solution)/shard_map/ppermute | solution.py:37
  75.5 3.7 %collective-permute-start.15 = (bf16[3,384,384]{2,1,0:T(8,128)(2,1)S(1)}, bf16[3,384,384]{2,1,0:T(8,128)(2,1)S(1)}, u32[]{:S(2)}, u32[]{:S(2)}) collective-permute-start(bf16[3,384,384]{2,1,0:T(8,128)(2,1)S(1)} %collective-permute-done.6), channel_id=1, source_target_pairs={{0,8},{1,9},{2,10},{3,11},{4,12},{5,13},{6,14},{7,15},{8,0},{9,1},... | collective-permute-start | bytes 2654216 | tf_op jit(solution)/shard_map/ppermute | solution.py:37
  76.0 4.4 %collective-permute-start.16 = (bf16[3,384,384]{2,1,0:T(8,128)(2,1)S(1)}, bf16[3,384,384]{2,1,0:T(8,128)(2,1)S(1)}, u32[]{:S(2)}, u32[]{:S(2)}) collective-permute-start(bf16[3,384,384]{2,1,0:T(8,128)(2,1)S(1)} %collective-permute-done.10), channel_id=1, source_target_pairs={{0,8},{1,9},{2,10},{3,11},{4,12},{5,13},{6,14},{7,15},{8,0},{9,1},... | collective-permute-start | bytes 2654216 | tf_op jit(solution)/shard_map/ppermute | solution.py:37
  76.0 14.3 %collective-permute-start.13 = (bf16[3,384,384]{2,1,0:T(8,128)(2,1)S(1)}, bf16[3,384,384]{2,1,0:T(8,128)(2,1)S(1)}, u32[]{:S(2)}, u32[]{:S(2)}) collective-permute-start(bf16[3,384,384]{2,1,0:T(8,128)(2,1)S(1)} %collective-permute-done.5), channel_id=1, source_target_pairs={{0,16},{1,17},{2,18},{3,19},{4,20},{5,21},{6,22},{7,23},{8,56},{9,... | collective-permute-start | bytes 2654216 | tf_op jit(solution)/shard_map/ppermute | solution.py:37
  80.5 9.7 %collective-permute-start.18 = (bf16[2,384,512]{2,1,0:T(8,128)(2,1)S(1)}, bf16[2,384,512]{2,1,0:T(8,128)(2,1)S(1)}, u32[]{:S(2)}, u32[]{:S(2)}) collective-permute-start(bf16[2,384,512]{2,1,0:T(8,128)(2,1)S(1)} %pad_maximum_fusion.4), channel_id=1, source_target_pairs={{0,8},{1,9},{2,10},{3,11},{4,12},{5,13},{6,14},{7,15},{8,0},{9,1},... | collective-permute-start | bytes 2359304 | tf_op jit(solution)/shard_map/ppermute | solution.py:37
  81.8 8.5 %collective-permute-start.17 = (bf16[2,384,384]{2,1,0:T(8,128)(2,1)S(1)}, bf16[2,384,384]{2,1,0:T(8,128)(2,1)S(1)}, u32[]{:S(2)}, u32[]{:S(2)}) collective-permute-start(bf16[2,384,384]{2,1,0:T(8,128)(2,1)S(1)} %pad_maximum_fusion.6), channel_id=1, source_target_pairs={{0,8},{1,9},{2,10},{3,11},{4,12},{5,13},{6,14},{7,15},{8,0},{9,1},... | collective-permute-start | bytes 1769480 | tf_op jit(solution)/shard_map/ppermute | solution.py:37
  91.4 17.7 %collective-permute-start.23 = (bf16[4,384,384]{2,1,0:T(8,128)(2,1)S(1)}, bf16[4,384,384]{2,1,0:T(8,128)(2,1)S(1)}, u32[]{:S(2)}, u32[]{:S(2)}) collective-permute-start(bf16[4,384,384]{2,1,0:T(8,128)(2,1)S(1)} %pad_maximum_fusion.1.refs_10_), channel_id=1, source_target_pairs={{0,16},{1,17},{2,18},{3,19},{4,20},{5,21},{6,22},{7,23},{8,56},{9,... | collective-permute-start | bytes 3538952 | tf_op jit(solution)/shard_map/ppermute | solution.py:37
  97.6 11.5 %collective-permute-start.20 = (bf16[512,384]{1,0:T(8,128)(2,1)S(1)}, bf16[512,384]{1,0:T(8,128)(2,1)S(1)}, u32[]{:S(2)}, u32[]{:S(2)}) collective-permute-start(bf16[512,384]{1,0:T(8,128)(2,1)S(1)} %accumulate.7.refs_0_), channel_id=1, source_target_pairs={{0,4},{1,5},{2,6},{3,7},{4,0},{5,1},{6,2},{7,3},{8,12},{9,13},{10,... | collective-permute-start | bytes 1179656 | tf_op jit(solution)/shard_map/ppermute | solution.py:37
  98.7 10.9 %collective-permute-start.21 = (bf16[512,384]{1,0:T(8,128)(2,1)S(1)}, bf16[512,384]{1,0:T(8,128)(2,1)S(1)}, u32[]{:S(2)}, u32[]{:S(2)}) collective-permute-start(bf16[512,384]{1,0:T(8,128)(2,1)S(1)} %accumulate.7.refs_0_), channel_id=1, source_target_pairs={{0,3},{1,0},{2,1},{3,2},{4,7},{5,4},{6,5},{7,6},{8,11},{9,8},{10,9... | collective-permute-start | bytes 1179656 | tf_op jit(solution)/shard_map/ppermute | solution.py:37
  99.4 12.8 %collective-permute-start.22 = (bf16[512,384]{1,0:T(8,128)(2,1)S(1)}, bf16[512,384]{1,0:T(8,128)(2,1)S(1)}, u32[]{:S(2)}, u32[]{:S(2)}) collective-permute-start(bf16[512,384]{1,0:T(8,128)(2,1)S(1)} %accumulate.7.refs_0_), channel_id=1, source_target_pairs={{0,1},{1,2},{2,3},{3,0},{4,5},{5,6},{6,7},{7,4},{8,9},{9,10},{10,1... | collective-permute-start | bytes 1179656 | tf_op jit(solution)/shard_map/ppermute | solution.py:37
  112.2 15.2 %collective-permute-start.28 = (bf16[4,384,384]{2,1,0:T(8,128)(2,1)S(1)}, bf16[4,384,384]{2,1,0:T(8,128)(2,1)S(1)}, u32[]{:S(2)}, u32[]{:S(2)}) collective-permute-start(bf16[4,384,384]{2,1,0:T(8,128)(2,1)S(1)} %collective-permute-done.23.refs_11_), channel_id=1, source_target_pairs={{0,8},{1,9},{2,10},{3,11},{4,12},{5,13},{6,14},{7,15},{8,0},{9,1},... | collective-permute-start | bytes 3538952 | tf_op jit(solution)/shard_map/ppermute | solution.py:37
  112.4 15.0 %collective-permute-start.27 = (bf16[2,384,384]{2,1,0:T(8,128)(2,1)S(1)}, bf16[2,384,384]{2,1,0:T(8,128)(2,1)}, u32[]{:S(2)}, u32[]{:S(2)}) collective-permute-start(bf16[2,384,384]{2,1,0:T(8,128)(2,1)S(1)} %slice.115), channel_id=1, source_target_pairs={{0,16},{1,17},{2,18},{3,19},{4,20},{5,21},{6,22},{7,23},{8,56},{9,... | collective-permute-start | bytes 1769480 | tf_op jit(solution)/shard_map/ppermute | solution.py:37
  113.2 14.1 %collective-permute-start.24 = (bf16[544,384]{1,0:T(8,128)(2,1)S(1)}, bf16[544,384]{1,0:T(8,128)(2,1)S(1)}, u32[]{:S(2)}, u32[]{:S(2)}) collective-permute-start(bf16[544,384]{1,0:T(8,128)(2,1)S(1)} %get-tuple-element.127), channel_id=1, source_target_pairs={{0,1},{1,2},{2,3},{3,0},{4,5},{5,6},{6,7},{7,4},{8,9},{9,10},{10,1... | collective-permute-start | bytes 1253384 | tf_op jit(solution)/shard_map/ppermute | solution.py:37
  113.3 14.1 %collective-permute-start.25 = (bf16[544,384]{1,0:T(8,128)(2,1)S(1)}, bf16[544,384]{1,0:T(8,128)(2,1)S(1)}, u32[]{:S(2)}, u32[]{:S(2)}) collective-permute-start(bf16[544,384]{1,0:T(8,128)(2,1)S(1)} %get-tuple-element.126), channel_id=1, source_target_pairs={{0,3},{1,0},{2,1},{3,2},{4,7},{5,4},{6,5},{7,6},{8,11},{9,8},{10,9... | collective-permute-start | bytes 1253384 | tf_op jit(solution)/shard_map/ppermute | solution.py:37
  116.6 10.1 %collective-permute-start.26 = (bf16[448,384]{1,0:T(8,128)(2,1)S(1)}, bf16[448,384]{1,0:T(8,128)(2,1)S(1)}, u32[]{:S(2)}, u32[]{:S(2)}) collective-permute-start(bf16[448,384]{1,0:T(8,128)(2,1)S(1)} %pad_maximum_fusion.9), channel_id=1, source_target_pairs={{0,4},{1,5},{2,6},{3,7},{4,0},{5,1},{6,2},{7,3},{8,12},{9,13},{10,... | collective-permute-start | bytes 1032200 | tf_op jit(solution)/shard_map/ppermute | solution.py:37
  129.2 63.0 %collective-permute-start.36 = (bf16[4,384,512]{2,1,0:T(8,128)(2,1)S(1)}, bf16[4,384,512]{2,1,0:T(8,128)(2,1)}, u32[]{:S(2)}, u32[]{:S(2)}) collective-permute-start(bf16[4,384,512]{2,1,0:T(8,128)(2,1)S(1)} %pad_maximum_fusion.refs_15_), channel_id=1, source_target_pairs={{0,16},{1,17},{2,18},{3,19},{4,20},{5,21},{6,22},{7,23},{8,56},{9,... | collective-permute-start | bytes 4718600 | tf_op jit(solution)/shard_map/ppermute | solution.py:37
  130.2 11.0 %collective-permute-start.32 = (bf16[2,384,384]{2,1,0:T(8,128)(2,1)}, bf16[2,384,384]{2,1,0:T(8,128)(2,1)}, u32[]{:S(2)}, u32[]{:S(2)}) collective-permute-start(bf16[2,384,384]{2,1,0:T(8,128)(2,1)} %collective-permute-done.27.refs_13_), channel_id=1, source_target_pairs={{0,8},{1,9},{2,10},{3,11},{4,12},{5,13},{6,14},{7,15},{8,0},{9,1},... | collective-permute-start | bytes 1769480 | tf_op jit(solution)/shard_map/ppermute | solution.py:37
  131.2 10.1 %collective-permute-start.31 = (bf16[224,384]{1,0:T(8,128)(2,1)S(1)}, bf16[224,384]{1,0:T(8,128)(2,1)S(1)}, u32[]{:S(2)}, u32[]{:S(2)}) collective-permute-start(bf16[224,384]{1,0:T(8,128)(2,1)S(1)} %slice.118), channel_id=1, source_target_pairs={{0,4},{1,5},{2,6},{3,7},{4,0},{5,1},{6,2},{7,3},{8,12},{9,13},{10,... | collective-permute-start | bytes 516104 | tf_op jit(solution)/shard_map/ppermute | solution.py:37
  134.8 6.5 %collective-permute-start.29 = (bf16[144,384]{1,0:T(8,128)(2,1)S(1)}, bf16[144,384]{1,0:T(8,128)(2,1)S(1)}, u32[]{:S(2)}, u32[]{:S(2)}) collective-permute-start(bf16[144,384]{1,0:T(8,128)(2,1)S(1)} %slice.116), channel_id=1, source_target_pairs={{0,1},{1,2},{2,3},{3,0},{4,5},{5,6},{6,7},{7,4},{8,9},{9,10},{10,1... | collective-permute-start | bytes 331784 | tf_op jit(solution)/shard_map/ppermute | solution.py:37
  134.9 6.4 %collective-permute-start.30 = (bf16[144,384]{1,0:T(8,128)(2,1)S(1)}, bf16[144,384]{1,0:T(8,128)(2,1)S(1)}, u32[]{:S(2)}, u32[]{:S(2)}) collective-permute-start(bf16[144,384]{1,0:T(8,128)(2,1)S(1)} %slice.117), channel_id=1, source_target_pairs={{0,3},{1,0},{2,1},{3,2},{4,7},{5,4},{6,5},{7,6},{8,11},{9,8},{10,9... | collective-permute-start | bytes 331784 | tf_op jit(solution)/shard_map/ppermute | solution.py:37
  159.2 32.9 %collective-permute-start.33 = (bf16[512,768]{1,0:T(8,128)(2,1)}, bf16[512,768]{1,0:T(8,128)(2,1)S(1)}, u32[]{:S(2)}, u32[]{:S(2)}) collective-permute-start(bf16[512,768]{1,0:T(8,128)(2,1)} %get-tuple-element.61.refs_0_), channel_id=1, source_target_pairs={{0,4},{1,5},{2,6},{3,7},{4,0},{5,1},{6,2},{7,3},{8,12},{9,13},{10,... | collective-permute-start | bytes 2359304 | tf_op jit(solution)/shard_map/ppermute | solution.py:37
  160.3 31.8 %collective-permute-start.34 = (bf16[512,768]{1,0:T(8,128)(2,1)}, bf16[512,768]{1,0:T(8,128)(2,1)S(1)}, u32[]{:S(2)}, u32[]{:S(2)}) collective-permute-start(bf16[512,768]{1,0:T(8,128)(2,1)} %get-tuple-element.61.refs_0_), channel_id=1, source_target_pairs={{0,3},{1,0},{2,1},{3,2},{4,7},{5,4},{6,5},{7,6},{8,11},{9,8},{10,9... | collective-permute-start | bytes 2359304 | tf_op jit(solution)/shard_map/ppermute | solution.py:37
  163.3 28.9 %collective-permute-start.35 = (bf16[512,768]{1,0:T(8,128)(2,1)}, bf16[512,768]{1,0:T(8,128)(2,1)S(1)}, u32[]{:S(2)}, u32[]{:S(2)}) collective-permute-start(bf16[512,768]{1,0:T(8,128)(2,1)} %get-tuple-element.61.refs_0_), channel_id=1, source_target_pairs={{0,1},{1,2},{2,3},{3,0},{4,5},{5,6},{6,7},{7,4},{8,9},{9,10},{10,1... | collective-permute-start | bytes 2359304 | tf_op jit(solution)/shard_map/ppermute | solution.py:37
  163.3 19.8 %collective-permute-start.37 = (f32[8,512]{1,0:T(8,128)S(1)}, f32[8,512]{1,0:T(8,128)S(1)}, u32[]{:S(2)}, u32[]{:S(2)}) collective-permute-start(f32[8,512]{1,0:T(8,128)S(1)} %get-tuple-element.107), channel_id=1, source_target_pairs={{0,1},{1,2},{2,3},{3,0},{4,5},{5,6},{6,7},{7,4},{8,9},{9,10},{10,1... | collective-permute-start | bytes 49160 | tf_op jit(solution)/shard_map/ppermute | solution.py:37
  183.1 3.7 %collective-permute-start.38 = (f32[8,512]{1,0:T(8,128)S(1)}, f32[8,512]{1,0:T(8,128)S(1)}, u32[]{:S(2)}, u32[]{:S(2)}) collective-permute-start(f32[8,512]{1,0:T(8,128)S(1)} %get-tuple-element.107), channel_id=1, source_target_pairs={{0,3},{1,0},{2,1},{3,2},{4,7},{5,4},{6,5},{7,6},{8,11},{9,8},{10,9... | collective-permute-start | bytes 49160 | tf_op jit(solution)/shard_map/ppermute | solution.py:37
  186.9 5.2 %collective-permute-start.39 = (f32[8,512]{1,0:T(8,128)S(1)}, f32[8,512]{1,0:T(8,128)S(1)}, u32[]{:S(2)}, u32[]{:S(2)}) collective-permute-start(f32[8,512]{1,0:T(8,128)S(1)} %get-tuple-element.107), channel_id=1, source_target_pairs={{0,2},{1,3},{2,0},{3,1},{4,6},{5,7},{6,4},{7,5},{8,10},{9,11},{10,... | collective-permute-start | bytes 49160 | tf_op jit(solution)/shard_map/ppermute | solution.py:37
  192.2 28.9 %collective-permute-start.44 = (bf16[4,384,512]{2,1,0:T(8,128)(2,1)}, bf16[4,384,512]{2,1,0:T(8,128)(2,1)S(1)}, u32[]{:S(2)}, u32[]{:S(2)}) collective-permute-start(bf16[4,384,512]{2,1,0:T(8,128)(2,1)} %collective-permute-done.36.refs_16_), channel_id=1, source_target_pairs={{0,8},{1,9},{2,10},{3,11},{4,12},{5,13},{6,14},{7,15},{8,0},{9,1},... | collective-permute-start | bytes 4718600 | tf_op jit(solution)/shard_map/ppermute | solution.py:37
  193.6 27.5 %collective-permute-start.40 = (bf16[544,768]{1,0:T(8,128)(2,1)S(1)}, bf16[544,768]{1,0:T(8,128)(2,1)S(1)}, u32[]{:S(2)}, u32[]{:S(2)}) collective-permute-start(bf16[544,768]{1,0:T(8,128)(2,1)S(1)} %get-tuple-element.125), channel_id=1, source_target_pairs={{0,1},{1,2},{2,3},{3,0},{4,5},{5,6},{6,7},{7,4},{8,9},{9,10},{10,1... | collective-permute-start | bytes 2506760 | tf_op jit(solution)/shard_map/ppermute | solution.py:37
  193.7 27.4 %collective-permute-start.41 = (bf16[544,768]{1,0:T(8,128)(2,1)S(1)}, bf16[544,768]{1,0:T(8,128)(2,1)S(1)}, u32[]{:S(2)}, u32[]{:S(2)}) collective-permute-start(bf16[544,768]{1,0:T(8,128)(2,1)S(1)} %get-tuple-element.124), channel_id=1, source_target_pairs={{0,3},{1,0},{2,1},{3,2},{4,7},{5,4},{6,5},{7,6},{8,11},{9,8},{10,9... | collective-permute-start | bytes 2506760 | tf_op jit(solution)/shard_map/ppermute | solution.py:37
  198.2 22.8 %collective-permute-start.43 = (bf16[2,384,512]{2,1,0:T(8,128)(2,1)S(1)}, bf16[2,384,512]{2,1,0:T(8,128)(2,1)}, u32[]{:S(2)}, u32[]{:S(2)}) collective-permute-start(bf16[2,384,512]{2,1,0:T(8,128)(2,1)S(1)} %slice.128), channel_id=1, source_target_pairs={{0,16},{1,17},{2,18},{3,19},{4,20},{5,21},{6,22},{7,23},{8,56},{9,... | collective-permute-start | bytes 2359304 | tf_op jit(solution)/shard_map/ppermute | solution.py:37
  198.8 3.8 %collective-permute-start.45 = (f32[8,512]{1,0:T(8,128)S(1)}, f32[8,512]{1,0:T(8,128)S(1)}, u32[]{:S(2)}, u32[]{:S(2)}) collective-permute-start(f32[8,512]{1,0:T(8,128)S(1)} %add_add_fusion), channel_id=1, source_target_pairs={{0,4},{1,5},{2,6},{3,7},{4,0},{5,1},{6,2},{7,3},{8,12},{9,13},{10,... | collective-permute-start | bytes 49160 | tf_op jit(solution)/shard_map/ppermute | solution.py:37
  202.6 17.5 %collective-permute-start.42 = (bf16[448,768]{1,0:T(8,128)(2,1)S(1)}, bf16[448,768]{1,0:T(8,128)(2,1)S(1)}, u32[]{:S(2)}, u32[]{:S(2)}) collective-permute-start(bf16[448,768]{1,0:T(8,128)(2,1)S(1)} %pad_maximum_fusion.5), channel_id=1, source_target_pairs={{0,4},{1,5},{2,6},{3,7},{4,0},{5,1},{6,2},{7,3},{8,12},{9,13},{10,... | collective-permute-start | bytes 2064392 | tf_op jit(solution)/shard_map/ppermute | solution.py:37
  222.3 11.2 %collective-permute-start.49 = (bf16[2,384,512]{2,1,0:T(8,128)(2,1)}, bf16[2,384,512]{2,1,0:T(8,128)(2,1)}, u32[]{:S(2)}, u32[]{:S(2)}) collective-permute-start(bf16[2,384,512]{2,1,0:T(8,128)(2,1)} %collective-permute-done.43.refs_18_), channel_id=1, source_target_pairs={{0,8},{1,9},{2,10},{3,11},{4,12},{5,13},{6,14},{7,15},{8,0},{9,1},... | collective-permute-start | bytes 2359304 | tf_op jit(solution)/shard_map/ppermute | solution.py:37
  222.7 26.0 %collective-permute-start.48 = (bf16[224,768]{1,0:T(8,128)(2,1)S(1)}, bf16[224,768]{1,0:T(8,128)(2,1)S(1)}, u32[]{:S(2)}, u32[]{:S(2)}) collective-permute-start(bf16[224,768]{1,0:T(8,128)(2,1)S(1)} %slice.131), channel_id=1, source_target_pairs={{0,4},{1,5},{2,6},{3,7},{4,0},{5,1},{6,2},{7,3},{8,12},{9,13},{10,... | collective-permute-start | bytes 1032200 | tf_op jit(solution)/shard_map/ppermute | solution.py:37
  228.2 20.5 %collective-permute-start.46 = (bf16[144,768]{1,0:T(8,128)(2,1)S(1)}, bf16[144,768]{1,0:T(8,128)(2,1)S(1)}, u32[]{:S(2)}, u32[]{:S(2)}) collective-permute-start(bf16[144,768]{1,0:T(8,128)(2,1)S(1)} %slice.129), channel_id=1, source_target_pairs={{0,1},{1,2},{2,3},{3,0},{4,5},{5,6},{6,7},{7,4},{8,9},{9,10},{10,1... | collective-permute-start | bytes 663560 | tf_op jit(solution)/shard_map/ppermute | solution.py:37
  228.2 20.4 %collective-permute-start.47 = (bf16[144,768]{1,0:T(8,128)(2,1)S(1)}, bf16[144,768]{1,0:T(8,128)(2,1)S(1)}, u32[]{:S(2)}, u32[]{:S(2)}) collective-permute-start(bf16[144,768]{1,0:T(8,128)(2,1)S(1)} %slice.130), channel_id=1, source_target_pairs={{0,3},{1,0},{2,1},{3,2},{4,7},{5,4},{6,5},{7,6},{8,11},{9,8},{10,9... | collective-permute-start | bytes 663560 | tf_op jit(solution)/shard_map/ppermute | solution.py:37
  251.6 19.1 %all-to-all-start = ((bf16[8,128,512]{2,1,0:T(8,128)(2,1)}), bf16[8,128,512]{2,1,0:T(8,128)(2,1)S(1)}, u32[]{:S(2)}, u32[]{:S(2)}) async-start(bf16[8,128,512]{2,1,0:T(8,128)(2,1)} %project.3), calls=%async_computation | async-start | bytes 2097152 | tf_op jit(solution)/shard_map/all_to_all | solution.py:611
  (43 other events, 216.6 us)

commit v2 on v1

--- a/solution.py
+++ b/solution.py
@@ -12,7 +12,7 @@
 PATCHES = 256
 HALF = 128
 AXES = ("dp", "mp")
-VMEM = 40 * 1024 * 1024
+MEGA = 1024 * 1024
 epsilon = 1e-06
 SMALL = pl.CostEstimate(flops=1, bytes_accessed=1, transcendentals=0)
 
@@ -105,7 +105,7 @@
     return order
 
 
-NEAR = [(0, 0), (1, 0), (0, 1), (0, 3), (1, 1), (1, 3), (0, 2), (1, 2)]
+NEAR = [(0, 0), (1, 0), (0, 1), (0, 3), (0, 2), (1, 1), (1, 3), (1, 2)]
 
 
 def place_tables():
@@ -146,7 +146,7 @@
         ],
         out_specs=pl.BlockSpec((chunks, block, width // chunks), lambda i: (0, i, 0)),
         out_shape=jax.ShapeDtypeStruct((chunks, rows, width // chunks), jnp.bfloat16),
-        compiler_params=pltpu.CompilerParams(vmem_limit_bytes=VMEM),
+        compiler_params=pltpu.CompilerParams(vmem_limit_bytes=16 * MEGA),
         cost_estimate=SMALL,
         name="norm_columns",
     )(values, gain.reshape(1, width))
@@ -175,7 +175,7 @@
     if not attend:
         refs[0][0] = total
         return
-    gain_ref, out_ref = refs
+    gain_ref, out_ref, *image_refs = refs
     size = gain_ref.shape[2]
     gains = gain_ref[0]
     query = row_norm(total[:, :size], gains[0:1]).astype(jnp.bfloat16)
@@ -188,9 +188,10 @@
         ) / math.sqrt(size)
         raised = jnp.exp(scores - jnp.max(scores, -1, keepdims=True))
         weights = (raised / jnp.sum(raised, -1, keepdims=True)).astype(jnp.bfloat16)
-        out_ref[rows, :] = jnp.dot(
-            weights, value[rows], preferred_element_type=jnp.float32
-        ).astype(jnp.bfloat16)
+        attended = jnp.dot(weights, value[rows], preferred_element_type=jnp.float32)
+        attended = attended.astype(jnp.bfloat16)
+        out_ref[rows, :] = attended
+        image_refs[image][...] = attended
 
 
 def accumulate(columns, shards, index, total=None, gains=None):
@@ -219,8 +220,11 @@
     else:
         in_specs.append(pl.BlockSpec((1, 2, wide // 3), lambda h, index: (h, 0, 0)))
         operands.append(gains)
-        out_spec = pl.BlockSpec((rows, wide // 3), lambda h, index: (0, h))
-        out_shape = jax.ShapeDtypeStruct((rows, heads * wide // 3), jnp.bfloat16)
+        sizes = [rows] + [PATCHES] * (rows // PATCHES)
+        out_spec = [pl.BlockSpec((size, wide // 3), lambda h, index: (0, h)) for size in sizes]
+        out_shape = [
+            jax.ShapeDtypeStruct((size, heads * wide // 3), jnp.bfloat16) for size in sizes
+        ]
     return pl.pallas_call(
         functools.partial(accumulate_kernel, counts, total is not None, gains is not None),
         grid_spec=pltpu.PrefetchScalarGridSpec(
@@ -228,7 +232,7 @@
         ),
         out_shape=out_shape,
         input_output_aliases=aliases,
-        compiler_params=pltpu.CompilerParams(vmem_limit_bytes=VMEM),
+        compiler_params=pltpu.CompilerParams(vmem_limit_bytes=20 * MEGA),
         cost_estimate=SMALL,
         name="accumulate",
     )(index, *operands)
@@ -248,36 +252,48 @@
 
 
 def read_piece(piece, refs):
-    parts = [refs[k][first:last] for k, first, last in piece]
+    parts = [refs[k][...] for k in piece]
     return parts[0] if len(parts) == 1 else jnp.concatenate(parts, 0)
 
 
-def out_kernel(pieces, held, count, index_ref, *refs):
+def out_kernel(pieces, held, count, kept, finish, index_ref, *refs):
     near, refs = refs[:held], refs[held:]
     parts, refs = refs[:count], refs[count:]
-    patches_ref, block_ref, stats_ref, held_ref, sems = refs
+    if finish:
+        given_ref, own_ref, block_ref, *half_refs, stats_ref, held_ref, sems = refs
+    else:
+        total_ref, kept_ref, held_ref, sems = refs
     load_shards(parts, held_ref, sems)
     depth = held_ref.shape[1]
-    rows = patches_ref.shape[0]
     sums, squares = 0.0, 0.0
     for half in range(2):
-        total = None
+        total = given_ref[half] if finish else None
         for k, piece in enumerate(pieces):
             term = lax.dot_general(
                 read_piece(piece, near),
-                held_ref[index_ref[2 * k + half]],
+                held_ref[2 * k + half if finish else index_ref[2 * k + half]],
                 (((1,), (1,)), ((), ())),
                 preferred_element_type=jnp.float32,
             )
             term = term.astype(jnp.bfloat16).astype(jnp.float32)
             total = term if total is None else total + term
+        if not finish:
+            total_ref[half] = total
+            continue
         cols = slice(half * depth, (half + 1) * depth)
-        block = (patches_ref[:, cols].astype(jnp.float32) + total).astype(jnp.bfloat16)
+        block = (own_ref[:, cols].astype(jnp.float32) + total).astype(jnp.bfloat16)
         block_ref[:, cols] = block
+        rows = block.shape[0] // 2
+        half_refs[0][:, cols] = block[:rows]
+        half_refs[1][:, cols] = block[rows:]
         block = block.astype(jnp.float32)
         sums += jnp.sum(block, 1, keepdims=True)
         squares += jnp.sum(block * block, 1, keepdims=True)
-    lane = lax.broadcasted_iota(jnp.int32, (rows, 128), 1)
+    if not finish:
+        for k in range(kept):
+            kept_ref[k] = held_ref[index_ref[2 * len(pieces) + k]]
+        return
+    lane = lax.broadcasted_iota(jnp.int32, (sums.shape[0], 128), 1)
     both = jnp.where(lane == 0, sums, squares)
     stats_ref[...] = both.T[:8]
 
@@ -286,32 +302,45 @@
     return pl.BlockSpec(shape, lambda i, index: (0,) * len(shape))
 
 
-def out_project(near, pieces, parts, index, patches):
-    rows, depth = near[0].shape
+def out_project(near, pieces, parts, index, kept=0, total=None, own=None):
+    depth = parts[0].shape[1]
+    finish = total is not None
     in_specs = [whole(part.shape) for part in near]
     in_specs += [pl.BlockSpec(memory_space=pl.ANY) for _ in parts]
-    in_specs.append(pl.BlockSpec((rows, 2 * depth), lambda i, index: (0, index[16])))
-    out_shape = [
-        jax.ShapeDtypeStruct((rows, 2 * depth), jnp.bfloat16),
-        jax.ShapeDtypeStruct((8, rows), jnp.float32),
-    ]
+    operands = list(near) + list(parts)
+    rows = near[0].shape[0]
+    if finish:
+        rows = own.shape[0]
+        in_specs += [whole(total.shape), whole(own.shape)]
+        operands += [total, own]
+        out_shape = [
+            jax.ShapeDtypeStruct((rows, 2 * depth), jnp.bfloat16),
+            jax.ShapeDtypeStruct((rows // 2, 2 * depth), jnp.bfloat16),
+            jax.ShapeDtypeStruct((rows // 2, 2 * depth), jnp.bfloat16),
+            jax.ShapeDtypeStruct((8, rows), jnp.float32),
+        ]
+    else:
+        out_shape = [
+            jax.ShapeDtypeStruct((2, rows, depth), jnp.float32),
+            jax.ShapeDtypeStruct((kept, depth, depth), jnp.bfloat16),
+        ]
     return pl.pallas_call(
-        functools.partial(out_kernel, pieces, len(near), len(parts)),
+        functools.partial(out_kernel, pieces, len(near), len(parts), kept, finish),
         grid_spec=pltpu.PrefetchScalarGridSpec(
             num_scalar_prefetch=1,
             grid=(1,),
             in_specs=in_specs,
             out_specs=[whole(out.shape) for out in out_shape],
             scratch_shapes=[
-                pltpu.VMEM((16, depth, depth), jnp.bfloat16),
+                pltpu.VMEM((sum(part.shape[0] for part in parts), depth, depth), jnp.bfloat16),
                 pltpu.SemaphoreType.DMA((len(parts),)),
             ],
         ),
         out_shape=out_shape,
-        compiler_params=pltpu.CompilerParams(vmem_limit_bytes=VMEM),
+        compiler_params=pltpu.CompilerParams(vmem_limit_bytes=20 * MEGA),
         cost_estimate=SMALL,
         name="out_project",
-    )(index, *near, *parts, patches)
+    )(index, *operands)
 
 
 def project_kernel(pieces, held, count, kept, finish, width, index_ref, *refs):
@@ -394,7 +423,7 @@
             scratch_shapes=scratch,
         ),
         out_shape=out_shape,
-        compiler_params=pltpu.CompilerParams(vmem_limit_bytes=VMEM),
+        compiler_params=pltpu.CompilerParams(vmem_limit_bytes=28 * MEGA),
         cost_estimate=SMALL,
         name="project",
     )(index, *operands)
@@ -434,7 +463,7 @@
             out_specs=whole(text.shape),
         ),
         out_shape=jax.ShapeDtypeStruct(text.shape, text.dtype),
-        compiler_params=pltpu.CompilerParams(vmem_limit_bytes=VMEM),
+        compiler_params=pltpu.CompilerParams(vmem_limit_bytes=8 * MEGA),
         cost_estimate=SMALL,
         name="pack",
     )(place, arrived, text)
@@ -464,11 +493,12 @@
     mp_slot = mp[None].astype(jnp.int32)
 
     own = qkv_weight.transpose(1, 0, 2)
+    first = spread_y(own)
+    other = swap_core(own)
+    far = swap_zh(own)
     turned = transpose_mesh(out_weight)
-    (other,) = join(swap_core(own))
-    first = spread_y(join(own, other)[0])
+    (other,) = join(other)
     beside = spread_y(other)
-    far = swap_zh(join(own, other)[0])
     columns = norm_columns(join(patches, other)[0], norm_gain, 16)
     total = accumulate(columns, [own, other], met[0:2])
 
@@ -488,17 +518,19 @@
         total,
     )
 
-    far_first, second, far_beside, turned_far, proj_far, total = join(
-        far_first, second, far_beside, turned_far, proj_far, total
+    turned_far, proj_far, total = join(turned_far, proj_far, total)
+    out_mine = jnp.stack([turned, turned_far])
+    proj_mine = jnp.stack([proj_weight, proj_far])
+    own_cols = lax.dynamic_slice_in_dim(patches, mp * (2 * 384), 2 * 384, 1)
+    far_first, second, far_beside, out_mine, proj_mine, own_cols, total = join(
+        far_first, second, far_beside, out_mine, proj_mine, own_cols, total
     )
     far_second = spread_y(far_first)
-    far_first_other, second_other, far_beside_other = join(
-        swap_core(far_first), swap_core(second), swap_core(far_beside)
-    )
-    out_mine = jnp.stack([turned, join(turned_far, second_other)[0]])
-    proj_mine = jnp.stack([proj_weight, join(proj_far, second_other)[0]])
-    out_other = swap_core(out_mine)
-    proj_other = swap_core(proj_mine)
+    far_first_other, second_other, far_beside_other, out_other = join(
+        swap_core(far_first), swap_core(second), swap_core(far_beside), swap_core(out_mine)
+    )
+    out_quad = jnp.concatenate([out_mine, out_other])
+    out_first = spread_y(out_quad)
     total = accumulate(
         columns,
         [far_first, far_first_other, second, second_other, far_beside, far_beside_other],
@@ -506,83 +538,69 @@
         total,
     )
 
-    far_second, out_other, proj_other, total = join(far_second, out_other, proj_other, total)
+    far_second, proj_mine, total = join(far_second, proj_mine, total)
     far_second_other = swap_core(far_second)
-    out_quad = jnp.concatenate([out_mine, out_other])
-    proj_quad = jnp.concatenate([proj_mine, proj_other])
-    out_first = spread_y(out_quad)
+    proj_other = swap_core(proj_mine)
     attended = accumulate(
         columns, [far_second, far_second_other], met[14:16], total, qk_gain.transpose(1, 0, 2)
     )
 
-    out_quad, proj_quad = join(out_quad, proj_quad)
-    rows = attended.shape[0]
-    half = rows // 2
-    middle = rows * 9 // 16
-    quarter = middle // 2
-    late = middle - half
-    pieces = (
-        ((0, 0, rows),),
-        ((1, 0, rows),),
-        ((2, 0, rows),),
-        ((3, 0, rows),),
-        ((5, half, half + middle), (6, 0, rows - middle)),
-        ((4, half, half + middle), (6, rows - middle, 2 * (rows - middle))),
-        ((4, 0, half), (5, 0, half)),
-        ((7, 0, quarter), (8, 0, quarter), (9, 0, rows - middle)),
-    )
-
-    def gather_first(mine):
-        return [swap_zl(mine), shift_x(mine, -1), shift_x(mine, 1)]
-
-    def gather_second(far, right, left):
-        return [
-            shift_x(jnp.concatenate([left[:half], far[:middle]]), 1),
-            shift_x(jnp.concatenate([right[half:], far[:middle]]), -1),
-            swap_zl(jnp.concatenate([right[middle:], left[middle:]])),
-        ]
-
-    def gather_third(from_left, from_right):
-        return [
-            shift_x(from_left[half : half + quarter], 1),
-            shift_x(from_right[half + quarter :], -1),
-            swap_zl(from_right[late:half]),
-        ]
-
-    near = [attended]
-    *got, out_first = join(*gather_first(attended), out_first)
-    near += got
+    whole_att, low, high, out_first, proj_other = join(*attended, out_first, proj_other)
+    proj_quad = jnp.concatenate([proj_mine, proj_other])
+    far = swap_zl(whole_att)
     out_second = spread_y(out_first[:2])
     out_first_other = swap_core(out_first)
-    *got, out_second, out_first_other = join(*gather_second(*got), out_second, out_first_other)
-    near += got
-    proj_first = spread_y(join(proj_quad, out_second)[0])
+    left_low, right_high, far, out_second, out_first_other, low, high = join(
+        shift_x(low, 1), shift_x(high, -1), far, out_second, out_first_other, low, high
+    )
+    near = [whole_att, far]
     out_second_other = swap_core(out_second)
-    *got, out_second_other = join(*gather_third(*got[:2]), out_second_other)
-    near += got
-    block_out, stats = out_project(
+    right_low, left_high, beyond_low, beyond_high, out_second_other = join(
+        shift_x(low, -1),
+        shift_x(high, 1),
+        shift_x(left_low, 1),
+        shift_x(right_high, -1),
+        out_second_other,
+    )
+    near += [right_low, right_high, left_low, left_high, beyond_low, beyond_high]
+    proj_first = spread_y(join(proj_quad, out_second_other)[0])
+    last = [shift_x(far, -1), shift_x(far, 1), swap_zl(beyond_low), swap_zl(beyond_high)]
+    pieces = ((0,), (1,), (2, 3), (4, 5), (6, 7))
+    last_pieces = ((0,), (1,), (2, 3))
+    total, left = out_project(
         near,
         pieces,
         [out_quad, out_first, out_first_other, out_second, out_second_other],
-        jnp.concatenate([shards, mp_slot]),
-        patches,
-    )
-
-    near = [block_out]
-    sent = gather_first(block_out)
+        shards,
+        kept=6,
+    )
+    *last, total, left = join(*last, total, left)
+    block_out, low, high, stats = out_project(
+        last, last_pieces, [left], shards, total=total, own=own_cols
+    )
+
     stats_x = join(shift_x(stats, 1), shift_x(stats, -1), shift_x(stats, 2))
     stats = stats + stats_x[0] + stats_x[1] + stats_x[2]
-    *got, proj_first, stats = join(*sent, proj_first, stats)
-    near += got
+    low, high, whole_block, stats, proj_first = join(low, high, block_out, stats, proj_first)
+    far = swap_zl(whole_block)
     proj_second = spread_y(proj_first[:2])
     proj_first_other = swap_core(proj_first)
-    *got, proj_second, proj_first_other, stats_z = join(
-        *gather_second(*got), proj_second, proj_first_other, swap_zl(stats)
-    )
-    near += got
+    left_low, right_high, stats_z, proj_first_other, low, high = join(
+        shift_x(low, 1), shift_x(high, -1), swap_zl(stats), proj_first_other, low, high
+    )
     stats = stats + stats_z
-    last = gather_third(*got[:2])
+    right_low, left_high, beyond_low, beyond_high, far, proj_second = join(
+        shift_x(low, -1),
+        shift_x(high, 1),
+        shift_x(left_low, 1),
+        shift_x(right_high, -1),
+        far,
+        proj_second,
+    )
+    near = [whole_block, far]
+    near += [right_low, right_high, left_low, left_high, beyond_low, beyond_high]
     proj_second_other = swap_core(proj_second)
+    last = [shift_x(far, -1), shift_x(far, 1), swap_zl(beyond_low), swap_zl(beyond_high)]
 
     slot = slot_offset // HALF
     block = jnp.arange(8, dtype=jnp.int32)
@@ -592,20 +610,21 @@
 
     total, left = project(
         near,
-        pieces[:7],
+        pieces,
         stats,
         final_gain,
         [proj_quad, proj_first, proj_first_other, proj_second, proj_second_other],
-        jnp.concatenate([shards, groups[:7]]),
-        kept=2,
-    )
+        jnp.concatenate([shards, groups[:5]]),
+        kept=6,
+    )
+    *last, total, left = join(*last, total, left)
     (outgoing,) = project(
         last,
-        (tuple((k - 7, first, last) for k, first, last in pieces[7]),),
+        last_pieces,
         stats,
         final_gain,
         [left],
-        jnp.concatenate([groups[7:], source]),
+        jnp.concatenate([groups[5:], source]),
         total=total,
     )
     arrived = lax.all_to_all(outgoing, "mp", split_axis=0, concat_axis=0, tiled=True)

time: 274 us -> 254 us (0.927)
  waiting for transfers between devices: 129 us -> 86.3 us
  starting transfers between devices: 54.5 us -> 65.8 us
  Pallas kernels: 43.6 us -> 52.2 us
  local copies, waits for them, and re-layouts: 37.7 us -> 41 us
    ppermute x50 -> x54, waiting for transfers between devices: 114 us -> 71.3 us  [move(): return lax.ppermute(values, AXES, pairs)]
    ppermute x50 -> x54, starting transfers between devices: 50.8 us -> 62.1 us  [move(): return lax.ppermute(values, AXES, pairs)]
    unnamed x76 -> x98, local copies, waits for them, and re-layouts: 28.1 us -> 35.7 us
    slice x20 -> x2, local copies, waits for them, and re-layouts: 5.47 us -> 0.07 us  [the longest x1 0.07 us: local(): groups[5:]]
    pallas_call x4, Pallas kernels: 18.2 us -> 21.9 us  [accumulate(): pl.pallas_call(functools.partial(accumulate_kernel, counts, total is not...]
    pallas_call x1 -> x2, Pallas kernels: 7.67 us -> 10.2 us  [out_project(): pl.pallas_call(functools.partial(out_kernel, pieces, len(near), len(parts...]
  transfers between devices with their start and end apart: 51 -> 55, of which waited for: 24 -> 27; matrix products, arithmetic and copies ran while one was open for 5% -> 4% of each run, Pallas kernels for 14% -> 18%
where the time goes in v2:
time: 254 us; the launch traced here: 252 us
  waiting for transfers between devices  86.3 us (34%)
  starting transfers between devices  65.8 us (26%)
  Pallas kernels  52.2 us (21%)
  local copies, waits for them, and re-layouts  41 us (16%)
  other arithmetic  3.76 us (1%)
  between operations  3.06 us (1%)
    ppermute x54, waiting for transfers between devices, move(): return lax.ppermute(values, AXES, pairs)  71.3 us
    ppermute x54, starting transfers between devices, move(): return lax.ppermute(values, AXES, pairs)  62.1 us
    unnamed x98, local copies, waits for them, and re-layouts  35.7 us
    pallas_call x4, Pallas kernels, accumulate(): pl.pallas_call(functools.partial(accumulate_kernel, counts, total is not...  21.9 us
    all_to_all x1, waiting for transfers between devices, local(): lax.all_to_all(outgoing, 'mp', split_axis=0, concat_axis=0, tiled=True)  15.1 us
    pallas_call x2, Pallas kernels, project(): pl.pallas_call(functools.partial(project_kernel, pieces, len(near), len(p...  12.2 us
    pallas_call x2, Pallas kernels, out_project(): pl.pallas_call(functools.partial(out_kernel, pieces, len(near), len(parts...  10.2 us
    pallas_call x1, Pallas kernels, norm_columns(): pl.pallas_call(norm_kernel, grid=(rows // block,), in_specs=[pl.BlockSpec...  6.11 us
  transfers between devices with their start and end apart: 55, of which 27 were waited for; matrix products, arithmetic and copies ran while one was open for 4% of the time, Pallas kernels for 18%

profile of v2, /device:TPU:0, one launch (start us, length us, event | category | flops | bytes accessed | tf_op | source)
XLA Modules:
  0.0 252.1 jit_solution(16423983787209383743)
XLA Ops:
  0.7 1.7 collective-permute-start.2
  2.5 3.9 %collective-permute-start.1 = (bf16[3,384,384]{2,1,0:T(8,128)(2,1)}, bf16[3,384,384]{2,1,0:T(8,128)(2,1)}, u32[]{:S(2)}, u32[]{:S(2)}) collective-permute-start(bf16[3,384,384]{2,1,0:T(8,128)(2,1)} %bitcast.61), channel_id=1, source_target_pairs={{0,64},{1,65},{2,66},{3,67},{4,68},{5,69},{6,70},{7,71},{8,72},{9,... | collective-permute-start | bytes 2654216 | tf_op jit(solution)/shard_map/ppermute | solution.py:37
  7.9 3.7 %collective-permute-start.4 = (bf16[384,384]{1,0:T(8,128)(2,1)}, bf16[384,384]{1,0:T(8,128)(2,1)}, u32[]{:S(2)}, u32[]{:S(2)}) collective-permute-start(bf16[384,384]{1,0:T(8,128)(2,1)} %param.17), channel_id=1, source_target_pairs={{0,0},{1,16},{2,32},{3,48},{4,64},{5,80},{6,96},{7,112},{8,8},{9,2... | collective-permute-start | bytes 884744 | tf_op jit(solution)/shard_map/ppermute | solution.py:37
  12.4 2.8 %copy-done.2 = bf16[512,6144]{1,0:T(8,128)(2,1)S(1)} copy-done((bf16[512,6144]{1,0:T(8,128)(2,1)S(1)}, bf16[512,6144]{1,0:T(8,128)(2,1)}, u32[]{:S(2)}) %copy-start.2) | copy-done | bytes 6291480
  16.0 6.1 %norm_columns.1.refs_0_.refs_1_.refs_2_.refs_3_.refs_4_.refs_5_ = bf16[16,512,384]{2,1,0:T(8,128)(2,1)S(1)} custom-call(bf16[512,6144]{1,0:T(8,128)(2,1)S(1)} %copy-done.2, f32[1,6144]{1,0:T(1,128)S(1)} %bitcast.65), custom_call_target="tpu_custom_call" | custom-call | flops 1 | bytes 1 | tf_op jit(solution)/shard_map/norm_columns/pallas_call | solution.py:140
  22.1 4.0 %accumulate.4.refs_12_ = f32[3,512,384]{2,1,0:T(8,128)S(1)} custom-call(s32[2]{0:T(128)S(1)} %get-tuple-element.184.index_ref, bf16[16,512,384]{2,1,0:T(8,128)(2,1)S(1)} %norm_columns.1.refs_0_.refs_1_.refs_2_.refs_3_.refs_4_.refs_5_, bf16[16,512,384]{2,1,0:T(8,128)(2,1)S(1)} %norm_columns.1.refs_0_.refs_1_.refs_2_.refs_3_.refs_4_.refs_5_, ...), custom_call_target="tpu_custom_call" | custom-call | flops 1 | bytes 1 | tf_op jit(solution)/shard_map/accumulate/pallas_call | solution.py:228
  26.3 9.1 %collective-permute-done.3 = bf16[3,384,384]{2,1,0:T(8,128)(2,1)} collective-permute-done((bf16[3,384,384]{2,1,0:T(8,128)(2,1)}, bf16[3,384,384]{2,1,0:T(8,128)(2,1)}, u32[]{:S(2)}, u32[]{:S(2)}) %collective-permute-start.3) | collective-permute-done | bytes 884768 | tf_op jit(solution)/shard_map/ppermute | solution.py:37
  36.0 2.5 collective-permute-start.5
  41.3 2.5 collective-permute-start.10
  43.8 3.9 %collective-permute-start.12 = (bf16[384,512]{1,0:T(8,128)(2,1)}, bf16[384,512]{1,0:T(8,128)(2,1)}, u32[]{:S(2)}, u32[]{:S(2)}) collective-permute-start(bf16[384,512]{1,0:T(8,128)(2,1)} %param.19), channel_id=1, source_target_pairs={{0,64},{1,65},{2,66},{3,67},{4,68},{5,69},{6,70},{7,71},{8,72},{9,... | collective-permute-start | bytes 1179656 | tf_op jit(solution)/shard_map/ppermute | solution.py:37
  47.7 2.1 constant_dynamic-slice_fusion.1.refs_6_
  49.9 2.8 %copy-done.1 = bf16[16,512,384]{2,1,0:T(8,128)(2,1)S(1)} copy-done((bf16[16,512,384]{2,1,0:T(8,128)(2,1)S(1)}, bf16[16,512,384]{2,1,0:T(8,128)(2,1)}, u32[]{:S(2)}) %copy-start.1) | copy-done | bytes 6291480
  53.9 6.5 %accumulate.5.refs_12_ = f32[3,512,384]{2,1,0:T(8,128)S(1)} custom-call(s32[6]{0:T(128)S(1)} %get-tuple-element.183.index_ref, bf16[16,512,384]{2,1,0:T(8,128)(2,1)S(1)} %copy-done.1, bf16[16,512,384]{2,1,0:T(8,128)(2,1)S(1)} %copy-done.1, bf16[16,512,384]{2,1,0:T(8,128)(2,1)S(1)} %copy-done.1, ...), custom_call_target="tpu_custom_call", output_to_operand_aliasing={{}: (13, {})} | custom-call | flops 1 | bytes 1 | tf_op jit(solution)/shard_map/accumulate/pallas_call | solution.py:228
  60.4 1.9 collective-permute-done.11
  64.5 5.0 %collective-permute-done.10 = bf16[3,384,384]{2,1,0:T(8,128)(2,1)} collective-permute-done((bf16[3,384,384]{2,1,0:T(8,128)(2,1)}, bf16[3,384,384]{2,1,0:T(8,128)(2,1)}, u32[]{:S(2)}, u32[]{:S(2)}) %collective-permute-start.10) | collective-permute-done | bytes 884768 | tf_op jit(solution)/shard_map/ppermute | solution.py:37
  71.9 1.8 collective-permute-done.17
  77.0 6.5 %accumulate.6.refs_4_ = f32[3,512,384]{2,1,0:T(8,128)S(1)} custom-call(s32[6]{0:T(128)S(1)} %get-tuple-element.182.index_ref, bf16[16,512,384]{2,1,0:T(8,128)(2,1)S(1)} %copy-done.1, bf16[16,512,384]{2,1,0:T(8,128)(2,1)S(1)} %copy-done.1, bf16[16,512,384]{2,1,0:T(8,128)(2,1)S(1)} %copy-done.1, ...), custom_call_target="tpu_custom_call", output_to_operand_aliasing={{}: (13, {})} | custom-call | flops 1 | bytes 1 | tf_op jit(solution)/shard_map/accumulate/pallas_call | solution.py:228
  85.5 1.9 collective-permute-done.18
  87.4 4.9 %accumulate.7 = (bf16[512,384]{1,0:T(8,128)(2,1)S(1)}, bf16[256,384]{1,0:T(8,128)(2,1)S(1)}, bf16[256,384]{1,0:T(8,128)(2,1)S(1)}) custom-call(s32[2]{0:T(128)S(1)} %get-tuple-element.185.index_ref, bf16[16,512,384]{2,1,0:T(8,128)(2,1)S(1)} %copy-done.1, bf16[16,512,384]{2,1,0:T(8,128)(2,1)S(1)} %copy-done.1, bf16[1,3,384,384]{3,2,1,0:T(8,128)(2,1)S(1)} %bitcast.63, ...), custom_call_target="tpu_custom_call" | custom-call | flops 1 | bytes 1 | tf_op jit(solution)/shard_map/accumulate/pallas_call | solution.py:228
  92.4 5.3 %collective-permute-done.19.refs_9_ = bf16[4,384,384]{2,1,0:T(8,128)(2,1)S(1)} collective-permute-done((bf16[4,384,384]{2,1,0:T(8,128)(2,1)S(1)}, bf16[4,384,384]{2,1,0:T(8,128)(2,1)S(1)}, u32[]{:S(2)}, u32[]{:S(2)}) %collective-permute-start.19) | collective-permute-done | bytes 1179680 | tf_op jit(solution)/shard_map/ppermute | solution.py:37
  97.8 1.9 collective-permute-start.23
  99.8 1.7 collective-permute-start.21
  103.0 5.0 %collective-permute-done.21.refs_4_ = bf16[256,384]{1,0:T(8,128)(2,1)S(1)} collective-permute-done((bf16[256,384]{1,0:T(8,128)(2,1)S(1)}, bf16[256,384]{1,0:T(8,128)(2,1)S(1)}, u32[]{:S(2)}, u32[]{:S(2)}) %collective-permute-start.21) | collective-permute-done | bytes 196640 | tf_op jit(solution)/shard_map/ppermute | solution.py:37
  111.9 1.7 collective-permute-start.30
  115.3 2.3 collective-permute-done.28.refs_2_
  118.3 1.9 collective-permute-done.29.refs_5_
  120.8 2.8 %collective-permute-done.30.refs_6_ = bf16[256,384]{1,0:T(8,128)(2,1)} collective-permute-done((bf16[256,384]{1,0:T(8,128)(2,1)S(1)}, bf16[256,384]{1,0:T(8,128)(2,1)}, u32[]{:S(2)}, u32[]{:S(2)}) %collective-permute-start.30) | collective-permute-done | bytes 196640 | tf_op jit(solution)/shard_map/ppermute | solution.py:37
  124.5 1.6 collective-permute-start.38
  126.1 3.2 %collective-permute-start.26 = (bf16[512,384]{1,0:T(8,128)(2,1)}, bf16[512,384]{1,0:T(8,128)(2,1)}, u32[]{:S(2)}, u32[]{:S(2)}) collective-permute-start(bf16[512,384]{1,0:T(8,128)(2,1)} %collective-permute-done.23.refs_1_), channel_id=1, source_target_pairs={{0,3},{1,0},{2,1},{3,2},{4,7},{5,4},{6,5},{7,6},{8,11},{9,8},{10,9... | collective-permute-start | bytes 1179656 | tf_op jit(solution)/shard_map/ppermute | solution.py:37
  129.4 1.7 collective-permute-start.33
  141.7 5.4 %out_project.2 = (f32[2,512,384]{2,1,0:T(8,128)S(1)}, bf16[6,384,384]{2,1,0:T(8,128)(2,1)S(1)}) custom-call(s32[16]{0:T(128)S(1)} %fusion.index_ref, bf16[512,384]{1,0:T(8,128)(2,1)S(1)} %get-tuple-element.123.refs_0_, bf16[512,384]{1,0:T(8,128)(2,1)} %collective-permute-done.23.refs_1_, bf16[256,384]{1,0:T(8,128)(2,1)S(1)} %copy-done.42, ...), custom_call_target="tpu_custom_call" | custom-call | flops 1 | bytes 1 | tf_op jit(solution)/shard_map/out_project/pallas_call | solution.py:327
  147.2 4.8 %out_project.3 = (bf16[512,768]{1,0:T(8,128)(2,1)}, bf16[256,768]{1,0:T(8,128)(2,1)S(1)}, bf16[256,768]{1,0:T(8,128)(2,1)S(1)}, f32[8,512]{1,0:T(8,128)S(1)}) custom-call(s32[16]{0:T(128)S(1)} %fusion.index_ref, bf16[512,384]{1,0:T(8,128)(2,1)} %collective-permute-done.26.refs_0_, bf16[512,384]{1,0:T(8,128)(2,1)} %collective-permute-done.27.refs_1_, ...), custom_call_target="tpu_custom_call" | custom-call | flops 1 | bytes 1 | tf_op jit(solution)/shard_map/out_project/pallas_call | solution.py:327
  154.5 2.9 %collective-permute-done.37 = f32[8,512]{1,0:T(8,128)S(1)} collective-permute-done((f32[8,512]{1,0:T(8,128)S(1)}, f32[8,512]{1,0:T(8,128)S(1)}, u32[]{:S(2)}, u32[]{:S(2)}) %collective-permute-start.37) | collective-permute-done | bytes 16416 | tf_op jit(solution)/shard_map/ppermute | solution.py:37
  159.5 1.7 collective-permute-start.41
  161.3 3.2 %collective-permute-start.40 = (bf16[256,768]{1,0:T(8,128)(2,1)S(1)}, bf16[256,768]{1,0:T(8,128)(2,1)S(1)}, u32[]{:S(2)}, u32[]{:S(2)}) collective-permute-start(bf16[256,768]{1,0:T(8,128)(2,1)S(1)} %get-tuple-element.160), channel_id=1, source_target_pairs={{0,3},{1,0},{2,1},{3,2},{4,7},{5,4},{6,5},{7,6},{8,11},{9,8},{10,9... | collective-permute-start | bytes 1179656 | tf_op jit(solution)/shard_map/ppermute | solution.py:37
  165.0 9.3 %collective-permute-done.39.refs_4_ = bf16[256,768]{1,0:T(8,128)(2,1)S(1)} collective-permute-done((bf16[256,768]{1,0:T(8,128)(2,1)S(1)}, bf16[256,768]{1,0:T(8,128)(2,1)S(1)}, u32[]{:S(2)}, u32[]{:S(2)}) %collective-permute-start.39) | collective-permute-done | bytes 393248 | tf_op jit(solution)/shard_map/ppermute | solution.py:37
  175.4 3.3 %collective-permute-start.43 = (bf16[256,768]{1,0:T(8,128)(2,1)S(1)}, bf16[256,768]{1,0:T(8,128)(2,1)S(1)}, u32[]{:S(2)}, u32[]{:S(2)}) collective-permute-start(bf16[256,768]{1,0:T(8,128)(2,1)S(1)} %get-tuple-element.159), channel_id=1, source_target_pairs={{0,3},{1,0},{2,1},{3,2},{4,7},{5,4},{6,5},{7,6},{8,11},{9,8},{10,9... | collective-permute-start | bytes 1179656 | tf_op jit(solution)/shard_map/ppermute | solution.py:37
  179.6 3.3 %collective-permute-start.46 = (bf16[256,768]{1,0:T(8,128)(2,1)S(1)}, bf16[256,768]{1,0:T(8,128)(2,1)S(1)}, u32[]{:S(2)}, u32[]{:S(2)}) collective-permute-start(bf16[256,768]{1,0:T(8,128)(2,1)S(1)} %collective-permute-done.40.refs_3_), channel_id=1, source_target_pairs={{0,3},{1,0},{2,1},{3,2},{4,7},{5,4},{6,5},{7,6},{8,11},{9,8},{10,9... | collective-permute-start | bytes 1179656 | tf_op jit(solution)/shard_map/ppermute | solution.py:37
  184.7 3.6 %collective-permute-done.43.refs_2_ = bf16[256,768]{1,0:T(8,128)(2,1)S(1)} collective-permute-done((bf16[256,768]{1,0:T(8,128)(2,1)S(1)}, bf16[256,768]{1,0:T(8,128)(2,1)S(1)}, u32[]{:S(2)}, u32[]{:S(2)}) %collective-permute-start.43) | collective-permute-done | bytes 393248 | tf_op jit(solution)/shard_map/ppermute | solution.py:37
  189.1 2.9 %collective-permute-done.44.refs_5_ = bf16[256,768]{1,0:T(8,128)(2,1)S(1)} collective-permute-done((bf16[256,768]{1,0:T(8,128)(2,1)S(1)}, bf16[256,768]{1,0:T(8,128)(2,1)S(1)}, u32[]{:S(2)}, u32[]{:S(2)}) %collective-permute-start.44) | collective-permute-done | bytes 393248 | tf_op jit(solution)/shard_map/ppermute | solution.py:37
  192.8 6.4 %collective-permute-done.45.refs_6_ = bf16[256,768]{1,0:T(8,128)(2,1)S(1)} collective-permute-done((bf16[256,768]{1,0:T(8,128)(2,1)S(1)}, bf16[256,768]{1,0:T(8,128)(2,1)S(1)}, u32[]{:S(2)}, u32[]{:S(2)}) %collective-permute-start.45) | collective-permute-done | bytes 393248 | tf_op jit(solution)/shard_map/ppermute | solution.py:37
  200.7 2.5 collective-permute-start.49
  205.5 1.7 collective-permute-start.52
  217.3 6.8 %project.2 = (f32[512,512]{1,0:T(8,128)S(1)}, bf16[6,384,512]{2,1,0:T(8,128)(2,1)S(1)}) custom-call(s32[21]{0:T(128)S(1)} %pad_add_fusion.2.index_ref, bf16[512,768]{1,0:T(8,128)(2,1)S(1)} %copy-done.20, bf16[512,768]{1,0:T(8,128)(2,1)} %collective-permute-done.47.refs_1_, bf16[256,768]{1,0:T(8,128)(2,1)S(1)} %copy-done.30, bf16[256,768]{1,0:T(8,128)(2,1)S(1)} %copy-done.28, ...), custom_call_target="tpu_custom_call" | custom-call | flops 1 | bytes 1 | tf_op jit(solution)/shard_map/project/pallas_call | solution.py:414
  225.4 5.4 %project.3 = bf16[8,128,512]{2,1,0:T(8,128)(2,1)} custom-call(s32[11]{0:T(128)S(1)} %pad_add_fusion.1.index_ref, bf16[512,768]{1,0:T(8,128)(2,1)} %collective-permute-done.49.refs_0_, bf16[512,768]{1,0:T(8,128)(2,1)} %collective-permute-done.50.refs_1_, bf16[256,768]{1,0:T(8,128)(2,1)S(1)} %collective-permute-done.51.refs_2_, ...), custom_call_target="tpu_custom_call" | custom-call | flops 1 | bytes 1 | tf_op jit(solution)/shard_map/project/pallas_call | solution.py:414
  230.9 3.7 %all-to-all-start = ((bf16[8,128,512]{2,1,0:T(8,128)(2,1)}), bf16[8,128,512]{2,1,0:T(8,128)(2,1)S(1)}, u32[]{:S(2)}, u32[]{:S(2)}) async-start(bf16[8,128,512]{2,1,0:T(8,128)(2,1)} %project.3), calls=%async_computation | async-start | bytes 2097152 | tf_op jit(solution)/shard_map/all_to_all | solution.py:630
  235.3 15.1 %all-to-all-done.arrived_ref = bf16[8,128,512]{2,1,0:T(8,128)(2,1)S(1)} async-done(((bf16[8,128,512]{2,1,0:T(8,128)(2,1)}), bf16[8,128,512]{2,1,0:T(8,128)(2,1)S(1)}, u32[]{:S(2)}, u32[]{:S(2)}) %all-to-all-start) | async-done | bytes 1048608 | tf_op jit(solution)/shard_map/all_to_all | solution.py:630
  250.4 1.7 pack.1
  (192 shorter events, 62.5 us)
Async XLA Ops:
  0.6 5.7 %collective-permute-start = (bf16[3,384,384]{2,1,0:T(8,128)(2,1)}, bf16[3,384,384]{2,1,0:T(8,128)(2,1)}, u32[]{:S(2)}, u32[]{:S(2)}) collective-permute-start(bf16[3,384,384]{2,1,0:T(8,128)(2,1)} %bitcast.59), channel_id=1, source_target_pairs={{0,8},{1,9},{2,10},{3,11},{4,12},{5,13},{6,14},{7,15},{8,0},{9,1},... | collective-permute-start | bytes 2654216 | tf_op jit(solution)/shard_map/ppermute | solution.py:37
  0.7 25.4 %collective-permute-start.2 = (bf16[3,384,384]{2,1,0:T(8,128)(2,1)}, bf16[3,384,384]{2,1,0:T(8,128)(2,1)S(1)}, u32[]{:S(2)}, u32[]{:S(2)}) collective-permute-start(bf16[3,384,384]{2,1,0:T(8,128)(2,1)} %bitcast.60), channel_id=1, source_target_pairs={{0,16},{1,17},{2,18},{3,19},{4,20},{5,21},{6,22},{7,23},{8,56},{9,... | collective-permute-start | bytes 2654216 | tf_op jit(solution)/shard_map/ppermute | solution.py:37
  2.5 23.8 %collective-permute-start.1 = (bf16[3,384,384]{2,1,0:T(8,128)(2,1)}, bf16[3,384,384]{2,1,0:T(8,128)(2,1)}, u32[]{:S(2)}, u32[]{:S(2)}) collective-permute-start(bf16[3,384,384]{2,1,0:T(8,128)(2,1)} %bitcast.61), channel_id=1, source_target_pairs={{0,64},{1,65},{2,66},{3,67},{4,68},{5,69},{6,70},{7,71},{8,72},{9,... | collective-permute-start | bytes 2654216 | tf_op jit(solution)/shard_map/ppermute | solution.py:37
  6.3 29.1 %collective-permute-start.3 = (bf16[3,384,384]{2,1,0:T(8,128)(2,1)}, bf16[3,384,384]{2,1,0:T(8,128)(2,1)}, u32[]{:S(2)}, u32[]{:S(2)}) collective-permute-start(bf16[3,384,384]{2,1,0:T(8,128)(2,1)} %collective-permute-done), channel_id=1, source_target_pairs={{0,16},{1,17},{2,18},{3,19},{4,20},{5,21},{6,22},{7,23},{8,56},{9,... | collective-permute-start | bytes 2654216 | tf_op jit(solution)/shard_map/ppermute | solution.py:37
  7.9 18.2 %collective-permute-start.4 = (bf16[384,384]{1,0:T(8,128)(2,1)}, bf16[384,384]{1,0:T(8,128)(2,1)}, u32[]{:S(2)}, u32[]{:S(2)}) collective-permute-start(bf16[384,384]{1,0:T(8,128)(2,1)} %param.17), channel_id=1, source_target_pairs={{0,0},{1,16},{2,32},{3,48},{4,64},{5,80},{6,96},{7,112},{8,8},{9,2... | collective-permute-start | bytes 884744 | tf_op jit(solution)/shard_map/ppermute | solution.py:37
  36.0 28.5 %collective-permute-start.5 = (bf16[3,384,384]{2,1,0:T(8,128)(2,1)}, bf16[3,384,384]{2,1,0:T(8,128)(2,1)}, u32[]{:S(2)}, u32[]{:S(2)}) collective-permute-start(bf16[3,384,384]{2,1,0:T(8,128)(2,1)} %collective-permute-done.1), channel_id=1, source_target_pairs={{0,16},{1,17},{2,18},{3,19},{4,20},{5,21},{6,22},{7,23},{8,56},{9,... | collective-permute-start | bytes 2654216 | tf_op jit(solution)/shard_map/ppermute | solution.py:37
  38.4 26.1 %collective-permute-start.6 = (bf16[3,384,384]{2,1,0:T(8,128)(2,1)S(1)}, bf16[3,384,384]{2,1,0:T(8,128)(2,1)}, u32[]{:S(2)}, u32[]{:S(2)}) collective-permute-start(bf16[3,384,384]{2,1,0:T(8,128)(2,1)S(1)} %collective-permute-done.2), channel_id=1, source_target_pairs={{0,16},{1,17},{2,18},{3,19},{4,20},{5,21},{6,22},{7,23},{8,56},{9,... | collective-permute-start | bytes 2654216 | tf_op jit(solution)/shard_map/ppermute | solution.py:37
  41.3 28.2 %collective-permute-start.10 = (bf16[3,384,384]{2,1,0:T(8,128)(2,1)}, bf16[3,384,384]{2,1,0:T(8,128)(2,1)}, u32[]{:S(2)}, u32[]{:S(2)}) collective-permute-start(bf16[3,384,384]{2,1,0:T(8,128)(2,1)} %collective-permute-done.7), channel_id=1, source_target_pairs={{0,16},{1,17},{2,18},{3,19},{4,20},{5,21},{6,22},{7,23},{8,56},{9,... | collective-permute-start | bytes 2654216 | tf_op jit(solution)/shard_map/ppermute | solution.py:37
  43.8 18.5 %collective-permute-start.12 = (bf16[384,512]{1,0:T(8,128)(2,1)}, bf16[384,512]{1,0:T(8,128)(2,1)}, u32[]{:S(2)}, u32[]{:S(2)}) collective-permute-start(bf16[384,512]{1,0:T(8,128)(2,1)} %param.19), channel_id=1, source_target_pairs={{0,64},{1,65},{2,66},{3,67},{4,68},{5,69},{6,70},{7,71},{8,72},{9,... | collective-permute-start | bytes 1179656 | tf_op jit(solution)/shard_map/ppermute | solution.py:37
  47.7 14.6 %collective-permute-start.11 = (bf16[384,384]{1,0:T(8,128)(2,1)}, bf16[384,384]{1,0:T(8,128)(2,1)S(1)}, u32[]{:S(2)}, u32[]{:S(2)}) collective-permute-start(bf16[384,384]{1,0:T(8,128)(2,1)} %collective-permute-done.4), channel_id=1, source_target_pairs={{0,64},{1,65},{2,66},{3,67},{4,68},{5,69},{6,70},{7,71},{8,72},{9,... | collective-permute-start | bytes 884744 | tf_op jit(solution)/shard_map/ppermute | solution.py:37
  70.0 5.5 %collective-permute-start.14 = (bf16[3,384,384]{2,1,0:T(8,128)(2,1)}, bf16[3,384,384]{2,1,0:T(8,128)(2,1)S(1)}, u32[]{:S(2)}, u32[]{:S(2)}) collective-permute-start(bf16[3,384,384]{2,1,0:T(8,128)(2,1)} %collective-permute-done.5), channel_id=1, source_target_pairs={{0,8},{1,9},{2,10},{3,11},{4,12},{5,13},{6,14},{7,15},{8,0},{9,1},... | collective-permute-start | bytes 2654216 | tf_op jit(solution)/shard_map/ppermute | solution.py:37
  70.5 14.5 %collective-permute-start.13 = (bf16[3,384,384]{2,1,0:T(8,128)(2,1)}, bf16[3,384,384]{2,1,0:T(8,128)(2,1)S(1)}, u32[]{:S(2)}, u32[]{:S(2)}) collective-permute-start(bf16[3,384,384]{2,1,0:T(8,128)(2,1)} %collective-permute-done.5), channel_id=1, source_target_pairs={{0,16},{1,17},{2,18},{3,19},{4,20},{5,21},{6,22},{7,23},{8,56},{9,... | collective-permute-start | bytes 2654216 | tf_op jit(solution)/shard_map/ppermute | solution.py:37
  75.6 22.0 %collective-permute-start.19 = (bf16[4,384,384]{2,1,0:T(8,128)(2,1)S(1)}, bf16[4,384,384]{2,1,0:T(8,128)(2,1)S(1)}, u32[]{:S(2)}, u32[]{:S(2)}) collective-permute-start(bf16[4,384,384]{2,1,0:T(8,128)(2,1)S(1)} %constant_dynamic-update-slice_fusion.refs_8_), channel_id=1, source_target_pairs={{0,16},{1,17},{2,18},{3,19},{4,20},{5,21},{6,22},{7,23},{8,56},{9,... | collective-permute-start | bytes 3538952 | tf_op jit(solution)/shard_map/ppermute | solution.py:37
  85.0 7.4 %collective-permute-start.20 = (bf16[2,384,512]{2,1,0:T(8,128)(2,1)S(1)}, bf16[2,384,512]{2,1,0:T(8,128)(2,1)S(1)}, u32[]{:S(2)}, u32[]{:S(2)}) collective-permute-start(bf16[2,384,512]{2,1,0:T(8,128)(2,1)S(1)} %pad_maximum_fusion), channel_id=1, source_target_pairs={{0,8},{1,9},{2,10},{3,11},{4,12},{5,13},{6,14},{7,15},{8,0},{9,1},... | collective-permute-start | bytes 2359304 | tf_op jit(solution)/shard_map/ppermute | solution.py:37
  97.6 12.0 %collective-permute-start.25 = (bf16[4,384,384]{2,1,0:T(8,128)(2,1)S(1)}, bf16[4,384,384]{2,1,0:T(8,128)(2,1)S(1)}, u32[]{:S(2)}, u32[]{:S(2)}) collective-permute-start(bf16[4,384,384]{2,1,0:T(8,128)(2,1)S(1)} %collective-permute-done.19.refs_9_), channel_id=1, source_target_pairs={{0,8},{1,9},{2,10},{3,11},{4,12},{5,13},{6,14},{7,15},{8,0},{9,1},... | collective-permute-start | bytes 3538952 | tf_op jit(solution)/shard_map/ppermute | solution.py:37
  97.7 12.0 %collective-permute-start.24 = (bf16[2,384,384]{2,1,0:T(8,128)(2,1)S(1)}, bf16[2,384,384]{2,1,0:T(8,128)(2,1)S(1)}, u32[]{:S(2)}, u32[]{:S(2)}) collective-permute-start(bf16[2,384,384]{2,1,0:T(8,128)(2,1)S(1)} %slice.60), channel_id=1, source_target_pairs={{0,16},{1,17},{2,18},{3,19},{4,20},{5,21},{6,22},{7,23},{8,56},{9,... | collective-permute-start | bytes 1769480 | tf_op jit(solution)/shard_map/ppermute | solution.py:37
  97.8 11.8 %collective-permute-start.23 = (bf16[512,384]{1,0:T(8,128)(2,1)S(1)}, bf16[512,384]{1,0:T(8,128)(2,1)}, u32[]{:S(2)}, u32[]{:S(2)}) collective-permute-start(bf16[512,384]{1,0:T(8,128)(2,1)S(1)} %get-tuple-element.123.refs_0_), channel_id=1, source_target_pairs={{0,4},{1,5},{2,6},{3,7},{4,0},{5,1},{6,2},{7,3},{8,12},{9,13},{10,... | collective-permute-start | bytes 1179656 | tf_op jit(solution)/shard_map/ppermute | solution.py:37
  99.8 8.2 %collective-permute-start.21 = (bf16[256,384]{1,0:T(8,128)(2,1)S(1)}, bf16[256,384]{1,0:T(8,128)(2,1)S(1)}, u32[]{:S(2)}, u32[]{:S(2)}) collective-permute-start(bf16[256,384]{1,0:T(8,128)(2,1)S(1)} %get-tuple-element.126), channel_id=1, source_target_pairs={{0,1},{1,2},{2,3},{3,0},{4,5},{5,6},{6,7},{7,4},{8,9},{9,10},{10,1... | collective-permute-start | bytes 589832 | tf_op jit(solution)/shard_map/ppermute | solution.py:37
  101.4 7.6 %collective-permute-start.22 = (bf16[256,384]{1,0:T(8,128)(2,1)S(1)}, bf16[256,384]{1,0:T(8,128)(2,1)S(1)}, u32[]{:S(2)}, u32[]{:S(2)}) collective-permute-start(bf16[256,384]{1,0:T(8,128)(2,1)S(1)} %get-tuple-element.127), channel_id=1, source_target_pairs={{0,3},{1,0},{2,1},{3,2},{4,7},{5,4},{6,5},{7,6},{8,11},{9,8},{10,9... | collective-permute-start | bytes 589832 | tf_op jit(solution)/shard_map/ppermute | solution.py:37
  109.7 14.0 %collective-permute-start.32 = (bf16[2,384,384]{2,1,0:T(8,128)(2,1)S(1)}, bf16[2,384,384]{2,1,0:T(8,128)(2,1)S(1)}, u32[]{:S(2)}, u32[]{:S(2)}) collective-permute-start(bf16[2,384,384]{2,1,0:T(8,128)(2,1)S(1)} %collective-permute-done.24.refs_11_), channel_id=1, source_target_pairs={{0,8},{1,9},{2,10},{3,11},{4,12},{5,13},{6,14},{7,15},{8,0},{9,1},... | collective-permute-start | bytes 1769480 | tf_op jit(solution)/shard_map/ppermute | solution.py:37
  109.8 7.8 %collective-permute-start.28 = (bf16[256,384]{1,0:T(8,128)(2,1)S(1)}, bf16[256,384]{1,0:T(8,128)(2,1)S(1)}, u32[]{:S(2)}, u32[]{:S(2)}) collective-permute-start(bf16[256,384]{1,0:T(8,128)(2,1)S(1)} %get-tuple-element.126), channel_id=1, source_target_pairs={{0,3},{1,0},{2,1},{3,2},{4,7},{5,4},{6,5},{7,6},{8,11},{9,8},{10,9... | collective-permute-start | bytes 589832 | tf_op jit(solution)/shard_map/ppermute | solution.py:37
  111.2 9.0 %collective-permute-start.29 = (bf16[256,384]{1,0:T(8,128)(2,1)S(1)}, bf16[256,384]{1,0:T(8,128)(2,1)S(1)}, u32[]{:S(2)}, u32[]{:S(2)}) collective-permute-start(bf16[256,384]{1,0:T(8,128)(2,1)S(1)} %get-tuple-element.127), channel_id=1, source_target_pairs={{0,1},{1,2},{2,3},{3,0},{4,5},{5,6},{6,7},{7,4},{8,9},{9,10},{10,1... | collective-permute-start | bytes 589832 | tf_op jit(solution)/shard_map/ppermute | solution.py:37
  111.9 11.8 %collective-permute-start.30 = (bf16[256,384]{1,0:T(8,128)(2,1)S(1)}, bf16[256,384]{1,0:T(8,128)(2,1)}, u32[]{:S(2)}, u32[]{:S(2)}) collective-permute-start(bf16[256,384]{1,0:T(8,128)(2,1)S(1)} %collective-permute-done.21.refs_4_), channel_id=1, source_target_pairs={{0,1},{1,2},{2,3},{3,0},{4,5},{5,6},{6,7},{7,4},{8,9},{9,10},{10,1... | collective-permute-start | bytes 589832 | tf_op jit(solution)/shard_map/ppermute | solution.py:37
  113.6 10.1 %collective-permute-start.31 = (bf16[256,384]{1,0:T(8,128)(2,1)S(1)}, bf16[256,384]{1,0:T(8,128)(2,1)}, u32[]{:S(2)}, u32[]{:S(2)}) collective-permute-start(bf16[256,384]{1,0:T(8,128)(2,1)S(1)} %collective-permute-done.22.refs_3_), channel_id=1, source_target_pairs={{0,3},{1,0},{2,1},{3,2},{4,7},{5,4},{6,5},{7,6},{8,11},{9,8},{10,9... | collective-permute-start | bytes 589832 | tf_op jit(solution)/shard_map/ppermute | solution.py:37
  124.5 34.0 %collective-permute-start.38 = (bf16[4,384,512]{2,1,0:T(8,128)(2,1)S(1)}, bf16[4,384,512]{2,1,0:T(8,128)(2,1)S(1)}, u32[]{:S(2)}, u32[]{:S(2)}) collective-permute-start(bf16[4,384,512]{2,1,0:T(8,128)(2,1)S(1)} %constant_dynamic-update-slice_fusion.2.refs_14_), channel_id=1, source_target_pairs={{0,16},{1,17},{2,18},{3,19},{4,20},{5,21},{6,22},{7,23},{8,56},{9,... | collective-permute-start | bytes 4718600 | tf_op jit(solution)/shard_map/ppermute | solution.py:37
  126.1 21.1 %collective-permute-start.27 = (bf16[512,384]{1,0:T(8,128)(2,1)}, bf16[512,384]{1,0:T(8,128)(2,1)}, u32[]{:S(2)}, u32[]{:S(2)}) collective-permute-start(bf16[512,384]{1,0:T(8,128)(2,1)} %collective-permute-done.23.refs_1_), channel_id=1, source_target_pairs={{0,1},{1,2},{2,3},{3,0},{4,5},{5,6},{6,7},{7,4},{8,9},{9,10},{10,1... | collective-permute-start | bytes 1179656 | tf_op jit(solution)/shard_map/ppermute | solution.py:37
  126.1 21.1 %collective-permute-start.26 = (bf16[512,384]{1,0:T(8,128)(2,1)}, bf16[512,384]{1,0:T(8,128)(2,1)}, u32[]{:S(2)}, u32[]{:S(2)}) collective-permute-start(bf16[512,384]{1,0:T(8,128)(2,1)} %collective-permute-done.23.refs_1_), channel_id=1, source_target_pairs={{0,3},{1,0},{2,1},{3,2},{4,7},{5,4},{6,5},{7,6},{8,11},{9,8},{10,9... | collective-permute-start | bytes 1179656 | tf_op jit(solution)/shard_map/ppermute | solution.py:37
  129.4 17.8 %collective-permute-start.33 = (bf16[256,384]{1,0:T(8,128)(2,1)}, bf16[256,384]{1,0:T(8,128)(2,1)}, u32[]{:S(2)}, u32[]{:S(2)}) collective-permute-start(bf16[256,384]{1,0:T(8,128)(2,1)} %collective-permute-done.30.refs_6_), channel_id=1, source_target_pairs={{0,4},{1,5},{2,6},{3,7},{4,0},{5,1},{6,2},{7,3},{8,12},{9,13},{10,... | collective-permute-start | bytes 589832 | tf_op jit(solution)/shard_map/ppermute | solution.py:37
  131.1 16.1 %collective-permute-start.34 = (bf16[256,384]{1,0:T(8,128)(2,1)}, bf16[256,384]{1,0:T(8,128)(2,1)}, u32[]{:S(2)}, u32[]{:S(2)}) collective-permute-start(bf16[256,384]{1,0:T(8,128)(2,1)} %collective-permute-done.31.refs_7_), channel_id=1, source_target_pairs={{0,4},{1,5},{2,6},{3,7},{4,0},{5,1},{6,2},{7,3},{8,12},{9,13},{10,... | collective-permute-start | bytes 589832 | tf_op jit(solution)/shard_map/ppermute | solution.py:37
  152.1 5.3 %collective-permute-start.37 = (f32[8,512]{1,0:T(8,128)S(1)}, f32[8,512]{1,0:T(8,128)S(1)}, u32[]{:S(2)}, u32[]{:S(2)}) collective-permute-start(f32[8,512]{1,0:T(8,128)S(1)} %get-tuple-element.149), channel_id=1, source_target_pairs={{0,2},{1,3},{2,0},{3,1},{4,6},{5,7},{6,4},{7,5},{8,10},{9,11},{10,... | collective-permute-start | bytes 49160 | tf_op jit(solution)/shard_map/ppermute | solution.py:37
  152.1 5.2 %collective-permute-start.36 = (f32[8,512]{1,0:T(8,128)S(1)}, f32[8,512]{1,0:T(8,128)S(1)}, u32[]{:S(2)}, u32[]{:S(2)}) collective-permute-start(f32[8,512]{1,0:T(8,128)S(1)} %get-tuple-element.149), channel_id=1, source_target_pairs={{0,3},{1,0},{2,1},{3,2},{4,7},{5,4},{6,5},{7,6},{8,11},{9,8},{10,9... | collective-permute-start | bytes 49160 | tf_op jit(solution)/shard_map/ppermute | solution.py:37
  153.6 4.9 %collective-permute-start.35 = (f32[8,512]{1,0:T(8,128)S(1)}, f32[8,512]{1,0:T(8,128)S(1)}, u32[]{:S(2)}, u32[]{:S(2)}) collective-permute-start(f32[8,512]{1,0:T(8,128)S(1)} %get-tuple-element.149), channel_id=1, source_target_pairs={{0,1},{1,2},{2,3},{3,0},{4,5},{5,6},{6,7},{7,4},{8,9},{9,10},{10,1... | collective-permute-start | bytes 49160 | tf_op jit(solution)/shard_map/ppermute | solution.py:37
  158.6 15.7 %collective-permute-start.42 = (bf16[4,384,512]{2,1,0:T(8,128)(2,1)S(1)}, bf16[4,384,512]{2,1,0:T(8,128)(2,1)S(1)}, u32[]{:S(2)}, u32[]{:S(2)}) collective-permute-start(bf16[4,384,512]{2,1,0:T(8,128)(2,1)S(1)} %collective-permute-done.38.refs_15_), channel_id=1, source_target_pairs={{0,8},{1,9},{2,10},{3,11},{4,12},{5,13},{6,14},{7,15},{8,0},{9,1},... | collective-permute-start | bytes 4718600 | tf_op jit(solution)/shard_map/ppermute | solution.py:37
  158.7 20.9 %collective-permute-start.48 = (bf16[2,384,512]{2,1,0:T(8,128)(2,1)S(1)}, bf16[2,384,512]{2,1,0:T(8,128)(2,1)}, u32[]{:S(2)}, u32[]{:S(2)}) collective-permute-start(bf16[2,384,512]{2,1,0:T(8,128)(2,1)S(1)} %slice.65), channel_id=1, source_target_pairs={{0,16},{1,17},{2,18},{3,19},{4,20},{5,21},{6,22},{7,23},{8,56},{9,... | collective-permute-start | bytes 2359304 | tf_op jit(solution)/shard_map/ppermute | solution.py:37
  159.5 5.0 %collective-permute-start.41 = (f32[8,512]{1,0:T(8,128)S(1)}, f32[8,512]{1,0:T(8,128)S(1)}, u32[]{:S(2)}, u32[]{:S(2)}) collective-permute-start(f32[8,512]{1,0:T(8,128)S(1)} %add_add_fusion), channel_id=1, source_target_pairs={{0,4},{1,5},{2,6},{3,7},{4,0},{5,1},{6,2},{7,3},{8,12},{9,13},{10,... | collective-permute-start | bytes 49160 | tf_op jit(solution)/shard_map/ppermute | solution.py:37
  161.3 13.0 %collective-permute-start.39 = (bf16[256,768]{1,0:T(8,128)(2,1)S(1)}, bf16[256,768]{1,0:T(8,128)(2,1)S(1)}, u32[]{:S(2)}, u32[]{:S(2)}) collective-permute-start(bf16[256,768]{1,0:T(8,128)(2,1)S(1)} %get-tuple-element.159), channel_id=1, source_target_pairs={{0,1},{1,2},{2,3},{3,0},{4,5},{5,6},{6,7},{7,4},{8,9},{9,10},{10,1... | collective-permute-start | bytes 1179656 | tf_op jit(solution)/shard_map/ppermute | solution.py:37
  161.3 13.0 %collective-permute-start.40 = (bf16[256,768]{1,0:T(8,128)(2,1)S(1)}, bf16[256,768]{1,0:T(8,128)(2,1)S(1)}, u32[]{:S(2)}, u32[]{:S(2)}) collective-permute-start(bf16[256,768]{1,0:T(8,128)(2,1)S(1)} %get-tuple-element.160), channel_id=1, source_target_pairs={{0,3},{1,0},{2,1},{3,2},{4,7},{5,4},{6,5},{7,6},{8,11},{9,8},{10,9... | collective-permute-start | bytes 1179656 | tf_op jit(solution)/shard_map/ppermute | solution.py:37
  164.5 20.2 %collective-permute-start.47 = (bf16[512,768]{1,0:T(8,128)(2,1)S(1)}, bf16[512,768]{1,0:T(8,128)(2,1)}, u32[]{:S(2)}, u32[]{:S(2)}) collective-permute-start(bf16[512,768]{1,0:T(8,128)(2,1)S(1)} %copy-done.19), channel_id=1, source_target_pairs={{0,4},{1,5},{2,6},{3,7},{4,0},{5,1},{6,2},{7,3},{8,12},{9,13},{10,... | collective-permute-start | bytes 2359304 | tf_op jit(solution)/shard_map/ppermute | solution.py:37
  175.4 12.8 %collective-permute-start.43 = (bf16[256,768]{1,0:T(8,128)(2,1)S(1)}, bf16[256,768]{1,0:T(8,128)(2,1)S(1)}, u32[]{:S(2)}, u32[]{:S(2)}) collective-permute-start(bf16[256,768]{1,0:T(8,128)(2,1)S(1)} %get-tuple-element.159), channel_id=1, source_target_pairs={{0,3},{1,0},{2,1},{3,2},{4,7},{5,4},{6,5},{7,6},{8,11},{9,8},{10,9... | collective-permute-start | bytes 1179656 | tf_op jit(solution)/shard_map/ppermute | solution.py:37
  178.8 13.2 %collective-permute-start.44 = (bf16[256,768]{1,0:T(8,128)(2,1)S(1)}, bf16[256,768]{1,0:T(8,128)(2,1)S(1)}, u32[]{:S(2)}, u32[]{:S(2)}) collective-permute-start(bf16[256,768]{1,0:T(8,128)(2,1)S(1)} %get-tuple-element.160), channel_id=1, source_target_pairs={{0,1},{1,2},{2,3},{3,0},{4,5},{5,6},{6,7},{7,4},{8,9},{9,10},{10,1... | collective-permute-start | bytes 1179656 | tf_op jit(solution)/shard_map/ppermute | solution.py:37
  178.8 20.4 %collective-permute-start.45 = (bf16[256,768]{1,0:T(8,128)(2,1)S(1)}, bf16[256,768]{1,0:T(8,128)(2,1)S(1)}, u32[]{:S(2)}, u32[]{:S(2)}) collective-permute-start(bf16[256,768]{1,0:T(8,128)(2,1)S(1)} %collective-permute-done.39.refs_4_), channel_id=1, source_target_pairs={{0,1},{1,2},{2,3},{3,0},{4,5},{5,6},{6,7},{7,4},{8,9},{9,10},{10,1... | collective-permute-start | bytes 1179656 | tf_op jit(solution)/shard_map/ppermute | solution.py:37
  179.6 19.6 %collective-permute-start.46 = (bf16[256,768]{1,0:T(8,128)(2,1)S(1)}, bf16[256,768]{1,0:T(8,128)(2,1)S(1)}, u32[]{:S(2)}, u32[]{:S(2)}) collective-permute-start(bf16[256,768]{1,0:T(8,128)(2,1)S(1)} %collective-permute-done.40.refs_3_), channel_id=1, source_target_pairs={{0,3},{1,0},{2,1},{3,2},{4,7},{5,4},{6,5},{7,6},{8,11},{9,8},{10,9... | collective-permute-start | bytes 1179656 | tf_op jit(solution)/shard_map/ppermute | solution.py:37
  199.9 25.5 %collective-permute-start.50 = (bf16[512,768]{1,0:T(8,128)(2,1)}, bf16[512,768]{1,0:T(8,128)(2,1)}, u32[]{:S(2)}, u32[]{:S(2)}) collective-permute-start(bf16[512,768]{1,0:T(8,128)(2,1)} %collective-permute-done.47.refs_1_), channel_id=1, source_target_pairs={{0,1},{1,2},{2,3},{3,0},{4,5},{5,6},{6,7},{7,4},{8,9},{9,10},{10,1... | collective-permute-start | bytes 2359304 | tf_op jit(solution)/shard_map/ppermute | solution.py:37
  200.7 24.7 %collective-permute-start.49 = (bf16[512,768]{1,0:T(8,128)(2,1)}, bf16[512,768]{1,0:T(8,128)(2,1)}, u32[]{:S(2)}, u32[]{:S(2)}) collective-permute-start(bf16[512,768]{1,0:T(8,128)(2,1)} %collective-permute-done.47.refs_1_), channel_id=1, source_target_pairs={{0,3},{1,0},{2,1},{3,2},{4,7},{5,4},{6,5},{7,6},{8,11},{9,8},{10,9... | collective-permute-start | bytes 2359304 | tf_op jit(solution)/shard_map/ppermute | solution.py:37
  203.2 5.6 %collective-permute-start.53 = (bf16[2,384,512]{2,1,0:T(8,128)(2,1)}, bf16[2,384,512]{2,1,0:T(8,128)(2,1)}, u32[]{:S(2)}, u32[]{:S(2)}) collective-permute-start(bf16[2,384,512]{2,1,0:T(8,128)(2,1)} %collective-permute-done.48.refs_17_), channel_id=1, source_target_pairs={{0,8},{1,9},{2,10},{3,11},{4,12},{5,13},{6,14},{7,15},{8,0},{9,1},... | collective-permute-start | bytes 2359304 | tf_op jit(solution)/shard_map/ppermute | solution.py:37
  205.2 18.8 %collective-permute-start.51 = (bf16[256,768]{1,0:T(8,128)(2,1)}, bf16[256,768]{1,0:T(8,128)(2,1)S(1)}, u32[]{:S(2)}, u32[]{:S(2)}) collective-permute-start(bf16[256,768]{1,0:T(8,128)(2,1)} %copy-done.33), channel_id=1, source_target_pairs={{0,4},{1,5},{2,6},{3,7},{4,0},{5,1},{6,2},{7,3},{8,12},{9,13},{10,... | collective-permute-start | bytes 1179656 | tf_op jit(solution)/shard_map/ppermute | solution.py:37
  205.5 19.9 %collective-permute-start.52 = (bf16[256,768]{1,0:T(8,128)(2,1)}, bf16[256,768]{1,0:T(8,128)(2,1)S(1)}, u32[]{:S(2)}, u32[]{:S(2)}) collective-permute-start(bf16[256,768]{1,0:T(8,128)(2,1)} %copy-done.35), channel_id=1, source_target_pairs={{0,4},{1,5},{2,6},{3,7},{4,0},{5,1},{6,2},{7,3},{8,12},{9,13},{10,... | collective-permute-start | bytes 1179656 | tf_op jit(solution)/shard_map/ppermute | solution.py:37
  230.9 19.5 %all-to-all-start = ((bf16[8,128,512]{2,1,0:T(8,128)(2,1)}), bf16[8,128,512]{2,1,0:T(8,128)(2,1)S(1)}, u32[]{:S(2)}, u32[]{:S(2)}) async-start(bf16[8,128,512]{2,1,0:T(8,128)(2,1)} %project.3), calls=%async_computation | async-start | bytes 2097152 | tf_op jit(solution)/shard_map/all_to_all | solution.py:630
  (55 other events, 262.4 us)

commit v3 on v2

--- a/solution.py
+++ b/solution.py
@@ -14,6 +14,7 @@
 AXES = ("dp", "mp")
 MEGA = 1024 * 1024
 epsilon = 1e-06
+EXTRA = 16
 SMALL = pl.CostEstimate(flops=1, bytes_accessed=1, transcendentals=0)
 
 
@@ -149,7 +150,7 @@
         compiler_params=pltpu.CompilerParams(vmem_limit_bytes=16 * MEGA),
         cost_estimate=SMALL,
         name="norm_columns",
-    )(values, gain.reshape(1, width))
+    )(*in_hbm([values]), gain.reshape(1, width))
 
 
 def row_norm(values, gain):
@@ -206,7 +207,7 @@
     in_specs += [
         pl.BlockSpec((number, 1, depth, wide), lambda h, index: (0, h, 0, 0)) for number in counts
     ]
-    operands = [columns] * sum(counts) + shards
+    operands = [columns] * sum(counts) + (in_hbm(shards) if gains is None else shards)
     total_spec = pl.BlockSpec((1, rows, wide), lambda h, index: (h, 0, 0))
     if total is not None:
         in_specs.append(total_spec)
@@ -238,85 +239,132 @@
     )(index, *operands)
 
 
-def load_shards(parts, held_ref, sems):
+def start_shards(parts, held_ref, sems):
     at = 0
     copies = []
     for k, part in enumerate(parts):
         number = part.shape[0]
         copies.append(pltpu.make_async_copy(part, held_ref.at[pl.ds(at, number)], sems.at[k]))
+        copies[-1].start()
         at += number
-    for copy in copies:
-        copy.start()
+    return copies
+
+
+def start_pieces(pieces, near, near_ref, sems):
+    copies = []
+    count = 0
+    for at, piece in enumerate(pieces):
+        copies.append([])
+        rows = near_ref.shape[1] // len(piece)
+        for part, (k, first) in enumerate(piece):
+            source = near[k].at[pl.ds(first, rows)]
+            place = near_ref.at[at, pl.ds(part * rows, rows)]
+            copies[-1].append(pltpu.make_async_copy(source, place, sems.at[count]))
+            copies[-1][-1].start()
+            count += 1
+    return copies
+
+
+def wait_all(copies):
     for copy in copies:
         copy.wait()
-
-
-def read_piece(piece, refs):
-    parts = [refs[k][...] for k in piece]
-    return parts[0] if len(parts) == 1 else jnp.concatenate(parts, 0)
 
 
 def out_kernel(pieces, held, count, kept, finish, index_ref, *refs):
     near, refs = refs[:held], refs[held:]
     parts, refs = refs[:count], refs[count:]
     if finish:
-        given_ref, own_ref, block_ref, *half_refs, stats_ref, held_ref, sems = refs
+        given_ref, own_ref, block_ref, *half_refs, stats_ref = refs[:-4]
     else:
-        total_ref, kept_ref, held_ref, sems = refs
-    load_shards(parts, held_ref, sems)
+        total_ref, kept_ref = refs[:-4]
+    near_ref, held_ref, near_sems, sems = refs[-4:]
+    shard_copies = start_shards(parts, held_ref, sems)
+    piece_copies = start_pieces(pieces, near, near_ref, near_sems)
+    wait_all(shard_copies)
     depth = held_ref.shape[1]
-    sums, squares = 0.0, 0.0
-    for half in range(2):
-        total = given_ref[half] if finish else None
-        for k, piece in enumerate(pieces):
+    total = [given_ref[0], given_ref[1]] if finish else [None, None]
+    for k in range(len(pieces)):
+        wait_all(piece_copies[k])
+        for half in range(2):
             term = lax.dot_general(
-                read_piece(piece, near),
+                near_ref[k],
                 held_ref[2 * k + half if finish else index_ref[2 * k + half]],
                 (((1,), (1,)), ((), ())),
                 preferred_element_type=jnp.float32,
             )
             term = term.astype(jnp.bfloat16).astype(jnp.float32)
-            total = term if total is None else total + term
-        if not finish:
-            total_ref[half] = total
-            continue
+            total[half] = term if total[half] is None else total[half] + term
+    if not finish:
+        total_ref[0] = total[0]
+        total_ref[1] = total[1]
+        for k in range(kept):
+            kept_ref[k] = held_ref[index_ref[2 * len(pieces) + k]]
+        return
+    sums, squares = 0.0, 0.0
+    for half in range(2):
         cols = slice(half * depth, (half + 1) * depth)
-        block = (own_ref[:, cols].astype(jnp.float32) + total).astype(jnp.bfloat16)
+        block = (own_ref[:, cols].astype(jnp.float32) + total[half]).astype(jnp.bfloat16)
         block_ref[:, cols] = block
         rows = block.shape[0] // 2
-        half_refs[0][:, cols] = block[:rows]
-        half_refs[1][:, cols] = block[rows:]
+        half_refs[0][:rows, cols] = block[:rows]
+        half_refs[1][:rows, cols] = block[rows:]
         block = block.astype(jnp.float32)
         sums += jnp.sum(block, 1, keepdims=True)
         squares += jnp.sum(block * block, 1, keepdims=True)
-    if not finish:
-        for k in range(kept):
-            kept_ref[k] = held_ref[index_ref[2 * len(pieces) + k]]
-        return
     lane = lax.broadcasted_iota(jnp.int32, (sums.shape[0], 128), 1)
-    both = jnp.where(lane == 0, sums, squares)
-    stats_ref[...] = both.T[:8]
+    both = jnp.where(lane == 0, sums, squares).T[:8]
+    stats_ref[...] = both
+    row = lax.broadcasted_iota(jnp.int32, (EXTRA, both.shape[1]), 0)
+    carried = jnp.zeros(row.shape, jnp.float32)
+    for k in range(2):
+        rest = both[k : k + 1]
+        for part in range(3):
+            rounded = rest.astype(jnp.bfloat16).astype(jnp.float32)
+            carried = jnp.where(row == 3 * k + part, rounded, carried)
+            rest = rest - rounded
+    carried = carried.astype(jnp.bfloat16)
+    for half_ref in half_refs:
+        half_ref[rows:, : carried.shape[1]] = carried
+        half_ref[rows:, carried.shape[1] :] = jnp.zeros(
+            (EXTRA, half_ref.shape[1] - carried.shape[1]), jnp.bfloat16
+        )
+
+
+def held_scratch(pieces, near, parts, wide):
+    rows = near[0].shape[0]
+    depth = parts[0].shape[1]
+    return [
+        pltpu.VMEM((len(pieces), rows, near[0].shape[1]), jnp.bfloat16),
+        pltpu.VMEM((sum(part.shape[0] for part in parts), depth, wide), jnp.bfloat16),
+        pltpu.SemaphoreType.DMA((sum(len(piece) for piece in pieces),)),
+        pltpu.SemaphoreType.DMA((len(parts),)),
+    ]
+
+
+def in_hbm(arrays):
+    return [pltpu.with_memory_space_constraint(array, pltpu.HBM) for array in arrays]
 
 
 def whole(shape):
     return pl.BlockSpec(shape, lambda i, index: (0,) * len(shape))
 
 
-def out_project(near, pieces, parts, index, kept=0, total=None, own=None):
+def out_project(near, pieces, parts, index, kept=0, total=None, patches=None):
     depth = parts[0].shape[1]
     finish = total is not None
-    in_specs = [whole(part.shape) for part in near]
-    in_specs += [pl.BlockSpec(memory_space=pl.ANY) for _ in parts]
-    operands = list(near) + list(parts)
+    in_specs = [pl.BlockSpec(memory_space=pltpu.HBM) for _ in near]
+    in_specs += [pl.BlockSpec(memory_space=pl.ANY if finish else pltpu.HBM) for _ in parts]
+    operands = in_hbm(near) + (parts if finish else in_hbm(parts))
     rows = near[0].shape[0]
     if finish:
-        rows = own.shape[0]
-        in_specs += [whole(total.shape), whole(own.shape)]
-        operands += [total, own]
+        rows = patches.shape[0]
+        in_specs.append(whole(total.shape))
+        in_specs.append(pl.BlockSpec((rows, 2 * depth), lambda i, index: (0, index[0])))
+        operands += [total, *in_hbm([patches])]
         out_shape = [
             jax.ShapeDtypeStruct((rows, 2 * depth), jnp.bfloat16),
-            jax.ShapeDtypeStruct((rows // 2, 2 * depth), jnp.bfloat16),
-            jax.ShapeDtypeStruct((rows // 2, 2 * depth), jnp.bfloat16),
+            jax.ShapeDtypeStruct((rows // 2 + EXTRA, 2 * depth), jnp.bfloat16),
+            jax.ShapeDtypeStruct((rows // 2 + EXTRA, 2 * depth), jnp.bfloat16),
             jax.ShapeDtypeStruct((8, rows), jnp.float32),
         ]
     else:
@@ -331,10 +379,7 @@
             grid=(1,),
             in_specs=in_specs,
             out_specs=[whole(out.shape) for out in out_shape],
-            scratch_shapes=[
-                pltpu.VMEM((sum(part.shape[0] for part in parts), depth, depth), jnp.bfloat16),
-                pltpu.SemaphoreType.DMA((len(parts),)),
-            ],
+            scratch_shapes=held_scratch(pieces, near, parts, depth),
         ),
         out_shape=out_shape,
         compiler_params=pltpu.CompilerParams(vmem_limit_bytes=20 * MEGA),
@@ -343,24 +388,61 @@
     )(index, *operands)
 
 
+def sums_kernel(own_ref, *refs):
+    *carried, out_ref = refs
+    total = own_ref[...]
+    row = lax.broadcasted_iota(jnp.int32, total.shape, 0)
+    for ref in carried:
+        parts = ref[...].astype(jnp.float32)
+        sums, squares = (
+            parts[k : k + 1] + parts[k + 1 : k + 2] + parts[k + 2 : k + 3] for k in (0, 3)
+        )
+        total = total + jnp.where(row == 0, sums, squares)
+    out_ref[...] = total
+
+
+def add_sums(own, carried):
+    rows = own.shape[1]
+    in_specs = [pl.BlockSpec(own.shape, lambda i: (0, 0))]
+    for _, first in carried:
+        place = (first + PATCHES) // EXTRA
+        in_specs.append(
+            pl.BlockSpec((EXTRA, rows), functools.partial(lambda place, i: (place, 0), place))
+        )
+    return pl.pallas_call(
+        sums_kernel,
+        grid=(1,),
+        in_specs=in_specs,
+        out_specs=pl.BlockSpec(own.shape, lambda i: (0, 0)),
+        out_shape=jax.ShapeDtypeStruct(own.shape, own.dtype),
+        compiler_params=pltpu.CompilerParams(vmem_limit_bytes=4 * MEGA),
+        cost_estimate=SMALL,
+        name="add_sums",
+    )(own, *in_hbm([array for array, _ in carried]))
+
+
 def project_kernel(pieces, held, count, kept, finish, width, index_ref, *refs):
     near, refs = refs[:held], refs[held:]
     stats_ref, refs = refs[0], refs[1:]
     gains, refs = refs[: len(pieces)], refs[len(pieces) :]
     parts, refs = refs[:count], refs[count:]
     if finish:
-        total, (out_ref, held_ref, sems, blocks_ref) = refs[0][...], refs[1:]
+        total, (out_ref, *refs, blocks_ref) = refs[0][...], refs[1:]
     else:
-        total, (out_ref, kept_ref, held_ref, sems) = None, refs
-    load_shards(parts, held_ref, sems)
+        total, (out_ref, kept_ref, *refs) = None, refs
+    near_ref, held_ref, near_sems, sems = refs
+    depth = held_ref.shape[1]
+    shard_copies = start_shards(parts, held_ref, sems)
+    piece_copies = start_pieces(pieces, near, near_ref, near_sems)
     rows = stats_ref.shape[1]
     row = lax.broadcasted_iota(jnp.int32, (128, rows), 0)
     stats = jnp.where(row == 0, stats_ref[0:1], stats_ref[1:2]).T
     row_mean = stats[:, 0:1] / width
     scale = lax.rsqrt(stats[:, 1:2] / width - row_mean * row_mean + epsilon)
-    depth = held_ref.shape[1]
-    for k, piece in enumerate(pieces):
-        values = read_piece(piece, near).astype(jnp.float32)
+    wait_all(shard_copies)
+    for k in range(len(pieces)):
+        wait_all(piece_copies[k])
+        values = near_ref[k].astype(jnp.float32)
         normed = ((values - row_mean) * scale * gains[k][...]).astype(jnp.bfloat16)
         for half in range(2):
             at = 2 * k + half if finish else index_ref[2 * k + half]
@@ -389,18 +471,16 @@
     count = len(pieces)
     finish = total is not None
     at = 0 if finish else 2 * count + kept
-    in_specs = [whole(part.shape) for part in near]
+    in_specs = [pl.BlockSpec(memory_space=pltpu.HBM) for _ in near]
     in_specs.append(whole(stats.shape))
     in_specs += [
         pl.BlockSpec((1, 2 * depth), functools.partial(lambda k, i, index: (0, index[k]), k))
         for k in range(at, at + count)
     ]
-    in_specs += [pl.BlockSpec(memory_space=pl.ANY) for _ in parts]
-    operands = list(near) + [stats] + [gain.reshape(1, width)] * count + list(parts)
-    scratch = [
-        pltpu.VMEM((sum(part.shape[0] for part in parts), depth, wide), jnp.bfloat16),
-        pltpu.SemaphoreType.DMA((len(parts),)),
-    ]
+    in_specs += [pl.BlockSpec(memory_space=pl.ANY if finish else pltpu.HBM) for _ in parts]
+    operands = in_hbm(near) + [stats] + [gain.reshape(1, width)] * count
+    operands += parts if finish else in_hbm(parts)
+    scratch = held_scratch(pieces, near, parts, wide)
     if finish:
         in_specs.append(whole(total.shape))
         operands.append(total)
@@ -473,6 +553,17 @@
     return lax.optimization_barrier(values)
 
 
+def piece_places(step):
+    first = (
+        ((0, 0),),
+        ((1, 0),),
+        ((5, step), (3, 0)),
+        ((2, 0), (4, step)),
+        ((4, 0), (5, 0)),
+    )
+    return first, (((0, 0),), ((1, 0),), ((2, 0), (2, PATCHES)))
+
+
 def local(
     patches,
     norm_gain,
@@ -495,9 +586,9 @@
     own = qkv_weight.transpose(1, 0, 2)
     first = spread_y(own)
     other = swap_core(own)
-    far = swap_zh(own)
     turned = transpose_mesh(out_weight)
     (other,) = join(other)
+    far = swap_zh(join(own, other)[0])
     beside = spread_y(other)
     columns = norm_columns(join(patches, other)[0], norm_gain, 16)
     total = accumulate(columns, [own, other], met[0:2])
@@ -517,20 +608,18 @@
         met[2:8],
         total,
     )
-
     turned_far, proj_far, total = join(turned_far, proj_far, total)
     out_mine = jnp.stack([turned, turned_far])
     proj_mine = jnp.stack([proj_weight, proj_far])
-    own_cols = lax.dynamic_slice_in_dim(patches, mp * (2 * 384), 2 * 384, 1)
-    far_first, second, far_beside, out_mine, proj_mine, own_cols, total = join(
-        far_first, second, far_beside, out_mine, proj_mine, own_cols, total
+
+    far_first, second, far_beside, out_mine, proj_mine, total = join(
+        far_first, second, far_beside, out_mine, proj_mine, total
     )
     far_second = spread_y(far_first)
     far_first_other, second_other, far_beside_other, out_other = join(
         swap_core(far_first), swap_core(second), swap_core(far_beside), swap_core(out_mine)
     )
     out_quad = jnp.concatenate([out_mine, out_other])
-    out_first = spread_y(out_quad)
     total = accumulate(
         columns,
         [far_first, far_first_other, second, second_other, far_beside, far_beside_other],
@@ -538,69 +627,62 @@
         total,
     )
 
-    far_second, proj_mine, total = join(far_second, proj_mine, total)
+    far_second, out_quad, proj_mine, total = join(far_second, out_quad, proj_mine, total)
     far_second_other = swap_core(far_second)
+    out_first = spread_y(out_quad)
     proj_other = swap_core(proj_mine)
     attended = accumulate(
         columns, [far_second, far_second_other], met[14:16], total, qk_gain.transpose(1, 0, 2)
     )
 
-    whole_att, low, high, out_first, proj_other = join(*attended, out_first, proj_other)
+    whole_att, low, high, proj_other = join(*attended, proj_other)
     proj_quad = jnp.concatenate([proj_mine, proj_other])
     far = swap_zl(whole_att)
+    left_low, right_high, far, out_first, low, high = join(
+        shift_x(low, 1), shift_x(high, -1), far, out_first, low, high
+    )
     out_second = spread_y(out_first[:2])
     out_first_other = swap_core(out_first)
-    left_low, right_high, far, out_second, out_first_other, low, high = join(
-        shift_x(low, 1), shift_x(high, -1), far, out_second, out_first_other, low, high
-    )
-    near = [whole_att, far]
+    from_left, from_right, out_second, out_first_other, proj_quad = join(
+        shift_x(jnp.concatenate([left_low, high]), 1),
+        shift_x(jnp.concatenate([right_high, low]), -1),
+        out_second,
+        out_first_other,
+        proj_quad,
+    )
+    near = [whole_att, far, left_low, right_high, from_left, from_right]
+    pieces, last_pieces = piece_places(PATCHES)
     out_second_other = swap_core(out_second)
-    right_low, left_high, beyond_low, beyond_high, out_second_other = join(
-        shift_x(low, -1),
-        shift_x(high, 1),
-        shift_x(left_low, 1),
-        shift_x(right_high, -1),
-        out_second_other,
-    )
-    near += [right_low, right_high, left_low, left_high, beyond_low, beyond_high]
-    proj_first = spread_y(join(proj_quad, out_second_other)[0])
-    last = [shift_x(far, -1), shift_x(far, 1), swap_zl(beyond_low), swap_zl(beyond_high)]
-    pieces = ((0,), (1,), (2, 3), (4, 5), (6, 7))
-    last_pieces = ((0,), (1,), (2, 3))
-    total, left = out_project(
-        near,
-        pieces,
-        [out_quad, out_first, out_first_other, out_second, out_second_other],
-        shards,
-        kept=6,
-    )
-    *last, total, left = join(*last, total, left)
+    proj_first = spread_y(proj_quad)
+    beyond = jnp.concatenate([from_left[:PATCHES], from_right[:PATCHES]])
+    last = [shift_x(far, -1), shift_x(far, 1), swap_zl(beyond)]
+    parts = [out_quad, out_first, out_first_other, out_second, out_second_other]
+    total, left = out_project(near, pieces, parts, shards, kept=6)
     block_out, low, high, stats = out_project(
-        last, last_pieces, [left], shards, total=total, own=own_cols
-    )
-
-    stats_x = join(shift_x(stats, 1), shift_x(stats, -1), shift_x(stats, 2))
-    stats = stats + stats_x[0] + stats_x[1] + stats_x[2]
-    low, high, whole_block, stats, proj_first = join(low, high, block_out, stats, proj_first)
+        last, last_pieces, [left], mp_slot, total=total, patches=patches
+    )
+
+    proj_first, whole_block, low, high, stats = join(proj_first, block_out, low, high, stats)
     far = swap_zl(whole_block)
     proj_second = spread_y(proj_first[:2])
     proj_first_other = swap_core(proj_first)
-    left_low, right_high, stats_z, proj_first_other, low, high = join(
-        shift_x(low, 1), shift_x(high, -1), swap_zl(stats), proj_first_other, low, high
-    )
+    left_low, right_high, proj_first_other, proj_second, low, high = join(
+        shift_x(low, 1), shift_x(high, -1), proj_first_other, proj_second, low, high
+    )
+    from_left, from_right, far = join(
+        shift_x(jnp.concatenate([left_low, high]), 1),
+        shift_x(jnp.concatenate([right_high, low]), -1),
+        far,
+    )
+    stats = add_sums(stats, [(left_low, 0), (right_high, 0), (from_left, 0)])
+    stats_z = swap_zl(stats)
     stats = stats + stats_z
-    right_low, left_high, beyond_low, beyond_high, far, proj_second = join(
-        shift_x(low, -1),
-        shift_x(high, 1),
-        shift_x(left_low, 1),
-        shift_x(right_high, -1),
-        far,
-        proj_second,
-    )
-    near = [whole_block, far]
-    near += [right_low, right_high, left_low, left_high, beyond_low, beyond_high]
-    proj_second_other = swap_core(proj_second)
-    last = [shift_x(far, -1), shift_x(far, 1), swap_zl(beyond_low), swap_zl(beyond_high)]
+    near = [whole_block, far, left_low, right_high, from_left, from_right]
+    pieces, last_pieces = piece_places(PATCHES + EXTRA)
+    beyond = jnp.concatenate([from_left[:PATCHES], from_right[:PATCHES]])
+    beyond = join(beyond, stats_z)[0]
+    last = [shift_x(far, -1), shift_x(far, 1), swap_zl(beyond)]
+    parts = [proj_quad, proj_first, proj_first_other, proj_second, swap_core(proj_second)]
 
     slot = slot_offset // HALF
     block = jnp.arange(8, dtype=jnp.int32)
@@ -613,11 +695,10 @@
         pieces,
         stats,
         final_gain,
-        [proj_quad, proj_first, proj_first_other, proj_second, proj_second_other],
+        parts,
         jnp.concatenate([shards, groups[:5]]),
         kept=6,
     )
-    *last, total, left = join(*last, total, left)
     (outgoing,) = project(
         last,
         last_pieces,

time: 254 us -> 228 us (0.90)
  local copies, waits for them, and re-layouts: 41 us -> 7.47 us
  waiting for transfers between devices: 86.3 us -> 98.4 us
  starting transfers between devices: 65.8 us -> 55.2 us
  Pallas kernels: 52.2 us -> 59.2 us
    unnamed x98 -> x74, local copies, waits for them, and re-layouts: 35.7 us -> 4.31 us
    ppermute x54 -> x45, waiting for transfers between devices: 71.3 us -> 86.8 us  [move(): return lax.ppermute(values, AXES, pairs)]
    ppermute x54 -> x45, starting transfers between devices: 62.1 us -> 51 us  [move(): return lax.ppermute(values, AXES, pairs)]
    all_to_all x1, waiting for transfers between devices: 15.1 us -> 11.6 us  [local(): lax.all_to_all(outgoing, 'mp', split_axis=0, concat_axis=0, tiled=True)]
  transfers between devices with their start and end apart: 55 -> 46, of which waited for: 27 -> 25; matrix products, arithmetic and copies ran while one was open for 4% -> 3% of each run, Pallas kernels for 18% -> 23%
where the time goes in v3:
time: 228 us; the launch traced here: 227 us
  waiting for transfers between devices  98.4 us (43%)
  Pallas kernels  59.2 us (26%)
  starting transfers between devices  55.2 us (24%)
  local copies, waits for them, and re-layouts  7.47 us (3%)
  other arithmetic  3.98 us (2%)
  between operations  3.25 us (1%)
    ppermute x45, waiting for transfers between devices, move(): return lax.ppermute(values, AXES, pairs)  86.8 us
    ppermute x45, starting transfers between devices, move(): return lax.ppermute(values, AXES, pairs)  51 us
    pallas_call x4, Pallas kernels, accumulate(): pl.pallas_call(functools.partial(accumulate_kernel, counts, total is not...  22.8 us
    pallas_call x2, Pallas kernels, project(): pl.pallas_call(functools.partial(project_kernel, pieces, len(near), len(p...  12.9 us
    pallas_call x2, Pallas kernels, out_project(): pl.pallas_call(functools.partial(out_kernel, pieces, len(near), len(parts...  12.5 us
    all_to_all x1, waiting for transfers between devices, local(): lax.all_to_all(outgoing, 'mp', split_axis=0, concat_axis=0, tiled=True)  11.6 us
    pallas_call x1, Pallas kernels, norm_columns(): pl.pallas_call(norm_kernel, grid=(rows // block,), in_specs=[pl.BlockSpec...  8.52 us
  transfers between devices with their start and end apart: 46, of which 25 were waited for; matrix products, arithmetic and copies ran while one was open for 3% of the time, Pallas kernels for 23%

profile of v3, /device:TPU:0, one launch (start us, length us, event | category | flops | bytes accessed | tf_op | source)
XLA Modules:
  0.0 227.4 jit_solution(18391954791091894822)
XLA Ops:
  0.7 1.7 collective-permute-start.2
  3.3 4.0 %collective-permute-start.1 = (bf16[3,384,384]{2,1,0:T(8,128)(2,1)}, bf16[3,384,384]{2,1,0:T(8,128)(2,1)S(1)}, u32[]{:S(2)}, u32[]{:S(2)}) collective-permute-start(bf16[3,384,384]{2,1,0:T(8,128)(2,1)} %bitcast.72), channel_id=1, source_target_pairs={{0,64},{1,65},{2,66},{3,67},{4,68},{5,69},{6,70},{7,71},{8,72},{9,... | collective-permute-start | bytes 2654216 | tf_op jit(solution)/shard_map/ppermute | solution.py:38
  7.3 1.6 collective-permute-start.3
  8.9 3.7 %collective-permute-start.4 = (bf16[384,384]{1,0:T(8,128)(2,1)}, bf16[384,384]{1,0:T(8,128)(2,1)}, u32[]{:S(2)}, u32[]{:S(2)}) collective-permute-start(bf16[384,384]{1,0:T(8,128)(2,1)} %param.17), channel_id=1, source_target_pairs={{0,0},{1,16},{2,32},{3,48},{4,64},{5,80},{6,96},{7,112},{8,8},{9,2... | collective-permute-start | bytes 884744 | tf_op jit(solution)/shard_map/ppermute | solution.py:38
  14.1 8.5 %norm_columns.1.refs_0_.refs_1_.refs_2_.refs_3_.refs_4_.refs_5_ = bf16[16,512,384]{2,1,0:T(8,128)(2,1)S(1)} custom-call(bf16[512,6144]{1,0:T(8,128)(2,1)} %refs_5_.1, f32[1,6144]{1,0:T(1,128)S(1)} %bitcast.55), custom_call_target="tpu_custom_call" | custom-call | flops 1 | bytes 1 | tf_op jit(solution)/shard_map/norm_columns/pallas_call | solution.py:141
  22.7 3.9 %accumulate.4.refs_12_ = f32[3,512,384]{2,1,0:T(8,128)S(1)} custom-call(s32[2]{0:T(128)S(1)} %get-tuple-element.146.index_ref, bf16[16,512,384]{2,1,0:T(8,128)(2,1)S(1)} %norm_columns.1.refs_0_.refs_1_.refs_2_.refs_3_.refs_4_.refs_5_, bf16[16,512,384]{2,1,0:T(8,128)(2,1)S(1)} %norm_columns.1.refs_0_.refs_1_.refs_2_.refs_3_.refs_4_.refs_5_, ...), custom_call_target="tpu_custom_call" | custom-call | flops 1 | bytes 1 | tf_op jit(solution)/shard_map/accumulate/pallas_call | solution.py:229
  26.7 1.3 collective-permute-done.1
  28.0 7.4 %collective-permute-done.3 = bf16[3,384,384]{2,1,0:T(8,128)(2,1)S(1)} collective-permute-done((bf16[3,384,384]{2,1,0:T(8,128)(2,1)S(1)}, bf16[3,384,384]{2,1,0:T(8,128)(2,1)S(1)}, u32[]{:S(2)}, u32[]{:S(2)}) %collective-permute-start.3) | collective-permute-done | bytes 884768 | tf_op jit(solution)/shard_map/ppermute | solution.py:38
  35.9 2.5 %collective-permute-start.5 = (bf16[3,384,384]{2,1,0:T(8,128)(2,1)S(1)}, bf16[3,384,384]{2,1,0:T(8,128)(2,1)S(1)}, u32[]{:S(2)}, u32[]{:S(2)}) collective-permute-start(bf16[3,384,384]{2,1,0:T(8,128)(2,1)S(1)} %collective-permute-done.1), channel_id=1, source_target_pairs={{0,16},{1,17},{2,18},{3,19},{4,20},{5,21},{6,22},{7,23},{8,56},{9,... | collective-permute-start | bytes 2654216 | tf_op jit(solution)/shard_map/ppermute | solution.py:38
  39.0 1.3 collective-permute-done.9
  40.3 2.5 %collective-permute-start.10 = (bf16[3,384,384]{2,1,0:T(8,128)(2,1)S(1)}, bf16[3,384,384]{2,1,0:T(8,128)(2,1)S(1)}, u32[]{:S(2)}, u32[]{:S(2)}) collective-permute-start(bf16[3,384,384]{2,1,0:T(8,128)(2,1)S(1)} %collective-permute-done.7), channel_id=1, source_target_pairs={{0,16},{1,17},{2,18},{3,19},{4,20},{5,21},{6,22},{7,23},{8,56},{9,... | collective-permute-start | bytes 2654216 | tf_op jit(solution)/shard_map/ppermute | solution.py:38
  42.8 3.9 %collective-permute-start.12 = (bf16[384,512]{1,0:T(8,128)(2,1)S(1)}, bf16[384,512]{1,0:T(8,128)(2,1)S(1)}, u32[]{:S(2)}, u32[]{:S(2)}) collective-permute-start(bf16[384,512]{1,0:T(8,128)(2,1)S(1)} %copy-done.35), channel_id=1, source_target_pairs={{0,64},{1,65},{2,66},{3,67},{4,68},{5,69},{6,70},{7,71},{8,72},{9,... | collective-permute-start | bytes 1179656 | tf_op jit(solution)/shard_map/ppermute | solution.py:38
  46.8 6.9 %accumulate.5.refs_12_ = f32[3,512,384]{2,1,0:T(8,128)S(1)} custom-call(s32[6]{0:T(128)S(1)} %get-tuple-element.145.index_ref, bf16[16,512,384]{2,1,0:T(8,128)(2,1)S(1)} %norm_columns.1.refs_0_.refs_1_.refs_2_.refs_3_.refs_4_.refs_5_, ...), custom_call_target="tpu_custom_call", output_to_operand_aliasing={{}: (13, {})} | custom-call | flops 1 | bytes 1 | tf_op jit(solution)/shard_map/accumulate/pallas_call | solution.py:229
  53.8 6.8 %collective-permute-done.11 = bf16[384,384]{1,0:T(8,128)(2,1)S(1)} collective-permute-done((bf16[384,384]{1,0:T(8,128)(2,1)}, bf16[384,384]{1,0:T(8,128)(2,1)S(1)}, u32[]{:S(2)}, u32[]{:S(2)}) %collective-permute-start.11) | collective-permute-done | bytes 294944 | tf_op jit(solution)/shard_map/ppermute | solution.py:38
  61.7 7.4 %collective-permute-done.10 = bf16[3,384,384]{2,1,0:T(8,128)(2,1)S(1)} collective-permute-done((bf16[3,384,384]{2,1,0:T(8,128)(2,1)S(1)}, bf16[3,384,384]{2,1,0:T(8,128)(2,1)S(1)}, u32[]{:S(2)}, u32[]{:S(2)}) %collective-permute-start.10) | collective-permute-done | bytes 884768 | tf_op jit(solution)/shard_map/ppermute | solution.py:38
  69.6 1.3 collective-permute-start.13
  70.9 4.0 %collective-permute-done.17 = bf16[2,384,384]{2,1,0:T(8,128)(2,1)S(1)} collective-permute-done((bf16[2,384,384]{2,1,0:T(8,128)(2,1)S(1)}, bf16[2,384,384]{2,1,0:T(8,128)(2,1)S(1)}, u32[]{:S(2)}, u32[]{:S(2)}) %collective-permute-start.17) | collective-permute-done | bytes 589856 | tf_op jit(solution)/shard_map/ppermute | solution.py:38
  76.4 6.9 %accumulate.6.refs_4_ = f32[3,512,384]{2,1,0:T(8,128)S(1)} custom-call(s32[6]{0:T(128)S(1)} %get-tuple-element.144.index_ref, bf16[16,512,384]{2,1,0:T(8,128)(2,1)S(1)} %norm_columns.1.refs_0_.refs_1_.refs_2_.refs_3_.refs_4_.refs_5_, ...), custom_call_target="tpu_custom_call", output_to_operand_aliasing={{}: (13, {})} | custom-call | flops 1 | bytes 1 | tf_op jit(solution)/shard_map/accumulate/pallas_call | solution.py:229
  86.3 5.0 %accumulate.7 = (bf16[512,384]{1,0:T(8,128)(2,1)S(1)}, bf16[256,384]{1,0:T(8,128)(2,1)S(1)}, bf16[256,384]{1,0:T(8,128)(2,1)S(1)}) custom-call(s32[2]{0:T(128)S(1)} %get-tuple-element.147.index_ref, bf16[16,512,384]{2,1,0:T(8,128)(2,1)S(1)} %norm_columns.1.refs_0_.refs_1_.refs_2_.refs_3_.refs_4_.refs_5_, ...), custom_call_target="tpu_custom_call" | custom-call | flops 1 | bytes 1 | tf_op jit(solution)/shard_map/accumulate/pallas_call | solution.py:229
  91.3 2.0 collective-permute-start.22
  93.3 1.7 collective-permute-start.20
  95.0 1.6 collective-permute-start.21
  96.5 4.6 %collective-permute-done.20.refs_2_ = bf16[256,384]{1,0:T(8,128)(2,1)S(1)} collective-permute-done((bf16[256,384]{1,0:T(8,128)(2,1)S(1)}, bf16[256,384]{1,0:T(8,128)(2,1)S(1)}, u32[]{:S(2)}, u32[]{:S(2)}) %collective-permute-start.20) | collective-permute-done | bytes 196640 | tf_op jit(solution)/shard_map/ppermute | solution.py:38
  104.0 1.5 collective-permute-start.27
  106.4 9.0 %collective-permute-done.27.refs_5_ = bf16[512,384]{1,0:T(8,128)(2,1)S(1)} collective-permute-done((bf16[512,384]{1,0:T(8,128)(2,1)S(1)}, bf16[512,384]{1,0:T(8,128)(2,1)S(1)}, u32[]{:S(2)}, u32[]{:S(2)}) %collective-permute-start.27) | collective-permute-done | bytes 393248 | tf_op jit(solution)/shard_map/ppermute | solution.py:38
  115.3 3.4 %collective-permute-done.26.refs_4_ = bf16[512,384]{1,0:T(8,128)(2,1)S(1)} collective-permute-done((bf16[512,384]{1,0:T(8,128)(2,1)S(1)}, bf16[512,384]{1,0:T(8,128)(2,1)S(1)}, u32[]{:S(2)}, u32[]{:S(2)}) %collective-permute-start.26) | collective-permute-done | bytes 393248 | tf_op jit(solution)/shard_map/ppermute | solution.py:38
  119.9 1.2 collective-permute-start.31
  121.5 1.6 collective-permute-start.25
  124.0 1.9 collective-permute-start.30
  126.6 7.0 %out_project.2 = (f32[2,512,384]{2,1,0:T(8,128)S(1)}, bf16[6,384,384]{2,1,0:T(8,128)(2,1)S(1)}) custom-call(s32[16]{0:T(128)S(1)} %fusion.index_ref, bf16[512,384]{1,0:T(8,128)(2,1)} %copy-done.2, bf16[512,384]{1,0:T(8,128)(2,1)} %collective-permute-done.22.refs_1_, bf16[256,384]{1,0:T(8,128)(2,1)} %copy-done.33, bf16[256,384]{1,0:T(8,128)(2,1)} %copy-done.34, ...), custom_call_target="tpu_custom_call" | custom-call | flops 1 | bytes 1 | tf_op jit(solution)/shard_map/out_project/pallas_call | solution.py:375
  134.9 5.5 %out_project.3 = (bf16[512,768]{1,0:T(8,128)(2,1)}, bf16[272,768]{1,0:T(8,128)(2,1)S(1)}, bf16[272,768]{1,0:T(8,128)(2,1)S(1)}, f32[8,512]{1,0:T(8,128)S(1)}) custom-call(s32[1]{0:T(128)} %bitcast.index_ref, bf16[512,384]{1,0:T(8,128)(2,1)} %collective-permute-done.24.refs_0_, bf16[512,384]{1,0:T(8,128)(2,1)} %collective-permute-done.25.refs_1_, ...), custom_call_target="tpu_custom_call" | custom-call | flops 1 | bytes 1 | tf_op jit(solution)/shard_map/out_project/pallas_call | solution.py:375
  141.9 3.2 %collective-permute-start.34 = (bf16[272,768]{1,0:T(8,128)(2,1)S(1)}, bf16[272,768]{1,0:T(8,128)(2,1)S(1)}, u32[]{:S(2)}, u32[]{:S(2)}) collective-permute-start(bf16[272,768]{1,0:T(8,128)(2,1)S(1)} %get-tuple-element.129), channel_id=1, source_target_pairs={{0,3},{1,0},{2,1},{3,2},{4,7},{5,4},{6,5},{7,6},{8,11},{9,8},{10,9... | collective-permute-start | bytes 1253384 | tf_op jit(solution)/shard_map/ppermute | solution.py:38
  145.1 10.0 %collective-permute-done.33.refs_0_.refs_2_ = bf16[272,768]{1,0:T(8,128)(2,1)S(1)} collective-permute-done((bf16[272,768]{1,0:T(8,128)(2,1)S(1)}, bf16[272,768]{1,0:T(8,128)(2,1)S(1)}, u32[]{:S(2)}, u32[]{:S(2)}) %collective-permute-start.33) | collective-permute-done | bytes 417824 | tf_op jit(solution)/shard_map/ppermute | solution.py:38
  155.3 3.5 %collective-permute-start.38 = (bf16[544,768]{1,0:T(8,128)(2,1)S(1)}, bf16[544,768]{1,0:T(8,128)(2,1)S(1)}, u32[]{:S(2)}, u32[]{:S(2)}) collective-permute-start(bf16[544,768]{1,0:T(8,128)(2,1)S(1)} %pad_maximum_fusion.3), channel_id=1, source_target_pairs={{0,3},{1,0},{2,1},{3,2},{4,7},{5,4},{6,5},{7,6},{8,11},{9,8},{10,9... | collective-permute-start | bytes 2506760 | tf_op jit(solution)/shard_map/ppermute | solution.py:38
  158.9 1.5 collective-permute-start.39
  161.1 17.2 %collective-permute-done.39.refs_1_ = bf16[512,768]{1,0:T(8,128)(2,1)S(1)} collective-permute-done((bf16[512,768]{1,0:T(8,128)(2,1)S(1)}, bf16[512,768]{1,0:T(8,128)(2,1)S(1)}, u32[]{:S(2)}, u32[]{:S(2)}) %collective-permute-start.39) | collective-permute-done | bytes 786464 | tf_op jit(solution)/shard_map/ppermute | solution.py:38
  178.3 2.2 collective-permute-done.37.refs_2_.refs_4_
  181.2 1.2 collective-permute-start.41
  183.3 1.5 collective-permute-start.42
  184.9 2.2 collective-permute-done.42
  187.1 1.4 collective-permute-start.43
  190.7 1.3 and_select_fusion.1
  193.1 7.9 %project.2 = (f32[512,512]{1,0:T(8,128)S(1)}, bf16[6,384,512]{2,1,0:T(8,128)(2,1)S(1)}) custom-call(s32[21]{0:T(128)S(1)} %pad_add_fusion.2.index_ref, bf16[512,768]{1,0:T(8,128)(2,1)} %get-tuple-element.132.refs_0_, bf16[512,768]{1,0:T(8,128)(2,1)} %copy-done.30, bf16[272,768]{1,0:T(8,128)(2,1)} %copy-done.8, bf16[272,768]{1,0:T(8,128)(2,1)} %copy-done.9, ...), custom_call_target="tpu_custom_call" | custom-call | flops 1 | bytes 1 | tf_op jit(solution)/shard_map/project/pallas_call | solution.py:494
  201.0 3.2 %collective-permute-done.43.refs_2_ = bf16[512,768]{1,0:T(8,128)(2,1)} collective-permute-done((bf16[512,768]{1,0:T(8,128)(2,1)S(1)}, bf16[512,768]{1,0:T(8,128)(2,1)}, u32[]{:S(2)}, u32[]{:S(2)}) %collective-permute-start.43) | collective-permute-done | bytes 786464 | tf_op jit(solution)/shard_map/ppermute | solution.py:38
  204.2 5.0 %project.3 = bf16[8,128,512]{2,1,0:T(8,128)(2,1)} custom-call(s32[11]{0:T(128)S(1)} %pad_add_fusion.1.index_ref, bf16[512,768]{1,0:T(8,128)(2,1)} %copy-done.32, bf16[512,768]{1,0:T(8,128)(2,1)} %collective-permute-done.41.refs_1_, bf16[512,768]{1,0:T(8,128)(2,1)} %collective-permute-done.43.refs_2_, f32[8,512]{1,0:T(8,128)S(1)} %add.26.refs_6_.refs_3_, ...), custom_call_target="tpu_custom_call" | custom-call | flops 1 | bytes 1 | tf_op jit(solution)/shard_map/project/pallas_call | solution.py:494
  209.3 4.1 %all-to-all-start = ((bf16[8,128,512]{2,1,0:T(8,128)(2,1)}), bf16[8,128,512]{2,1,0:T(8,128)(2,1)S(1)}, u32[]{:S(2)}, u32[]{:S(2)}) async-start(bf16[8,128,512]{2,1,0:T(8,128)(2,1)} %project.3), calls=%async_computation | async-start | bytes 2097152 | tf_op jit(solution)/shard_map/all_to_all | solution.py:711
  214.1 11.6 %all-to-all-done.arrived_ref = bf16[8,128,512]{2,1,0:T(8,128)(2,1)S(1)} async-done(((bf16[8,128,512]{2,1,0:T(8,128)(2,1)}), bf16[8,128,512]{2,1,0:T(8,128)(2,1)S(1)}, u32[]{:S(2)}, u32[]{:S(2)}) %all-to-all-start) | async-done | bytes 1048608 | tf_op jit(solution)/shard_map/all_to_all | solution.py:711
  225.7 1.7 pack.1
  (159 shorter events, 23.9 us)
Async XLA Ops:
  0.6 2.7 %collective-permute-start = (bf16[3,384,384]{2,1,0:T(8,128)(2,1)}, bf16[3,384,384]{2,1,0:T(8,128)(2,1)S(1)}, u32[]{:S(2)}, u32[]{:S(2)}) collective-permute-start(bf16[3,384,384]{2,1,0:T(8,128)(2,1)} %bitcast.70), channel_id=1, source_target_pairs={{0,8},{1,9},{2,10},{3,11},{4,12},{5,13},{6,14},{7,15},{8,0},{9,1},... | collective-permute-start | bytes 2654216 | tf_op jit(solution)/shard_map/ppermute | solution.py:38
  0.7 25.9 %collective-permute-start.2 = (bf16[3,384,384]{2,1,0:T(8,128)(2,1)}, bf16[3,384,384]{2,1,0:T(8,128)(2,1)S(1)}, u32[]{:S(2)}, u32[]{:S(2)}) collective-permute-start(bf16[3,384,384]{2,1,0:T(8,128)(2,1)} %bitcast.71), channel_id=1, source_target_pairs={{0,16},{1,17},{2,18},{3,19},{4,20},{5,21},{6,22},{7,23},{8,56},{9,... | collective-permute-start | bytes 2654216 | tf_op jit(solution)/shard_map/ppermute | solution.py:38
  3.3 24.6 %collective-permute-start.1 = (bf16[3,384,384]{2,1,0:T(8,128)(2,1)}, bf16[3,384,384]{2,1,0:T(8,128)(2,1)S(1)}, u32[]{:S(2)}, u32[]{:S(2)}) collective-permute-start(bf16[3,384,384]{2,1,0:T(8,128)(2,1)} %bitcast.72), channel_id=1, source_target_pairs={{0,64},{1,65},{2,66},{3,67},{4,68},{5,69},{6,70},{7,71},{8,72},{9,... | collective-permute-start | bytes 2654216 | tf_op jit(solution)/shard_map/ppermute | solution.py:38
  7.3 28.0 %collective-permute-start.3 = (bf16[3,384,384]{2,1,0:T(8,128)(2,1)S(1)}, bf16[3,384,384]{2,1,0:T(8,128)(2,1)S(1)}, u32[]{:S(2)}, u32[]{:S(2)}) collective-permute-start(bf16[3,384,384]{2,1,0:T(8,128)(2,1)S(1)} %collective-permute-done), channel_id=1, source_target_pairs={{0,16},{1,17},{2,18},{3,19},{4,20},{5,21},{6,22},{7,23},{8,56},{9,... | collective-permute-start | bytes 2654216 | tf_op jit(solution)/shard_map/ppermute | solution.py:38
  8.9 17.8 %collective-permute-start.4 = (bf16[384,384]{1,0:T(8,128)(2,1)}, bf16[384,384]{1,0:T(8,128)(2,1)}, u32[]{:S(2)}, u32[]{:S(2)}) collective-permute-start(bf16[384,384]{1,0:T(8,128)(2,1)} %param.17), channel_id=1, source_target_pairs={{0,0},{1,16},{2,32},{3,48},{4,64},{5,80},{6,96},{7,112},{8,8},{9,2... | collective-permute-start | bytes 884744 | tf_op jit(solution)/shard_map/ppermute | solution.py:38
  22.7 20.1 %copy-start.35 = (bf16[384,512]{1,0:T(8,128)(2,1)S(1)}, bf16[384,512]{1,0:T(8,128)(2,1)}, u32[]{:S(2)}) copy-start(bf16[384,512]{1,0:T(8,128)(2,1)} %param.19) | copy-start | bytes 1179652
  35.3 3.0 %collective-permute-start.7 = (bf16[3,384,384]{2,1,0:T(8,128)(2,1)S(1)}, bf16[3,384,384]{2,1,0:T(8,128)(2,1)S(1)}, u32[]{:S(2)}, u32[]{:S(2)}) collective-permute-start(bf16[3,384,384]{2,1,0:T(8,128)(2,1)S(1)} %collective-permute-done.1), channel_id=1, source_target_pairs={{0,8},{1,9},{2,10},{3,11},{4,12},{5,13},{6,14},{7,15},{8,0},{9,1},... | collective-permute-start | bytes 2654216 | tf_op jit(solution)/shard_map/ppermute | solution.py:38
  35.4 3.7 %collective-permute-start.8 = (bf16[3,384,384]{2,1,0:T(8,128)(2,1)S(1)}, bf16[3,384,384]{2,1,0:T(8,128)(2,1)S(1)}, u32[]{:S(2)}, u32[]{:S(2)}) collective-permute-start(bf16[3,384,384]{2,1,0:T(8,128)(2,1)S(1)} %collective-permute-done.2), channel_id=1, source_target_pairs={{0,8},{1,9},{2,10},{3,11},{4,12},{5,13},{6,14},{7,15},{8,0},{9,1},... | collective-permute-start | bytes 2654216 | tf_op jit(solution)/shard_map/ppermute | solution.py:38
  35.9 4.4 %collective-permute-start.9 = (bf16[3,384,384]{2,1,0:T(8,128)(2,1)S(1)}, bf16[3,384,384]{2,1,0:T(8,128)(2,1)S(1)}, u32[]{:S(2)}, u32[]{:S(2)}) collective-permute-start(bf16[3,384,384]{2,1,0:T(8,128)(2,1)S(1)} %collective-permute-done.3), channel_id=1, source_target_pairs={{0,8},{1,9},{2,10},{3,11},{4,12},{5,13},{6,14},{7,15},{8,0},{9,1},... | collective-permute-start | bytes 2654216 | tf_op jit(solution)/shard_map/ppermute | solution.py:38
  35.9 25.8 %collective-permute-start.5 = (bf16[3,384,384]{2,1,0:T(8,128)(2,1)S(1)}, bf16[3,384,384]{2,1,0:T(8,128)(2,1)S(1)}, u32[]{:S(2)}, u32[]{:S(2)}) collective-permute-start(bf16[3,384,384]{2,1,0:T(8,128)(2,1)S(1)} %collective-permute-done.1), channel_id=1, source_target_pairs={{0,16},{1,17},{2,18},{3,19},{4,20},{5,21},{6,22},{7,23},{8,56},{9,... | collective-permute-start | bytes 2654216 | tf_op jit(solution)/shard_map/ppermute | solution.py:38
  38.3 23.3 %collective-permute-start.6 = (bf16[3,384,384]{2,1,0:T(8,128)(2,1)S(1)}, bf16[3,384,384]{2,1,0:T(8,128)(2,1)S(1)}, u32[]{:S(2)}, u32[]{:S(2)}) collective-permute-start(bf16[3,384,384]{2,1,0:T(8,128)(2,1)S(1)} %collective-permute-done.2), channel_id=1, source_target_pairs={{0,16},{1,17},{2,18},{3,19},{4,20},{5,21},{6,22},{7,23},{8,56},{9,... | collective-permute-start | bytes 2654216 | tf_op jit(solution)/shard_map/ppermute | solution.py:38
  40.3 28.8 %collective-permute-start.10 = (bf16[3,384,384]{2,1,0:T(8,128)(2,1)S(1)}, bf16[3,384,384]{2,1,0:T(8,128)(2,1)S(1)}, u32[]{:S(2)}, u32[]{:S(2)}) collective-permute-start(bf16[3,384,384]{2,1,0:T(8,128)(2,1)S(1)} %collective-permute-done.7), channel_id=1, source_target_pairs={{0,16},{1,17},{2,18},{3,19},{4,20},{5,21},{6,22},{7,23},{8,56},{9,... | collective-permute-start | bytes 2654216 | tf_op jit(solution)/shard_map/ppermute | solution.py:38
  42.8 17.8 %collective-permute-start.12 = (bf16[384,512]{1,0:T(8,128)(2,1)S(1)}, bf16[384,512]{1,0:T(8,128)(2,1)S(1)}, u32[]{:S(2)}, u32[]{:S(2)}) collective-permute-start(bf16[384,512]{1,0:T(8,128)(2,1)S(1)} %copy-done.35), channel_id=1, source_target_pairs={{0,64},{1,65},{2,66},{3,67},{4,68},{5,69},{6,70},{7,71},{8,72},{9,... | collective-permute-start | bytes 1179656 | tf_op jit(solution)/shard_map/ppermute | solution.py:38
  46.7 13.9 %collective-permute-start.11 = (bf16[384,384]{1,0:T(8,128)(2,1)}, bf16[384,384]{1,0:T(8,128)(2,1)S(1)}, u32[]{:S(2)}, u32[]{:S(2)}) collective-permute-start(bf16[384,384]{1,0:T(8,128)(2,1)} %collective-permute-done.4), channel_id=1, source_target_pairs={{0,64},{1,65},{2,66},{3,67},{4,68},{5,69},{6,70},{7,71},{8,72},{9,... | collective-permute-start | bytes 884744 | tf_op jit(solution)/shard_map/ppermute | solution.py:38
  69.1 5.8 %collective-permute-start.14 = (bf16[3,384,384]{2,1,0:T(8,128)(2,1)S(1)}, bf16[3,384,384]{2,1,0:T(8,128)(2,1)S(1)}, u32[]{:S(2)}, u32[]{:S(2)}) collective-permute-start(bf16[3,384,384]{2,1,0:T(8,128)(2,1)S(1)} %collective-permute-done.5), channel_id=1, source_target_pairs={{0,8},{1,9},{2,10},{3,11},{4,12},{5,13},{6,14},{7,15},{8,0},{9,1},... | collective-permute-start | bytes 2654216 | tf_op jit(solution)/shard_map/ppermute | solution.py:38
  69.1 5.8 %collective-permute-start.15 = (bf16[3,384,384]{2,1,0:T(8,128)(2,1)S(1)}, bf16[3,384,384]{2,1,0:T(8,128)(2,1)S(1)}, u32[]{:S(2)}, u32[]{:S(2)}) collective-permute-start(bf16[3,384,384]{2,1,0:T(8,128)(2,1)S(1)} %collective-permute-done.6), channel_id=1, source_target_pairs={{0,8},{1,9},{2,10},{3,11},{4,12},{5,13},{6,14},{7,15},{8,0},{9,1},... | collective-permute-start | bytes 2654216 | tf_op jit(solution)/shard_map/ppermute | solution.py:38
  69.6 5.3 %collective-permute-start.16 = (bf16[3,384,384]{2,1,0:T(8,128)(2,1)S(1)}, bf16[3,384,384]{2,1,0:T(8,128)(2,1)S(1)}, u32[]{:S(2)}, u32[]{:S(2)}) collective-permute-start(bf16[3,384,384]{2,1,0:T(8,128)(2,1)S(1)} %collective-permute-done.10), channel_id=1, source_target_pairs={{0,8},{1,9},{2,10},{3,11},{4,12},{5,13},{6,14},{7,15},{8,0},{9,1},... | collective-permute-start | bytes 2654216 | tf_op jit(solution)/shard_map/ppermute | solution.py:38
  69.6 14.3 %collective-permute-start.13 = (bf16[3,384,384]{2,1,0:T(8,128)(2,1)S(1)}, bf16[3,384,384]{2,1,0:T(8,128)(2,1)S(1)}, u32[]{:S(2)}, u32[]{:S(2)}) collective-permute-start(bf16[3,384,384]{2,1,0:T(8,128)(2,1)S(1)} %collective-permute-done.5), channel_id=1, source_target_pairs={{0,16},{1,17},{2,18},{3,19},{4,20},{5,21},{6,22},{7,23},{8,56},{9,... | collective-permute-start | bytes 2654216 | tf_op jit(solution)/shard_map/ppermute | solution.py:38
  70.9 4.0 %collective-permute-start.17 = (bf16[2,384,384]{2,1,0:T(8,128)(2,1)S(1)}, bf16[2,384,384]{2,1,0:T(8,128)(2,1)S(1)}, u32[]{:S(2)}, u32[]{:S(2)}) collective-permute-start(bf16[2,384,384]{2,1,0:T(8,128)(2,1)S(1)} %pad_maximum_fusion.6), channel_id=1, source_target_pairs={{0,8},{1,9},{2,10},{3,11},{4,12},{5,13},{6,14},{7,15},{8,0},{9,1},... | collective-permute-start | bytes 1769480 | tf_op jit(solution)/shard_map/ppermute | solution.py:38
  83.8 2.4 %collective-permute-start.18 = (bf16[3,384,384]{2,1,0:T(8,128)(2,1)S(1)}, bf16[3,384,384]{2,1,0:T(8,128)(2,1)S(1)}, u32[]{:S(2)}, u32[]{:S(2)}) collective-permute-start(bf16[3,384,384]{2,1,0:T(8,128)(2,1)S(1)} %collective-permute-done.13), channel_id=1, source_target_pairs={{0,8},{1,9},{2,10},{3,11},{4,12},{5,13},{6,14},{7,15},{8,0},{9,1},... | collective-permute-start | bytes 2654216 | tf_op jit(solution)/shard_map/ppermute | solution.py:38
  83.9 7.4 %collective-permute-start.19 = (bf16[2,384,512]{2,1,0:T(8,128)(2,1)S(1)}, bf16[2,384,512]{2,1,0:T(8,128)(2,1)S(1)}, u32[]{:S(2)}, u32[]{:S(2)}) collective-permute-start(bf16[2,384,512]{2,1,0:T(8,128)(2,1)S(1)} %pad_maximum_fusion.4), channel_id=1, source_target_pairs={{0,8},{1,9},{2,10},{3,11},{4,12},{5,13},{6,14},{7,15},{8,0},{9,1},... | collective-permute-start | bytes 2359304 | tf_op jit(solution)/shard_map/ppermute | solution.py:38
  84.4 17.4 %collective-permute-start.23 = (bf16[4,384,384]{2,1,0:T(8,128)(2,1)S(1)}, bf16[4,384,384]{2,1,0:T(8,128)(2,1)S(1)}, u32[]{:S(2)}, u32[]{:S(2)}) collective-permute-start(bf16[4,384,384]{2,1,0:T(8,128)(2,1)S(1)} %pad_maximum_fusion.1.refs_6_), channel_id=1, source_target_pairs={{0,16},{1,17},{2,18},{3,19},{4,20},{5,21},{6,22},{7,23},{8,56},{9,... | collective-permute-start | bytes 3538952 | tf_op jit(solution)/shard_map/ppermute | solution.py:38
  91.3 11.5 %collective-permute-start.22 = (bf16[512,384]{1,0:T(8,128)(2,1)S(1)}, bf16[512,384]{1,0:T(8,128)(2,1)}, u32[]{:S(2)}, u32[]{:S(2)}) collective-permute-start(bf16[512,384]{1,0:T(8,128)(2,1)S(1)} %get-tuple-element.105.refs_0_), channel_id=1, source_target_pairs={{0,4},{1,5},{2,6},{3,7},{4,0},{5,1},{6,2},{7,3},{8,12},{9,13},{10,... | collective-permute-start | bytes 1179656 | tf_op jit(solution)/shard_map/ppermute | solution.py:38
  93.3 7.9 %collective-permute-start.20 = (bf16[256,384]{1,0:T(8,128)(2,1)S(1)}, bf16[256,384]{1,0:T(8,128)(2,1)S(1)}, u32[]{:S(2)}, u32[]{:S(2)}) collective-permute-start(bf16[256,384]{1,0:T(8,128)(2,1)S(1)} %get-tuple-element.111), channel_id=1, source_target_pairs={{0,1},{1,2},{2,3},{3,0},{4,5},{5,6},{6,7},{7,4},{8,9},{9,10},{10,1... | collective-permute-start | bytes 589832 | tf_op jit(solution)/shard_map/ppermute | solution.py:38
  95.0 6.6 %collective-permute-start.21 = (bf16[256,384]{1,0:T(8,128)(2,1)S(1)}, bf16[256,384]{1,0:T(8,128)(2,1)S(1)}, u32[]{:S(2)}, u32[]{:S(2)}) collective-permute-start(bf16[256,384]{1,0:T(8,128)(2,1)S(1)} %get-tuple-element.109), channel_id=1, source_target_pairs={{0,3},{1,0},{2,1},{3,2},{4,7},{5,4},{6,5},{7,6},{8,11},{9,8},{10,9... | collective-permute-start | bytes 589832 | tf_op jit(solution)/shard_map/ppermute | solution.py:38
  102.8 15.9 %collective-permute-start.29 = (bf16[4,384,384]{2,1,0:T(8,128)(2,1)S(1)}, bf16[4,384,384]{2,1,0:T(8,128)(2,1)S(1)}, u32[]{:S(2)}, u32[]{:S(2)}) collective-permute-start(bf16[4,384,384]{2,1,0:T(8,128)(2,1)S(1)} %collective-permute-done.23.refs_7_), channel_id=1, source_target_pairs={{0,8},{1,9},{2,10},{3,11},{4,12},{5,13},{6,14},{7,15},{8,0},{9,1},... | collective-permute-start | bytes 3538952 | tf_op jit(solution)/shard_map/ppermute | solution.py:38
  102.9 15.8 %collective-permute-start.28 = (bf16[2,384,384]{2,1,0:T(8,128)(2,1)S(1)}, bf16[2,384,384]{2,1,0:T(8,128)(2,1)}, u32[]{:S(2)}, u32[]{:S(2)}) collective-permute-start(bf16[2,384,384]{2,1,0:T(8,128)(2,1)S(1)} %slice.72), channel_id=1, source_target_pairs={{0,16},{1,17},{2,18},{3,19},{4,20},{5,21},{6,22},{7,23},{8,56},{9,... | collective-permute-start | bytes 1769480 | tf_op jit(solution)/shard_map/ppermute | solution.py:38
  104.0 11.4 %collective-permute-start.27 = (bf16[512,384]{1,0:T(8,128)(2,1)S(1)}, bf16[512,384]{1,0:T(8,128)(2,1)S(1)}, u32[]{:S(2)}, u32[]{:S(2)}) collective-permute-start(bf16[512,384]{1,0:T(8,128)(2,1)S(1)} %pad_maximum_fusion.8), channel_id=1, source_target_pairs={{0,3},{1,0},{2,1},{3,2},{4,7},{5,4},{6,5},{7,6},{8,11},{9,8},{10,9... | collective-permute-start | bytes 1179656 | tf_op jit(solution)/shard_map/ppermute | solution.py:38
  105.5 13.2 %collective-permute-start.26 = (bf16[512,384]{1,0:T(8,128)(2,1)S(1)}, bf16[512,384]{1,0:T(8,128)(2,1)S(1)}, u32[]{:S(2)}, u32[]{:S(2)}) collective-permute-start(bf16[512,384]{1,0:T(8,128)(2,1)S(1)} %pad_maximum_fusion.7), channel_id=1, source_target_pairs={{0,1},{1,2},{2,3},{3,0},{4,5},{5,6},{6,7},{7,4},{8,9},{9,10},{10,1... | collective-permute-start | bytes 1179656 | tf_op jit(solution)/shard_map/ppermute | solution.py:38
  106.4 27.2 %copy-start.5 = (bf16[4,384,512]{2,1,0:T(8,128)(2,1)}, bf16[4,384,512]{2,1,0:T(8,128)(2,1)S(1)}, u32[]{:S(2)}) copy-start(bf16[4,384,512]{2,1,0:T(8,128)(2,1)S(1)} %pad_maximum_fusion.refs_12_) | copy-start | bytes 4718596
  119.8 21.6 %collective-permute-start.32 = (bf16[4,384,512]{2,1,0:T(8,128)(2,1)S(1)}, bf16[4,384,512]{2,1,0:T(8,128)(2,1)S(1)}, u32[]{:S(2)}, u32[]{:S(2)}) collective-permute-start(bf16[4,384,512]{2,1,0:T(8,128)(2,1)S(1)} %pad_maximum_fusion.refs_12_), channel_id=1, source_target_pairs={{0,16},{1,17},{2,18},{3,19},{4,20},{5,21},{6,22},{7,23},{8,56},{9,... | collective-permute-start | bytes 4718600 | tf_op jit(solution)/shard_map/ppermute | solution.py:38
  119.9 6.7 %collective-permute-start.31 = (bf16[2,384,384]{2,1,0:T(8,128)(2,1)}, bf16[2,384,384]{2,1,0:T(8,128)(2,1)}, u32[]{:S(2)}, u32[]{:S(2)}) collective-permute-start(bf16[2,384,384]{2,1,0:T(8,128)(2,1)} %collective-permute-done.28.refs_9_), channel_id=1, source_target_pairs={{0,8},{1,9},{2,10},{3,11},{4,12},{5,13},{6,14},{7,15},{8,0},{9,1},... | collective-permute-start | bytes 1769480 | tf_op jit(solution)/shard_map/ppermute | solution.py:38
  121.1 12.5 %collective-permute-start.24 = (bf16[512,384]{1,0:T(8,128)(2,1)}, bf16[512,384]{1,0:T(8,128)(2,1)}, u32[]{:S(2)}, u32[]{:S(2)}) collective-permute-start(bf16[512,384]{1,0:T(8,128)(2,1)} %collective-permute-done.22.refs_1_), channel_id=1, source_target_pairs={{0,3},{1,0},{2,1},{3,2},{4,7},{5,4},{6,5},{7,6},{8,11},{9,8},{10,9... | collective-permute-start | bytes 1179656 | tf_op jit(solution)/shard_map/ppermute | solution.py:38
  121.5 12.3 %collective-permute-start.25 = (bf16[512,384]{1,0:T(8,128)(2,1)}, bf16[512,384]{1,0:T(8,128)(2,1)}, u32[]{:S(2)}, u32[]{:S(2)}) collective-permute-start(bf16[512,384]{1,0:T(8,128)(2,1)} %collective-permute-done.22.refs_1_), channel_id=1, source_target_pairs={{0,1},{1,2},{2,3},{3,0},{4,5},{5,6},{6,7},{7,4},{8,9},{9,10},{10,1... | collective-permute-start | bytes 1179656 | tf_op jit(solution)/shard_map/ppermute | solution.py:38
  124.0 10.9 %collective-permute-start.30 = (bf16[512,384]{1,0:T(8,128)(2,1)}, bf16[512,384]{1,0:T(8,128)(2,1)}, u32[]{:S(2)}, u32[]{:S(2)}) collective-permute-start(bf16[512,384]{1,0:T(8,128)(2,1)} %pad_maximum_fusion.9), channel_id=1, source_target_pairs={{0,4},{1,5},{2,6},{3,7},{4,0},{5,1},{6,2},{7,3},{8,12},{9,13},{10,... | collective-permute-start | bytes 1179656 | tf_op jit(solution)/shard_map/ppermute | solution.py:38
  141.4 13.7 %collective-permute-start.35 = (bf16[4,384,512]{2,1,0:T(8,128)(2,1)S(1)}, bf16[4,384,512]{2,1,0:T(8,128)(2,1)}, u32[]{:S(2)}, u32[]{:S(2)}) collective-permute-start(bf16[4,384,512]{2,1,0:T(8,128)(2,1)S(1)} %collective-permute-done.32.refs_13_), channel_id=1, source_target_pairs={{0,8},{1,9},{2,10},{3,11},{4,12},{5,13},{6,14},{7,15},{8,0},{9,1},... | collective-permute-start | bytes 4718600 | tf_op jit(solution)/shard_map/ppermute | solution.py:38
  141.5 13.6 %collective-permute-start.36 = (bf16[2,384,512]{2,1,0:T(8,128)(2,1)S(1)}, bf16[2,384,512]{2,1,0:T(8,128)(2,1)}, u32[]{:S(2)}, u32[]{:S(2)}) collective-permute-start(bf16[2,384,512]{2,1,0:T(8,128)(2,1)S(1)} %slice.79), channel_id=1, source_target_pairs={{0,16},{1,17},{2,18},{3,19},{4,20},{5,21},{6,22},{7,23},{8,56},{9,... | collective-permute-start | bytes 2359304 | tf_op jit(solution)/shard_map/ppermute | solution.py:38
  141.8 13.3 %collective-permute-start.33 = (bf16[272,768]{1,0:T(8,128)(2,1)S(1)}, bf16[272,768]{1,0:T(8,128)(2,1)S(1)}, u32[]{:S(2)}, u32[]{:S(2)}) collective-permute-start(bf16[272,768]{1,0:T(8,128)(2,1)S(1)} %get-tuple-element.131), channel_id=1, source_target_pairs={{0,1},{1,2},{2,3},{3,0},{4,5},{5,6},{6,7},{7,4},{8,9},{9,10},{10,1... | collective-permute-start | bytes 1253384 | tf_op jit(solution)/shard_map/ppermute | solution.py:38
  141.9 13.2 %collective-permute-start.34 = (bf16[272,768]{1,0:T(8,128)(2,1)S(1)}, bf16[272,768]{1,0:T(8,128)(2,1)S(1)}, u32[]{:S(2)}, u32[]{:S(2)}) collective-permute-start(bf16[272,768]{1,0:T(8,128)(2,1)S(1)} %get-tuple-element.129), channel_id=1, source_target_pairs={{0,3},{1,0},{2,1},{3,2},{4,7},{5,4},{6,5},{7,6},{8,11},{9,8},{10,9... | collective-permute-start | bytes 1253384 | tf_op jit(solution)/shard_map/ppermute | solution.py:38
  155.3 23.0 %collective-permute-start.38 = (bf16[544,768]{1,0:T(8,128)(2,1)S(1)}, bf16[544,768]{1,0:T(8,128)(2,1)S(1)}, u32[]{:S(2)}, u32[]{:S(2)}) collective-permute-start(bf16[544,768]{1,0:T(8,128)(2,1)S(1)} %pad_maximum_fusion.3), channel_id=1, source_target_pairs={{0,3},{1,0},{2,1},{3,2},{4,7},{5,4},{6,5},{7,6},{8,11},{9,8},{10,9... | collective-permute-start | bytes 2506760 | tf_op jit(solution)/shard_map/ppermute | solution.py:38
  158.8 21.6 %collective-permute-start.37 = (bf16[544,768]{1,0:T(8,128)(2,1)S(1)}, bf16[544,768]{1,0:T(8,128)(2,1)S(1)}, u32[]{:S(2)}, u32[]{:S(2)}) collective-permute-start(bf16[544,768]{1,0:T(8,128)(2,1)S(1)} %pad_maximum_fusion.2), channel_id=1, source_target_pairs={{0,1},{1,2},{2,3},{3,0},{4,5},{5,6},{6,7},{7,4},{8,9},{9,10},{10,1... | collective-permute-start | bytes 2506760 | tf_op jit(solution)/shard_map/ppermute | solution.py:38
  158.9 19.4 %collective-permute-start.39 = (bf16[512,768]{1,0:T(8,128)(2,1)S(1)}, bf16[512,768]{1,0:T(8,128)(2,1)S(1)}, u32[]{:S(2)}, u32[]{:S(2)}) collective-permute-start(bf16[512,768]{1,0:T(8,128)(2,1)S(1)} %copy-done.29), channel_id=1, source_target_pairs={{0,4},{1,5},{2,6},{3,7},{4,0},{5,1},{6,2},{7,3},{8,12},{9,13},{10,... | collective-permute-start | bytes 2359304 | tf_op jit(solution)/shard_map/ppermute | solution.py:38
  161.1 31.0 %collective-permute-start.44 = (bf16[2,384,512]{2,1,0:T(8,128)(2,1)}, bf16[2,384,512]{2,1,0:T(8,128)(2,1)S(1)}, u32[]{:S(2)}, u32[]{:S(2)}) collective-permute-start(bf16[2,384,512]{2,1,0:T(8,128)(2,1)} %collective-permute-done.36.refs_15_), channel_id=1, source_target_pairs={{0,8},{1,9},{2,10},{3,11},{4,12},{5,13},{6,14},{7,15},{8,0},{9,1},... | collective-permute-start | bytes 2359304 | tf_op jit(solution)/shard_map/ppermute | solution.py:38
  180.5 20.5 %collective-permute-start.40 = (bf16[512,768]{1,0:T(8,128)(2,1)S(1)}, bf16[512,768]{1,0:T(8,128)(2,1)S(1)}, u32[]{:S(2)}, u32[]{:S(2)}) collective-permute-start(bf16[512,768]{1,0:T(8,128)(2,1)S(1)} %collective-permute-done.39.refs_1_), channel_id=1, source_target_pairs={{0,3},{1,0},{2,1},{3,2},{4,7},{5,4},{6,5},{7,6},{8,11},{9,8},{10,9... | collective-permute-start | bytes 2359304 | tf_op jit(solution)/shard_map/ppermute | solution.py:38
  181.2 19.8 %collective-permute-start.41 = (bf16[512,768]{1,0:T(8,128)(2,1)S(1)}, bf16[512,768]{1,0:T(8,128)(2,1)}, u32[]{:S(2)}, u32[]{:S(2)}) collective-permute-start(bf16[512,768]{1,0:T(8,128)(2,1)S(1)} %collective-permute-done.39.refs_1_), channel_id=1, source_target_pairs={{0,1},{1,2},{2,3},{3,0},{4,5},{5,6},{6,7},{7,4},{8,9},{9,10},{10,1... | collective-permute-start | bytes 2359304 | tf_op jit(solution)/shard_map/ppermute | solution.py:38
  183.3 3.8 %collective-permute-start.42 = (f32[8,512]{1,0:T(8,128)S(1)}, f32[8,512]{1,0:T(8,128)S(1)}, u32[]{:S(2)}, u32[]{:S(2)}) collective-permute-start(f32[8,512]{1,0:T(8,128)S(1)} %add_sums.1), channel_id=1, source_target_pairs={{0,4},{1,5},{2,6},{3,7},{4,0},{5,1},{6,2},{7,3},{8,12},{9,13},{10,... | collective-permute-start | bytes 49160 | tf_op jit(solution)/shard_map/ppermute | solution.py:38
  187.1 17.1 %collective-permute-start.43 = (bf16[512,768]{1,0:T(8,128)(2,1)S(1)}, bf16[512,768]{1,0:T(8,128)(2,1)}, u32[]{:S(2)}, u32[]{:S(2)}) collective-permute-start(bf16[512,768]{1,0:T(8,128)(2,1)S(1)} %pad_maximum_fusion.5), channel_id=1, source_target_pairs={{0,4},{1,5},{2,6},{3,7},{4,0},{5,1},{6,2},{7,3},{8,12},{9,13},{10,... | collective-permute-start | bytes 2359304 | tf_op jit(solution)/shard_map/ppermute | solution.py:38
  209.3 16.4 %all-to-all-start = ((bf16[8,128,512]{2,1,0:T(8,128)(2,1)}), bf16[8,128,512]{2,1,0:T(8,128)(2,1)S(1)}, u32[]{:S(2)}, u32[]{:S(2)}) async-start(bf16[8,128,512]{2,1,0:T(8,128)(2,1)} %project.3), calls=%async_computation | async-start | bytes 2097152 | tf_op jit(solution)/shard_map/all_to_all | solution.py:711
  (35 other events, 287.2 us)

commit v4 on v3

--- a/solution.py
+++ b/solution.py
@@ -58,8 +58,12 @@
     return move(values, lambda zh, y, c, zl, x: (zh, y, c, zl, (x + step) % 4))
 
 
-def transpose_mesh(values):
-    return move(values, lambda zh, y, c, zl, x: (zl, x, c, zh, y))
+def turn_first(values):
+    return move(values, lambda zh, y, c, zl, x: (zl, (x + y) % 4, c, zh, x))
+
+
+def turn_second(values):
+    return move(values, lambda zh, y, c, zl, x: (zh, y, c, zl, (y - x) % 4))
 
 
 def per_device(order):
@@ -112,14 +116,16 @@
 def place_tables():
     met = per_device(late_order)
     groups = np.zeros((8, 8), np.int32)
-    shards = np.zeros((16, 8, 16), np.int32)
+    shards = np.zeros((2, 16, 8, 16), np.int32)
     for mp in range(8):
         for r, (dz, dx) in enumerate(NEAR):
             group = (mp // 4 ^ dz) * 4 + (mp + dx) % 4
             groups[mp, r] = group
+            turned = group // 4 * 4 + (group + mp) % 4
             for dp in range(16):
                 for half in range(2):
-                    shards[dp, mp, 2 * r + half] = np.argmax(met[dp] == 2 * group + half)
+                    shards[0, dp, mp, 2 * r + half] = np.argmax(met[dp] == 2 * group + half)
+                    shards[1, dp, mp, 2 * r + half] = np.argmax(met[dp] == 2 * turned + half)
     return groups, shards
 
 
@@ -167,12 +173,13 @@
     total = None
     if has_total:
         total, refs = refs[0][0], refs[1:]
-    at = 0
-    for held, number in zip(shards, shard_counts):
-        for k in range(number):
-            term = jnp.dot(columns[at][0], held[k, 0], preferred_element_type=jnp.float32)
-            total = term if total is None else total + term
-            at += 1
+    held = [ref[k, 0] for ref, number in zip(shards, shard_counts) for k in range(number)]
+    term = jnp.dot(
+        jnp.concatenate([ref[0] for ref in columns], 1),
+        jnp.concatenate(held, 0),
+        preferred_element_type=jnp.float32,
+    )
+    total = term if total is None else total + term
     if not attend:
         refs[0][0] = total
         return
@@ -352,9 +359,9 @@
 def out_project(near, pieces, parts, index, kept=0, total=None, patches=None):
     depth = parts[0].shape[1]
     finish = total is not None
-    in_specs = [pl.BlockSpec(memory_space=pltpu.HBM) for _ in near]
-    in_specs += [pl.BlockSpec(memory_space=pl.ANY if finish else pltpu.HBM) for _ in parts]
-    operands = in_hbm(near) + (parts if finish else in_hbm(parts))
+    place = pl.ANY if finish else pltpu.HBM
+    in_specs = [pl.BlockSpec(memory_space=place) for _ in (*near, *parts)]
+    operands = [*near, *parts] if finish else in_hbm((*near, *parts))
     rows = near[0].shape[0]
     if finish:
         rows = patches.shape[0]
@@ -431,7 +438,6 @@
     else:
         total, (out_ref, kept_ref, *refs) = None, refs
     near_ref, held_ref, near_sems, sems = refs
-    depth = held_ref.shape[1]
     shard_copies = start_shards(parts, held_ref, sems)
     piece_copies = start_pieces(pieces, near, near_ref, near_sems)
     rows = stats_ref.shape[1]
@@ -444,14 +450,11 @@
         wait_all(piece_copies[k])
         values = near_ref[k].astype(jnp.float32)
         normed = ((values - row_mean) * scale * gains[k][...]).astype(jnp.bfloat16)
-        for half in range(2):
-            at = 2 * k + half if finish else index_ref[2 * k + half]
-            term = jnp.dot(
-                normed[:, half * depth : (half + 1) * depth],
-                held_ref[at],
-                preferred_element_type=jnp.float32,
-            )
-            total = term if total is None else total + term
+        held = [
+            held_ref[2 * k + half if finish else index_ref[2 * k + half]] for half in range(2)
+        ]
+        term = jnp.dot(normed, jnp.concatenate(held, 0), preferred_element_type=jnp.float32)
+        total = term if total is None else total + term
     if not finish:
         out_ref[...] = total
         for k in range(kept):
@@ -471,14 +474,16 @@
     count = len(pieces)
     finish = total is not None
     at = 0 if finish else 2 * count + kept
-    in_specs = [pl.BlockSpec(memory_space=pltpu.HBM) for _ in near]
+    place = pl.ANY if finish else pltpu.HBM
+    in_specs = [pl.BlockSpec(memory_space=place) for _ in near]
     in_specs.append(whole(stats.shape))
     in_specs += [
         pl.BlockSpec((1, 2 * depth), functools.partial(lambda k, i, index: (0, index[k]), k))
         for k in range(at, at + count)
     ]
-    in_specs += [pl.BlockSpec(memory_space=pl.ANY if finish else pltpu.HBM) for _ in parts]
-    operands = in_hbm(near) + [stats] + [gain.reshape(1, width)] * count
+    in_specs += [pl.BlockSpec(memory_space=place) for _ in parts]
+    operands = (list(near) if finish else in_hbm(near)) + [stats]
+    operands += [gain.reshape(1, width)] * count
     operands += parts if finish else in_hbm(parts)
     scratch = held_scratch(pieces, near, parts, wide)
     if finish:
@@ -576,50 +581,57 @@
     slot_offset,
     text_len,
 ):
+    own = qkv_weight.transpose(1, 0, 2)
+    first = spread_y(own)
+    other = swap_core(own)
+    far = swap_zh(own)
+    half_turned = turn_first(out_weight)
+    (other,) = join(other)
+    beside = spread_y(other)
+    columns = norm_columns(join(patches, other)[0], norm_gain, 16)
     dp = lax.axis_index("dp")
     mp = lax.axis_index("mp")
     met = jnp.asarray(per_device(early_order))[dp]
-    groups, shards = place_tables()
-    groups, shards = jnp.asarray(groups)[mp], jnp.asarray(shards)[dp, mp]
-    mp_slot = mp[None].astype(jnp.int32)
-
-    own = qkv_weight.transpose(1, 0, 2)
-    first = spread_y(own)
-    other = swap_core(own)
-    turned = transpose_mesh(out_weight)
-    (other,) = join(other)
-    far = swap_zh(join(own, other)[0])
-    beside = spread_y(other)
-    columns = norm_columns(join(patches, other)[0], norm_gain, 16)
     total = accumulate(columns, [own, other], met[0:2])
 
-    far, first, beside, turned, total = join(far, first, beside, turned, total)
+    far, first, beside, half_turned, total = join(far, first, beside, half_turned, total)
     far_first = spread_y(far)
     second = spread_y(first)
+    far_beside = swap_zh(beside)
+    turned = turn_second(half_turned)
     far_other, first_other, beside_other = join(
         swap_core(far), swap_core(first), swap_core(beside)
     )
-    far_beside = spread_y(far_other)
-    turned_far = swap_zh(join(turned, far_other)[0])
-    proj_far = swap_zh(join(proj_weight, far_other)[0])
     total = accumulate(
         columns,
         [far, far_other, first, first_other, beside, beside_other],
         met[2:8],
         total,
     )
-    turned_far, proj_far, total = join(turned_far, proj_far, total)
-    out_mine = jnp.stack([turned, turned_far])
-    proj_mine = jnp.stack([proj_weight, proj_far])
-
-    far_first, second, far_beside, out_mine, proj_mine, total = join(
-        far_first, second, far_beside, out_mine, proj_mine, total
+    total, slot_offset, text_len, dp, mp = join(total, slot_offset, text_len, dp, mp)
+    groups, shards = place_tables()
+    groups, shards = jnp.asarray(groups)[mp], jnp.asarray(shards)[:, dp, mp]
+    shards, out_shards = shards[0], shards[1]
+    mp_slot = mp[None].astype(jnp.int32)
+    slot = slot_offset // HALF
+    block = jnp.arange(8, dtype=jnp.int32)
+    in_first = (block >= slot[0]) & (block < slot[0] + 2)
+    in_second = (block >= slot[1]) & (block < slot[1] + 2)
+    source = jnp.where(in_first, block - slot[0], jnp.where(in_second, block - slot[1] + 2, -1))
+
+    first_index = jnp.concatenate([shards, groups[:5]])
+    last_index = jnp.concatenate([groups[5:], source])
+    pack_index = jnp.concatenate([mp_slot * HALF, slot_offset, text_len])
+
+    far_first, second, far_beside, turned, total, first_index, last_index, pack_index = join(
+        far_first, second, far_beside, turned, total, first_index, last_index, pack_index
     )
     far_second = spread_y(far_first)
-    far_first_other, second_other, far_beside_other, out_other = join(
-        swap_core(far_first), swap_core(second), swap_core(far_beside), swap_core(out_mine)
-    )
-    out_quad = jnp.concatenate([out_mine, out_other])
+    turned_far = swap_zh(turned)
+    proj_far = swap_zh(join(proj_weight, turned)[0])
+    far_first_other, second_other, far_beside_other = join(
+        swap_core(far_first), swap_core(second), swap_core(far_beside)
+    )
     total = accumulate(
         columns,
         [far_first, far_first_other, second, second_other, far_beside, far_beside_other],
@@ -627,29 +639,33 @@
         total,
     )
 
-    far_second, out_quad, proj_mine, total = join(far_second, out_quad, proj_mine, total)
+    far_second, turned_far, proj_far, total = join(far_second, turned_far, proj_far, total)
     far_second_other = swap_core(far_second)
+    out_mine = jnp.stack([turned, turned_far])
+    out_other = swap_core(out_mine)
+    out_quad = jnp.concatenate([out_mine, out_other])
     out_first = spread_y(out_quad)
-    proj_other = swap_core(proj_mine)
     attended = accumulate(
         columns, [far_second, far_second_other], met[14:16], total, qk_gain.transpose(1, 0, 2)
     )
 
-    whole_att, low, high, proj_other = join(*attended, proj_other)
-    proj_quad = jnp.concatenate([proj_mine, proj_other])
+    whole_att, low, high = join(*attended)
     far = swap_zl(whole_att)
-    left_low, right_high, far, out_first, low, high = join(
-        shift_x(low, 1), shift_x(high, -1), far, out_first, low, high
-    )
+    left_low, right_high, far, out_first, low, high, proj_far = join(
+        shift_x(low, 1), shift_x(high, -1), far, out_first, low, high, proj_far
+    )
+    proj_mine = jnp.stack([proj_weight, proj_far])
+    proj_other = swap_core(proj_mine)
     out_second = spread_y(out_first[:2])
     out_first_other = swap_core(out_first)
-    from_left, from_right, out_second, out_first_other, proj_quad = join(
+    from_left, from_right, out_second, out_first_other, proj_other = join(
         shift_x(jnp.concatenate([left_low, high]), 1),
         shift_x(jnp.concatenate([right_high, low]), -1),
         out_second,
         out_first_other,
-        proj_quad,
-    )
+        proj_other,
+    )
+    proj_quad = jnp.concatenate([proj_mine, proj_other])
     near = [whole_att, far, left_low, right_high, from_left, from_right]
     pieces, last_pieces = piece_places(PATCHES)
     out_second_other = swap_core(out_second)
@@ -657,7 +673,7 @@
     beyond = jnp.concatenate([from_left[:PATCHES], from_right[:PATCHES]])
     last = [shift_x(far, -1), shift_x(far, 1), swap_zl(beyond)]
     parts = [out_quad, out_first, out_first_other, out_second, out_second_other]
-    total, left = out_project(near, pieces, parts, shards, kept=6)
+    total, left = out_project(near, pieces, parts, out_shards, kept=6)
     block_out, low, high, stats = out_project(
         last, last_pieces, [left], mp_slot, total=total, patches=patches
     )
@@ -684,19 +700,13 @@
     last = [shift_x(far, -1), shift_x(far, 1), swap_zl(beyond)]
     parts = [proj_quad, proj_first, proj_first_other, proj_second, swap_core(proj_second)]
 
-    slot = slot_offset // HALF
-    block = jnp.arange(8, dtype=jnp.int32)
-    in_first = (block >= slot[0]) & (block < slot[0] + 2)
-    in_second = (block >= slot[1]) & (block < slot[1] + 2)
-    source = jnp.where(in_first, block - slot[0], jnp.where(in_second, block - slot[1] + 2, -1))
-
     total, left = project(
         near,
         pieces,
         stats,
         final_gain,
         parts,
-        jnp.concatenate([shards, groups[:5]]),
+        first_index,
         kept=6,
     )
     (outgoing,) = project(
@@ -705,12 +715,11 @@
         stats,
         final_gain,
         [left],
-        jnp.concatenate([groups[5:], source]),
+        last_index,
         total=total,
     )
     arrived = lax.all_to_all(outgoing, "mp", split_axis=0, concat_axis=0, tiled=True)
-    place = jnp.concatenate([mp_slot * HALF, slot_offset, text_len])
-    sequence = pack(arrived, text_embed[0], place)
+    sequence = pack(arrived, text_embed[0], pack_index)
     return (block_out, sequence[None])
 
 

time: 228 us -> 225 us (0.987)
  blocking collectives: 0 us -> 14.9 us
  waiting for transfers between devices: 98.4 us -> 87.3 us
  starting transfers between devices: 55.2 us -> 46.6 us
  local copies, waits for them, and re-layouts: 7.47 us -> 13.3 us
  Pallas kernels: 59.2 us -> 55.3 us
    all_to_all x0 -> x1, blocking collectives: none -> 14.9 us  [local(): lax.all_to_all(outgoing, 'mp', split_axis=0, concat_axis=0, tiled=True)]
    all_to_all x1 -> x0, waiting for transfers between devices: 11.6 us -> none  [local(): lax.all_to_all(outgoing, 'mp', split_axis=0, concat_axis=0, tiled=True)]
    unnamed x74 -> x72, local copies, waits for them, and re-layouts: 4.31 us -> 10.2 us
    ppermute x45 -> x46, starting transfers between devices: 51 us -> 46.6 us  [move(): return lax.ppermute(values, AXES, pairs)]
    all_to_all x1 -> x0, starting transfers between devices: 4.13 us -> none  [local(): lax.all_to_all(outgoing, 'mp', split_axis=0, concat_axis=0, tiled=True)]
    ppermute x45 -> x46, waiting for transfers between devices: 86.8 us -> 87.3 us  [move(): return lax.ppermute(values, AXES, pairs)]
  transfers between devices with their start and end apart: 46 -> 46, of which waited for: 25 -> 22; matrix products, arithmetic and copies ran while one was open for 3% -> 2% of each run, Pallas kernels for 23% -> 23%
where the time goes in v4:
time: 225 us; the launch traced here: 223 us
  waiting for transfers between devices  87.3 us (39%)
  Pallas kernels  55.3 us (25%)
  starting transfers between devices  46.6 us (21%)
  blocking collectives  14.9 us (7%)
  local copies, waits for them, and re-layouts  13.3 us (6%)
  between operations  3.2 us (1%)
  other arithmetic  2.28 us (1%)
    ppermute x46, waiting for transfers between devices, move(): return lax.ppermute(values, AXES, pairs)  87.3 us
    ppermute x46, starting transfers between devices, move(): return lax.ppermute(values, AXES, pairs)  46.6 us
    pallas_call x4, Pallas kernels, accumulate(): pl.pallas_call(functools.partial(accumulate_kernel, counts, total is not...  21.2 us
    all_to_all x1, blocking collectives, local(): lax.all_to_all(outgoing, 'mp', split_axis=0, concat_axis=0, tiled=True)  14.9 us
    pallas_call x2, Pallas kernels, out_project(): pl.pallas_call(functools.partial(out_kernel, pieces, len(near), len(parts...  12.5 us
    pallas_call x2, Pallas kernels, project(): pl.pallas_call(functools.partial(project_kernel, pieces, len(near), len(p...  10.7 us
    unnamed x72, local copies, waits for them, and re-layouts  10.2 us
    pallas_call x1, Pallas kernels, norm_columns(): pl.pallas_call(norm_kernel, grid=(rows // block,), in_specs=[pl.BlockSpec...  8.52 us
  transfers between devices with their start and end apart: 46, of which 22 were waited for; matrix products, arithmetic and copies ran while one was open for 2% of the time, Pallas kernels for 23%

profile of v4, /device:TPU:0, one launch (start us, length us, event | category | flops | bytes accessed | tf_op | source)
XLA Modules:
  0.0 222.9 jit_solution(1658073638298756961)
XLA Ops:
  0.7 4.0 %collective-permute-start.1 = (bf16[3,384,384]{2,1,0:T(8,128)(2,1)}, bf16[3,384,384]{2,1,0:T(8,128)(2,1)}, u32[]{:S(2)}, u32[]{:S(2)}) collective-permute-start(bf16[3,384,384]{2,1,0:T(8,128)(2,1)} %bitcast.73), channel_id=1, source_target_pairs={{0,64},{1,65},{2,66},{3,67},{4,68},{5,69},{6,70},{7,71},{8,72},{9,... | collective-permute-start | bytes 2654216 | tf_op jit(solution)/shard_map/ppermute | solution.py:38
  4.8 1.6 collective-permute-start.2
  6.3 1.6 collective-permute-start.3
  7.9 1.6 collective-permute-start.4
  11.0 8.5 %norm_columns.1.refs_0_.refs_1_.refs_2_.refs_3_.refs_4_.refs_5_ = bf16[16,512,384]{2,1,0:T(8,128)(2,1)S(1)} custom-call(bf16[512,6144]{1,0:T(8,128)(2,1)} %refs_5_.1, f32[1,6144]{1,0:T(1,128)S(1)} %bitcast.57), custom_call_target="tpu_custom_call" | custom-call | flops 1 | bytes 1 | tf_op jit(solution)/shard_map/norm_columns/pallas_call | solution.py:147
  19.6 4.2 %accumulate.4.refs_12_ = f32[3,512,384]{2,1,0:T(8,128)S(1)} custom-call(s32[2]{0:T(128)S(1)} %get-tuple-element.145.index_ref, bf16[16,512,384]{2,1,0:T(8,128)(2,1)S(1)} %norm_columns.1.refs_0_.refs_1_.refs_2_.refs_3_.refs_4_.refs_5_, bf16[16,512,384]{2,1,0:T(8,128)(2,1)S(1)} %norm_columns.1.refs_0_.refs_1_.refs_2_.refs_3_.refs_4_.refs_5_, ...), custom_call_target="tpu_custom_call" | custom-call | flops 1 | bytes 1 | tf_op jit(solution)/shard_map/accumulate/pallas_call | solution.py:236
  23.9 1.4 collective-permute-done.1
  25.3 3.5 %collective-permute-done.3 = bf16[3,384,384]{2,1,0:T(8,128)(2,1)} collective-permute-done((bf16[3,384,384]{2,1,0:T(8,128)(2,1)S(1)}, bf16[3,384,384]{2,1,0:T(8,128)(2,1)}, u32[]{:S(2)}, u32[]{:S(2)}) %collective-permute-start.3) | collective-permute-done | bytes 884768 | tf_op jit(solution)/shard_map/ppermute | solution.py:38
  30.1 6.2 %collective-permute-start.10 = (bf16[3,384,384]{2,1,0:T(8,128)(2,1)}, bf16[3,384,384]{2,1,0:T(8,128)(2,1)}, u32[]{:S(2)}, u32[]{:S(2)}) collective-permute-start(bf16[3,384,384]{2,1,0:T(8,128)(2,1)} %collective-permute-done.3), channel_id=1, source_target_pairs={{0,64},{1,65},{2,66},{3,67},{4,68},{5,69},{6,70},{7,71},{8,72},{9,... | collective-permute-start | bytes 2654216 | tf_op jit(solution)/shard_map/ppermute | solution.py:38
  36.3 1.5 collective-permute-start.8
  37.8 1.6 collective-permute-start.9
  40.1 2.8 %copy-done.1 = bf16[16,512,384]{2,1,0:T(8,128)(2,1)S(1)} copy-done((bf16[16,512,384]{2,1,0:T(8,128)(2,1)S(1)}, bf16[16,512,384]{2,1,0:T(8,128)(2,1)}, u32[]{:S(2)}) %copy-start.1) | copy-done | bytes 6291480
  42.9 6.2 %accumulate.5.refs_12_ = f32[3,512,384]{2,1,0:T(8,128)S(1)} custom-call(s32[6]{0:T(128)S(1)} %get-tuple-element.141.index_ref, bf16[16,512,384]{2,1,0:T(8,128)(2,1)S(1)} %copy-done.1, bf16[16,512,384]{2,1,0:T(8,128)(2,1)S(1)} %copy-done.1, bf16[16,512,384]{2,1,0:T(8,128)(2,1)S(1)} %copy-done.1, ...), custom_call_target="tpu_custom_call", output_to_operand_aliasing={{}: (13, {})} | custom-call | flops 1 | bytes 1 | tf_op jit(solution)/shard_map/accumulate/pallas_call | solution.py:236
  51.1 1.3 and_select_fusion.1
  54.1 2.7 %collective-permute-done.10 = bf16[3,384,384]{2,1,0:T(8,128)(2,1)} collective-permute-done((bf16[3,384,384]{2,1,0:T(8,128)(2,1)}, bf16[3,384,384]{2,1,0:T(8,128)(2,1)}, u32[]{:S(2)}, u32[]{:S(2)}) %collective-permute-start.10) | collective-permute-done | bytes 884768 | tf_op jit(solution)/shard_map/ppermute | solution.py:38
  56.8 3.6 %collective-permute-done.9 = bf16[3,384,384]{2,1,0:T(8,128)(2,1)} collective-permute-done((bf16[3,384,384]{2,1,0:T(8,128)(2,1)}, bf16[3,384,384]{2,1,0:T(8,128)(2,1)}, u32[]{:S(2)}, u32[]{:S(2)}) %collective-permute-start.9) | collective-permute-done | bytes 884768 | tf_op jit(solution)/shard_map/ppermute | solution.py:38
  63.0 1.7 collective-permute-start.13
  66.4 2.8 %copy-done.2 = bf16[16,512,384]{2,1,0:T(8,128)(2,1)S(1)} copy-done((bf16[16,512,384]{2,1,0:T(8,128)(2,1)S(1)}, bf16[16,512,384]{2,1,0:T(8,128)(2,1)}, u32[]{:S(2)}) %copy-start.2) | copy-done | bytes 6291480
  69.2 6.2 %accumulate.6.refs_4_ = f32[3,512,384]{2,1,0:T(8,128)S(1)} custom-call(s32[6]{0:T(128)S(1)} %get-tuple-element.140.index_ref, bf16[16,512,384]{2,1,0:T(8,128)(2,1)S(1)} %copy-done.2, bf16[16,512,384]{2,1,0:T(8,128)(2,1)S(1)} %copy-done.2, bf16[16,512,384]{2,1,0:T(8,128)(2,1)S(1)} %copy-done.2, ...), custom_call_target="tpu_custom_call", output_to_operand_aliasing={{}: (13, {})} | custom-call | flops 1 | bytes 1 | tf_op jit(solution)/shard_map/accumulate/pallas_call | solution.py:236
  75.4 4.9 %collective-permute-done.13 = bf16[384,384]{1,0:T(8,128)(2,1)S(1)} collective-permute-done((bf16[384,384]{1,0:T(8,128)(2,1)S(1)}, bf16[384,384]{1,0:T(8,128)(2,1)S(1)}, u32[]{:S(2)}, u32[]{:S(2)}) %collective-permute-start.13) | collective-permute-done | bytes 294944 | tf_op jit(solution)/shard_map/ppermute | solution.py:38
  81.1 1.5 collective-permute-done.22
  82.8 1.6 collective-permute-start.23
  84.3 4.5 %accumulate.7 = (bf16[512,384]{1,0:T(8,128)(2,1)S(1)}, bf16[256,384]{1,0:T(8,128)(2,1)S(1)}, bf16[256,384]{1,0:T(8,128)(2,1)S(1)}) custom-call(s32[2]{0:T(128)S(1)} %get-tuple-element.144.index_ref, bf16[16,512,384]{2,1,0:T(8,128)(2,1)S(1)} %copy-done.2, bf16[16,512,384]{2,1,0:T(8,128)(2,1)S(1)} %copy-done.2, bf16[1,3,384,384]{3,2,1,0:T(8,128)(2,1)S(1)} %bitcast.55, ...), custom_call_target="tpu_custom_call" | custom-call | flops 1 | bytes 1 | tf_op jit(solution)/shard_map/accumulate/pallas_call | solution.py:236
  89.0 4.1 %collective-permute-start.19 = (bf16[256,384]{1,0:T(8,128)(2,1)S(1)}, bf16[256,384]{1,0:T(8,128)(2,1)S(1)}, u32[]{:S(2)}, u32[]{:S(2)}) collective-permute-start(bf16[256,384]{1,0:T(8,128)(2,1)S(1)} %get-tuple-element.104), channel_id=1, source_target_pairs={{0,1},{1,2},{2,3},{3,0},{4,5},{5,6},{6,7},{7,4},{8,9},{9,10},{10,1... | collective-permute-start | bytes 589832 | tf_op jit(solution)/shard_map/ppermute | solution.py:38
  93.1 5.2 %collective-permute-done.19.refs_2_ = bf16[256,384]{1,0:T(8,128)(2,1)S(1)} collective-permute-done((bf16[256,384]{1,0:T(8,128)(2,1)S(1)}, bf16[256,384]{1,0:T(8,128)(2,1)S(1)}, u32[]{:S(2)}, u32[]{:S(2)}) %collective-permute-start.19) | collective-permute-done | bytes 196640 | tf_op jit(solution)/shard_map/ppermute | solution.py:38
  98.2 2.2 collective-permute-done.20.refs_3_
  102.1 3.6 %collective-permute-start.27 = (bf16[512,384]{1,0:T(8,128)(2,1)S(1)}, bf16[512,384]{1,0:T(8,128)(2,1)S(1)}, u32[]{:S(2)}, u32[]{:S(2)}) collective-permute-start(bf16[512,384]{1,0:T(8,128)(2,1)S(1)} %pad_maximum_fusion.8), channel_id=1, source_target_pairs={{0,3},{1,0},{2,1},{3,2},{4,7},{5,4},{6,5},{7,6},{8,11},{9,8},{10,9... | collective-permute-start | bytes 1179656 | tf_op jit(solution)/shard_map/ppermute | solution.py:38
  105.9 9.1 %collective-permute-done.27.refs_5_ = bf16[512,384]{1,0:T(8,128)(2,1)S(1)} collective-permute-done((bf16[512,384]{1,0:T(8,128)(2,1)S(1)}, bf16[512,384]{1,0:T(8,128)(2,1)S(1)}, u32[]{:S(2)}, u32[]{:S(2)}) %collective-permute-start.27) | collective-permute-done | bytes 393248 | tf_op jit(solution)/shard_map/ppermute | solution.py:38
  114.9 3.5 %collective-permute-done.26.refs_4_ = bf16[512,384]{1,0:T(8,128)(2,1)S(1)} collective-permute-done((bf16[512,384]{1,0:T(8,128)(2,1)S(1)}, bf16[512,384]{1,0:T(8,128)(2,1)S(1)}, u32[]{:S(2)}, u32[]{:S(2)}) %collective-permute-start.26) | collective-permute-done | bytes 393248 | tf_op jit(solution)/shard_map/ppermute | solution.py:38
  123.8 7.0 %out_project.2 = (f32[2,512,384]{2,1,0:T(8,128)S(1)}, bf16[6,384,384]{2,1,0:T(8,128)(2,1)S(1)}) custom-call(s32[16]{0:T(128)S(1)} %get-tuple-element.138.index_ref, bf16[512,384]{1,0:T(8,128)(2,1)} %copy-done.5, bf16[512,384]{1,0:T(8,128)(2,1)} %copy-done.34, bf16[256,384]{1,0:T(8,128)(2,1)} %copy-done.30, bf16[256,384]{1,0:T(8,128)(2,1)} %copy-done.31, ...), custom_call_target="tpu_custom_call" | custom-call | flops 1 | bytes 1 | tf_op jit(solution)/shard_map/out_project/pallas_call | solution.py:382
  130.8 1.4 collective-permute-done.24.refs_0_
  132.3 1.8 collective-permute-done.25.refs_1_
  134.0 5.5 %out_project.3 = (bf16[512,768]{1,0:T(8,128)(2,1)}, bf16[272,768]{1,0:T(8,128)(2,1)S(1)}, bf16[272,768]{1,0:T(8,128)(2,1)S(1)}, f32[8,512]{1,0:T(8,128)S(1)}) custom-call(s32[1]{0:T(128)} %bitcast.12.index_ref, bf16[512,384]{1,0:T(8,128)(2,1)S(1)} %collective-permute-done.24.refs_0_, bf16[512,384]{1,0:T(8,128)(2,1)S(1)} %collective-permute-done.25.refs_1_, ...), custom_call_target="tpu_custom_call" | custom-call | flops 1 | bytes 1 | tf_op jit(solution)/shard_map/out_project/pallas_call | solution.py:382
  139.5 1.9 collective-permute-done.33.refs_13_
  141.7 3.2 %collective-permute-start.35 = (bf16[272,768]{1,0:T(8,128)(2,1)S(1)}, bf16[272,768]{1,0:T(8,128)(2,1)S(1)}, u32[]{:S(2)}, u32[]{:S(2)}) collective-permute-start(bf16[272,768]{1,0:T(8,128)(2,1)S(1)} %get-tuple-element.124), channel_id=1, source_target_pairs={{0,3},{1,0},{2,1},{3,2},{4,7},{5,4},{6,5},{7,6},{8,11},{9,8},{10,9... | collective-permute-start | bytes 1253384 | tf_op jit(solution)/shard_map/ppermute | solution.py:38
  144.9 10.3 %collective-permute-done.34.refs_0_.refs_2_ = bf16[272,768]{1,0:T(8,128)(2,1)S(1)} collective-permute-done((bf16[272,768]{1,0:T(8,128)(2,1)S(1)}, bf16[272,768]{1,0:T(8,128)(2,1)S(1)}, u32[]{:S(2)}, u32[]{:S(2)}) %collective-permute-start.34) | collective-permute-done | bytes 417824 | tf_op jit(solution)/shard_map/ppermute | solution.py:38
  155.3 3.0 %collective-permute-start.39 = (bf16[544,768]{1,0:T(8,128)(2,1)S(1)}, bf16[544,768]{1,0:T(8,128)(2,1)S(1)}, u32[]{:S(2)}, u32[]{:S(2)}) collective-permute-start(bf16[544,768]{1,0:T(8,128)(2,1)S(1)} %pad_maximum_fusion.3), channel_id=1, source_target_pairs={{0,3},{1,0},{2,1},{3,2},{4,7},{5,4},{6,5},{7,6},{8,11},{9,8},{10,9... | collective-permute-start | bytes 2506760 | tf_op jit(solution)/shard_map/ppermute | solution.py:38
  158.9 18.7 %collective-permute-done.40.refs_1_ = bf16[512,768]{1,0:T(8,128)(2,1)S(1)} collective-permute-done((bf16[512,768]{1,0:T(8,128)(2,1)S(1)}, bf16[512,768]{1,0:T(8,128)(2,1)S(1)}, u32[]{:S(2)}, u32[]{:S(2)}) %collective-permute-start.40) | collective-permute-done | bytes 786464 | tf_op jit(solution)/shard_map/ppermute | solution.py:38
  177.6 2.2 collective-permute-done.38.refs_2_.refs_4_
  180.6 1.2 collective-permute-start.42
  182.8 3.8 %collective-permute-done.43 = f32[8,512]{1,0:T(8,128)S(1)} collective-permute-done((f32[8,512]{1,0:T(8,128)S(1)}, f32[8,512]{1,0:T(8,128)S(1)}, u32[]{:S(2)}, u32[]{:S(2)}) %collective-permute-start.43) | collective-permute-done | bytes 16416 | tf_op jit(solution)/shard_map/ppermute | solution.py:38
  187.6 7.5 %project.2 = (f32[512,512]{1,0:T(8,128)S(1)}, bf16[6,384,512]{2,1,0:T(8,128)(2,1)S(1)}) custom-call(s32[21]{0:T(128)S(1)} %pad_add_fusion.index_ref, bf16[512,768]{1,0:T(8,128)(2,1)} %get-tuple-element.127.refs_0_, bf16[512,768]{1,0:T(8,128)(2,1)} %copy-done.28, bf16[272,768]{1,0:T(8,128)(2,1)} %copy-done.11, bf16[272,768]{1,0:T(8,128)(2,1)} %copy-done.12, ...), custom_call_target="tpu_custom_call" | custom-call | flops 1 | bytes 1 | tf_op jit(solution)/shard_map/project/pallas_call | solution.py:499
  195.1 2.6 %collective-permute-done.41.refs_0_ = bf16[512,768]{1,0:T(8,128)(2,1)S(1)} collective-permute-done((bf16[512,768]{1,0:T(8,128)(2,1)S(1)}, bf16[512,768]{1,0:T(8,128)(2,1)S(1)}, u32[]{:S(2)}, u32[]{:S(2)}) %collective-permute-start.41) | collective-permute-done | bytes 786464 | tf_op jit(solution)/shard_map/ppermute | solution.py:38
  197.7 1.4 collective-permute-done.42.refs_1_
  199.2 4.0 %collective-permute-done.44.refs_2_ = bf16[512,768]{1,0:T(8,128)(2,1)S(1)} collective-permute-done((bf16[512,768]{1,0:T(8,128)(2,1)S(1)}, bf16[512,768]{1,0:T(8,128)(2,1)S(1)}, u32[]{:S(2)}, u32[]{:S(2)}) %collective-permute-start.44) | collective-permute-done | bytes 786464 | tf_op jit(solution)/shard_map/ppermute | solution.py:38
  203.2 3.3 %project.3 = bf16[8,128,512]{2,1,0:T(8,128)(2,1)S(1)} custom-call(s32[11]{0:T(128)S(1)} %pad_add_fusion.1.index_ref, bf16[512,768]{1,0:T(8,128)(2,1)S(1)} %collective-permute-done.41.refs_0_, bf16[512,768]{1,0:T(8,128)(2,1)S(1)} %collective-permute-done.42.refs_1_, bf16[512,768]{1,0:T(8,128)(2,1)S(1)} %collective-permute-done.44.refs_2_, ...), custom_call_target="tpu_custom_call" | custom-call | flops 1 | bytes 1 | tf_op jit(solution)/shard_map/project/pallas_call | solution.py:499
  206.4 14.9 %all_to_all.5.arrived_ref = bf16[8,128,512]{2,1,0:T(8,128)(2,1)S(1)} all-to-all(bf16[8,128,512]{2,1,0:T(8,128)(2,1)S(1)} %project.3), channel_id=1, replica_groups=mesh['dp'=16,'mp'=8] {'mp'}, dimensions={0} | all-to-all | bytes 2097152 | tf_op jit(solution)/shard_map/all_to_all | solution.py:721
  221.3 1.6 pack.1
  (158 shorter events, 21.1 us)
Async XLA Ops:
  0.6 5.7 %collective-permute-start = (bf16[3,384,384]{2,1,0:T(8,128)(2,1)}, bf16[3,384,384]{2,1,0:T(8,128)(2,1)S(1)}, u32[]{:S(2)}, u32[]{:S(2)}) collective-permute-start(bf16[3,384,384]{2,1,0:T(8,128)(2,1)} %bitcast.72), channel_id=1, source_target_pairs={{0,8},{1,9},{2,10},{3,11},{4,12},{5,13},{6,14},{7,15},{8,0},{9,1},... | collective-permute-start | bytes 2654216 | tf_op jit(solution)/shard_map/ppermute | solution.py:38
  0.7 24.6 %collective-permute-start.1 = (bf16[3,384,384]{2,1,0:T(8,128)(2,1)}, bf16[3,384,384]{2,1,0:T(8,128)(2,1)}, u32[]{:S(2)}, u32[]{:S(2)}) collective-permute-start(bf16[3,384,384]{2,1,0:T(8,128)(2,1)} %bitcast.73), channel_id=1, source_target_pairs={{0,64},{1,65},{2,66},{3,67},{4,68},{5,69},{6,70},{7,71},{8,72},{9,... | collective-permute-start | bytes 2654216 | tf_op jit(solution)/shard_map/ppermute | solution.py:38
  4.8 20.5 %collective-permute-start.2 = (bf16[3,384,384]{2,1,0:T(8,128)(2,1)}, bf16[3,384,384]{2,1,0:T(8,128)(2,1)}, u32[]{:S(2)}, u32[]{:S(2)}) collective-permute-start(bf16[3,384,384]{2,1,0:T(8,128)(2,1)} %bitcast.74), channel_id=1, source_target_pairs={{0,16},{1,17},{2,18},{3,19},{4,20},{5,21},{6,22},{7,23},{8,56},{9,... | collective-permute-start | bytes 2654216 | tf_op jit(solution)/shard_map/ppermute | solution.py:38
  6.3 22.5 %collective-permute-start.3 = (bf16[3,384,384]{2,1,0:T(8,128)(2,1)S(1)}, bf16[3,384,384]{2,1,0:T(8,128)(2,1)}, u32[]{:S(2)}, u32[]{:S(2)}) collective-permute-start(bf16[3,384,384]{2,1,0:T(8,128)(2,1)S(1)} %collective-permute-done), channel_id=1, source_target_pairs={{0,16},{1,17},{2,18},{3,19},{4,20},{5,21},{6,22},{7,23},{8,56},{9,... | collective-permute-start | bytes 2654216 | tf_op jit(solution)/shard_map/ppermute | solution.py:38
  7.9 15.9 %collective-permute-start.4 = (bf16[384,384]{1,0:T(8,128)(2,1)}, bf16[384,384]{1,0:T(8,128)(2,1)S(1)}, u32[]{:S(2)}, u32[]{:S(2)}) collective-permute-start(bf16[384,384]{1,0:T(8,128)(2,1)} %param.17), channel_id=1, source_target_pairs={{0,0},{1,17},{2,34},{3,51},{4,64},{5,81},{6,98},{7,115},{8,8},{9,2... | collective-permute-start | bytes 884744 | tf_op jit(solution)/shard_map/ppermute | solution.py:38
  28.8 9.0 %collective-permute-start.5 = (bf16[3,384,384]{2,1,0:T(8,128)(2,1)}, bf16[3,384,384]{2,1,0:T(8,128)(2,1)S(1)}, u32[]{:S(2)}, u32[]{:S(2)}) collective-permute-start(bf16[3,384,384]{2,1,0:T(8,128)(2,1)} %collective-permute-done.1), channel_id=1, source_target_pairs={{0,8},{1,9},{2,10},{3,11},{4,12},{5,13},{6,14},{7,15},{8,0},{9,1},... | collective-permute-start | bytes 2654216 | tf_op jit(solution)/shard_map/ppermute | solution.py:38
  28.8 10.6 %collective-permute-start.6 = (bf16[3,384,384]{2,1,0:T(8,128)(2,1)}, bf16[3,384,384]{2,1,0:T(8,128)(2,1)}, u32[]{:S(2)}, u32[]{:S(2)}) collective-permute-start(bf16[3,384,384]{2,1,0:T(8,128)(2,1)} %collective-permute-done.2), channel_id=1, source_target_pairs={{0,8},{1,9},{2,10},{3,11},{4,12},{5,13},{6,14},{7,15},{8,0},{9,1},... | collective-permute-start | bytes 2654216 | tf_op jit(solution)/shard_map/ppermute | solution.py:38
  29.3 10.7 %collective-permute-start.7 = (bf16[3,384,384]{2,1,0:T(8,128)(2,1)}, bf16[3,384,384]{2,1,0:T(8,128)(2,1)}, u32[]{:S(2)}, u32[]{:S(2)}) collective-permute-start(bf16[3,384,384]{2,1,0:T(8,128)(2,1)} %collective-permute-done.3), channel_id=1, source_target_pairs={{0,8},{1,9},{2,10},{3,11},{4,12},{5,13},{6,14},{7,15},{8,0},{9,1},... | collective-permute-start | bytes 2654216 | tf_op jit(solution)/shard_map/ppermute | solution.py:38
  30.1 26.7 %collective-permute-start.10 = (bf16[3,384,384]{2,1,0:T(8,128)(2,1)}, bf16[3,384,384]{2,1,0:T(8,128)(2,1)}, u32[]{:S(2)}, u32[]{:S(2)}) collective-permute-start(bf16[3,384,384]{2,1,0:T(8,128)(2,1)} %collective-permute-done.3), channel_id=1, source_target_pairs={{0,64},{1,65},{2,66},{3,67},{4,68},{5,69},{6,70},{7,71},{8,72},{9,... | collective-permute-start | bytes 2654216 | tf_op jit(solution)/shard_map/ppermute | solution.py:38
  36.3 20.5 %collective-permute-start.8 = (bf16[3,384,384]{2,1,0:T(8,128)(2,1)}, bf16[3,384,384]{2,1,0:T(8,128)(2,1)}, u32[]{:S(2)}, u32[]{:S(2)}) collective-permute-start(bf16[3,384,384]{2,1,0:T(8,128)(2,1)} %collective-permute-done.1), channel_id=1, source_target_pairs={{0,16},{1,17},{2,18},{3,19},{4,20},{5,21},{6,22},{7,23},{8,56},{9,... | collective-permute-start | bytes 2654216 | tf_op jit(solution)/shard_map/ppermute | solution.py:38
  37.8 22.5 %collective-permute-start.9 = (bf16[3,384,384]{2,1,0:T(8,128)(2,1)}, bf16[3,384,384]{2,1,0:T(8,128)(2,1)}, u32[]{:S(2)}, u32[]{:S(2)}) collective-permute-start(bf16[3,384,384]{2,1,0:T(8,128)(2,1)} %collective-permute-done.2), channel_id=1, source_target_pairs={{0,16},{1,17},{2,18},{3,19},{4,20},{5,21},{6,22},{7,23},{8,56},{9,... | collective-permute-start | bytes 2654216 | tf_op jit(solution)/shard_map/ppermute | solution.py:38
  39.4 14.7 %collective-permute-start.11 = (bf16[384,384]{1,0:T(8,128)(2,1)S(1)}, bf16[384,384]{1,0:T(8,128)(2,1)S(1)}, u32[]{:S(2)}, u32[]{:S(2)}) collective-permute-start(bf16[384,384]{1,0:T(8,128)(2,1)S(1)} %collective-permute-done.4), channel_id=1, source_target_pairs={{0,0},{1,3},{2,2},{3,1},{4,4},{5,7},{6,6},{7,5},{8,8},{9,11},{10,1... | collective-permute-start | bytes 884744 | tf_op jit(solution)/shard_map/ppermute | solution.py:38
  42.9 18.3 %copy-start.17 = (bf16[384,512]{1,0:T(8,128)(2,1)S(1)}, bf16[384,512]{1,0:T(8,128)(2,1)}, u32[]{:S(2)}) copy-start(bf16[384,512]{1,0:T(8,128)(2,1)} %param.19) | copy-start | bytes 1179652
  60.3 2.6 %collective-permute-start.15 = (bf16[3,384,384]{2,1,0:T(8,128)(2,1)}, bf16[3,384,384]{2,1,0:T(8,128)(2,1)S(1)}, u32[]{:S(2)}, u32[]{:S(2)}) collective-permute-start(bf16[3,384,384]{2,1,0:T(8,128)(2,1)} %collective-permute-done.8), channel_id=1, source_target_pairs={{0,8},{1,9},{2,10},{3,11},{4,12},{5,13},{6,14},{7,15},{8,0},{9,1},... | collective-permute-start | bytes 2654216 | tf_op jit(solution)/shard_map/ppermute | solution.py:38
  60.3 4.4 %collective-permute-start.16 = (bf16[3,384,384]{2,1,0:T(8,128)(2,1)}, bf16[3,384,384]{2,1,0:T(8,128)(2,1)S(1)}, u32[]{:S(2)}, u32[]{:S(2)}) collective-permute-start(bf16[3,384,384]{2,1,0:T(8,128)(2,1)} %collective-permute-done.9), channel_id=1, source_target_pairs={{0,8},{1,9},{2,10},{3,11},{4,12},{5,13},{6,14},{7,15},{8,0},{9,1},... | collective-permute-start | bytes 2654216 | tf_op jit(solution)/shard_map/ppermute | solution.py:38
  60.8 4.7 %collective-permute-start.17 = (bf16[3,384,384]{2,1,0:T(8,128)(2,1)}, bf16[3,384,384]{2,1,0:T(8,128)(2,1)S(1)}, u32[]{:S(2)}, u32[]{:S(2)}) collective-permute-start(bf16[3,384,384]{2,1,0:T(8,128)(2,1)} %collective-permute-done.10), channel_id=1, source_target_pairs={{0,8},{1,9},{2,10},{3,11},{4,12},{5,13},{6,14},{7,15},{8,0},{9,1},... | collective-permute-start | bytes 2654216 | tf_op jit(solution)/shard_map/ppermute | solution.py:38
  60.8 19.5 %collective-permute-start.12 = (bf16[3,384,384]{2,1,0:T(8,128)(2,1)}, bf16[3,384,384]{2,1,0:T(8,128)(2,1)S(1)}, u32[]{:S(2)}, u32[]{:S(2)}) collective-permute-start(bf16[3,384,384]{2,1,0:T(8,128)(2,1)} %collective-permute-done.8), channel_id=1, source_target_pairs={{0,16},{1,17},{2,18},{3,19},{4,20},{5,21},{6,22},{7,23},{8,56},{9,... | collective-permute-start | bytes 2654216 | tf_op jit(solution)/shard_map/ppermute | solution.py:38
  61.2 19.2 %collective-permute-start.14 = (bf16[384,512]{1,0:T(8,128)(2,1)S(1)}, bf16[384,512]{1,0:T(8,128)(2,1)S(1)}, u32[]{:S(2)}, u32[]{:S(2)}) collective-permute-start(bf16[384,512]{1,0:T(8,128)(2,1)S(1)} %copy-done.17), channel_id=1, source_target_pairs={{0,64},{1,65},{2,66},{3,67},{4,68},{5,69},{6,70},{7,71},{8,72},{9,... | collective-permute-start | bytes 1179656 | tf_op jit(solution)/shard_map/ppermute | solution.py:38
  63.0 17.4 %collective-permute-start.13 = (bf16[384,384]{1,0:T(8,128)(2,1)S(1)}, bf16[384,384]{1,0:T(8,128)(2,1)S(1)}, u32[]{:S(2)}, u32[]{:S(2)}) collective-permute-start(bf16[384,384]{1,0:T(8,128)(2,1)S(1)} %collective-permute-done.11), channel_id=1, source_target_pairs={{0,64},{1,65},{2,66},{3,67},{4,68},{5,69},{6,70},{7,71},{8,72},{9,... | collective-permute-start | bytes 884744 | tf_op jit(solution)/shard_map/ppermute | solution.py:38
  80.4 2.2 collective-permute-start.22
  81.0 3.4 %collective-permute-start.18 = (bf16[3,384,384]{2,1,0:T(8,128)(2,1)S(1)}, bf16[3,384,384]{2,1,0:T(8,128)(2,1)S(1)}, u32[]{:S(2)}, u32[]{:S(2)}) collective-permute-start(bf16[3,384,384]{2,1,0:T(8,128)(2,1)S(1)} %collective-permute-done.12), channel_id=1, source_target_pairs={{0,8},{1,9},{2,10},{3,11},{4,12},{5,13},{6,14},{7,15},{8,0},{9,1},... | collective-permute-start | bytes 2654216 | tf_op jit(solution)/shard_map/ppermute | solution.py:38
  82.8 17.7 %collective-permute-start.23 = (bf16[4,384,384]{2,1,0:T(8,128)(2,1)S(1)}, bf16[4,384,384]{2,1,0:T(8,128)(2,1)S(1)}, u32[]{:S(2)}, u32[]{:S(2)}) collective-permute-start(bf16[4,384,384]{2,1,0:T(8,128)(2,1)S(1)} %pad_maximum_fusion.1.refs_6_), channel_id=1, source_target_pairs={{0,16},{1,17},{2,18},{3,19},{4,20},{5,21},{6,22},{7,23},{8,56},{9,... | collective-permute-start | bytes 3538952 | tf_op jit(solution)/shard_map/ppermute | solution.py:38
  88.9 11.5 %collective-permute-start.21 = (bf16[512,384]{1,0:T(8,128)(2,1)S(1)}, bf16[512,384]{1,0:T(8,128)(2,1)S(1)}, u32[]{:S(2)}, u32[]{:S(2)}) collective-permute-start(bf16[512,384]{1,0:T(8,128)(2,1)S(1)} %get-tuple-element.97.refs_0_), channel_id=1, source_target_pairs={{0,4},{1,5},{2,6},{3,7},{4,0},{5,1},{6,2},{7,3},{8,12},{9,13},{10,... | collective-permute-start | bytes 1179656 | tf_op jit(solution)/shard_map/ppermute | solution.py:38
  89.0 9.2 %collective-permute-start.19 = (bf16[256,384]{1,0:T(8,128)(2,1)S(1)}, bf16[256,384]{1,0:T(8,128)(2,1)S(1)}, u32[]{:S(2)}, u32[]{:S(2)}) collective-permute-start(bf16[256,384]{1,0:T(8,128)(2,1)S(1)} %get-tuple-element.104), channel_id=1, source_target_pairs={{0,1},{1,2},{2,3},{3,0},{4,5},{5,6},{6,7},{7,4},{8,9},{9,10},{10,1... | collective-permute-start | bytes 589832 | tf_op jit(solution)/shard_map/ppermute | solution.py:38
  93.1 7.4 %collective-permute-start.20 = (bf16[256,384]{1,0:T(8,128)(2,1)S(1)}, bf16[256,384]{1,0:T(8,128)(2,1)S(1)}, u32[]{:S(2)}, u32[]{:S(2)}) collective-permute-start(bf16[256,384]{1,0:T(8,128)(2,1)S(1)} %get-tuple-element.102), channel_id=1, source_target_pairs={{0,3},{1,0},{2,1},{3,2},{4,7},{5,4},{6,5},{7,6},{8,11},{9,8},{10,9... | collective-permute-start | bytes 589832 | tf_op jit(solution)/shard_map/ppermute | solution.py:38
  100.4 21.2 %copy-start.34 = (bf16[512,384]{1,0:T(8,128)(2,1)}, bf16[512,384]{1,0:T(8,128)(2,1)S(1)}, u32[]{:S(2)}) copy-start(bf16[512,384]{1,0:T(8,128)(2,1)S(1)} %collective-permute-done.21.refs_1_) | copy-start | bytes 1179652
  100.4 18.0 %collective-permute-start.29 = (bf16[4,384,384]{2,1,0:T(8,128)(2,1)S(1)}, bf16[4,384,384]{2,1,0:T(8,128)(2,1)S(1)}, u32[]{:S(2)}, u32[]{:S(2)}) collective-permute-start(bf16[4,384,384]{2,1,0:T(8,128)(2,1)S(1)} %collective-permute-done.23.refs_7_), channel_id=1, source_target_pairs={{0,8},{1,9},{2,10},{3,11},{4,12},{5,13},{6,14},{7,15},{8,0},{9,1},... | collective-permute-start | bytes 3538952 | tf_op jit(solution)/shard_map/ppermute | solution.py:38
  100.9 17.5 %collective-permute-start.30 = (bf16[2,384,512]{2,1,0:T(8,128)(2,1)S(1)}, bf16[2,384,512]{2,1,0:T(8,128)(2,1)S(1)}, u32[]{:S(2)}, u32[]{:S(2)}) collective-permute-start(bf16[2,384,512]{2,1,0:T(8,128)(2,1)S(1)} %pad_maximum_fusion.4), channel_id=1, source_target_pairs={{0,8},{1,9},{2,10},{3,11},{4,12},{5,13},{6,14},{7,15},{8,0},{9,1},... | collective-permute-start | bytes 2359304 | tf_op jit(solution)/shard_map/ppermute | solution.py:38
  101.2 17.2 %collective-permute-start.28 = (bf16[2,384,384]{2,1,0:T(8,128)(2,1)S(1)}, bf16[2,384,384]{2,1,0:T(8,128)(2,1)S(1)}, u32[]{:S(2)}, u32[]{:S(2)}) collective-permute-start(bf16[2,384,384]{2,1,0:T(8,128)(2,1)S(1)} %slice.87), channel_id=1, source_target_pairs={{0,16},{1,17},{2,18},{3,19},{4,20},{5,21},{6,22},{7,23},{8,56},{9,... | collective-permute-start | bytes 1769480 | tf_op jit(solution)/shard_map/ppermute | solution.py:38
  102.1 12.8 %collective-permute-start.27 = (bf16[512,384]{1,0:T(8,128)(2,1)S(1)}, bf16[512,384]{1,0:T(8,128)(2,1)S(1)}, u32[]{:S(2)}, u32[]{:S(2)}) collective-permute-start(bf16[512,384]{1,0:T(8,128)(2,1)S(1)} %pad_maximum_fusion.8), channel_id=1, source_target_pairs={{0,3},{1,0},{2,1},{3,2},{4,7},{5,4},{6,5},{7,6},{8,11},{9,8},{10,9... | collective-permute-start | bytes 1179656 | tf_op jit(solution)/shard_map/ppermute | solution.py:38
  105.8 12.7 %collective-permute-start.26 = (bf16[512,384]{1,0:T(8,128)(2,1)S(1)}, bf16[512,384]{1,0:T(8,128)(2,1)S(1)}, u32[]{:S(2)}, u32[]{:S(2)}) collective-permute-start(bf16[512,384]{1,0:T(8,128)(2,1)S(1)} %pad_maximum_fusion.7), channel_id=1, source_target_pairs={{0,1},{1,2},{2,3},{3,0},{4,5},{5,6},{6,7},{7,4},{8,9},{9,10},{10,1... | collective-permute-start | bytes 1179656 | tf_op jit(solution)/shard_map/ppermute | solution.py:38
  119.8 21.6 %collective-permute-start.33 = (bf16[4,384,512]{2,1,0:T(8,128)(2,1)S(1)}, bf16[4,384,512]{2,1,0:T(8,128)(2,1)S(1)}, u32[]{:S(2)}, u32[]{:S(2)}) collective-permute-start(bf16[4,384,512]{2,1,0:T(8,128)(2,1)S(1)} %pad_maximum_fusion.refs_12_), channel_id=1, source_target_pairs={{0,16},{1,17},{2,18},{3,19},{4,20},{5,21},{6,22},{7,23},{8,56},{9,... | collective-permute-start | bytes 4718600 | tf_op jit(solution)/shard_map/ppermute | solution.py:38
  120.7 2.2 %collective-permute-start.32 = (bf16[2,384,384]{2,1,0:T(8,128)(2,1)S(1)}, bf16[2,384,384]{2,1,0:T(8,128)(2,1)S(1)}, u32[]{:S(2)}, u32[]{:S(2)}) collective-permute-start(bf16[2,384,384]{2,1,0:T(8,128)(2,1)S(1)} %collective-permute-done.28.refs_9_), channel_id=1, source_target_pairs={{0,8},{1,9},{2,10},{3,11},{4,12},{5,13},{6,14},{7,15},{8,0},{9,1},... | collective-permute-start | bytes 1769480 | tf_op jit(solution)/shard_map/ppermute | solution.py:38
  120.7 11.5 %collective-permute-start.24 = (bf16[512,384]{1,0:T(8,128)(2,1)S(1)}, bf16[512,384]{1,0:T(8,128)(2,1)S(1)}, u32[]{:S(2)}, u32[]{:S(2)}) collective-permute-start(bf16[512,384]{1,0:T(8,128)(2,1)S(1)} %collective-permute-done.21.refs_1_), channel_id=1, source_target_pairs={{0,3},{1,0},{2,1},{3,2},{4,7},{5,4},{6,5},{7,6},{8,11},{9,8},{10,9... | collective-permute-start | bytes 1179656 | tf_op jit(solution)/shard_map/ppermute | solution.py:38
  121.6 12.5 %collective-permute-start.25 = (bf16[512,384]{1,0:T(8,128)(2,1)S(1)}, bf16[512,384]{1,0:T(8,128)(2,1)S(1)}, u32[]{:S(2)}, u32[]{:S(2)}) collective-permute-start(bf16[512,384]{1,0:T(8,128)(2,1)S(1)} %collective-permute-done.21.refs_1_), channel_id=1, source_target_pairs={{0,1},{1,2},{2,3},{3,0},{4,5},{5,6},{6,7},{7,4},{8,9},{9,10},{10,1... | collective-permute-start | bytes 1179656 | tf_op jit(solution)/shard_map/ppermute | solution.py:38
  122.9 11.1 %collective-permute-start.31 = (bf16[512,384]{1,0:T(8,128)(2,1)S(1)}, bf16[512,384]{1,0:T(8,128)(2,1)S(1)}, u32[]{:S(2)}, u32[]{:S(2)}) collective-permute-start(bf16[512,384]{1,0:T(8,128)(2,1)S(1)} %pad_maximum_fusion.9), channel_id=1, source_target_pairs={{0,4},{1,5},{2,6},{3,7},{4,0},{5,1},{6,2},{7,3},{8,12},{9,13},{10,... | collective-permute-start | bytes 1179656 | tf_op jit(solution)/shard_map/ppermute | solution.py:38
  141.4 13.8 %collective-permute-start.36 = (bf16[4,384,512]{2,1,0:T(8,128)(2,1)S(1)}, bf16[4,384,512]{2,1,0:T(8,128)(2,1)S(1)}, u32[]{:S(2)}, u32[]{:S(2)}) collective-permute-start(bf16[4,384,512]{2,1,0:T(8,128)(2,1)S(1)} %collective-permute-done.33.refs_13_), channel_id=1, source_target_pairs={{0,8},{1,9},{2,10},{3,11},{4,12},{5,13},{6,14},{7,15},{8,0},{9,1},... | collective-permute-start | bytes 4718600 | tf_op jit(solution)/shard_map/ppermute | solution.py:38
  141.5 13.7 %collective-permute-start.37 = (bf16[2,384,512]{2,1,0:T(8,128)(2,1)S(1)}, bf16[2,384,512]{2,1,0:T(8,128)(2,1)S(1)}, u32[]{:S(2)}, u32[]{:S(2)}) collective-permute-start(bf16[2,384,512]{2,1,0:T(8,128)(2,1)S(1)} %slice.91), channel_id=1, source_target_pairs={{0,16},{1,17},{2,18},{3,19},{4,20},{5,21},{6,22},{7,23},{8,56},{9,... | collective-permute-start | bytes 2359304 | tf_op jit(solution)/shard_map/ppermute | solution.py:38
  141.6 13.6 %collective-permute-start.34 = (bf16[272,768]{1,0:T(8,128)(2,1)S(1)}, bf16[272,768]{1,0:T(8,128)(2,1)S(1)}, u32[]{:S(2)}, u32[]{:S(2)}) collective-permute-start(bf16[272,768]{1,0:T(8,128)(2,1)S(1)} %get-tuple-element.126), channel_id=1, source_target_pairs={{0,1},{1,2},{2,3},{3,0},{4,5},{5,6},{6,7},{7,4},{8,9},{9,10},{10,1... | collective-permute-start | bytes 1253384 | tf_op jit(solution)/shard_map/ppermute | solution.py:38
  141.7 13.5 %collective-permute-start.35 = (bf16[272,768]{1,0:T(8,128)(2,1)S(1)}, bf16[272,768]{1,0:T(8,128)(2,1)S(1)}, u32[]{:S(2)}, u32[]{:S(2)}) collective-permute-start(bf16[272,768]{1,0:T(8,128)(2,1)S(1)} %get-tuple-element.124), channel_id=1, source_target_pairs={{0,3},{1,0},{2,1},{3,2},{4,7},{5,4},{6,5},{7,6},{8,11},{9,8},{10,9... | collective-permute-start | bytes 1253384 | tf_op jit(solution)/shard_map/ppermute | solution.py:38
  155.3 22.4 %collective-permute-start.39 = (bf16[544,768]{1,0:T(8,128)(2,1)S(1)}, bf16[544,768]{1,0:T(8,128)(2,1)S(1)}, u32[]{:S(2)}, u32[]{:S(2)}) collective-permute-start(bf16[544,768]{1,0:T(8,128)(2,1)S(1)} %pad_maximum_fusion.3), channel_id=1, source_target_pairs={{0,3},{1,0},{2,1},{3,2},{4,7},{5,4},{6,5},{7,6},{8,11},{9,8},{10,9... | collective-permute-start | bytes 2506760 | tf_op jit(solution)/shard_map/ppermute | solution.py:38
  158.4 21.4 %collective-permute-start.38 = (bf16[544,768]{1,0:T(8,128)(2,1)S(1)}, bf16[544,768]{1,0:T(8,128)(2,1)S(1)}, u32[]{:S(2)}, u32[]{:S(2)}) collective-permute-start(bf16[544,768]{1,0:T(8,128)(2,1)S(1)} %pad_maximum_fusion.2), channel_id=1, source_target_pairs={{0,1},{1,2},{2,3},{3,0},{4,5},{5,6},{6,7},{7,4},{8,9},{9,10},{10,1... | collective-permute-start | bytes 2506760 | tf_op jit(solution)/shard_map/ppermute | solution.py:38
  158.7 18.9 %collective-permute-start.40 = (bf16[512,768]{1,0:T(8,128)(2,1)S(1)}, bf16[512,768]{1,0:T(8,128)(2,1)S(1)}, u32[]{:S(2)}, u32[]{:S(2)}) collective-permute-start(bf16[512,768]{1,0:T(8,128)(2,1)S(1)} %copy-done.26), channel_id=1, source_target_pairs={{0,4},{1,5},{2,6},{3,7},{4,0},{5,1},{6,2},{7,3},{8,12},{9,13},{10,... | collective-permute-start | bytes 2359304 | tf_op jit(solution)/shard_map/ppermute | solution.py:38
  158.8 27.8 %collective-permute-start.45 = (bf16[2,384,512]{2,1,0:T(8,128)(2,1)S(1)}, bf16[2,384,512]{2,1,0:T(8,128)(2,1)S(1)}, u32[]{:S(2)}, u32[]{:S(2)}) collective-permute-start(bf16[2,384,512]{2,1,0:T(8,128)(2,1)S(1)} %collective-permute-done.37.refs_15_), channel_id=1, source_target_pairs={{0,8},{1,9},{2,10},{3,11},{4,12},{5,13},{6,14},{7,15},{8,0},{9,1},... | collective-permute-start | bytes 2359304 | tf_op jit(solution)/shard_map/ppermute | solution.py:38
  179.8 17.9 %collective-permute-start.41 = (bf16[512,768]{1,0:T(8,128)(2,1)S(1)}, bf16[512,768]{1,0:T(8,128)(2,1)S(1)}, u32[]{:S(2)}, u32[]{:S(2)}) collective-permute-start(bf16[512,768]{1,0:T(8,128)(2,1)S(1)} %collective-permute-done.40.refs_1_), channel_id=1, source_target_pairs={{0,3},{1,0},{2,1},{3,2},{4,7},{5,4},{6,5},{7,6},{8,11},{9,8},{10,9... | collective-permute-start | bytes 2359304 | tf_op jit(solution)/shard_map/ppermute | solution.py:38
  180.6 18.6 %collective-permute-start.42 = (bf16[512,768]{1,0:T(8,128)(2,1)S(1)}, bf16[512,768]{1,0:T(8,128)(2,1)S(1)}, u32[]{:S(2)}, u32[]{:S(2)}) collective-permute-start(bf16[512,768]{1,0:T(8,128)(2,1)S(1)} %collective-permute-done.40.refs_1_), channel_id=1, source_target_pairs={{0,1},{1,2},{2,3},{3,0},{4,5},{5,6},{6,7},{7,4},{8,9},{9,10},{10,1... | collective-permute-start | bytes 2359304 | tf_op jit(solution)/shard_map/ppermute | solution.py:38
  182.6 4.0 %collective-permute-start.43 = (f32[8,512]{1,0:T(8,128)S(1)}, f32[8,512]{1,0:T(8,128)S(1)}, u32[]{:S(2)}, u32[]{:S(2)}) collective-permute-start(f32[8,512]{1,0:T(8,128)S(1)} %add_sums.1), channel_id=1, source_target_pairs={{0,4},{1,5},{2,6},{3,7},{4,0},{5,1},{6,2},{7,3},{8,12},{9,13},{10,... | collective-permute-start | bytes 49160 | tf_op jit(solution)/shard_map/ppermute | solution.py:38
  186.6 16.5 %collective-permute-start.44 = (bf16[512,768]{1,0:T(8,128)(2,1)S(1)}, bf16[512,768]{1,0:T(8,128)(2,1)S(1)}, u32[]{:S(2)}, u32[]{:S(2)}) collective-permute-start(bf16[512,768]{1,0:T(8,128)(2,1)S(1)} %pad_maximum_fusion.5), channel_id=1, source_target_pairs={{0,4},{1,5},{2,6},{3,7},{4,0},{5,1},{6,2},{7,3},{8,12},{9,13},{10,... | collective-permute-start | bytes 2359304 | tf_op jit(solution)/shard_map/ppermute | solution.py:38
  (34 other events, 179.3 us)

commit v5 on v4

--- a/solution.py
+++ b/solution.py
@@ -690,14 +690,15 @@
         shift_x(jnp.concatenate([right_high, low]), -1),
         far,
     )
+    near = [whole_block, far, left_low, right_high, from_left, from_right]
+    pieces, last_pieces = piece_places(PATCHES + EXTRA)
+    last = [shift_x(far, -1), shift_x(far, 1), swap_zl(from_left[:PATCHES])]
     stats = add_sums(stats, [(left_low, 0), (right_high, 0), (from_left, 0)])
     stats_z = swap_zl(stats)
+    from_right_held, stats = join(from_right, stats)
+    last.append(swap_zl(from_right_held[:PATCHES]))
+    last_pieces = (*last_pieces[:2], ((2, 0), (3, 0)))
     stats = stats + stats_z
-    near = [whole_block, far, left_low, right_high, from_left, from_right]
-    pieces, last_pieces = piece_places(PATCHES + EXTRA)
-    beyond = jnp.concatenate([from_left[:PATCHES], from_right[:PATCHES]])
-    beyond = join(beyond, stats_z)[0]
-    last = [shift_x(far, -1), shift_x(far, 1), swap_zl(beyond)]
     parts = [proj_quad, proj_first, proj_first_other, proj_second, swap_core(proj_second)]
 
     total, left = project(

time: 225 us -> 225 us (level)
  waiting for transfers between devices: 87.3 us -> 82.5 us
    ppermute x46 -> x47, waiting for transfers between devices: 87.3 us -> 82.5 us  [move(): return lax.ppermute(values, AXES, pairs)]
    ppermute x46 -> x47, starting transfers between devices: 46.6 us -> 48.7 us  [move(): return lax.ppermute(values, AXES, pairs)]
  transfers between devices with their start and end apart: 46 -> 47, of which waited for: 22 -> 21; matrix products, arithmetic and copies ran while one was open for 2% -> 3% of each run, Pallas kernels for 23% -> 23%
where the time goes in v5:
time: 225 us; the launch traced here: 223 us
  waiting for transfers between devices  82.5 us (37%)
  Pallas kernels  55.5 us (25%)
  starting transfers between devices  48.7 us (22%)
  blocking collectives  16.6 us (7%)
  local copies, waits for them, and re-layouts  14.3 us (6%)
  between operations  3.19 us (1%)
    ppermute x47, waiting for transfers between devices, move(): return lax.ppermute(values, AXES, pairs)  82.5 us
    ppermute x47, starting transfers between devices, move(): return lax.ppermute(values, AXES, pairs)  48.7 us
    pallas_call x4, Pallas kernels, accumulate(): pl.pallas_call(functools.partial(accumulate_kernel, counts, total is not...  21.2 us
    all_to_all x1, blocking collectives, local(): lax.all_to_all(outgoing, 'mp', split_axis=0, concat_axis=0, tiled=True)  16.6 us
    pallas_call x2, Pallas kernels, out_project(): pl.pallas_call(functools.partial(out_kernel, pieces, len(near), len(parts...  12.5 us
    pallas_call x2, Pallas kernels, project(): pl.pallas_call(functools.partial(project_kernel, pieces, len(near), len(p...  10.7 us
    unnamed x72, local copies, waits for them, and re-layouts  10.2 us
    pallas_call x1, Pallas kernels, norm_columns(): pl.pallas_call(norm_kernel, grid=(rows // block,), in_specs=[pl.BlockSpec...  8.52 us
  transfers between devices with their start and end apart: 47, of which 21 were waited for; matrix products, arithmetic and copies ran while one was open for 3% of the time, Pallas kernels for 23%

profile of v5, /device:TPU:0, one launch (start us, length us, event | category | flops | bytes accessed | tf_op | source)
XLA Modules:
  0.0 223.0 jit_solution(7397766560649895822)
XLA Ops:
  0.7 4.0 %collective-permute-start.1 = (bf16[3,384,384]{2,1,0:T(8,128)(2,1)}, bf16[3,384,384]{2,1,0:T(8,128)(2,1)}, u32[]{:S(2)}, u32[]{:S(2)}) collective-permute-start(bf16[3,384,384]{2,1,0:T(8,128)(2,1)} %bitcast.73), channel_id=1, source_target_pairs={{0,64},{1,65},{2,66},{3,67},{4,68},{5,69},{6,70},{7,71},{8,72},{9,... | collective-permute-start | bytes 2654216 | tf_op jit(solution)/shard_map/ppermute | solution.py:38
  4.8 1.6 collective-permute-start.2
  6.3 1.6 collective-permute-start.3
  7.9 1.6 collective-permute-start.4
  11.0 8.5 %norm_columns.1.refs_0_.refs_1_.refs_2_.refs_3_.refs_4_.refs_5_ = bf16[16,512,384]{2,1,0:T(8,128)(2,1)S(1)} custom-call(bf16[512,6144]{1,0:T(8,128)(2,1)} %refs_5_.1, f32[1,6144]{1,0:T(1,128)S(1)} %bitcast.57), custom_call_target="tpu_custom_call" | custom-call | flops 1 | bytes 1 | tf_op jit(solution)/shard_map/norm_columns/pallas_call | solution.py:147
  19.6 4.2 %accumulate.4.refs_12_ = f32[3,512,384]{2,1,0:T(8,128)S(1)} custom-call(s32[2]{0:T(128)S(1)} %get-tuple-element.147.index_ref, bf16[16,512,384]{2,1,0:T(8,128)(2,1)S(1)} %norm_columns.1.refs_0_.refs_1_.refs_2_.refs_3_.refs_4_.refs_5_, bf16[16,512,384]{2,1,0:T(8,128)(2,1)S(1)} %norm_columns.1.refs_0_.refs_1_.refs_2_.refs_3_.refs_4_.refs_5_, ...), custom_call_target="tpu_custom_call" | custom-call | flops 1 | bytes 1 | tf_op jit(solution)/shard_map/accumulate/pallas_call | solution.py:236
  23.9 1.4 collective-permute-done.1
  25.3 3.5 %collective-permute-done.3 = bf16[3,384,384]{2,1,0:T(8,128)(2,1)} collective-permute-done((bf16[3,384,384]{2,1,0:T(8,128)(2,1)S(1)}, bf16[3,384,384]{2,1,0:T(8,128)(2,1)}, u32[]{:S(2)}, u32[]{:S(2)}) %collective-permute-start.3) | collective-permute-done | bytes 884768 | tf_op jit(solution)/shard_map/ppermute | solution.py:38
  30.1 6.2 %collective-permute-start.10 = (bf16[3,384,384]{2,1,0:T(8,128)(2,1)}, bf16[3,384,384]{2,1,0:T(8,128)(2,1)}, u32[]{:S(2)}, u32[]{:S(2)}) collective-permute-start(bf16[3,384,384]{2,1,0:T(8,128)(2,1)} %collective-permute-done.3), channel_id=1, source_target_pairs={{0,64},{1,65},{2,66},{3,67},{4,68},{5,69},{6,70},{7,71},{8,72},{9,... | collective-permute-start | bytes 2654216 | tf_op jit(solution)/shard_map/ppermute | solution.py:38
  36.3 1.5 collective-permute-start.8
  37.8 1.6 collective-permute-start.9
  40.1 2.8 %copy-done.1 = bf16[16,512,384]{2,1,0:T(8,128)(2,1)S(1)} copy-done((bf16[16,512,384]{2,1,0:T(8,128)(2,1)S(1)}, bf16[16,512,384]{2,1,0:T(8,128)(2,1)}, u32[]{:S(2)}) %copy-start.1) | copy-done | bytes 6291480
  42.9 6.2 %accumulate.5.refs_12_ = f32[3,512,384]{2,1,0:T(8,128)S(1)} custom-call(s32[6]{0:T(128)S(1)} %get-tuple-element.143.index_ref, bf16[16,512,384]{2,1,0:T(8,128)(2,1)S(1)} %copy-done.1, bf16[16,512,384]{2,1,0:T(8,128)(2,1)S(1)} %copy-done.1, bf16[16,512,384]{2,1,0:T(8,128)(2,1)S(1)} %copy-done.1, ...), custom_call_target="tpu_custom_call", output_to_operand_aliasing={{}: (13, {})} | custom-call | flops 1 | bytes 1 | tf_op jit(solution)/shard_map/accumulate/pallas_call | solution.py:236
  51.1 1.3 and_select_fusion.1
  54.1 2.7 %collective-permute-done.10 = bf16[3,384,384]{2,1,0:T(8,128)(2,1)} collective-permute-done((bf16[3,384,384]{2,1,0:T(8,128)(2,1)}, bf16[3,384,384]{2,1,0:T(8,128)(2,1)}, u32[]{:S(2)}, u32[]{:S(2)}) %collective-permute-start.10) | collective-permute-done | bytes 884768 | tf_op jit(solution)/shard_map/ppermute | solution.py:38
  56.8 3.6 %collective-permute-done.9 = bf16[3,384,384]{2,1,0:T(8,128)(2,1)} collective-permute-done((bf16[3,384,384]{2,1,0:T(8,128)(2,1)}, bf16[3,384,384]{2,1,0:T(8,128)(2,1)}, u32[]{:S(2)}, u32[]{:S(2)}) %collective-permute-start.9) | collective-permute-done | bytes 884768 | tf_op jit(solution)/shard_map/ppermute | solution.py:38
  63.0 1.7 collective-permute-start.13
  66.4 2.8 %copy-done.2 = bf16[16,512,384]{2,1,0:T(8,128)(2,1)S(1)} copy-done((bf16[16,512,384]{2,1,0:T(8,128)(2,1)S(1)}, bf16[16,512,384]{2,1,0:T(8,128)(2,1)}, u32[]{:S(2)}) %copy-start.2) | copy-done | bytes 6291480
  69.2 6.2 %accumulate.6.refs_4_ = f32[3,512,384]{2,1,0:T(8,128)S(1)} custom-call(s32[6]{0:T(128)S(1)} %get-tuple-element.142.index_ref, bf16[16,512,384]{2,1,0:T(8,128)(2,1)S(1)} %copy-done.2, bf16[16,512,384]{2,1,0:T(8,128)(2,1)S(1)} %copy-done.2, bf16[16,512,384]{2,1,0:T(8,128)(2,1)S(1)} %copy-done.2, ...), custom_call_target="tpu_custom_call", output_to_operand_aliasing={{}: (13, {})} | custom-call | flops 1 | bytes 1 | tf_op jit(solution)/shard_map/accumulate/pallas_call | solution.py:236
  75.4 4.9 %collective-permute-done.13 = bf16[384,384]{1,0:T(8,128)(2,1)S(1)} collective-permute-done((bf16[384,384]{1,0:T(8,128)(2,1)S(1)}, bf16[384,384]{1,0:T(8,128)(2,1)S(1)}, u32[]{:S(2)}, u32[]{:S(2)}) %collective-permute-start.13) | collective-permute-done | bytes 294944 | tf_op jit(solution)/shard_map/ppermute | solution.py:38
  81.1 1.5 collective-permute-done.22
  82.8 1.6 collective-permute-start.23
  84.3 4.5 %accumulate.7 = (bf16[512,384]{1,0:T(8,128)(2,1)S(1)}, bf16[256,384]{1,0:T(8,128)(2,1)S(1)}, bf16[256,384]{1,0:T(8,128)(2,1)S(1)}) custom-call(s32[2]{0:T(128)S(1)} %get-tuple-element.146.index_ref, bf16[16,512,384]{2,1,0:T(8,128)(2,1)S(1)} %copy-done.2, bf16[16,512,384]{2,1,0:T(8,128)(2,1)S(1)} %copy-done.2, bf16[1,3,384,384]{3,2,1,0:T(8,128)(2,1)S(1)} %bitcast.55, ...), custom_call_target="tpu_custom_call" | custom-call | flops 1 | bytes 1 | tf_op jit(solution)/shard_map/accumulate/pallas_call | solution.py:236
  89.0 4.1 %collective-permute-start.19 = (bf16[256,384]{1,0:T(8,128)(2,1)S(1)}, bf16[256,384]{1,0:T(8,128)(2,1)S(1)}, u32[]{:S(2)}, u32[]{:S(2)}) collective-permute-start(bf16[256,384]{1,0:T(8,128)(2,1)S(1)} %get-tuple-element.105), channel_id=1, source_target_pairs={{0,1},{1,2},{2,3},{3,0},{4,5},{5,6},{6,7},{7,4},{8,9},{9,10},{10,1... | collective-permute-start | bytes 589832 | tf_op jit(solution)/shard_map/ppermute | solution.py:38
  93.1 5.2 %collective-permute-done.19.refs_2_ = bf16[256,384]{1,0:T(8,128)(2,1)S(1)} collective-permute-done((bf16[256,384]{1,0:T(8,128)(2,1)S(1)}, bf16[256,384]{1,0:T(8,128)(2,1)S(1)}, u32[]{:S(2)}, u32[]{:S(2)}) %collective-permute-start.19) | collective-permute-done | bytes 196640 | tf_op jit(solution)/shard_map/ppermute | solution.py:38
  98.2 2.2 collective-permute-done.20.refs_3_
  102.1 3.6 %collective-permute-start.27 = (bf16[512,384]{1,0:T(8,128)(2,1)S(1)}, bf16[512,384]{1,0:T(8,128)(2,1)S(1)}, u32[]{:S(2)}, u32[]{:S(2)}) collective-permute-start(bf16[512,384]{1,0:T(8,128)(2,1)S(1)} %pad_maximum_fusion.7), channel_id=1, source_target_pairs={{0,3},{1,0},{2,1},{3,2},{4,7},{5,4},{6,5},{7,6},{8,11},{9,8},{10,9... | collective-permute-start | bytes 1179656 | tf_op jit(solution)/shard_map/ppermute | solution.py:38
  105.9 9.1 %collective-permute-done.27.refs_5_ = bf16[512,384]{1,0:T(8,128)(2,1)S(1)} collective-permute-done((bf16[512,384]{1,0:T(8,128)(2,1)S(1)}, bf16[512,384]{1,0:T(8,128)(2,1)S(1)}, u32[]{:S(2)}, u32[]{:S(2)}) %collective-permute-start.27) | collective-permute-done | bytes 393248 | tf_op jit(solution)/shard_map/ppermute | solution.py:38
  114.9 3.5 %collective-permute-done.26.refs_4_ = bf16[512,384]{1,0:T(8,128)(2,1)S(1)} collective-permute-done((bf16[512,384]{1,0:T(8,128)(2,1)S(1)}, bf16[512,384]{1,0:T(8,128)(2,1)S(1)}, u32[]{:S(2)}, u32[]{:S(2)}) %collective-permute-start.26) | collective-permute-done | bytes 393248 | tf_op jit(solution)/shard_map/ppermute | solution.py:38
  118.6 1.1 copy-done.18
  121.6 1.2 collective-permute-start.25
  123.8 7.0 %out_project.2 = (f32[2,512,384]{2,1,0:T(8,128)S(1)}, bf16[6,384,384]{2,1,0:T(8,128)(2,1)S(1)}) custom-call(s32[16]{0:T(128)S(1)} %get-tuple-element.140.index_ref, bf16[512,384]{1,0:T(8,128)(2,1)} %copy-done.5, bf16[512,384]{1,0:T(8,128)(2,1)} %copy-done.34, bf16[256,384]{1,0:T(8,128)(2,1)} %copy-done.30, bf16[256,384]{1,0:T(8,128)(2,1)} %copy-done.31, ...), custom_call_target="tpu_custom_call" | custom-call | flops 1 | bytes 1 | tf_op jit(solution)/shard_map/out_project/pallas_call | solution.py:382
  130.8 1.4 collective-permute-done.24.refs_0_
  132.3 1.8 collective-permute-done.25.refs_1_
  134.0 5.5 %out_project.3 = (bf16[512,768]{1,0:T(8,128)(2,1)}, bf16[272,768]{1,0:T(8,128)(2,1)S(1)}, bf16[272,768]{1,0:T(8,128)(2,1)S(1)}, f32[8,512]{1,0:T(8,128)S(1)}) custom-call(s32[1]{0:T(128)} %bitcast.12.index_ref, bf16[512,384]{1,0:T(8,128)(2,1)S(1)} %collective-permute-done.24.refs_0_, bf16[512,384]{1,0:T(8,128)(2,1)S(1)} %collective-permute-done.25.refs_1_, ...), custom_call_target="tpu_custom_call" | custom-call | flops 1 | bytes 1 | tf_op jit(solution)/shard_map/out_project/pallas_call | solution.py:382
  139.5 1.9 collective-permute-done.33.refs_13_
  141.7 3.2 %collective-permute-start.35 = (bf16[272,768]{1,0:T(8,128)(2,1)S(1)}, bf16[272,768]{1,0:T(8,128)(2,1)S(1)}, u32[]{:S(2)}, u32[]{:S(2)}) collective-permute-start(bf16[272,768]{1,0:T(8,128)(2,1)S(1)} %get-tuple-element.125), channel_id=1, source_target_pairs={{0,3},{1,0},{2,1},{3,2},{4,7},{5,4},{6,5},{7,6},{8,11},{9,8},{10,9... | collective-permute-start | bytes 1253384 | tf_op jit(solution)/shard_map/ppermute | solution.py:38
  144.9 10.3 %collective-permute-done.34.refs_0_.refs_2_ = bf16[272,768]{1,0:T(8,128)(2,1)S(1)} collective-permute-done((bf16[272,768]{1,0:T(8,128)(2,1)S(1)}, bf16[272,768]{1,0:T(8,128)(2,1)S(1)}, u32[]{:S(2)}, u32[]{:S(2)}) %collective-permute-start.34) | collective-permute-done | bytes 417824 | tf_op jit(solution)/shard_map/ppermute | solution.py:38
  155.3 3.0 %collective-permute-start.39 = (bf16[544,768]{1,0:T(8,128)(2,1)S(1)}, bf16[544,768]{1,0:T(8,128)(2,1)S(1)}, u32[]{:S(2)}, u32[]{:S(2)}) collective-permute-start(bf16[544,768]{1,0:T(8,128)(2,1)S(1)} %pad_maximum_fusion.3), channel_id=1, source_target_pairs={{0,3},{1,0},{2,1},{3,2},{4,7},{5,4},{6,5},{7,6},{8,11},{9,8},{10,9... | collective-permute-start | bytes 2506760 | tf_op jit(solution)/shard_map/ppermute | solution.py:38
  158.9 18.7 %collective-permute-done.40.refs_1_ = bf16[512,768]{1,0:T(8,128)(2,1)S(1)} collective-permute-done((bf16[512,768]{1,0:T(8,128)(2,1)S(1)}, bf16[512,768]{1,0:T(8,128)(2,1)S(1)}, u32[]{:S(2)}, u32[]{:S(2)}) %collective-permute-start.40) | collective-permute-done | bytes 786464 | tf_op jit(solution)/shard_map/ppermute | solution.py:38
  177.7 2.2 collective-permute-done.38.refs_2_.refs_4_
  180.6 1.2 collective-permute-start.42
  183.8 2.1 collective-permute-start.44
  187.7 7.5 %project.2 = (f32[512,512]{1,0:T(8,128)S(1)}, bf16[6,384,512]{2,1,0:T(8,128)(2,1)S(1)}) custom-call(s32[21]{0:T(128)S(1)} %pad_add_fusion.index_ref, bf16[512,768]{1,0:T(8,128)(2,1)} %get-tuple-element.128.refs_0_, bf16[512,768]{1,0:T(8,128)(2,1)} %copy-done.28, bf16[272,768]{1,0:T(8,128)(2,1)} %copy-done.11, bf16[272,768]{1,0:T(8,128)(2,1)} %copy-done.12, ...), custom_call_target="tpu_custom_call" | custom-call | flops 1 | bytes 1 | tf_op jit(solution)/shard_map/project/pallas_call | solution.py:499
  195.9 5.5 %collective-permute-done.43.refs_2_ = bf16[256,768]{1,0:T(8,128)(2,1)S(1)} collective-permute-done((bf16[256,768]{1,0:T(8,128)(2,1)S(1)}, bf16[256,768]{1,0:T(8,128)(2,1)S(1)}, u32[]{:S(2)}, u32[]{:S(2)}) %collective-permute-start.43) | collective-permute-done | bytes 393248 | tf_op jit(solution)/shard_map/ppermute | solution.py:38
  201.4 3.3 %project.3 = bf16[8,128,512]{2,1,0:T(8,128)(2,1)S(1)} custom-call(s32[11]{0:T(128)S(1)} %pad_add_fusion.1.index_ref, bf16[512,768]{1,0:T(8,128)(2,1)S(1)} %collective-permute-done.41.refs_0_, bf16[512,768]{1,0:T(8,128)(2,1)S(1)} %collective-permute-done.42.refs_1_, bf16[256,768]{1,0:T(8,128)(2,1)S(1)} %collective-permute-done.43.refs_2_, ...), custom_call_target="tpu_custom_call" | custom-call | flops 1 | bytes 1 | tf_op jit(solution)/shard_map/project/pallas_call | solution.py:499
  204.7 16.6 %all_to_all.5.arrived_ref = bf16[8,128,512]{2,1,0:T(8,128)(2,1)S(1)} all-to-all(bf16[8,128,512]{2,1,0:T(8,128)(2,1)S(1)} %project.3), channel_id=1, replica_groups=mesh['dp'=16,'mp'=8] {'mp'}, dimensions={0} | all-to-all | bytes 2097152 | tf_op jit(solution)/shard_map/all_to_all | solution.py:722
  221.3 1.7 pack.1
  (159 shorter events, 21.3 us)
Async XLA Ops:
  0.6 5.7 %collective-permute-start = (bf16[3,384,384]{2,1,0:T(8,128)(2,1)}, bf16[3,384,384]{2,1,0:T(8,128)(2,1)S(1)}, u32[]{:S(2)}, u32[]{:S(2)}) collective-permute-start(bf16[3,384,384]{2,1,0:T(8,128)(2,1)} %bitcast.72), channel_id=1, source_target_pairs={{0,8},{1,9},{2,10},{3,11},{4,12},{5,13},{6,14},{7,15},{8,0},{9,1},... | collective-permute-start | bytes 2654216 | tf_op jit(solution)/shard_map/ppermute | solution.py:38
  0.7 24.6 %collective-permute-start.1 = (bf16[3,384,384]{2,1,0:T(8,128)(2,1)}, bf16[3,384,384]{2,1,0:T(8,128)(2,1)}, u32[]{:S(2)}, u32[]{:S(2)}) collective-permute-start(bf16[3,384,384]{2,1,0:T(8,128)(2,1)} %bitcast.73), channel_id=1, source_target_pairs={{0,64},{1,65},{2,66},{3,67},{4,68},{5,69},{6,70},{7,71},{8,72},{9,... | collective-permute-start | bytes 2654216 | tf_op jit(solution)/shard_map/ppermute | solution.py:38
  4.8 20.5 %collective-permute-start.2 = (bf16[3,384,384]{2,1,0:T(8,128)(2,1)}, bf16[3,384,384]{2,1,0:T(8,128)(2,1)}, u32[]{:S(2)}, u32[]{:S(2)}) collective-permute-start(bf16[3,384,384]{2,1,0:T(8,128)(2,1)} %bitcast.74), channel_id=1, source_target_pairs={{0,16},{1,17},{2,18},{3,19},{4,20},{5,21},{6,22},{7,23},{8,56},{9,... | collective-permute-start | bytes 2654216 | tf_op jit(solution)/shard_map/ppermute | solution.py:38
  6.3 22.5 %collective-permute-start.3 = (bf16[3,384,384]{2,1,0:T(8,128)(2,1)S(1)}, bf16[3,384,384]{2,1,0:T(8,128)(2,1)}, u32[]{:S(2)}, u32[]{:S(2)}) collective-permute-start(bf16[3,384,384]{2,1,0:T(8,128)(2,1)S(1)} %collective-permute-done), channel_id=1, source_target_pairs={{0,16},{1,17},{2,18},{3,19},{4,20},{5,21},{6,22},{7,23},{8,56},{9,... | collective-permute-start | bytes 2654216 | tf_op jit(solution)/shard_map/ppermute | solution.py:38
  7.9 15.9 %collective-permute-start.4 = (bf16[384,384]{1,0:T(8,128)(2,1)}, bf16[384,384]{1,0:T(8,128)(2,1)S(1)}, u32[]{:S(2)}, u32[]{:S(2)}) collective-permute-start(bf16[384,384]{1,0:T(8,128)(2,1)} %param.17), channel_id=1, source_target_pairs={{0,0},{1,17},{2,34},{3,51},{4,64},{5,81},{6,98},{7,115},{8,8},{9,2... | collective-permute-start | bytes 884744 | tf_op jit(solution)/shard_map/ppermute | solution.py:38
  28.8 9.0 %collective-permute-start.5 = (bf16[3,384,384]{2,1,0:T(8,128)(2,1)}, bf16[3,384,384]{2,1,0:T(8,128)(2,1)S(1)}, u32[]{:S(2)}, u32[]{:S(2)}) collective-permute-start(bf16[3,384,384]{2,1,0:T(8,128)(2,1)} %collective-permute-done.1), channel_id=1, source_target_pairs={{0,8},{1,9},{2,10},{3,11},{4,12},{5,13},{6,14},{7,15},{8,0},{9,1},... | collective-permute-start | bytes 2654216 | tf_op jit(solution)/shard_map/ppermute | solution.py:38
  28.8 10.6 %collective-permute-start.6 = (bf16[3,384,384]{2,1,0:T(8,128)(2,1)}, bf16[3,384,384]{2,1,0:T(8,128)(2,1)}, u32[]{:S(2)}, u32[]{:S(2)}) collective-permute-start(bf16[3,384,384]{2,1,0:T(8,128)(2,1)} %collective-permute-done.2), channel_id=1, source_target_pairs={{0,8},{1,9},{2,10},{3,11},{4,12},{5,13},{6,14},{7,15},{8,0},{9,1},... | collective-permute-start | bytes 2654216 | tf_op jit(solution)/shard_map/ppermute | solution.py:38
  29.3 10.7 %collective-permute-start.7 = (bf16[3,384,384]{2,1,0:T(8,128)(2,1)}, bf16[3,384,384]{2,1,0:T(8,128)(2,1)}, u32[]{:S(2)}, u32[]{:S(2)}) collective-permute-start(bf16[3,384,384]{2,1,0:T(8,128)(2,1)} %collective-permute-done.3), channel_id=1, source_target_pairs={{0,8},{1,9},{2,10},{3,11},{4,12},{5,13},{6,14},{7,15},{8,0},{9,1},... | collective-permute-start | bytes 2654216 | tf_op jit(solution)/shard_map/ppermute | solution.py:38
  30.1 26.7 %collective-permute-start.10 = (bf16[3,384,384]{2,1,0:T(8,128)(2,1)}, bf16[3,384,384]{2,1,0:T(8,128)(2,1)}, u32[]{:S(2)}, u32[]{:S(2)}) collective-permute-start(bf16[3,384,384]{2,1,0:T(8,128)(2,1)} %collective-permute-done.3), channel_id=1, source_target_pairs={{0,64},{1,65},{2,66},{3,67},{4,68},{5,69},{6,70},{7,71},{8,72},{9,... | collective-permute-start | bytes 2654216 | tf_op jit(solution)/shard_map/ppermute | solution.py:38
  36.3 20.5 %collective-permute-start.8 = (bf16[3,384,384]{2,1,0:T(8,128)(2,1)}, bf16[3,384,384]{2,1,0:T(8,128)(2,1)}, u32[]{:S(2)}, u32[]{:S(2)}) collective-permute-start(bf16[3,384,384]{2,1,0:T(8,128)(2,1)} %collective-permute-done.1), channel_id=1, source_target_pairs={{0,16},{1,17},{2,18},{3,19},{4,20},{5,21},{6,22},{7,23},{8,56},{9,... | collective-permute-start | bytes 2654216 | tf_op jit(solution)/shard_map/ppermute | solution.py:38
  37.8 22.5 %collective-permute-start.9 = (bf16[3,384,384]{2,1,0:T(8,128)(2,1)}, bf16[3,384,384]{2,1,0:T(8,128)(2,1)}, u32[]{:S(2)}, u32[]{:S(2)}) collective-permute-start(bf16[3,384,384]{2,1,0:T(8,128)(2,1)} %collective-permute-done.2), channel_id=1, source_target_pairs={{0,16},{1,17},{2,18},{3,19},{4,20},{5,21},{6,22},{7,23},{8,56},{9,... | collective-permute-start | bytes 2654216 | tf_op jit(solution)/shard_map/ppermute | solution.py:38
  39.4 14.7 %collective-permute-start.11 = (bf16[384,384]{1,0:T(8,128)(2,1)S(1)}, bf16[384,384]{1,0:T(8,128)(2,1)S(1)}, u32[]{:S(2)}, u32[]{:S(2)}) collective-permute-start(bf16[384,384]{1,0:T(8,128)(2,1)S(1)} %collective-permute-done.4), channel_id=1, source_target_pairs={{0,0},{1,3},{2,2},{3,1},{4,4},{5,7},{6,6},{7,5},{8,8},{9,11},{10,1... | collective-permute-start | bytes 884744 | tf_op jit(solution)/shard_map/ppermute | solution.py:38
  60.3 2.6 %collective-permute-start.15 = (bf16[3,384,384]{2,1,0:T(8,128)(2,1)}, bf16[3,384,384]{2,1,0:T(8,128)(2,1)S(1)}, u32[]{:S(2)}, u32[]{:S(2)}) collective-permute-start(bf16[3,384,384]{2,1,0:T(8,128)(2,1)} %collective-permute-done.8), channel_id=1, source_target_pairs={{0,8},{1,9},{2,10},{3,11},{4,12},{5,13},{6,14},{7,15},{8,0},{9,1},... | collective-permute-start | bytes 2654216 | tf_op jit(solution)/shard_map/ppermute | solution.py:38
  60.3 4.4 %collective-permute-start.16 = (bf16[3,384,384]{2,1,0:T(8,128)(2,1)}, bf16[3,384,384]{2,1,0:T(8,128)(2,1)S(1)}, u32[]{:S(2)}, u32[]{:S(2)}) collective-permute-start(bf16[3,384,384]{2,1,0:T(8,128)(2,1)} %collective-permute-done.9), channel_id=1, source_target_pairs={{0,8},{1,9},{2,10},{3,11},{4,12},{5,13},{6,14},{7,15},{8,0},{9,1},... | collective-permute-start | bytes 2654216 | tf_op jit(solution)/shard_map/ppermute | solution.py:38
  60.8 4.7 %collective-permute-start.17 = (bf16[3,384,384]{2,1,0:T(8,128)(2,1)}, bf16[3,384,384]{2,1,0:T(8,128)(2,1)S(1)}, u32[]{:S(2)}, u32[]{:S(2)}) collective-permute-start(bf16[3,384,384]{2,1,0:T(8,128)(2,1)} %collective-permute-done.10), channel_id=1, source_target_pairs={{0,8},{1,9},{2,10},{3,11},{4,12},{5,13},{6,14},{7,15},{8,0},{9,1},... | collective-permute-start | bytes 2654216 | tf_op jit(solution)/shard_map/ppermute | solution.py:38
  60.8 19.5 %collective-permute-start.12 = (bf16[3,384,384]{2,1,0:T(8,128)(2,1)}, bf16[3,384,384]{2,1,0:T(8,128)(2,1)S(1)}, u32[]{:S(2)}, u32[]{:S(2)}) collective-permute-start(bf16[3,384,384]{2,1,0:T(8,128)(2,1)} %collective-permute-done.8), channel_id=1, source_target_pairs={{0,16},{1,17},{2,18},{3,19},{4,20},{5,21},{6,22},{7,23},{8,56},{9,... | collective-permute-start | bytes 2654216 | tf_op jit(solution)/shard_map/ppermute | solution.py:38
  61.2 19.2 %collective-permute-start.14 = (bf16[384,512]{1,0:T(8,128)(2,1)S(1)}, bf16[384,512]{1,0:T(8,128)(2,1)S(1)}, u32[]{:S(2)}, u32[]{:S(2)}) collective-permute-start(bf16[384,512]{1,0:T(8,128)(2,1)S(1)} %copy-done.17), channel_id=1, source_target_pairs={{0,64},{1,65},{2,66},{3,67},{4,68},{5,69},{6,70},{7,71},{8,72},{9,... | collective-permute-start | bytes 1179656 | tf_op jit(solution)/shard_map/ppermute | solution.py:38
  63.0 17.4 %collective-permute-start.13 = (bf16[384,384]{1,0:T(8,128)(2,1)S(1)}, bf16[384,384]{1,0:T(8,128)(2,1)S(1)}, u32[]{:S(2)}, u32[]{:S(2)}) collective-permute-start(bf16[384,384]{1,0:T(8,128)(2,1)S(1)} %collective-permute-done.11), channel_id=1, source_target_pairs={{0,64},{1,65},{2,66},{3,67},{4,68},{5,69},{6,70},{7,71},{8,72},{9,... | collective-permute-start | bytes 884744 | tf_op jit(solution)/shard_map/ppermute | solution.py:38
  80.4 2.2 collective-permute-start.22
  81.0 3.4 %collective-permute-start.18 = (bf16[3,384,384]{2,1,0:T(8,128)(2,1)S(1)}, bf16[3,384,384]{2,1,0:T(8,128)(2,1)S(1)}, u32[]{:S(2)}, u32[]{:S(2)}) collective-permute-start(bf16[3,384,384]{2,1,0:T(8,128)(2,1)S(1)} %collective-permute-done.12), channel_id=1, source_target_pairs={{0,8},{1,9},{2,10},{3,11},{4,12},{5,13},{6,14},{7,15},{8,0},{9,1},... | collective-permute-start | bytes 2654216 | tf_op jit(solution)/shard_map/ppermute | solution.py:38
  82.8 17.7 %collective-permute-start.23 = (bf16[4,384,384]{2,1,0:T(8,128)(2,1)S(1)}, bf16[4,384,384]{2,1,0:T(8,128)(2,1)S(1)}, u32[]{:S(2)}, u32[]{:S(2)}) collective-permute-start(bf16[4,384,384]{2,1,0:T(8,128)(2,1)S(1)} %pad_maximum_fusion.1.refs_6_), channel_id=1, source_target_pairs={{0,16},{1,17},{2,18},{3,19},{4,20},{5,21},{6,22},{7,23},{8,56},{9,... | collective-permute-start | bytes 3538952 | tf_op jit(solution)/shard_map/ppermute | solution.py:38
  88.9 11.5 %collective-permute-start.21 = (bf16[512,384]{1,0:T(8,128)(2,1)S(1)}, bf16[512,384]{1,0:T(8,128)(2,1)S(1)}, u32[]{:S(2)}, u32[]{:S(2)}) collective-permute-start(bf16[512,384]{1,0:T(8,128)(2,1)S(1)} %get-tuple-element.98.refs_0_), channel_id=1, source_target_pairs={{0,4},{1,5},{2,6},{3,7},{4,0},{5,1},{6,2},{7,3},{8,12},{9,13},{10,... | collective-permute-start | bytes 1179656 | tf_op jit(solution)/shard_map/ppermute | solution.py:38
  89.0 9.2 %collective-permute-start.19 = (bf16[256,384]{1,0:T(8,128)(2,1)S(1)}, bf16[256,384]{1,0:T(8,128)(2,1)S(1)}, u32[]{:S(2)}, u32[]{:S(2)}) collective-permute-start(bf16[256,384]{1,0:T(8,128)(2,1)S(1)} %get-tuple-element.105), channel_id=1, source_target_pairs={{0,1},{1,2},{2,3},{3,0},{4,5},{5,6},{6,7},{7,4},{8,9},{9,10},{10,1... | collective-permute-start | bytes 589832 | tf_op jit(solution)/shard_map/ppermute | solution.py:38
  93.1 7.4 %collective-permute-start.20 = (bf16[256,384]{1,0:T(8,128)(2,1)S(1)}, bf16[256,384]{1,0:T(8,128)(2,1)S(1)}, u32[]{:S(2)}, u32[]{:S(2)}) collective-permute-start(bf16[256,384]{1,0:T(8,128)(2,1)S(1)} %get-tuple-element.103), channel_id=1, source_target_pairs={{0,3},{1,0},{2,1},{3,2},{4,7},{5,4},{6,5},{7,6},{8,11},{9,8},{10,9... | collective-permute-start | bytes 589832 | tf_op jit(solution)/shard_map/ppermute | solution.py:38
  100.4 18.0 %collective-permute-start.29 = (bf16[4,384,384]{2,1,0:T(8,128)(2,1)S(1)}, bf16[4,384,384]{2,1,0:T(8,128)(2,1)S(1)}, u32[]{:S(2)}, u32[]{:S(2)}) collective-permute-start(bf16[4,384,384]{2,1,0:T(8,128)(2,1)S(1)} %collective-permute-done.23.refs_7_), channel_id=1, source_target_pairs={{0,8},{1,9},{2,10},{3,11},{4,12},{5,13},{6,14},{7,15},{8,0},{9,1},... | collective-permute-start | bytes 3538952 | tf_op jit(solution)/shard_map/ppermute | solution.py:38
  100.9 17.5 %collective-permute-start.30 = (bf16[2,384,512]{2,1,0:T(8,128)(2,1)S(1)}, bf16[2,384,512]{2,1,0:T(8,128)(2,1)S(1)}, u32[]{:S(2)}, u32[]{:S(2)}) collective-permute-start(bf16[2,384,512]{2,1,0:T(8,128)(2,1)S(1)} %pad_maximum_fusion.4), channel_id=1, source_target_pairs={{0,8},{1,9},{2,10},{3,11},{4,12},{5,13},{6,14},{7,15},{8,0},{9,1},... | collective-permute-start | bytes 2359304 | tf_op jit(solution)/shard_map/ppermute | solution.py:38
  101.2 17.2 %collective-permute-start.28 = (bf16[2,384,384]{2,1,0:T(8,128)(2,1)S(1)}, bf16[2,384,384]{2,1,0:T(8,128)(2,1)S(1)}, u32[]{:S(2)}, u32[]{:S(2)}) collective-permute-start(bf16[2,384,384]{2,1,0:T(8,128)(2,1)S(1)} %slice.87), channel_id=1, source_target_pairs={{0,16},{1,17},{2,18},{3,19},{4,20},{5,21},{6,22},{7,23},{8,56},{9,... | collective-permute-start | bytes 1769480 | tf_op jit(solution)/shard_map/ppermute | solution.py:38
  102.1 12.8 %collective-permute-start.27 = (bf16[512,384]{1,0:T(8,128)(2,1)S(1)}, bf16[512,384]{1,0:T(8,128)(2,1)S(1)}, u32[]{:S(2)}, u32[]{:S(2)}) collective-permute-start(bf16[512,384]{1,0:T(8,128)(2,1)S(1)} %pad_maximum_fusion.7), channel_id=1, source_target_pairs={{0,3},{1,0},{2,1},{3,2},{4,7},{5,4},{6,5},{7,6},{8,11},{9,8},{10,9... | collective-permute-start | bytes 1179656 | tf_op jit(solution)/shard_map/ppermute | solution.py:38
  105.8 12.7 %collective-permute-start.26 = (bf16[512,384]{1,0:T(8,128)(2,1)S(1)}, bf16[512,384]{1,0:T(8,128)(2,1)S(1)}, u32[]{:S(2)}, u32[]{:S(2)}) collective-permute-start(bf16[512,384]{1,0:T(8,128)(2,1)S(1)} %pad_maximum_fusion.6), channel_id=1, source_target_pairs={{0,1},{1,2},{2,3},{3,0},{4,5},{5,6},{6,7},{7,4},{8,9},{9,10},{10,1... | collective-permute-start | bytes 1179656 | tf_op jit(solution)/shard_map/ppermute | solution.py:38
  119.8 21.6 %collective-permute-start.33 = (bf16[4,384,512]{2,1,0:T(8,128)(2,1)S(1)}, bf16[4,384,512]{2,1,0:T(8,128)(2,1)S(1)}, u32[]{:S(2)}, u32[]{:S(2)}) collective-permute-start(bf16[4,384,512]{2,1,0:T(8,128)(2,1)S(1)} %pad_maximum_fusion.refs_12_), channel_id=1, source_target_pairs={{0,16},{1,17},{2,18},{3,19},{4,20},{5,21},{6,22},{7,23},{8,56},{9,... | collective-permute-start | bytes 4718600 | tf_op jit(solution)/shard_map/ppermute | solution.py:38
  120.7 2.2 %collective-permute-start.32 = (bf16[2,384,384]{2,1,0:T(8,128)(2,1)S(1)}, bf16[2,384,384]{2,1,0:T(8,128)(2,1)S(1)}, u32[]{:S(2)}, u32[]{:S(2)}) collective-permute-start(bf16[2,384,384]{2,1,0:T(8,128)(2,1)S(1)} %collective-permute-done.28.refs_9_), channel_id=1, source_target_pairs={{0,8},{1,9},{2,10},{3,11},{4,12},{5,13},{6,14},{7,15},{8,0},{9,1},... | collective-permute-start | bytes 1769480 | tf_op jit(solution)/shard_map/ppermute | solution.py:38
  120.8 11.5 %collective-permute-start.24 = (bf16[512,384]{1,0:T(8,128)(2,1)S(1)}, bf16[512,384]{1,0:T(8,128)(2,1)S(1)}, u32[]{:S(2)}, u32[]{:S(2)}) collective-permute-start(bf16[512,384]{1,0:T(8,128)(2,1)S(1)} %collective-permute-done.21.refs_1_), channel_id=1, source_target_pairs={{0,3},{1,0},{2,1},{3,2},{4,7},{5,4},{6,5},{7,6},{8,11},{9,8},{10,9... | collective-permute-start | bytes 1179656 | tf_op jit(solution)/shard_map/ppermute | solution.py:38
  121.6 12.5 %collective-permute-start.25 = (bf16[512,384]{1,0:T(8,128)(2,1)S(1)}, bf16[512,384]{1,0:T(8,128)(2,1)S(1)}, u32[]{:S(2)}, u32[]{:S(2)}) collective-permute-start(bf16[512,384]{1,0:T(8,128)(2,1)S(1)} %collective-permute-done.21.refs_1_), channel_id=1, source_target_pairs={{0,1},{1,2},{2,3},{3,0},{4,5},{5,6},{6,7},{7,4},{8,9},{9,10},{10,1... | collective-permute-start | bytes 1179656 | tf_op jit(solution)/shard_map/ppermute | solution.py:38
  122.9 11.1 %collective-permute-start.31 = (bf16[512,384]{1,0:T(8,128)(2,1)S(1)}, bf16[512,384]{1,0:T(8,128)(2,1)S(1)}, u32[]{:S(2)}, u32[]{:S(2)}) collective-permute-start(bf16[512,384]{1,0:T(8,128)(2,1)S(1)} %pad_maximum_fusion.8), channel_id=1, source_target_pairs={{0,4},{1,5},{2,6},{3,7},{4,0},{5,1},{6,2},{7,3},{8,12},{9,13},{10,... | collective-permute-start | bytes 1179656 | tf_op jit(solution)/shard_map/ppermute | solution.py:38
  141.4 13.8 %collective-permute-start.36 = (bf16[4,384,512]{2,1,0:T(8,128)(2,1)S(1)}, bf16[4,384,512]{2,1,0:T(8,128)(2,1)S(1)}, u32[]{:S(2)}, u32[]{:S(2)}) collective-permute-start(bf16[4,384,512]{2,1,0:T(8,128)(2,1)S(1)} %collective-permute-done.33.refs_13_), channel_id=1, source_target_pairs={{0,8},{1,9},{2,10},{3,11},{4,12},{5,13},{6,14},{7,15},{8,0},{9,1},... | collective-permute-start | bytes 4718600 | tf_op jit(solution)/shard_map/ppermute | solution.py:38
  141.5 13.7 %collective-permute-start.37 = (bf16[2,384,512]{2,1,0:T(8,128)(2,1)S(1)}, bf16[2,384,512]{2,1,0:T(8,128)(2,1)S(1)}, u32[]{:S(2)}, u32[]{:S(2)}) collective-permute-start(bf16[2,384,512]{2,1,0:T(8,128)(2,1)S(1)} %slice.91), channel_id=1, source_target_pairs={{0,16},{1,17},{2,18},{3,19},{4,20},{5,21},{6,22},{7,23},{8,56},{9,... | collective-permute-start | bytes 2359304 | tf_op jit(solution)/shard_map/ppermute | solution.py:38
  141.6 13.6 %collective-permute-start.34 = (bf16[272,768]{1,0:T(8,128)(2,1)S(1)}, bf16[272,768]{1,0:T(8,128)(2,1)S(1)}, u32[]{:S(2)}, u32[]{:S(2)}) collective-permute-start(bf16[272,768]{1,0:T(8,128)(2,1)S(1)} %get-tuple-element.127), channel_id=1, source_target_pairs={{0,1},{1,2},{2,3},{3,0},{4,5},{5,6},{6,7},{7,4},{8,9},{9,10},{10,1... | collective-permute-start | bytes 1253384 | tf_op jit(solution)/shard_map/ppermute | solution.py:38
  141.7 13.5 %collective-permute-start.35 = (bf16[272,768]{1,0:T(8,128)(2,1)S(1)}, bf16[272,768]{1,0:T(8,128)(2,1)S(1)}, u32[]{:S(2)}, u32[]{:S(2)}) collective-permute-start(bf16[272,768]{1,0:T(8,128)(2,1)S(1)} %get-tuple-element.125), channel_id=1, source_target_pairs={{0,3},{1,0},{2,1},{3,2},{4,7},{5,4},{6,5},{7,6},{8,11},{9,8},{10,9... | collective-permute-start | bytes 1253384 | tf_op jit(solution)/shard_map/ppermute | solution.py:38
  155.3 22.4 %collective-permute-start.39 = (bf16[544,768]{1,0:T(8,128)(2,1)S(1)}, bf16[544,768]{1,0:T(8,128)(2,1)S(1)}, u32[]{:S(2)}, u32[]{:S(2)}) collective-permute-start(bf16[544,768]{1,0:T(8,128)(2,1)S(1)} %pad_maximum_fusion.3), channel_id=1, source_target_pairs={{0,3},{1,0},{2,1},{3,2},{4,7},{5,4},{6,5},{7,6},{8,11},{9,8},{10,9... | collective-permute-start | bytes 2506760 | tf_op jit(solution)/shard_map/ppermute | solution.py:38
  158.4 29.3 %copy-start.3 = (f32[6144]{0:T(1024)S(1)}, f32[6144]{0:T(1024)}, u32[]{:S(2)}) copy-start(f32[6144]{0:T(1024)} %param.18) | copy-start | bytes 73732
  158.4 21.4 %collective-permute-start.38 = (bf16[544,768]{1,0:T(8,128)(2,1)S(1)}, bf16[544,768]{1,0:T(8,128)(2,1)S(1)}, u32[]{:S(2)}, u32[]{:S(2)}) collective-permute-start(bf16[544,768]{1,0:T(8,128)(2,1)S(1)} %pad_maximum_fusion.2), channel_id=1, source_target_pairs={{0,1},{1,2},{2,3},{3,0},{4,5},{5,6},{6,7},{7,4},{8,9},{9,10},{10,1... | collective-permute-start | bytes 2506760 | tf_op jit(solution)/shard_map/ppermute | solution.py:38
  158.7 18.9 %collective-permute-start.40 = (bf16[512,768]{1,0:T(8,128)(2,1)S(1)}, bf16[512,768]{1,0:T(8,128)(2,1)S(1)}, u32[]{:S(2)}, u32[]{:S(2)}) collective-permute-start(bf16[512,768]{1,0:T(8,128)(2,1)S(1)} %copy-done.26), channel_id=1, source_target_pairs={{0,4},{1,5},{2,6},{3,7},{4,0},{5,1},{6,2},{7,3},{8,12},{9,13},{10,... | collective-permute-start | bytes 2359304 | tf_op jit(solution)/shard_map/ppermute | solution.py:38
  158.8 27.8 %collective-permute-start.46 = (bf16[2,384,512]{2,1,0:T(8,128)(2,1)S(1)}, bf16[2,384,512]{2,1,0:T(8,128)(2,1)S(1)}, u32[]{:S(2)}, u32[]{:S(2)}) collective-permute-start(bf16[2,384,512]{2,1,0:T(8,128)(2,1)S(1)} %collective-permute-done.37.refs_15_), channel_id=1, source_target_pairs={{0,8},{1,9},{2,10},{3,11},{4,12},{5,13},{6,14},{7,15},{8,0},{9,1},... | collective-permute-start | bytes 2359304 | tf_op jit(solution)/shard_map/ppermute | solution.py:38
  179.8 21.6 %collective-permute-start.41 = (bf16[512,768]{1,0:T(8,128)(2,1)S(1)}, bf16[512,768]{1,0:T(8,128)(2,1)S(1)}, u32[]{:S(2)}, u32[]{:S(2)}) collective-permute-start(bf16[512,768]{1,0:T(8,128)(2,1)S(1)} %collective-permute-done.40.refs_1_), channel_id=1, source_target_pairs={{0,3},{1,0},{2,1},{3,2},{4,7},{5,4},{6,5},{7,6},{8,11},{9,8},{10,9... | collective-permute-start | bytes 2359304 | tf_op jit(solution)/shard_map/ppermute | solution.py:38
  180.6 20.8 %collective-permute-start.42 = (bf16[512,768]{1,0:T(8,128)(2,1)S(1)}, bf16[512,768]{1,0:T(8,128)(2,1)S(1)}, u32[]{:S(2)}, u32[]{:S(2)}) collective-permute-start(bf16[512,768]{1,0:T(8,128)(2,1)S(1)} %collective-permute-done.40.refs_1_), channel_id=1, source_target_pairs={{0,1},{1,2},{2,3},{3,0},{4,5},{5,6},{6,7},{7,4},{8,9},{9,10},{10,1... | collective-permute-start | bytes 2359304 | tf_op jit(solution)/shard_map/ppermute | solution.py:38
  182.6 4.1 %collective-permute-start.45 = (f32[8,512]{1,0:T(8,128)S(1)}, f32[8,512]{1,0:T(8,128)S(1)}, u32[]{:S(2)}, u32[]{:S(2)}) collective-permute-start(f32[8,512]{1,0:T(8,128)S(1)} %add_sums.1), channel_id=1, source_target_pairs={{0,4},{1,5},{2,6},{3,7},{4,0},{5,1},{6,2},{7,3},{8,12},{9,13},{10,... | collective-permute-start | bytes 49160 | tf_op jit(solution)/shard_map/ppermute | solution.py:38
  183.8 12.1 %collective-permute-start.44 = (bf16[256,768]{1,0:T(8,128)(2,1)S(1)}, bf16[256,768]{1,0:T(8,128)(2,1)S(1)}, u32[]{:S(2)}, u32[]{:S(2)}) collective-permute-start(bf16[256,768]{1,0:T(8,128)(2,1)S(1)} %slice.93), channel_id=1, source_target_pairs={{0,4},{1,5},{2,6},{3,7},{4,0},{5,1},{6,2},{7,3},{8,12},{9,13},{10,... | collective-permute-start | bytes 1179656 | tf_op jit(solution)/shard_map/ppermute | solution.py:38
  186.7 14.7 %collective-permute-start.43 = (bf16[256,768]{1,0:T(8,128)(2,1)S(1)}, bf16[256,768]{1,0:T(8,128)(2,1)S(1)}, u32[]{:S(2)}, u32[]{:S(2)}) collective-permute-start(bf16[256,768]{1,0:T(8,128)(2,1)S(1)} %slice.92), channel_id=1, source_target_pairs={{0,4},{1,5},{2,6},{3,7},{4,0},{5,1},{6,2},{7,3},{8,12},{9,13},{10,... | collective-permute-start | bytes 1179656 | tf_op jit(solution)/shard_map/ppermute | solution.py:38
  (35 other events, 219.4 us)

commit v6 on v5

--- a/solution.py
+++ b/solution.py
@@ -628,7 +628,6 @@
     )
     far_second = spread_y(far_first)
     turned_far = swap_zh(turned)
-    proj_far = swap_zh(join(proj_weight, turned)[0])
     far_first_other, second_other, far_beside_other = join(
         swap_core(far_first), swap_core(second), swap_core(far_beside)
     )
@@ -639,7 +638,8 @@
         total,
     )
 
-    far_second, turned_far, proj_far, total = join(far_second, turned_far, proj_far, total)
+    far_second, turned_far, proj_held, total = join(far_second, turned_far, proj_weight, total)
+    proj_far = swap_zh(proj_held)
     far_second_other = swap_core(far_second)
     out_mine = jnp.stack([turned, turned_far])
     out_other = swap_core(out_mine)

time: 225 us -> 223 us (level)
  waiting for transfers between devices: 82.5 us -> 74.7 us
  starting transfers between devices: 48.7 us -> 56.2 us
    ppermute x47, waiting for transfers between devices: 82.5 us -> 74.7 us  [move(): return lax.ppermute(values, AXES, pairs)]
    ppermute x47, starting transfers between devices: 48.7 us -> 56.2 us  [move(): return lax.ppermute(values, AXES, pairs)]
  transfers between devices with their start and end apart: 47 -> 47, of which waited for: 21 -> 22; matrix products, arithmetic and copies ran while one was open for 3% -> 3% of each run, Pallas kernels for 23% -> 23%
where the time goes in v6:
time: 223 us; the launch traced here: 222 us
  waiting for transfers between devices  74.7 us (33%)
  starting transfers between devices  56.2 us (25%)
  Pallas kernels  55.5 us (25%)
  blocking collectives  16.3 us (7%)
  local copies, waits for them, and re-layouts  14.3 us (6%)
  between operations  3.04 us (1%)
    ppermute x47, waiting for transfers between devices, move(): return lax.ppermute(values, AXES, pairs)  74.7 us
    ppermute x47, starting transfers between devices, move(): return lax.ppermute(values, AXES, pairs)  56.2 us
    pallas_call x4, Pallas kernels, accumulate(): pl.pallas_call(functools.partial(accumulate_kernel, counts, total is not...  21.4 us
    all_to_all x1, blocking collectives, local(): lax.all_to_all(outgoing, 'mp', split_axis=0, concat_axis=0, tiled=True)  16.3 us
    pallas_call x2, Pallas kernels, out_project(): pl.pallas_call(functools.partial(out_kernel, pieces, len(near), len(parts...  12.5 us
    pallas_call x2, Pallas kernels, project(): pl.pallas_call(functools.partial(project_kernel, pieces, len(near), len(p...  10.7 us
    unnamed x72, local copies, waits for them, and re-layouts  10.2 us
    pallas_call x1, Pallas kernels, norm_columns(): pl.pallas_call(norm_kernel, grid=(rows // block,), in_specs=[pl.BlockSpec...  8.55 us
  transfers between devices with their start and end apart: 47, of which 22 were waited for; matrix products, arithmetic and copies ran while one was open for 3% of the time, Pallas kernels for 23%

profile of v6, /device:TPU:0, one launch (start us, length us, event | category | flops | bytes accessed | tf_op | source)
XLA Modules:
  0.0 222.3 jit_solution(76128510629900216)
XLA Ops:
  0.7 4.0 %collective-permute-start.1 = (bf16[3,384,384]{2,1,0:T(8,128)(2,1)}, bf16[3,384,384]{2,1,0:T(8,128)(2,1)S(1)}, u32[]{:S(2)}, u32[]{:S(2)}) collective-permute-start(bf16[3,384,384]{2,1,0:T(8,128)(2,1)} %bitcast.73), channel_id=1, source_target_pairs={{0,64},{1,65},{2,66},{3,67},{4,68},{5,69},{6,70},{7,71},{8,72},{9,... | collective-permute-start | bytes 2654216 | tf_op jit(solution)/shard_map/ppermute | solution.py:38
  4.8 1.6 collective-permute-start.2
  6.3 1.6 collective-permute-start.3
  7.9 1.6 collective-permute-start.4
  11.0 8.6 %norm_columns.1.refs_0_.refs_1_.refs_2_.refs_3_.refs_4_.refs_5_ = bf16[16,512,384]{2,1,0:T(8,128)(2,1)S(1)} custom-call(bf16[512,6144]{1,0:T(8,128)(2,1)} %refs_5_.1, f32[1,6144]{1,0:T(1,128)S(1)} %bitcast.57), custom_call_target="tpu_custom_call" | custom-call | flops 1 | bytes 1 | tf_op jit(solution)/shard_map/norm_columns/pallas_call | solution.py:147
  19.6 4.3 %accumulate.4.refs_12_ = f32[3,512,384]{2,1,0:T(8,128)S(1)} custom-call(s32[2]{0:T(128)S(1)} %get-tuple-element.145.index_ref, bf16[16,512,384]{2,1,0:T(8,128)(2,1)S(1)} %norm_columns.1.refs_0_.refs_1_.refs_2_.refs_3_.refs_4_.refs_5_, bf16[16,512,384]{2,1,0:T(8,128)(2,1)S(1)} %norm_columns.1.refs_0_.refs_1_.refs_2_.refs_3_.refs_4_.refs_5_, ...), custom_call_target="tpu_custom_call" | custom-call | flops 1 | bytes 1 | tf_op jit(solution)/shard_map/accumulate/pallas_call | solution.py:236
  23.9 1.3 collective-permute-done.1
  25.2 3.6 %collective-permute-done.3 = bf16[3,384,384]{2,1,0:T(8,128)(2,1)} collective-permute-done((bf16[3,384,384]{2,1,0:T(8,128)(2,1)}, bf16[3,384,384]{2,1,0:T(8,128)(2,1)}, u32[]{:S(2)}, u32[]{:S(2)}) %collective-permute-start.3) | collective-permute-done | bytes 884768 | tf_op jit(solution)/shard_map/ppermute | solution.py:38
  30.1 6.2 %collective-permute-start.10 = (bf16[3,384,384]{2,1,0:T(8,128)(2,1)}, bf16[3,384,384]{2,1,0:T(8,128)(2,1)}, u32[]{:S(2)}, u32[]{:S(2)}) collective-permute-start(bf16[3,384,384]{2,1,0:T(8,128)(2,1)} %collective-permute-done.3), channel_id=1, source_target_pairs={{0,64},{1,65},{2,66},{3,67},{4,68},{5,69},{6,70},{7,71},{8,72},{9,... | collective-permute-start | bytes 2654216 | tf_op jit(solution)/shard_map/ppermute | solution.py:38
  36.3 1.5 collective-permute-start.8
  37.8 1.6 collective-permute-start.9
  39.4 1.6 collective-permute-start.11
  41.0 2.8 %copy-done.1 = bf16[16,512,384]{2,1,0:T(8,128)(2,1)S(1)} copy-done((bf16[16,512,384]{2,1,0:T(8,128)(2,1)S(1)}, bf16[16,512,384]{2,1,0:T(8,128)(2,1)}, u32[]{:S(2)}) %copy-start.1) | copy-done | bytes 6291480
  43.8 6.3 %accumulate.5.refs_12_ = f32[3,512,384]{2,1,0:T(8,128)S(1)} custom-call(s32[6]{0:T(128)S(1)} %get-tuple-element.141.index_ref, bf16[16,512,384]{2,1,0:T(8,128)(2,1)S(1)} %copy-done.1, bf16[16,512,384]{2,1,0:T(8,128)(2,1)S(1)} %copy-done.1, bf16[16,512,384]{2,1,0:T(8,128)(2,1)S(1)} %copy-done.1, ...), custom_call_target="tpu_custom_call", output_to_operand_aliasing={{}: (13, {})} | custom-call | flops 1 | bytes 1 | tf_op jit(solution)/shard_map/accumulate/pallas_call | solution.py:236
  54.9 1.9 collective-permute-done.10
  56.8 3.3 %collective-permute-done.9 = bf16[3,384,384]{2,1,0:T(8,128)(2,1)} collective-permute-done((bf16[3,384,384]{2,1,0:T(8,128)(2,1)}, bf16[3,384,384]{2,1,0:T(8,128)(2,1)}, u32[]{:S(2)}, u32[]{:S(2)}) %collective-permute-start.9) | collective-permute-done | bytes 884768 | tf_op jit(solution)/shard_map/ppermute | solution.py:38
  66.2 2.8 %copy-done.2 = bf16[16,512,384]{2,1,0:T(8,128)(2,1)S(1)} copy-done((bf16[16,512,384]{2,1,0:T(8,128)(2,1)S(1)}, bf16[16,512,384]{2,1,0:T(8,128)(2,1)}, u32[]{:S(2)}) %copy-start.2) | copy-done | bytes 6291480
  69.0 6.3 %accumulate.6.refs_4_ = f32[3,512,384]{2,1,0:T(8,128)S(1)} custom-call(s32[6]{0:T(128)S(1)} %get-tuple-element.140.index_ref, bf16[16,512,384]{2,1,0:T(8,128)(2,1)S(1)} %copy-done.2, bf16[16,512,384]{2,1,0:T(8,128)(2,1)S(1)} %copy-done.2, bf16[16,512,384]{2,1,0:T(8,128)(2,1)S(1)} %copy-done.2, ...), custom_call_target="tpu_custom_call", output_to_operand_aliasing={{}: (13, {})} | custom-call | flops 1 | bytes 1 | tf_op jit(solution)/shard_map/accumulate/pallas_call | solution.py:236
  76.0 1.5 collective-permute-done.21
  78.4 2.5 %collective-permute-start.23 = (bf16[384,512]{1,0:T(8,128)(2,1)S(1)}, bf16[384,512]{1,0:T(8,128)(2,1)S(1)}, u32[]{:S(2)}, u32[]{:S(2)}) collective-permute-start(bf16[384,512]{1,0:T(8,128)(2,1)S(1)} %copy-done.17), channel_id=1, source_target_pairs={{0,64},{1,65},{2,66},{3,67},{4,68},{5,69},{6,70},{7,71},{8,72},{9,... | collective-permute-start | bytes 1179656 | tf_op jit(solution)/shard_map/ppermute | solution.py:38
  80.9 4.6 %accumulate.7 = (bf16[512,384]{1,0:T(8,128)(2,1)S(1)}, bf16[256,384]{1,0:T(8,128)(2,1)S(1)}, bf16[256,384]{1,0:T(8,128)(2,1)S(1)}) custom-call(s32[2]{0:T(128)S(1)} %get-tuple-element.144.index_ref, bf16[16,512,384]{2,1,0:T(8,128)(2,1)S(1)} %copy-done.2, bf16[16,512,384]{2,1,0:T(8,128)(2,1)S(1)} %copy-done.2, bf16[1,3,384,384]{3,2,1,0:T(8,128)(2,1)S(1)} %bitcast.55, ...), custom_call_target="tpu_custom_call" | custom-call | flops 1 | bytes 1 | tf_op jit(solution)/shard_map/accumulate/pallas_call | solution.py:236
  85.6 2.3 %collective-permute-start.18 = (bf16[256,384]{1,0:T(8,128)(2,1)S(1)}, bf16[256,384]{1,0:T(8,128)(2,1)S(1)}, u32[]{:S(2)}, u32[]{:S(2)}) collective-permute-start(bf16[256,384]{1,0:T(8,128)(2,1)S(1)} %get-tuple-element.103), channel_id=1, source_target_pairs={{0,1},{1,2},{2,3},{3,0},{4,5},{5,6},{6,7},{7,4},{8,9},{9,10},{10,1... | collective-permute-start | bytes 589832 | tf_op jit(solution)/shard_map/ppermute | solution.py:38
  89.1 2.7 %collective-permute-done.23 = bf16[384,512]{1,0:T(8,128)(2,1)S(1)} collective-permute-done((bf16[384,512]{1,0:T(8,128)(2,1)S(1)}, bf16[384,512]{1,0:T(8,128)(2,1)S(1)}, u32[]{:S(2)}, u32[]{:S(2)}) %collective-permute-start.23) | collective-permute-done | bytes 393248 | tf_op jit(solution)/shard_map/ppermute | solution.py:38
  91.9 2.6 %collective-permute-done.18.refs_2_ = bf16[256,384]{1,0:T(8,128)(2,1)S(1)} collective-permute-done((bf16[256,384]{1,0:T(8,128)(2,1)S(1)}, bf16[256,384]{1,0:T(8,128)(2,1)S(1)}, u32[]{:S(2)}, u32[]{:S(2)}) %collective-permute-start.18) | collective-permute-done | bytes 196640 | tf_op jit(solution)/shard_map/ppermute | solution.py:38
  94.5 1.8 collective-permute-done.19.refs_3_
  96.3 2.1 collective-permute-done.20.refs_1_
  99.5 3.5 %collective-permute-start.27 = (bf16[512,384]{1,0:T(8,128)(2,1)S(1)}, bf16[512,384]{1,0:T(8,128)(2,1)S(1)}, u32[]{:S(2)}, u32[]{:S(2)}) collective-permute-start(bf16[512,384]{1,0:T(8,128)(2,1)S(1)} %pad_maximum_fusion.7), channel_id=1, source_target_pairs={{0,3},{1,0},{2,1},{3,2},{4,7},{5,4},{6,5},{7,6},{8,11},{9,8},{10,9... | collective-permute-start | bytes 1179656 | tf_op jit(solution)/shard_map/ppermute | solution.py:38
  103.1 8.7 %collective-permute-done.27.refs_5_ = bf16[512,384]{1,0:T(8,128)(2,1)S(1)} collective-permute-done((bf16[512,384]{1,0:T(8,128)(2,1)S(1)}, bf16[512,384]{1,0:T(8,128)(2,1)S(1)}, u32[]{:S(2)}, u32[]{:S(2)}) %collective-permute-start.27) | collective-permute-done | bytes 393248 | tf_op jit(solution)/shard_map/ppermute | solution.py:38
  111.8 3.3 %collective-permute-done.26.refs_4_ = bf16[512,384]{1,0:T(8,128)(2,1)S(1)} collective-permute-done((bf16[512,384]{1,0:T(8,128)(2,1)S(1)}, bf16[512,384]{1,0:T(8,128)(2,1)S(1)}, u32[]{:S(2)}, u32[]{:S(2)}) %collective-permute-start.26) | collective-permute-done | bytes 393248 | tf_op jit(solution)/shard_map/ppermute | solution.py:38
  117.5 1.8 collective-permute-start.24
  119.7 2.4 %collective-permute-start.31 = (bf16[512,384]{1,0:T(8,128)(2,1)S(1)}, bf16[512,384]{1,0:T(8,128)(2,1)S(1)}, u32[]{:S(2)}, u32[]{:S(2)}) collective-permute-start(bf16[512,384]{1,0:T(8,128)(2,1)S(1)} %pad_maximum_fusion.8), channel_id=1, source_target_pairs={{0,4},{1,5},{2,6},{3,7},{4,0},{5,1},{6,2},{7,3},{8,12},{9,13},{10,... | collective-permute-start | bytes 1179656 | tf_op jit(solution)/shard_map/ppermute | solution.py:38
  122.9 7.0 %out_project.2 = (f32[2,512,384]{2,1,0:T(8,128)S(1)}, bf16[6,384,384]{2,1,0:T(8,128)(2,1)S(1)}) custom-call(s32[16]{0:T(128)S(1)} %get-tuple-element.138.index_ref, bf16[512,384]{1,0:T(8,128)(2,1)} %copy-done.5, bf16[512,384]{1,0:T(8,128)(2,1)} %copy-done.33, bf16[256,384]{1,0:T(8,128)(2,1)} %copy-done.29, bf16[256,384]{1,0:T(8,128)(2,1)} %copy-done.30, ...), custom_call_target="tpu_custom_call" | custom-call | flops 1 | bytes 1 | tf_op jit(solution)/shard_map/out_project/pallas_call | solution.py:382
  129.9 1.9 collective-permute-done.25.refs_1_
  131.8 5.5 %out_project.3 = (bf16[512,768]{1,0:T(8,128)(2,1)}, bf16[272,768]{1,0:T(8,128)(2,1)S(1)}, bf16[272,768]{1,0:T(8,128)(2,1)S(1)}, f32[8,512]{1,0:T(8,128)S(1)}) custom-call(s32[1]{0:T(128)} %bitcast.12.index_ref, bf16[512,384]{1,0:T(8,128)(2,1)S(1)} %collective-permute-done.24.refs_0_, bf16[512,384]{1,0:T(8,128)(2,1)S(1)} %collective-permute-done.25.refs_1_, ...), custom_call_target="tpu_custom_call" | custom-call | flops 1 | bytes 1 | tf_op jit(solution)/shard_map/out_project/pallas_call | solution.py:382
  138.3 3.2 %collective-permute-start.35 = (bf16[272,768]{1,0:T(8,128)(2,1)S(1)}, bf16[272,768]{1,0:T(8,128)(2,1)S(1)}, u32[]{:S(2)}, u32[]{:S(2)}) collective-permute-start(bf16[272,768]{1,0:T(8,128)(2,1)S(1)} %get-tuple-element.123), channel_id=1, source_target_pairs={{0,3},{1,0},{2,1},{3,2},{4,7},{5,4},{6,5},{7,6},{8,11},{9,8},{10,9... | collective-permute-start | bytes 1253384 | tf_op jit(solution)/shard_map/ppermute | solution.py:38
  141.5 10.1 %collective-permute-done.34.refs_0_.refs_2_ = bf16[272,768]{1,0:T(8,128)(2,1)S(1)} collective-permute-done((bf16[272,768]{1,0:T(8,128)(2,1)S(1)}, bf16[272,768]{1,0:T(8,128)(2,1)S(1)}, u32[]{:S(2)}, u32[]{:S(2)}) %collective-permute-start.34) | collective-permute-done | bytes 417824 | tf_op jit(solution)/shard_map/ppermute | solution.py:38
  151.8 3.5 %collective-permute-start.39 = (bf16[544,768]{1,0:T(8,128)(2,1)S(1)}, bf16[544,768]{1,0:T(8,128)(2,1)S(1)}, u32[]{:S(2)}, u32[]{:S(2)}) collective-permute-start(bf16[544,768]{1,0:T(8,128)(2,1)S(1)} %pad_maximum_fusion.3), channel_id=1, source_target_pairs={{0,3},{1,0},{2,1},{3,2},{4,7},{5,4},{6,5},{7,6},{8,11},{9,8},{10,9... | collective-permute-start | bytes 2506760 | tf_op jit(solution)/shard_map/ppermute | solution.py:38
  155.7 2.3 %collective-permute-start.40 = (bf16[512,768]{1,0:T(8,128)(2,1)S(1)}, bf16[512,768]{1,0:T(8,128)(2,1)S(1)}, u32[]{:S(2)}, u32[]{:S(2)}) collective-permute-start(bf16[512,768]{1,0:T(8,128)(2,1)S(1)} %copy-done.25), channel_id=1, source_target_pairs={{0,4},{1,5},{2,6},{3,7},{4,0},{5,1},{6,2},{7,3},{8,12},{9,13},{10,... | collective-permute-start | bytes 2359304 | tf_op jit(solution)/shard_map/ppermute | solution.py:38
  158.1 17.5 %collective-permute-done.40.refs_1_ = bf16[512,768]{1,0:T(8,128)(2,1)S(1)} collective-permute-done((bf16[512,768]{1,0:T(8,128)(2,1)S(1)}, bf16[512,768]{1,0:T(8,128)(2,1)S(1)}, u32[]{:S(2)}, u32[]{:S(2)}) %collective-permute-start.40) | collective-permute-done | bytes 786464 | tf_op jit(solution)/shard_map/ppermute | solution.py:38
  175.6 1.6 collective-permute-done.38.refs_2_.refs_4_
  177.2 1.3 collective-permute-start.41
  180.0 2.3 %collective-permute-start.45 = (f32[8,512]{1,0:T(8,128)S(1)}, f32[8,512]{1,0:T(8,128)S(1)}, u32[]{:S(2)}, u32[]{:S(2)}) collective-permute-start(f32[8,512]{1,0:T(8,128)S(1)} %add_sums.1), channel_id=1, source_target_pairs={{0,4},{1,5},{2,6},{3,7},{4,0},{5,1},{6,2},{7,3},{8,12},{9,13},{10,... | collective-permute-start | bytes 49160 | tf_op jit(solution)/shard_map/ppermute | solution.py:38
  184.1 2.2 %collective-permute-start.43 = (bf16[256,768]{1,0:T(8,128)(2,1)S(1)}, bf16[256,768]{1,0:T(8,128)(2,1)S(1)}, u32[]{:S(2)}, u32[]{:S(2)}) collective-permute-start(bf16[256,768]{1,0:T(8,128)(2,1)S(1)} %slice.92), channel_id=1, source_target_pairs={{0,4},{1,5},{2,6},{3,7},{4,0},{5,1},{6,2},{7,3},{8,12},{9,13},{10,... | collective-permute-start | bytes 1179656 | tf_op jit(solution)/shard_map/ppermute | solution.py:38
  187.3 7.4 %project.2 = (f32[512,512]{1,0:T(8,128)S(1)}, bf16[6,384,512]{2,1,0:T(8,128)(2,1)S(1)}) custom-call(s32[21]{0:T(128)S(1)} %pad_add_fusion.index_ref, bf16[512,768]{1,0:T(8,128)(2,1)} %get-tuple-element.126.refs_0_, bf16[512,768]{1,0:T(8,128)(2,1)} %copy-done.27, bf16[272,768]{1,0:T(8,128)(2,1)} %copy-done.11, bf16[272,768]{1,0:T(8,128)(2,1)} %copy-done.12, ...), custom_call_target="tpu_custom_call" | custom-call | flops 1 | bytes 1 | tf_op jit(solution)/shard_map/project/pallas_call | solution.py:499
  195.6 5.5 %collective-permute-done.43.refs_2_ = bf16[256,768]{1,0:T(8,128)(2,1)S(1)} collective-permute-done((bf16[256,768]{1,0:T(8,128)(2,1)S(1)}, bf16[256,768]{1,0:T(8,128)(2,1)S(1)}, u32[]{:S(2)}, u32[]{:S(2)}) %collective-permute-start.43) | collective-permute-done | bytes 393248 | tf_op jit(solution)/shard_map/ppermute | solution.py:38
  201.1 3.3 %project.3 = bf16[8,128,512]{2,1,0:T(8,128)(2,1)S(1)} custom-call(s32[11]{0:T(128)S(1)} %pad_add_fusion.1.index_ref, bf16[512,768]{1,0:T(8,128)(2,1)S(1)} %collective-permute-done.41.refs_0_, bf16[512,768]{1,0:T(8,128)(2,1)S(1)} %collective-permute-done.42.refs_1_, bf16[256,768]{1,0:T(8,128)(2,1)S(1)} %collective-permute-done.43.refs_2_, ...), custom_call_target="tpu_custom_call" | custom-call | flops 1 | bytes 1 | tf_op jit(solution)/shard_map/project/pallas_call | solution.py:499
  204.4 16.3 %all_to_all.5.arrived_ref = bf16[8,128,512]{2,1,0:T(8,128)(2,1)S(1)} all-to-all(bf16[8,128,512]{2,1,0:T(8,128)(2,1)S(1)} %project.3), channel_id=1, replica_groups=mesh['dp'=16,'mp'=8] {'mp'}, dimensions={0} | all-to-all | bytes 2097152 | tf_op jit(solution)/shard_map/all_to_all | solution.py:722
  220.7 1.6 pack.1
  (159 shorter events, 25.9 us)
Async XLA Ops:
  0.6 5.7 %collective-permute-start = (bf16[3,384,384]{2,1,0:T(8,128)(2,1)}, bf16[3,384,384]{2,1,0:T(8,128)(2,1)}, u32[]{:S(2)}, u32[]{:S(2)}) collective-permute-start(bf16[3,384,384]{2,1,0:T(8,128)(2,1)} %bitcast.72), channel_id=1, source_target_pairs={{0,8},{1,9},{2,10},{3,11},{4,12},{5,13},{6,14},{7,15},{8,0},{9,1},... | collective-permute-start | bytes 2654216 | tf_op jit(solution)/shard_map/ppermute | solution.py:38
  0.7 24.5 %collective-permute-start.1 = (bf16[3,384,384]{2,1,0:T(8,128)(2,1)}, bf16[3,384,384]{2,1,0:T(8,128)(2,1)S(1)}, u32[]{:S(2)}, u32[]{:S(2)}) collective-permute-start(bf16[3,384,384]{2,1,0:T(8,128)(2,1)} %bitcast.73), channel_id=1, source_target_pairs={{0,64},{1,65},{2,66},{3,67},{4,68},{5,69},{6,70},{7,71},{8,72},{9,... | collective-permute-start | bytes 2654216 | tf_op jit(solution)/shard_map/ppermute | solution.py:38
  4.8 20.4 %collective-permute-start.2 = (bf16[3,384,384]{2,1,0:T(8,128)(2,1)}, bf16[3,384,384]{2,1,0:T(8,128)(2,1)}, u32[]{:S(2)}, u32[]{:S(2)}) collective-permute-start(bf16[3,384,384]{2,1,0:T(8,128)(2,1)} %bitcast.74), channel_id=1, source_target_pairs={{0,16},{1,17},{2,18},{3,19},{4,20},{5,21},{6,22},{7,23},{8,56},{9,... | collective-permute-start | bytes 2654216 | tf_op jit(solution)/shard_map/ppermute | solution.py:38
  6.3 22.5 %collective-permute-start.3 = (bf16[3,384,384]{2,1,0:T(8,128)(2,1)}, bf16[3,384,384]{2,1,0:T(8,128)(2,1)}, u32[]{:S(2)}, u32[]{:S(2)}) collective-permute-start(bf16[3,384,384]{2,1,0:T(8,128)(2,1)} %collective-permute-done), channel_id=1, source_target_pairs={{0,16},{1,17},{2,18},{3,19},{4,20},{5,21},{6,22},{7,23},{8,56},{9,... | collective-permute-start | bytes 2654216 | tf_op jit(solution)/shard_map/ppermute | solution.py:38
  7.9 16.0 %collective-permute-start.4 = (bf16[384,384]{1,0:T(8,128)(2,1)}, bf16[384,384]{1,0:T(8,128)(2,1)S(1)}, u32[]{:S(2)}, u32[]{:S(2)}) collective-permute-start(bf16[384,384]{1,0:T(8,128)(2,1)} %param.17), channel_id=1, source_target_pairs={{0,0},{1,17},{2,34},{3,51},{4,64},{5,81},{6,98},{7,115},{8,8},{9,2... | collective-permute-start | bytes 884744 | tf_op jit(solution)/shard_map/ppermute | solution.py:38
  28.8 9.0 %collective-permute-start.5 = (bf16[3,384,384]{2,1,0:T(8,128)(2,1)S(1)}, bf16[3,384,384]{2,1,0:T(8,128)(2,1)}, u32[]{:S(2)}, u32[]{:S(2)}) collective-permute-start(bf16[3,384,384]{2,1,0:T(8,128)(2,1)S(1)} %collective-permute-done.1), channel_id=1, source_target_pairs={{0,8},{1,9},{2,10},{3,11},{4,12},{5,13},{6,14},{7,15},{8,0},{9,1},... | collective-permute-start | bytes 2654216 | tf_op jit(solution)/shard_map/ppermute | solution.py:38
  28.8 10.6 %collective-permute-start.6 = (bf16[3,384,384]{2,1,0:T(8,128)(2,1)}, bf16[3,384,384]{2,1,0:T(8,128)(2,1)}, u32[]{:S(2)}, u32[]{:S(2)}) collective-permute-start(bf16[3,384,384]{2,1,0:T(8,128)(2,1)} %collective-permute-done.2), channel_id=1, source_target_pairs={{0,8},{1,9},{2,10},{3,11},{4,12},{5,13},{6,14},{7,15},{8,0},{9,1},... | collective-permute-start | bytes 2654216 | tf_op jit(solution)/shard_map/ppermute | solution.py:38
  29.3 11.7 %collective-permute-start.7 = (bf16[3,384,384]{2,1,0:T(8,128)(2,1)}, bf16[3,384,384]{2,1,0:T(8,128)(2,1)}, u32[]{:S(2)}, u32[]{:S(2)}) collective-permute-start(bf16[3,384,384]{2,1,0:T(8,128)(2,1)} %collective-permute-done.3), channel_id=1, source_target_pairs={{0,8},{1,9},{2,10},{3,11},{4,12},{5,13},{6,14},{7,15},{8,0},{9,1},... | collective-permute-start | bytes 2654216 | tf_op jit(solution)/shard_map/ppermute | solution.py:38
  30.1 26.7 %collective-permute-start.10 = (bf16[3,384,384]{2,1,0:T(8,128)(2,1)}, bf16[3,384,384]{2,1,0:T(8,128)(2,1)}, u32[]{:S(2)}, u32[]{:S(2)}) collective-permute-start(bf16[3,384,384]{2,1,0:T(8,128)(2,1)} %collective-permute-done.3), channel_id=1, source_target_pairs={{0,64},{1,65},{2,66},{3,67},{4,68},{5,69},{6,70},{7,71},{8,72},{9,... | collective-permute-start | bytes 2654216 | tf_op jit(solution)/shard_map/ppermute | solution.py:38
  36.3 20.5 %collective-permute-start.8 = (bf16[3,384,384]{2,1,0:T(8,128)(2,1)S(1)}, bf16[3,384,384]{2,1,0:T(8,128)(2,1)}, u32[]{:S(2)}, u32[]{:S(2)}) collective-permute-start(bf16[3,384,384]{2,1,0:T(8,128)(2,1)S(1)} %collective-permute-done.1), channel_id=1, source_target_pairs={{0,16},{1,17},{2,18},{3,19},{4,20},{5,21},{6,22},{7,23},{8,56},{9,... | collective-permute-start | bytes 2654216 | tf_op jit(solution)/shard_map/ppermute | solution.py:38
  37.8 22.3 %collective-permute-start.9 = (bf16[3,384,384]{2,1,0:T(8,128)(2,1)}, bf16[3,384,384]{2,1,0:T(8,128)(2,1)}, u32[]{:S(2)}, u32[]{:S(2)}) collective-permute-start(bf16[3,384,384]{2,1,0:T(8,128)(2,1)} %collective-permute-done.2), channel_id=1, source_target_pairs={{0,16},{1,17},{2,18},{3,19},{4,20},{5,21},{6,22},{7,23},{8,56},{9,... | collective-permute-start | bytes 2654216 | tf_op jit(solution)/shard_map/ppermute | solution.py:38
  39.4 15.4 %collective-permute-start.11 = (bf16[384,384]{1,0:T(8,128)(2,1)}, bf16[384,384]{1,0:T(8,128)(2,1)S(1)}, u32[]{:S(2)}, u32[]{:S(2)}) collective-permute-start(bf16[384,384]{1,0:T(8,128)(2,1)} %copy-done.35), channel_id=1, source_target_pairs={{0,0},{1,3},{2,2},{3,1},{4,4},{5,7},{6,6},{7,5},{8,8},{9,11},{10,1... | collective-permute-start | bytes 884744 | tf_op jit(solution)/shard_map/ppermute | solution.py:38
  60.1 2.6 %collective-permute-start.14 = (bf16[3,384,384]{2,1,0:T(8,128)(2,1)}, bf16[3,384,384]{2,1,0:T(8,128)(2,1)S(1)}, u32[]{:S(2)}, u32[]{:S(2)}) collective-permute-start(bf16[3,384,384]{2,1,0:T(8,128)(2,1)} %collective-permute-done.8), channel_id=1, source_target_pairs={{0,8},{1,9},{2,10},{3,11},{4,12},{5,13},{6,14},{7,15},{8,0},{9,1},... | collective-permute-start | bytes 2654216 | tf_op jit(solution)/shard_map/ppermute | solution.py:38
  60.1 3.9 %collective-permute-start.15 = (bf16[3,384,384]{2,1,0:T(8,128)(2,1)}, bf16[3,384,384]{2,1,0:T(8,128)(2,1)S(1)}, u32[]{:S(2)}, u32[]{:S(2)}) collective-permute-start(bf16[3,384,384]{2,1,0:T(8,128)(2,1)} %collective-permute-done.9), channel_id=1, source_target_pairs={{0,8},{1,9},{2,10},{3,11},{4,12},{5,13},{6,14},{7,15},{8,0},{9,1},... | collective-permute-start | bytes 2654216 | tf_op jit(solution)/shard_map/ppermute | solution.py:38
  60.6 4.7 %collective-permute-start.16 = (bf16[3,384,384]{2,1,0:T(8,128)(2,1)}, bf16[3,384,384]{2,1,0:T(8,128)(2,1)S(1)}, u32[]{:S(2)}, u32[]{:S(2)}) collective-permute-start(bf16[3,384,384]{2,1,0:T(8,128)(2,1)} %collective-permute-done.10), channel_id=1, source_target_pairs={{0,8},{1,9},{2,10},{3,11},{4,12},{5,13},{6,14},{7,15},{8,0},{9,1},... | collective-permute-start | bytes 2654216 | tf_op jit(solution)/shard_map/ppermute | solution.py:38
  60.6 14.6 %collective-permute-start.12 = (bf16[3,384,384]{2,1,0:T(8,128)(2,1)}, bf16[3,384,384]{2,1,0:T(8,128)(2,1)S(1)}, u32[]{:S(2)}, u32[]{:S(2)}) collective-permute-start(bf16[3,384,384]{2,1,0:T(8,128)(2,1)} %collective-permute-done.8), channel_id=1, source_target_pairs={{0,16},{1,17},{2,18},{3,19},{4,20},{5,21},{6,22},{7,23},{8,56},{9,... | collective-permute-start | bytes 2654216 | tf_op jit(solution)/shard_map/ppermute | solution.py:38
  61.0 14.3 %collective-permute-start.13 = (bf16[384,384]{1,0:T(8,128)(2,1)S(1)}, bf16[384,384]{1,0:T(8,128)(2,1)S(1)}, u32[]{:S(2)}, u32[]{:S(2)}) collective-permute-start(bf16[384,384]{1,0:T(8,128)(2,1)S(1)} %collective-permute-done.11), channel_id=1, source_target_pairs={{0,64},{1,65},{2,66},{3,67},{4,68},{5,69},{6,70},{7,71},{8,72},{9,... | collective-permute-start | bytes 884744 | tf_op jit(solution)/shard_map/ppermute | solution.py:38
  75.4 2.1 collective-permute-start.21
  75.6 5.3 %collective-permute-start.17 = (bf16[3,384,384]{2,1,0:T(8,128)(2,1)S(1)}, bf16[3,384,384]{2,1,0:T(8,128)(2,1)S(1)}, u32[]{:S(2)}, u32[]{:S(2)}) collective-permute-start(bf16[3,384,384]{2,1,0:T(8,128)(2,1)S(1)} %collective-permute-done.12), channel_id=1, source_target_pairs={{0,8},{1,9},{2,10},{3,11},{4,12},{5,13},{6,14},{7,15},{8,0},{9,1},... | collective-permute-start | bytes 2654216 | tf_op jit(solution)/shard_map/ppermute | solution.py:38
  77.6 20.7 %collective-permute-start.22 = (bf16[4,384,384]{2,1,0:T(8,128)(2,1)S(1)}, bf16[4,384,384]{2,1,0:T(8,128)(2,1)S(1)}, u32[]{:S(2)}, u32[]{:S(2)}) collective-permute-start(bf16[4,384,384]{2,1,0:T(8,128)(2,1)S(1)} %pad_maximum_fusion.1.refs_6_), channel_id=1, source_target_pairs={{0,16},{1,17},{2,18},{3,19},{4,20},{5,21},{6,22},{7,23},{8,56},{9,... | collective-permute-start | bytes 3538952 | tf_op jit(solution)/shard_map/ppermute | solution.py:38
  78.4 13.5 %collective-permute-start.23 = (bf16[384,512]{1,0:T(8,128)(2,1)S(1)}, bf16[384,512]{1,0:T(8,128)(2,1)S(1)}, u32[]{:S(2)}, u32[]{:S(2)}) collective-permute-start(bf16[384,512]{1,0:T(8,128)(2,1)S(1)} %copy-done.17), channel_id=1, source_target_pairs={{0,64},{1,65},{2,66},{3,67},{4,68},{5,69},{6,70},{7,71},{8,72},{9,... | collective-permute-start | bytes 1179656 | tf_op jit(solution)/shard_map/ppermute | solution.py:38
  85.5 12.8 %collective-permute-start.20 = (bf16[512,384]{1,0:T(8,128)(2,1)S(1)}, bf16[512,384]{1,0:T(8,128)(2,1)S(1)}, u32[]{:S(2)}, u32[]{:S(2)}) collective-permute-start(bf16[512,384]{1,0:T(8,128)(2,1)S(1)} %get-tuple-element.96.refs_0_), channel_id=1, source_target_pairs={{0,4},{1,5},{2,6},{3,7},{4,0},{5,1},{6,2},{7,3},{8,12},{9,13},{10,... | collective-permute-start | bytes 1179656 | tf_op jit(solution)/shard_map/ppermute | solution.py:38
  85.6 8.9 %collective-permute-start.18 = (bf16[256,384]{1,0:T(8,128)(2,1)S(1)}, bf16[256,384]{1,0:T(8,128)(2,1)S(1)}, u32[]{:S(2)}, u32[]{:S(2)}) collective-permute-start(bf16[256,384]{1,0:T(8,128)(2,1)S(1)} %get-tuple-element.103), channel_id=1, source_target_pairs={{0,1},{1,2},{2,3},{3,0},{4,5},{5,6},{6,7},{7,4},{8,9},{9,10},{10,1... | collective-permute-start | bytes 589832 | tf_op jit(solution)/shard_map/ppermute | solution.py:38
  88.0 8.3 %collective-permute-start.19 = (bf16[256,384]{1,0:T(8,128)(2,1)S(1)}, bf16[256,384]{1,0:T(8,128)(2,1)S(1)}, u32[]{:S(2)}, u32[]{:S(2)}) collective-permute-start(bf16[256,384]{1,0:T(8,128)(2,1)S(1)} %get-tuple-element.101), channel_id=1, source_target_pairs={{0,3},{1,0},{2,1},{3,2},{4,7},{5,4},{6,5},{7,6},{8,11},{9,8},{10,9... | collective-permute-start | bytes 589832 | tf_op jit(solution)/shard_map/ppermute | solution.py:38
  98.4 16.7 %collective-permute-start.29 = (bf16[4,384,384]{2,1,0:T(8,128)(2,1)S(1)}, bf16[4,384,384]{2,1,0:T(8,128)(2,1)S(1)}, u32[]{:S(2)}, u32[]{:S(2)}) collective-permute-start(bf16[4,384,384]{2,1,0:T(8,128)(2,1)S(1)} %collective-permute-done.22.refs_7_), channel_id=1, source_target_pairs={{0,8},{1,9},{2,10},{3,11},{4,12},{5,13},{6,14},{7,15},{8,0},{9,1},... | collective-permute-start | bytes 3538952 | tf_op jit(solution)/shard_map/ppermute | solution.py:38
  98.6 16.4 %collective-permute-start.30 = (bf16[2,384,512]{2,1,0:T(8,128)(2,1)S(1)}, bf16[2,384,512]{2,1,0:T(8,128)(2,1)S(1)}, u32[]{:S(2)}, u32[]{:S(2)}) collective-permute-start(bf16[2,384,512]{2,1,0:T(8,128)(2,1)S(1)} %pad_maximum_fusion.4), channel_id=1, source_target_pairs={{0,8},{1,9},{2,10},{3,11},{4,12},{5,13},{6,14},{7,15},{8,0},{9,1},... | collective-permute-start | bytes 2359304 | tf_op jit(solution)/shard_map/ppermute | solution.py:38
  99.2 15.9 %collective-permute-start.28 = (bf16[2,384,384]{2,1,0:T(8,128)(2,1)S(1)}, bf16[2,384,384]{2,1,0:T(8,128)(2,1)S(1)}, u32[]{:S(2)}, u32[]{:S(2)}) collective-permute-start(bf16[2,384,384]{2,1,0:T(8,128)(2,1)S(1)} %slice.87), channel_id=1, source_target_pairs={{0,16},{1,17},{2,18},{3,19},{4,20},{5,21},{6,22},{7,23},{8,56},{9,... | collective-permute-start | bytes 1769480 | tf_op jit(solution)/shard_map/ppermute | solution.py:38
  99.5 12.3 %collective-permute-start.27 = (bf16[512,384]{1,0:T(8,128)(2,1)S(1)}, bf16[512,384]{1,0:T(8,128)(2,1)S(1)}, u32[]{:S(2)}, u32[]{:S(2)}) collective-permute-start(bf16[512,384]{1,0:T(8,128)(2,1)S(1)} %pad_maximum_fusion.7), channel_id=1, source_target_pairs={{0,3},{1,0},{2,1},{3,2},{4,7},{5,4},{6,5},{7,6},{8,11},{9,8},{10,9... | collective-permute-start | bytes 1179656 | tf_op jit(solution)/shard_map/ppermute | solution.py:38
  103.0 12.0 %collective-permute-start.26 = (bf16[512,384]{1,0:T(8,128)(2,1)S(1)}, bf16[512,384]{1,0:T(8,128)(2,1)S(1)}, u32[]{:S(2)}, u32[]{:S(2)}) collective-permute-start(bf16[512,384]{1,0:T(8,128)(2,1)S(1)} %pad_maximum_fusion.6), channel_id=1, source_target_pairs={{0,1},{1,2},{2,3},{3,0},{4,5},{5,6},{6,7},{7,4},{8,9},{9,10},{10,1... | collective-permute-start | bytes 1179656 | tf_op jit(solution)/shard_map/ppermute | solution.py:38
  116.4 21.6 %collective-permute-start.33 = (bf16[4,384,512]{2,1,0:T(8,128)(2,1)S(1)}, bf16[4,384,512]{2,1,0:T(8,128)(2,1)S(1)}, u32[]{:S(2)}, u32[]{:S(2)}) collective-permute-start(bf16[4,384,512]{2,1,0:T(8,128)(2,1)S(1)} %pad_maximum_fusion.refs_12_), channel_id=1, source_target_pairs={{0,16},{1,17},{2,18},{3,19},{4,20},{5,21},{6,22},{7,23},{8,56},{9,... | collective-permute-start | bytes 4718600 | tf_op jit(solution)/shard_map/ppermute | solution.py:38
  117.5 4.5 %collective-permute-start.32 = (bf16[2,384,384]{2,1,0:T(8,128)(2,1)S(1)}, bf16[2,384,384]{2,1,0:T(8,128)(2,1)S(1)}, u32[]{:S(2)}, u32[]{:S(2)}) collective-permute-start(bf16[2,384,384]{2,1,0:T(8,128)(2,1)S(1)} %collective-permute-done.28.refs_9_), channel_id=1, source_target_pairs={{0,8},{1,9},{2,10},{3,11},{4,12},{5,13},{6,14},{7,15},{8,0},{9,1},... | collective-permute-start | bytes 1769480 | tf_op jit(solution)/shard_map/ppermute | solution.py:38
  117.5 12.4 %collective-permute-start.24 = (bf16[512,384]{1,0:T(8,128)(2,1)S(1)}, bf16[512,384]{1,0:T(8,128)(2,1)S(1)}, u32[]{:S(2)}, u32[]{:S(2)}) collective-permute-start(bf16[512,384]{1,0:T(8,128)(2,1)S(1)} %collective-permute-done.20.refs_1_), channel_id=1, source_target_pairs={{0,3},{1,0},{2,1},{3,2},{4,7},{5,4},{6,5},{7,6},{8,11},{9,8},{10,9... | collective-permute-start | bytes 1179656 | tf_op jit(solution)/shard_map/ppermute | solution.py:38
  119.3 12.5 %collective-permute-start.25 = (bf16[512,384]{1,0:T(8,128)(2,1)S(1)}, bf16[512,384]{1,0:T(8,128)(2,1)S(1)}, u32[]{:S(2)}, u32[]{:S(2)}) collective-permute-start(bf16[512,384]{1,0:T(8,128)(2,1)S(1)} %collective-permute-done.20.refs_1_), channel_id=1, source_target_pairs={{0,1},{1,2},{2,3},{3,0},{4,5},{5,6},{6,7},{7,4},{8,9},{9,10},{10,1... | collective-permute-start | bytes 1179656 | tf_op jit(solution)/shard_map/ppermute | solution.py:38
  119.7 12.1 %collective-permute-start.31 = (bf16[512,384]{1,0:T(8,128)(2,1)S(1)}, bf16[512,384]{1,0:T(8,128)(2,1)S(1)}, u32[]{:S(2)}, u32[]{:S(2)}) collective-permute-start(bf16[512,384]{1,0:T(8,128)(2,1)S(1)} %pad_maximum_fusion.8), channel_id=1, source_target_pairs={{0,4},{1,5},{2,6},{3,7},{4,0},{5,1},{6,2},{7,3},{8,12},{9,13},{10,... | collective-permute-start | bytes 1179656 | tf_op jit(solution)/shard_map/ppermute | solution.py:38
  138.0 13.7 %collective-permute-start.36 = (bf16[4,384,512]{2,1,0:T(8,128)(2,1)S(1)}, bf16[4,384,512]{2,1,0:T(8,128)(2,1)S(1)}, u32[]{:S(2)}, u32[]{:S(2)}) collective-permute-start(bf16[4,384,512]{2,1,0:T(8,128)(2,1)S(1)} %collective-permute-done.33.refs_13_), channel_id=1, source_target_pairs={{0,8},{1,9},{2,10},{3,11},{4,12},{5,13},{6,14},{7,15},{8,0},{9,1},... | collective-permute-start | bytes 4718600 | tf_op jit(solution)/shard_map/ppermute | solution.py:38
  138.1 13.6 %collective-permute-start.37 = (bf16[2,384,512]{2,1,0:T(8,128)(2,1)S(1)}, bf16[2,384,512]{2,1,0:T(8,128)(2,1)S(1)}, u32[]{:S(2)}, u32[]{:S(2)}) collective-permute-start(bf16[2,384,512]{2,1,0:T(8,128)(2,1)S(1)} %slice.91), channel_id=1, source_target_pairs={{0,16},{1,17},{2,18},{3,19},{4,20},{5,21},{6,22},{7,23},{8,56},{9,... | collective-permute-start | bytes 2359304 | tf_op jit(solution)/shard_map/ppermute | solution.py:38
  138.3 13.4 %collective-permute-start.34 = (bf16[272,768]{1,0:T(8,128)(2,1)S(1)}, bf16[272,768]{1,0:T(8,128)(2,1)S(1)}, u32[]{:S(2)}, u32[]{:S(2)}) collective-permute-start(bf16[272,768]{1,0:T(8,128)(2,1)S(1)} %get-tuple-element.125), channel_id=1, source_target_pairs={{0,1},{1,2},{2,3},{3,0},{4,5},{5,6},{6,7},{7,4},{8,9},{9,10},{10,1... | collective-permute-start | bytes 1253384 | tf_op jit(solution)/shard_map/ppermute | solution.py:38
  138.3 13.4 %collective-permute-start.35 = (bf16[272,768]{1,0:T(8,128)(2,1)S(1)}, bf16[272,768]{1,0:T(8,128)(2,1)S(1)}, u32[]{:S(2)}, u32[]{:S(2)}) collective-permute-start(bf16[272,768]{1,0:T(8,128)(2,1)S(1)} %get-tuple-element.123), channel_id=1, source_target_pairs={{0,3},{1,0},{2,1},{3,2},{4,7},{5,4},{6,5},{7,6},{8,11},{9,8},{10,9... | collective-permute-start | bytes 1253384 | tf_op jit(solution)/shard_map/ppermute | solution.py:38
  151.8 23.8 %collective-permute-start.39 = (bf16[544,768]{1,0:T(8,128)(2,1)S(1)}, bf16[544,768]{1,0:T(8,128)(2,1)S(1)}, u32[]{:S(2)}, u32[]{:S(2)}) collective-permute-start(bf16[544,768]{1,0:T(8,128)(2,1)S(1)} %pad_maximum_fusion.3), channel_id=1, source_target_pairs={{0,3},{1,0},{2,1},{3,2},{4,7},{5,4},{6,5},{7,6},{8,11},{9,8},{10,9... | collective-permute-start | bytes 2506760 | tf_op jit(solution)/shard_map/ppermute | solution.py:38
  155.4 31.9 %copy-start.3 = (f32[6144]{0:T(1024)S(1)}, f32[6144]{0:T(1024)}, u32[]{:S(2)}) copy-start(f32[6144]{0:T(1024)} %param.18) | copy-start | bytes 73732
  155.4 21.8 %collective-permute-start.38 = (bf16[544,768]{1,0:T(8,128)(2,1)S(1)}, bf16[544,768]{1,0:T(8,128)(2,1)S(1)}, u32[]{:S(2)}, u32[]{:S(2)}) collective-permute-start(bf16[544,768]{1,0:T(8,128)(2,1)S(1)} %pad_maximum_fusion.2), channel_id=1, source_target_pairs={{0,1},{1,2},{2,3},{3,0},{4,5},{5,6},{6,7},{7,4},{8,9},{9,10},{10,1... | collective-permute-start | bytes 2506760 | tf_op jit(solution)/shard_map/ppermute | solution.py:38
  155.7 19.9 %collective-permute-start.40 = (bf16[512,768]{1,0:T(8,128)(2,1)S(1)}, bf16[512,768]{1,0:T(8,128)(2,1)S(1)}, u32[]{:S(2)}, u32[]{:S(2)}) collective-permute-start(bf16[512,768]{1,0:T(8,128)(2,1)S(1)} %copy-done.25), channel_id=1, source_target_pairs={{0,4},{1,5},{2,6},{3,7},{4,0},{5,1},{6,2},{7,3},{8,12},{9,13},{10,... | collective-permute-start | bytes 2359304 | tf_op jit(solution)/shard_map/ppermute | solution.py:38
  158.1 28.3 %collective-permute-start.46 = (bf16[2,384,512]{2,1,0:T(8,128)(2,1)S(1)}, bf16[2,384,512]{2,1,0:T(8,128)(2,1)S(1)}, u32[]{:S(2)}, u32[]{:S(2)}) collective-permute-start(bf16[2,384,512]{2,1,0:T(8,128)(2,1)S(1)} %collective-permute-done.37.refs_15_), channel_id=1, source_target_pairs={{0,8},{1,9},{2,10},{3,11},{4,12},{5,13},{6,14},{7,15},{8,0},{9,1},... | collective-permute-start | bytes 2359304 | tf_op jit(solution)/shard_map/ppermute | solution.py:38
  177.2 23.9 %collective-permute-start.41 = (bf16[512,768]{1,0:T(8,128)(2,1)S(1)}, bf16[512,768]{1,0:T(8,128)(2,1)S(1)}, u32[]{:S(2)}, u32[]{:S(2)}) collective-permute-start(bf16[512,768]{1,0:T(8,128)(2,1)S(1)} %collective-permute-done.40.refs_1_), channel_id=1, source_target_pairs={{0,3},{1,0},{2,1},{3,2},{4,7},{5,4},{6,5},{7,6},{8,11},{9,8},{10,9... | collective-permute-start | bytes 2359304 | tf_op jit(solution)/shard_map/ppermute | solution.py:38
  178.5 22.6 %collective-permute-start.42 = (bf16[512,768]{1,0:T(8,128)(2,1)S(1)}, bf16[512,768]{1,0:T(8,128)(2,1)S(1)}, u32[]{:S(2)}, u32[]{:S(2)}) collective-permute-start(bf16[512,768]{1,0:T(8,128)(2,1)S(1)} %collective-permute-done.40.refs_1_), channel_id=1, source_target_pairs={{0,1},{1,2},{2,3},{3,0},{4,5},{5,6},{6,7},{7,4},{8,9},{9,10},{10,1... | collective-permute-start | bytes 2359304 | tf_op jit(solution)/shard_map/ppermute | solution.py:38
  180.0 4.1 %collective-permute-start.45 = (f32[8,512]{1,0:T(8,128)S(1)}, f32[8,512]{1,0:T(8,128)S(1)}, u32[]{:S(2)}, u32[]{:S(2)}) collective-permute-start(f32[8,512]{1,0:T(8,128)S(1)} %add_sums.1), channel_id=1, source_target_pairs={{0,4},{1,5},{2,6},{3,7},{4,0},{5,1},{6,2},{7,3},{8,12},{9,13},{10,... | collective-permute-start | bytes 49160 | tf_op jit(solution)/shard_map/ppermute | solution.py:38
  183.4 12.1 %collective-permute-start.44 = (bf16[256,768]{1,0:T(8,128)(2,1)S(1)}, bf16[256,768]{1,0:T(8,128)(2,1)S(1)}, u32[]{:S(2)}, u32[]{:S(2)}) collective-permute-start(bf16[256,768]{1,0:T(8,128)(2,1)S(1)} %slice.93), channel_id=1, source_target_pairs={{0,4},{1,5},{2,6},{3,7},{4,0},{5,1},{6,2},{7,3},{8,12},{9,13},{10,... | collective-permute-start | bytes 1179656 | tf_op jit(solution)/shard_map/ppermute | solution.py:38
  184.1 17.0 %collective-permute-start.43 = (bf16[256,768]{1,0:T(8,128)(2,1)S(1)}, bf16[256,768]{1,0:T(8,128)(2,1)S(1)}, u32[]{:S(2)}, u32[]{:S(2)}) collective-permute-start(bf16[256,768]{1,0:T(8,128)(2,1)S(1)} %slice.92), channel_id=1, source_target_pairs={{0,4},{1,5},{2,6},{3,7},{4,0},{5,1},{6,2},{7,3},{8,12},{9,13},{10,... | collective-permute-start | bytes 1179656 | tf_op jit(solution)/shard_map/ppermute | solution.py:38
  (35 other events, 237.3 us)
